TPU v7x, 32 devices: a whole 2x2x4 slice. The times are simulated.
32 devices in a mesh: sec: 2 (over core), dev: 16 (over z, y, x).
Axes of the slice: x: 2, y: 2, z: 4, core: 2. Of those that a mesh axis runs over, the one named last changes fastest.
Arguments:
- queries: bfloat16 [256, 8192], P('dev', 'sec'), may hold values from -160 to 160
- key_cache: bfloat16 [256, 768, 512], P('dev', None, 'sec'), may hold values from -5 to 5
- value_cache: bfloat16 [256, 768, 512], P('dev', None, 'sec'), may hold values from -6 to 6
- new_key: bfloat16 [256, 512], P('dev', 'sec'), may hold values from -4 to 4
- new_value: bfloat16 [256, 512], P('dev', 'sec'), may hold values from -6 to 6
- cache_lengths: int32 [256], P('dev'), may hold values from 1 to 768, 98304 in all
- residual_in: bfloat16 [256, 4096], P('dev'), may hold values from -14 to 14
- out_weight: bfloat16 [8192, 4096], P('sec', 'dev'), may hold values from -0.5 to 0.5
- norm_gain: float32 [4096], replicated, may hold values from 0.1 to 1.9
- router_weight: bfloat16 [4096, 16], replicated, may hold values from -8 to 8
- expert_ids: int32 [256, 8], P('dev'), may hold values from 0 to 15, all different within a row; in each aligned block of 16 rows (0 to 15, 16 to 31, ...) at most 16 rows name the same one
- gate_weight: bfloat16 [16, 4096, 768], P('dev', None, 'sec'), may hold values from -0.09375 to 0.09375
- up_weight: bfloat16 [16, 4096, 768], P('dev', None, 'sec'), may hold values from -0.09375 to 0.09375
- down_weight: bfloat16 [16, 768, 4096], P('dev', 'sec'), may hold values from -0.625 to 0.625
Outputs:
- layer_out: bfloat16 [256, 4096], P('dev')
Inputs may be any that keep to these rules, and one draw needn't show every extreme that they name: `cache_lengths`: the longest row has exactly 768 filled slots. `expert_ids`: in each aligned block of 16 rows (the rows of one chip) no expert is named by more than 16 rows, a bound that some block reaches.
All inputs are finite; a program needn't handle non-finite values. No bound on the sum of `cache_lengths` on one device may be relied on, other than what follows from the above.
Results may differ from a plain program's by a relative error of at most 0.012.
Values may be sent and summed in bfloat16 or wider, within the bound.
No kernel may reach another device: no remote copies, remote signals or barrier semaphores. Data moves between devices by JAX's collectives and lax.ppermute only.
A program may use at most 128 MiB of HBM per device.

v0:
```python
import math

import jax
import jax.numpy as jnp
from jax import lax
from jax.sharding import PartitionSpec as P

HEAD = 128


masked_score = -1e30


def local(
    queries,
    key_cache,
    value_cache,
    new_key,
    new_value,
    cache_lengths,
    residual_in,
    out_weight,
    norm_gain,
    router_weight,
    expert_ids,
    gate_weight,
    up_weight,
    down_weight,
):
    row_count = queries.shape[0]
    group_count = new_key.shape[1] // HEAD
    per_group = queries.shape[1] // (group_count * HEAD)
    cache_span = key_cache.shape[1]
    score_scale = 1.0 / math.sqrt(HEAD)
    query_heads = queries.reshape(row_count, group_count, per_group, HEAD)
    fresh_keys = new_key.reshape(row_count, group_count, HEAD)
    fresh_values = new_value.reshape(row_count, group_count, HEAD)
    fresh_score = (
        jnp.einsum("rgqh,rgh->rgq", query_heads, fresh_keys, preferred_element_type=jnp.float32)
        * score_scale
    )
    keys_whole = key_cache.reshape(row_count, cache_span, group_count, HEAD)
    scores = (
        jnp.einsum("rgqh,rcgh->rgqc", query_heads, keys_whole, preferred_element_type=jnp.float32)
        * score_scale
    )
    positions = jnp.arange(cache_span, dtype=jnp.int32)
    live_mask = positions[None, :] < cache_lengths[:, None]
    scores = jnp.where(live_mask[:, None, None, :], scores, masked_score)
    row_max = jnp.maximum(jnp.max(scores, axis=-1), fresh_score)
    exp_cache = jnp.exp(scores - row_max[..., None])
    denominator = jnp.sum(exp_cache, axis=-1) + jnp.exp(fresh_score - row_max)
    weights_bf = (exp_cache / denominator[..., None]).astype(jnp.bfloat16)
    values_whole = value_cache.reshape(row_count, cache_span, group_count, HEAD)
    attended = jnp.einsum(
        "rgqc,rcgh->rgqh", weights_bf, values_whole, preferred_element_type=jnp.float32
    )
    fresh_weight = (jnp.exp(fresh_score - row_max) / denominator).astype(jnp.bfloat16)
    attended = (
        attended
        + fresh_weight.astype(jnp.float32)[..., None]
        * fresh_values.astype(jnp.float32)[:, :, None, :]
    )
    attended = attended.reshape(row_count, group_count * per_group * HEAD).astype(jnp.bfloat16)
    partial_value = jnp.dot(
        lax.all_gather(attended, "dev", axis=0, tiled=True),
        out_weight,
        preferred_element_type=jnp.float32,
    )
    summed = lax.psum(partial_value, "sec")
    projected = lax.all_to_all(
        summed.astype(jnp.bfloat16), "dev", split_axis=0, concat_axis=1, tiled=True
    )
    mixed = (residual_in.astype(jnp.float32) + projected.astype(jnp.float32)).astype(jnp.bfloat16)
    mixed_f = mixed.astype(jnp.float32)
    mean_square = jnp.mean(mixed_f * mixed_f, axis=-1, keepdims=True)
    normed = (mixed_f * lax.rsqrt(mean_square + 1e-06) * norm_gain).astype(jnp.bfloat16)
    model_width = normed.shape[1]
    expert_total = router_weight.shape[1]
    topk_count = expert_ids.shape[1]
    capacity = max(2, 2 * row_count * topk_count // lax.axis_size("dev"))
    logits = jnp.dot(normed, router_weight, preferred_element_type=jnp.float32)
    pair_total = row_count * topk_count
    flat_ids = expert_ids.reshape(pair_total)
    expert_hot = (flat_ids[:, None] == jnp.arange(expert_total, dtype=jnp.int32)[None, :]).astype(
        jnp.int32
    )
    chosen = jnp.sum(
        expert_hot.astype(jnp.float32).reshape(row_count, topk_count, expert_total)
        * logits[:, None, :],
        axis=-1,
    )
    route_weights = jax.nn.softmax(chosen, axis=-1)
    rank = jnp.sum((jnp.cumsum(expert_hot, axis=0) - expert_hot) * expert_hot, axis=1)
    destination = flat_ids * capacity + rank
    dest_hot = (
        destination[:, None] == jnp.arange(expert_total * capacity, dtype=jnp.int32)[None, :]
    ).astype(jnp.float32)
    row_hot = (
        (jnp.arange(pair_total, dtype=jnp.int32) // topk_count)[:, None]
        == jnp.arange(row_count, dtype=jnp.int32)[None, :]
    ).astype(jnp.float32)
    placement = jnp.dot(dest_hot.T, row_hot, precision=lax.Precision.HIGHEST).astype(jnp.bfloat16)
    weighted_rows = row_hot * route_weights.reshape(pair_total)[:, None]
    combine_map = jnp.dot(weighted_rows.T, dest_hot, precision=lax.Precision.HIGHEST)
    half_width = model_width // 2
    normed_part = lax.dynamic_slice_in_dim(
        normed, lax.axis_index("sec") * half_width, half_width, 1
    )
    outgoing = jnp.dot(placement, normed_part, preferred_element_type=jnp.float32).astype(
        jnp.bfloat16
    )
    outgoing = outgoing.reshape(expert_total, capacity, half_width)
    completed = lax.all_gather(
        lax.all_to_all(outgoing, "dev", split_axis=0, concat_axis=0, tiled=True),
        "sec",
        axis=2,
        tiled=True,
    )
    source_count = completed.shape[0]
    item_count = completed.shape[1]
    flat_rows = completed.reshape(source_count * item_count, model_width)
    gate_act = jnp.dot(flat_rows, gate_weight[0], preferred_element_type=jnp.float32)
    up_act = jnp.dot(flat_rows, up_weight[0], preferred_element_type=jnp.float32)
    hidden = (jax.nn.silu(gate_act) * up_act).astype(jnp.bfloat16)
    result = jnp.dot(hidden, down_weight[0], preferred_element_type=jnp.float32).astype(
        jnp.bfloat16
    )
    result = result.reshape(source_count, item_count, model_width)
    returned = lax.all_to_all(result, "dev", split_axis=0, concat_axis=0, tiled=True)
    combined = jnp.dot(
        combine_map,
        returned.reshape(expert_total * capacity, model_width).astype(jnp.float32),
        precision=lax.Precision.HIGHEST,
    )
    expert_sum = lax.psum(combined.astype(jnp.bfloat16), "sec").astype(jnp.float32)
    return (mixed_f + expert_sum).astype(jnp.bfloat16)


def solution(mesh):
    placed = (
        P("dev", "sec"),
        P("dev", None, "sec"),
        P("dev", None, "sec"),
        P("dev", "sec"),
        P("dev", "sec"),
        P("dev"),
        P("dev", None),
        P("sec", "dev"),
        P(),
        P(),
        P("dev", None),
        P("dev", None, "sec"),
        P("dev", None, "sec"),
        P("dev", "sec", None),
    )
    return jax.shard_map(
        local, mesh=mesh, in_specs=placed, out_specs=P("dev", None), check_vma=False
    )
```

profile of v0, /device:TPU:0, one launch (start us, length us, event | category | flops | bytes accessed | tf_op | source)
XLA Modules:
  0.0 235.9 jit_solution(18083482707833663183)
XLA Ops:
  6.5 0.0 copy-start
  6.5 0.0 all-gather.3.cloned.1.call-start
  6.5 0.9 iota_compare_fusion.8
  7.4 0.8 reshape.141
  8.2 0.7 reshape.136
  8.9 0.9 copy.35
  9.8 0.2 fusion.58
  10.0 0.0 copy-start.8
  10.0 4.8 %fusion.57 = (f32[16,2,16]{2,1,0:T(2,128)S(1)}, f32[16,2,16,768]{3,2,1,0:T(8,128)S(1)}) fusion(bf16[16,2,16,128]{3,2,1,0:T(8,128)(2,1)S(1)} %bitcast.72, pred[16,768]{1,0:T(8,128)(4,1)S(1)} %iota_compare_fusion.8, bf16[16,768,256]{2,1,0:T(8,128)(2,1)} %param.15), kind=kOutput, calls=%fused_computation.75 | convolution fusion | flops 101842432 | bytes 8009728 | tf_op jit(solution)/shard_map/rgqh,rcgh->rgqc/dot_general | solution.py:44
  14.8 0.5 fusion.13
  15.3 0.0 copy-done.8
  15.4 0.0 copy-start.3
  15.4 1.1 fusion.23
  16.5 0.7 copy.54
  17.2 0.0 all-gather.3.cloned.1.call-update
  17.2 0.0 copy-done.3
  17.2 0.1 copy.28
  17.3 0.1 reshape.131
  17.4 0.1 fusion.44
  17.5 0.2 reduce_window_sum.11
  17.7 0.2 select_reduce_fusion
  17.8 0.0 copy-start.1
  17.8 62.9 %all-gather.3.cloned.1.call-done = bf16[256,4096]{1,0:T(8,128)(2,1)} async-done(((bf16[16,4096]{1,0:T(8,128)(2,1)}), bf16[256,4096]{1,0:T(8,128)(2,1)}) %all-gather.3.cloned.1.call-update) | async-done | bytes 2097168 | tf_op jit(solution)/shard_map/all_gather | solution.py:66
  80.8 2.9 %fusion.59 = f32[256,256]{1,0:T(8,128)S(1)} fusion(bf16[256,4096]{1,0:T(8,128)(2,1)} %all-gather.3.cloned.1.call-done, bf16[4096,256]{1,0:T(8,128)(2,1)} %param.21), kind=kOutput, calls=%fused_computation.77 | convolution fusion | flops 536870912 | bytes 4456448 | tf_op jit(solution)/shard_map/dot_general | solution.py:65
  83.7 4.7 %all-reduce.4 = bf16[256,256]{1,0:T(8,128)(2,1)} all-reduce(f32[256,256]{1,0:T(8,128)S(1)} %fusion.59), channel_id=1, replica_groups=mesh['sec'=2,'dev'=16] {'sec'}, use_global_device_ids=true, to_apply=%region_2.3 | all-reduce | flops 65536 | bytes 393216 | tf_op jit(solution)/shard_map/psum | solution.py:70
  88.4 4.3 %all-to-all-start = ((bf16[16,16,256]{2,1,0:T(8,128)(2,1)}), bf16[16,16,256]{2,1,0:T(8,128)(2,1)S(1)}, u32[]{:S(2)}, u32[]{:S(2)}) async-start(bf16[16,16,256]{2,1,0:T(8,128)(2,1)} %bitcast.2), calls=%async_computation | async-start | bytes 262144 | tf_op jit(solution)/shard_map/all_to_all | solution.py:71
  92.7 0.0 all-gather.5.cloned.1.call-start
  92.7 0.0 copy-start.4
  92.7 0.0 copy-start.6
  92.8 0.2 convolution_convert_fusion.3
  93.0 7.6 %all-to-all-done = bf16[16,16,256]{2,1,0:T(8,128)(2,1)S(1)} async-done(((bf16[16,16,256]{2,1,0:T(8,128)(2,1)}), bf16[16,16,256]{2,1,0:T(8,128)(2,1)S(1)}, u32[]{:S(2)}, u32[]{:S(2)}) %all-to-all-start) | async-done | bytes 131104 | tf_op jit(solution)/shard_map/all_to_all | solution.py:71
  100.7 0.0 copy-done.4
  100.7 0.0 copy-done.1
  100.7 0.2 fusion.35
  100.9 0.0 copy-done.6
  100.9 0.8 fusion.37
  101.7 0.5 convolution_convert_fusion.2
  102.2 29.3 %all_to_all.23 = bf16[16,16,2048]{2,1,0:T(8,128)(2,1)} all-to-all(bf16[16,16,2048]{2,1,0:T(8,128)(2,1)S(1)} %bitcast.68), channel_id=1, replica_groups=mesh['sec'=2,'dev'=16] {'dev'}, dimensions={0} | all-to-all | bytes 2097152 | tf_op jit(solution)/shard_map/all_to_all | solution.py:115
  131.4 0.0 all-gather.5.cloned.1.call-update
  131.5 9.0 %all-gather.5.cloned.1.call-done = bf16[16,16,4096]{2,1,0:T(8,128)(2,1)} async-done(((bf16[16,16,2048]{2,1,0:T(8,128)(2,1)}), bf16[16,16,4096]{2,1,0:T(8,128)(2,1)}) %all-gather.5.cloned.1.call-update) | async-done | bytes 2097168 | tf_op jit(solution)/shard_map/all_gather | solution.py:114
  140.5 4.5 %fusion.9 = f32[256,384]{1,0:T(8,128)} fusion(bf16[256,4096]{1,0:T(8,128)(2,1)} %bitcast.78, bf16[1,4096,384]{2,1,0:T(8,128)(2,1)} %param.25), kind=kOutput, calls=%fused_computation.11 | convolution fusion | flops 805306368 | bytes 5636096 | tf_op jit(solution)/shard_map/dot_general | solution.py:123
  145.0 0.0 copy-done
  145.0 6.4 %convolution_convert_fusion = bf16[256,4096]{1,0:T(8,128)(2,1)} fusion(bf16[1,384,4096]{2,1,0:T(8,128)(2,1)S(1)} %copy-done, bf16[256,4096]{1,0:T(8,128)(2,1)} %bitcast.79, bf16[1,4096,384]{2,1,0:T(8,128)(2,1)} %param.26, f32[256,384]{1,0:T(8,128)} %fusion.9), kind=kOutput, calls=%fused_computation.6 | convolution fusion | flops 1612251136 | bytes 10878976 | tf_op jit(solution)/shard_map/dot_general | solution.py:126
  151.4 0.0 copy-start.2
  151.4 0.0 copy-start.5
  151.4 0.0 copy-start.7
  151.4 7.0 %all-to-all-start.2 = ((bf16[16,16,4096]{2,1,0:T(8,128)(2,1)}), bf16[16,16,4096]{2,1,0:T(8,128)(2,1)}, u32[]{:S(2)}, u32[]{:S(2)}) async-start(bf16[16,16,4096]{2,1,0:T(8,128)(2,1)} %bitcast.69), calls=%async_computation.2 | async-start | bytes 4194304 | tf_op jit(solution)/shard_map/all_to_all | solution.py:130
  158.4 0.0 all-reduce.3.cloned.1.call-start
  158.4 0.0 copy-done.2
  158.4 0.2 fusion.60
  158.6 0.2 multiply_reduce_fusion
  158.8 0.1 reduce_max.19
  158.9 0.2 fusion.52
  159.1 0.1 fusion.51
  159.1 0.1 div.51
  159.2 0.0 copy-done.5
  159.3 0.0 copy-done.7
  159.3 0.3 fusion.40
  159.5 42.1 %all-to-all-done.2 = bf16[16,16,4096]{2,1,0:T(8,128)(2,1)} async-done(((bf16[16,16,4096]{2,1,0:T(8,128)(2,1)}), bf16[16,16,4096]{2,1,0:T(8,128)(2,1)}, u32[]{:S(2)}, u32[]{:S(2)}) %all-to-all-start.2) | async-done | bytes 2097184 | tf_op jit(solution)/shard_map/all_to_all | solution.py:130
  201.6 3.2 %convolution_convert_fusion.1 = bf16[16,4096]{1,0:T(8,128)(2,1)} fusion(f32[16,256]{1,0:T(8,128)S(1)} %fusion.40, bf16[256,4096]{1,0:T(8,128)(2,1)} %bitcast.10), kind=kOutput, calls=%fused_computation.7 | convolution fusion | flops 201392128 | bytes 2244608 | tf_op jit(solution)/shard_map/dot_general | solution.py:131
  204.8 0.0 all-reduce.3.cloned.1.call-update
  204.8 22.9 %all-reduce.3.cloned.1.call-done = bf16[16,4096]{1,0:T(8,128)(2,1)} async-done(((bf16[16,4096]{1,0:T(8,128)(2,1)}), bf16[16,4096]{1,0:T(8,128)(2,1)}) %all-reduce.3.cloned.1.call-update) | async-done | bytes 131088 | tf_op jit(solution)/shard_map/psum | solution.py:136
  227.8 1.6 fusion.38
  (6 shorter events, 0.1 us)
Async XLA Ops:
  6.5 138.5 %copy-start = (bf16[1,384,4096]{2,1,0:T(8,128)(2,1)S(1)}, bf16[1,384,4096]{2,1,0:T(8,128)(2,1)}, u32[]{:S(2)}) copy-start(bf16[1,384,4096]{2,1,0:T(8,128)(2,1)} %param.27) | copy-start | bytes 9437188
  6.5 74.2 %all-gather.3.cloned.1.call-start = ((), (), s32[]{:S(2)}) async-start(), calls=%async_computation.3 | async-start | bytes 2228224 | tf_op jit(solution)/shard_map/all_gather | solution.py:66
  10.0 5.3 %copy-start.8 = (bf16[16,768,256]{2,1,0:T(8,128)(2,1)S(1)}, bf16[16,768,256]{2,1,0:T(8,128)(2,1)}, u32[]{:S(2)}) copy-start(bf16[16,768,256]{2,1,0:T(8,128)(2,1)} %param.16) | copy-start | bytes 18874372
  15.4 1.9 copy-start.3
  17.8 82.8 %copy-start.1 = (bf16[16,4096]{1,0:T(8,128)(2,1)S(1)}, bf16[16,4096]{1,0:T(8,128)(2,1)}, u32[]{:S(2)}) copy-start(bf16[16,4096]{1,0:T(8,128)(2,1)} %param.20) | copy-start | bytes 393220
  88.4 12.2 %all-to-all-start = ((bf16[16,16,256]{2,1,0:T(8,128)(2,1)}), bf16[16,16,256]{2,1,0:T(8,128)(2,1)S(1)}, u32[]{:S(2)}, u32[]{:S(2)}) async-start(bf16[16,16,256]{2,1,0:T(8,128)(2,1)} %bitcast.2), calls=%async_computation | async-start | bytes 262144 | tf_op jit(solution)/shard_map/all_to_all | solution.py:71
  92.7 47.8 %all-gather.5.cloned.1.call-start = ((), (), s32[]{:S(2)}) async-start(), calls=%async_computation.4 | async-start | bytes 3145728 | tf_op jit(solution)/shard_map/all_gather | solution.py:114
  92.7 7.9 %copy-start.4 = (s32[128]{0:T(128)}, s32[128]{0:T(128)S(1)}, u32[]{:S(2)}) copy-start(s32[128]{0:T(128)S(1)} %get-tuple-element.11) | copy-start | bytes 1540
  92.7 8.1 %copy-start.6 = (s32[128]{0:T(128)}, s32[128]{0:T(128)S(1)}, u32[]{:S(2)}) copy-start(s32[128]{0:T(128)S(1)} %get-tuple-element.12) | copy-start | bytes 1540
  151.4 7.0 %copy-start.2 = (bf16[4096,16]{0,1:T(8,128)(2,1)S(1)}, bf16[4096,16]{0,1:T(8,128)(2,1)}, u32[]{:S(2)}) copy-start(bf16[4096,16]{0,1:T(8,128)(2,1)} %param.23) | copy-start | bytes 393220
  151.4 7.9 %copy-start.5 = (s32[128]{0:T(128)S(1)}, s32[128]{0:T(128)}, u32[]{:S(2)}) copy-start(s32[128]{0:T(128)} %copy-done.4) | copy-start | bytes 1540
  151.4 7.9 %copy-start.7 = (s32[128]{0:T(128)S(1)}, s32[128]{0:T(128)}, u32[]{:S(2)}) copy-start(s32[128]{0:T(128)} %copy-done.6) | copy-start | bytes 1540
  151.4 50.2 %all-to-all-start.2 = ((bf16[16,16,4096]{2,1,0:T(8,128)(2,1)}), bf16[16,16,4096]{2,1,0:T(8,128)(2,1)}, u32[]{:S(2)}, u32[]{:S(2)}) async-start(bf16[16,16,4096]{2,1,0:T(8,128)(2,1)} %bitcast.69), calls=%async_computation.2 | async-start | bytes 4194304 | tf_op jit(solution)/shard_map/all_to_all | solution.py:130
  158.4 69.4 %all-reduce.3.cloned.1.call-start = ((), (), s32[]{:S(2)}) async-start(), calls=%async_computation.5 | async-start | bytes 262144 | tf_op jit(solution)/shard_map/psum | solution.py:136
Sparse Core Ops, SparseCore 0:
  17.3 63.3 all-gather.2
  131.6 8.8 all-gather.4
  205.0 22.7 all-reduce.2
where the time goes:
time: 236 us
  waiting for transfers between devices  145 us (61%)
  blocking collectives  34 us (14%)
  matrix products  24.2 us (10%)
  between operations  13.3 us (6%)
  starting transfers between devices  11.3 us (5%)
  other arithmetic  5.03 us (2%)
  local copies, waits for them, and re-layouts  3.45 us (1%)
    all_gather x1, waiting for transfers between devices, local(): lax.all_gather(attended, 'dev', axis=0, tiled=True)  62.9 us
    all_to_all x1, waiting for transfers between devices, local(): lax.all_to_all(result, 'dev', split_axis=0, concat_axis=0, tiled=True)  42.1 us
    all_to_all x1, blocking collectives, local(): lax.all_to_all(outgoing, 'dev', split_axis=0, concat_axis=0, tiled=True)  29.3 us
    psum x1, waiting for transfers between devices, local(): lax.psum(combined.astype(jnp.bfloat16), 'sec').astype(jnp.float32)  22.9 us
    all_gather x1, waiting for transfers between devices, local(): lax.all_gather(lax.all_to_all(outgoing, 'dev', split_axis=0, concat_axis=...  9.01 us
    all_to_all x1, waiting for transfers between devices, local(): lax.all_to_all(summed.astype(jnp.bfloat16), 'dev', split_axis=0, concat_a...  7.61 us
    all_to_all x1, starting transfers between devices, local(): lax.all_to_all(result, 'dev', split_axis=0, concat_axis=0, tiled=True)  6.97 us
    dot_general x1, matrix products, local(): jnp.dot(hidden, down_weight[0], preferred_element_type=jnp.float32)  6.37 us
  transfers between devices with their start and end apart: 5, of which 5 were waited for; matrix products, arithmetic and copies ran while one was open for 1% of the time, Pallas kernels for 0%

commit v1 on v0

v1 whole, which is shorter than its diff:
```python
import functools
import math

import jax
import jax.numpy as jnp
from jax import lax
from jax.experimental import pallas as pl
from jax.experimental.pallas import tpu as pltpu
from jax.sharding import PartitionSpec as P

HEAD = 128
masked_score = -1e30
BF = jnp.bfloat16
F32 = jnp.float32


def grid_of(n):
    known = {16: (4, 2, 2), 64: (4, 4, 4)}
    return known.get(n, (n, 1, 1))


def strides_of(dims):
    return {"z": dims[1] * dims[2], "y": dims[2], "x": 1}


def rotate(value, dims, axis, step):
    nz, ny, nx = dims
    pairs = []
    for z in range(nz):
        for y in range(ny):
            for x in range(nx):
                src = (z * ny + y) * nx + x
                tz, ty, tx = z, y, x
                if axis == "z":
                    tz = (z + step) % nz
                elif axis == "y":
                    ty = (y + step) % ny
                else:
                    tx = (x + step) % nx
                pairs.append((src, (tz * ny + ty) * nx + tx))
    return lax.ppermute(value, "dev", pairs)


def swap_sec(value):
    return lax.ppermute(value, "sec", [(0, 1), (1, 0)])


def spread(block, dims, first, second):
    extent = dict(zip("zyx", dims))
    stacked = jnp.concatenate(
        [block] + [rotate(block, dims, "z", k) for k in range(1, extent["z"])], axis=0
    )
    found = {}
    for a in range(extent[first]):
        near = stacked if a == 0 else rotate(stacked, dims, first, a)
        for b in range(extent[second]):
            far = near if b == 0 else rotate(near, dims, second, b)
            found[(a, b) if first == "y" else (b, a)] = far
    return found


def position(dims):
    nz, ny, nx = dims
    d = lax.axis_index("dev")
    return d // (ny * nx), (d // nx) % ny, d % nx


def back(dims, pos, kz, ky, kx):
    nz, ny, nx = dims
    z, y, x = pos
    return (
        (lax.rem(z - kz + nz, nz) * ny + lax.rem(y - ky + ny, ny)) * nx + lax.rem(x - kx + nx, nx)
    )


def ahead(dims, pos, kz, ky, kx):
    nz, ny, nx = dims
    z, y, x = pos
    return (lax.rem(z + kz, nz) * ny + lax.rem(y + ky, ny)) * nx + lax.rem(x + kx, nx)


ANY = pl.BlockSpec(memory_space=pl.ANY)
VM = pl.BlockSpec(memory_space=pltpu.VMEM)


def project_kernel(dims, keys, rows, *refs):
    nz, ny, nx = dims
    count = len(keys)
    a_refs, b_refs = refs[:count], refs[count : 2 * count]
    w_ref, keep_ref, send_ref, held, weight, sems, wsem = refs[2 * count :]
    depth = held.shape[1]
    half = depth // 2
    pos = position(dims)
    sec = lax.axis_index("sec")
    wcopy = pltpu.make_async_copy(w_ref, weight, wsem)
    wcopy.start()
    copies = []
    for i, (ky, kx) in enumerate(keys):
        for kz in range(nz):
            place = pl.multiple_of(back(dims, pos, kz, ky, kx) * rows, rows)
            for h, group in enumerate((a_refs, b_refs)):
                copies.append(
                    pltpu.make_async_copy(
                        group[i].at[pl.ds(kz * rows, rows)],
                        held.at[pl.ds(place, rows), pl.ds(h * half, half)],
                        sems.at[(i * nz + kz) * 2 + h],
                    )
                )
    for c in copies:
        c.start()
    wcopy.wait()
    for c in copies:
        c.wait()
    total = jnp.dot(held[...], weight[...], preferred_element_type=F32)
    part = total.shape[1] // 2
    low, high = total[:, :part], total[:, part:]
    keep_ref[...] = jnp.where(sec == 0, low, high)
    send_ref[...] = jnp.where(sec == 0, high, low)


def project(a, b, weight, dims, rows):
    keys = sorted(a)
    n = dims[0] * dims[1] * dims[2]
    depth, cols = weight.shape
    out = jax.ShapeDtypeStruct((n * rows, cols // 2), F32)
    return pl.pallas_call(
        functools.partial(project_kernel, dims, keys, rows),
        out_shape=(out, out),
        in_specs=[ANY] * (2 * len(keys) + 1),
        out_specs=(VM, VM),
        scratch_shapes=[
            pltpu.VMEM((n * rows, depth), BF),
            pltpu.VMEM((depth, cols), BF),
            pltpu.SemaphoreType.DMA((2 * n,)),
            pltpu.SemaphoreType.DMA,
        ],
        compiler_params=pltpu.CompilerParams(vmem_limit_bytes=48 * 1024 * 1024),
        cost_estimate=pl.CostEstimate(
            flops=2 * n * rows * depth * cols,
            bytes_accessed=2 * depth * (cols + n * rows),
            transcendentals=0,
        ),
        name="project",
    )(*[a[k] for k in keys], *[b[k] for k in keys], weight)


STEPS = 8


def expert_kernel(dims, keys, rows, eps, *refs):
    nz, ny, nx = dims
    n = nz * ny * nx
    count = len(keys)
    groups = [refs[i * count : (i + 1) * count] for i in range(4)]
    (
        mask_ref,
        gain_ref,
        router_ref,
        gate_ref,
        up_ref,
        down_ref,
        keep_refs,
        send_refs,
        own_ref,
        held,
        gate_w,
        up_w,
        down_w,
        gate_acc,
        up_acc,
        route_acc,
        square,
        hidden,
        hidden_a,
        hidden_b,
        xsems,
        gsems,
        dsems,
    ) = (
        refs[4 * count],
        refs[4 * count + 1],
        refs[4 * count + 2],
        refs[4 * count + 3],
        refs[4 * count + 4],
        refs[4 * count + 5],
        refs[4 * count + 6 : 4 * count + 8],
        refs[4 * count + 8 : 4 * count + 10],
        *refs[4 * count + 10 :],
    )
    total_rows, width = held.shape
    half_rows = total_rows // 2
    part = width // n // 2
    pos = position(dims)
    me = lax.axis_index("dev")
    sec = lax.axis_index("sec")
    step = width // STEPS
    weight_copies = []
    for c in range(STEPS):
        span = pl.ds(c * step, step)
        weight_copies.append(
            (
                pltpu.make_async_copy(gate_ref.at[0, span], gate_w.at[span], gsems.at[c]),
                pltpu.make_async_copy(up_ref.at[0, span], up_w.at[span], gsems.at[STEPS + c]),
            )
        )
    copies = []
    if part % 128:
        copies.append(pltpu.make_async_copy(groups[0][0], held, xsems.at[0]))
    for i, (ky, kx) in enumerate(keys if part % 128 == 0 else ()):
        for kz in range(nz):
            owner = back(dims, pos, kz, ky, kx)
            for g in range(4):
                whose = sec if g < 2 else 1 - sec
                column = pl.multiple_of((owner * 2 + whose) * part, part)
                copies.append(
                    pltpu.make_async_copy(
                        groups[g][i].at[pl.ds(kz * half_rows, half_rows)],
                        held.at[pl.ds((g % 2) * half_rows, half_rows), pl.ds(column, part)],
                        xsems.at[(i * nz + kz) * 4 + g],
                    )
                )
    for c in copies:
        c.start()
    for pair in weight_copies:
        for c in pair:
            c.start()
    halves = []
    for h, whose in enumerate((sec, 1 - sec)):
        span = pl.ds(pl.multiple_of(whose * (width // 2), width // 2), width // 2)
        halves.append(pltpu.make_async_copy(down_ref.at[0, :, span], down_w.at[h], dsems.at[h]))
    for c in halves:
        c.start()
    for c in copies:
        c.wait()
    gate_acc[...] = jnp.zeros_like(gate_acc)
    up_acc[...] = jnp.zeros_like(up_acc)
    route_acc[...] = jnp.zeros_like(route_acc)
    square[...] = jnp.zeros_like(square)

    def body(c, carry):
        span = pl.ds(pl.multiple_of(c * step, step), step)
        x = held[:, span].astype(F32)
        square[...] += jnp.sum(x * x, axis=1, keepdims=True)
        scaled = (x * gain_ref[:, span]).astype(BF)
        pltpu.make_async_copy(gate_ref.at[0, span], gate_w.at[span], gsems.at[c]).wait()
        pltpu.make_async_copy(up_ref.at[0, span], up_w.at[span], gsems.at[STEPS + c]).wait()
        gate_acc[...] += jnp.dot(scaled, gate_w[span], preferred_element_type=F32)
        up_acc[...] += jnp.dot(scaled, up_w[span], preferred_element_type=F32)
        route_acc[...] += jnp.dot(scaled, router_ref[span], preferred_element_type=F32)
        return carry

    lax.fori_loop(0, STEPS, body, 0)
    inverse = lax.rsqrt(square[:, :1] * (1.0 / width) + eps)
    mask = mask_ref[...].astype(F32)
    live = mask > 0.5
    logits = jnp.where(live, route_acc[...] * inverse, masked_score)
    top = jnp.max(logits, axis=1, keepdims=True)
    powers = jnp.where(live, jnp.exp(logits - top), 0.0)
    lane = lax.broadcasted_iota(jnp.int32, powers.shape, 1)
    mine = jnp.sum(jnp.where(lane == me, powers, 0.0), axis=1, keepdims=True)
    weight = mine / jnp.sum(powers, axis=1, keepdims=True)
    gate = gate_acc[...] * inverse
    up = up_acc[...] * inverse
    hidden[...] = (gate / (1.0 + jnp.exp(-gate)) * up * weight).astype(BF)
    own_ref[...] = held[pl.ds(pl.multiple_of(me * rows, rows), rows)]
    for kz in range(nz):
        for ky in range(ny):
            for kx in range(nx):
                place = pl.multiple_of(ahead(dims, pos, kz, ky, kx) * rows, rows)
                block = hidden[pl.ds(place, rows)]
                hidden_a[pl.ds(((kx * ny + ky) * nz + kz) * rows, rows)] = block
                hidden_b[pl.ds(((ky * nx + kx) * nz + kz) * rows, rows)] = block
    quarter = width // 4
    for c in halves:
        c.wait()
    for h, outs in enumerate((keep_refs, send_refs)):
        for q, source in enumerate((hidden_a, hidden_b)):
            for t in range(2):
                wide = quarter // 2
                outs[q][:, t * wide : (t + 1) * wide] = jnp.dot(
                    source[...],
                    down_w[h, :, pl.ds(q * quarter + t * wide, wide)],
                    preferred_element_type=F32,
                ).astype(BF)


def in_order(own, other, dims):
    nz, ny, nx = dims
    pos = position(dims)
    sides = []
    for pair in (own, other):
        parts = []
        for found in pair:
            stacked = jnp.stack([jnp.stack([found[(b, a)] for a in range(nx)]) for b in range(ny)])
            half = stacked.shape[2] // nz
            stacked = stacked.reshape(ny, nx, nz, half, -1).transpose(2, 0, 1, 3, 4)
            for axis in range(3):
                order = (pos[axis] - jnp.arange(dims[axis], dtype=jnp.int32)) % dims[axis]
                stacked = jnp.take(stacked, order, axis=axis)
            parts.append(stacked.reshape(nz * ny * nx, half, -1))
        sides.append(jnp.concatenate(parts, axis=1))
    first = lax.axis_index("sec") == 0
    both = jnp.stack([jnp.where(first, sides[0], sides[1]), jnp.where(first, sides[1], sides[0])])
    return both.transpose(2, 1, 0, 3).reshape(both.shape[2], -1)


def experts(own, other, mask, gain, router, gate, up, down, dims, rows):
    keys = sorted(own[0])
    n = dims[0] * dims[1] * dims[2]
    total_rows = n * rows
    _, width, units = gate.shape
    quarter = width // 4
    lanes = router.shape[1]
    result = jax.ShapeDtypeStruct((total_rows, quarter), BF)
    arrays = [g[k] for g in (*own, *other) for k in keys]
    if (width // n // 2) % 128:
        arrays = [in_order(own, other, dims)] * len(arrays)
    outs = pl.pallas_call(
        functools.partial(expert_kernel, dims, keys, rows, 1e-6),
        out_shape=(result,) * 4 + (jax.ShapeDtypeStruct((rows, width), BF),),
        in_specs=[ANY] * len(arrays) + [VM, VM, VM, ANY, ANY, ANY],
        out_specs=(VM,) * 5,
        scratch_shapes=[
            pltpu.VMEM((total_rows, width), BF),
            pltpu.VMEM((width, units), BF),
            pltpu.VMEM((width, units), BF),
            pltpu.VMEM((2, units, width // 2), BF),
            pltpu.VMEM((total_rows, units), F32),
            pltpu.VMEM((total_rows, units), F32),
            pltpu.VMEM((total_rows, lanes), F32),
            pltpu.VMEM((total_rows, 128), F32),
            pltpu.VMEM((total_rows, units), BF),
            pltpu.VMEM((total_rows, units), BF),
            pltpu.VMEM((total_rows, units), BF),
            pltpu.SemaphoreType.DMA((4 * n,)),
            pltpu.SemaphoreType.DMA((2 * STEPS,)),
            pltpu.SemaphoreType.DMA((2,)),
        ],
        compiler_params=pltpu.CompilerParams(vmem_limit_bytes=56 * 1024 * 1024),
        cost_estimate=pl.CostEstimate(
            flops=6 * total_rows * width * units,
            bytes_accessed=6 * width * units + 6 * total_rows * width,
            transcendentals=0,
        ),
        name="experts",
    )(*arrays, mask, gain, router, gate, up, down)
    return outs[:2], outs[2:4], outs[4]


def attention(queries, key_cache, value_cache, new_key, new_value, cache_lengths):
    row_count = queries.shape[0]
    group_count = new_key.shape[1] // HEAD
    per_group = queries.shape[1] // (group_count * HEAD)
    cache_span = key_cache.shape[1]
    score_scale = 1.0 / math.sqrt(HEAD)
    query_heads = queries.reshape(row_count, group_count, per_group, HEAD)
    fresh_keys = new_key.reshape(row_count, group_count, HEAD)
    fresh_values = new_value.reshape(row_count, group_count, HEAD)
    fresh_score = (
        jnp.einsum("rgqh,rgh->rgq", query_heads, fresh_keys, preferred_element_type=F32)
        * score_scale
    )
    keys_whole = key_cache.reshape(row_count, cache_span, group_count, HEAD)
    scores = (
        jnp.einsum("rgqh,rcgh->rgqc", query_heads, keys_whole, preferred_element_type=F32)
        * score_scale
    )
    positions = jnp.arange(cache_span, dtype=jnp.int32)
    live_mask = positions[None, :] < cache_lengths[:, None]
    scores = jnp.where(live_mask[:, None, None, :], scores, masked_score)
    row_max = jnp.maximum(jnp.max(scores, axis=-1), fresh_score)
    exp_cache = jnp.exp(scores - row_max[..., None])
    denominator = jnp.sum(exp_cache, axis=-1) + jnp.exp(fresh_score - row_max)
    weights_bf = (exp_cache / denominator[..., None]).astype(BF)
    values_whole = value_cache.reshape(row_count, cache_span, group_count, HEAD)
    attended = jnp.einsum("rgqc,rcgh->rgqh", weights_bf, values_whole, preferred_element_type=F32)
    fresh_weight = (jnp.exp(fresh_score - row_max) / denominator).astype(BF)
    attended = (
        attended
        + fresh_weight.astype(F32)[..., None] * fresh_values.astype(F32)[:, :, None, :]
    )
    return attended.reshape(row_count, group_count * per_group * HEAD).astype(BF)


def local(
    dims,
    queries,
    key_cache,
    value_cache,
    new_key,
    new_value,
    cache_lengths,
    residual_in,
    out_weight,
    norm_gain,
    router_weight,
    expert_ids,
    gate_weight,
    up_weight,
    down_weight,
):
    nz, ny, nx = dims
    n = nz * ny * nx
    rows, width = residual_in.shape
    expert_total = router_weight.shape[1]
    sec = lax.axis_index("sec")
    lanes = -(-expert_total // 128) * 128
    part = width // n // 2
    chosen = jnp.any(
        expert_ids[:, :, None] == jnp.arange(lanes, dtype=jnp.int32)[None, None, :], axis=1
    ).astype(BF)
    mine = lax.dynamic_index_in_dim(
        residual_in.reshape(rows, n, 2, part), sec, axis=2, keepdims=False
    )
    outgoing = jnp.concatenate(
        [jnp.swapaxes(mine, 0, 1), jnp.broadcast_to(chosen[None], (n, rows, lanes))], axis=2
    )
    incoming = lax.all_to_all(outgoing, "dev", split_axis=0, concat_axis=0, tiled=True)
    residual = incoming[:, :, :part].reshape(n * rows, part)
    mask = incoming[:, :, part:].reshape(n * rows, lanes)

    attended = attention(queries, key_cache, value_cache, new_key, new_value, cache_lengths)
    middle = attended.shape[1] // 2
    a = spread(attended[:, :middle], dims, "x", "y")
    b = spread(attended[:, middle:], dims, "y", "x")
    keep, send = project(a, b, out_weight, dims, rows)
    projected = (keep + swap_sec(send)).astype(BF)
    mixed = (residual.astype(F32) + projected.astype(F32)).astype(BF)

    half_rows = n * rows // 2
    ma = spread(mixed[:half_rows], dims, "x", "y")
    mb = spread(mixed[half_rows:], dims, "y", "x")
    other_a = {k: swap_sec(v) for k, v in ma.items()}
    other_b = {k: swap_sec(v) for k, v in mb.items()}
    router = jnp.pad(router_weight, ((0, 0), (0, lanes - expert_total)))
    keeps, sends, own_mixed = experts(
        (ma, mb),
        (other_a, other_b),
        mask,
        norm_gain.reshape(1, width),
        router,
        gate_weight,
        up_weight,
        down_weight,
        dims,
        rows,
    )
    finals = []
    for q, (first, second) in enumerate((("x", "y"), ("y", "x"))):
        extent = dict(zip("zyx", dims))
        nf, ns = extent[first], extent[second]
        quarter = keeps[q].shape[1]
        summed = keeps[q].astype(F32) + swap_sec(sends[q]).astype(F32)
        summed = summed.reshape(nf, ns * nz * rows, quarter)
        total = summed[0]
        for k in range(1, nf):
            total = total + rotate(summed[k].astype(BF), dims, first, k).astype(F32)
        total = total.reshape(ns, nz * rows, quarter)
        inner = total[0]
        for k in range(1, ns):
            inner = inner + rotate(total[k].astype(BF), dims, second, k).astype(F32)
        inner = inner.reshape(nz, rows, quarter)
        last = inner[0]
        for k in range(1, nz):
            last = last + rotate(inner[k].astype(BF), dims, "z", k).astype(F32)
        finals.append(last)
    own_half = lax.dynamic_slice_in_dim(own_mixed, sec * (width // 2), width // 2, 1)
    done = (own_half.astype(F32) + jnp.concatenate(finals, axis=1)).astype(BF)
    other = swap_sec(done)
    return jnp.where(
        sec == 0, jnp.concatenate([done, other], axis=1), jnp.concatenate([other, done], axis=1)
    )


def solution(mesh):
    dims = grid_of(mesh.shape["dev"])
    placed = (
        P("dev", "sec"),
        P("dev", None, "sec"),
        P("dev", None, "sec"),
        P("dev", "sec"),
        P("dev", "sec"),
        P("dev"),
        P("dev", None),
        P("sec", "dev"),
        P(),
        P(),
        P("dev", None),
        P("dev", None, "sec"),
        P("dev", None, "sec"),
        P("dev", "sec", None),
    )
    return jax.shard_map(
        functools.partial(local, dims),
        mesh=mesh,
        in_specs=placed,
        out_specs=P("dev", None),
        check_vma=False,
    )
```

time: 236 us -> 124 us (0.53)
  waiting for transfers between devices: 145 us -> 28.7 us
  starting transfers between devices: 11.3 us -> 57.5 us
  blocking collectives: 34 us -> 0 us
  Pallas kernels: 0 us -> 16.8 us
  matrix products: 24.2 us -> 8.68 us
  between operations: 13.3 us -> 0.61 us
  local copies, waits for them, and re-layouts: 3.45 us -> 7.12 us
    all_gather x2 -> x0, waiting for transfers between devices: 71.9 us -> none  [the longest x1 62.9 us: local(): lax.all_gather(attended, 'dev', axis=0, tiled=True)]
    ppermute x0 -> x46, starting transfers between devices: none -> 52.1 us  [the longest x34 50.4 us: rotate(): return lax.ppermute(value, 'dev', pairs)]
    all_to_all x2 -> x1, waiting for transfers between devices: 49.7 us -> 1 us  [local(): lax.all_to_all(outgoing, 'dev', split_axis=0, concat_axis=0, tiled=True)]
    all_to_all x1 -> x0, blocking collectives: 29.3 us -> none  [local(): lax.all_to_all(outgoing, 'dev', split_axis=0, concat_axis=0, tiled=True)]
    ppermute x0 -> x46, waiting for transfers between devices: none -> 27.7 us  [the longest x34 24.8 us: rotate(): return lax.ppermute(value, 'dev', pairs)]
    psum x1 -> x0, waiting for transfers between devices: 22.9 us -> none  [local(): lax.psum(combined.astype(jnp.bfloat16), 'sec').astype(jnp.float32)]
    pallas_call x0 -> x2, Pallas kernels: none -> 16.8 us  [the longest x1 13 us: experts(): pl.pallas_call(functools.partial(expert_kernel, dims, keys, rows, 1e-06),...]
    dot_general x11 -> x3, matrix products: 24.2 us -> 8.68 us  [the longest x1 4.62 us: attention(): jnp.einsum('rgqh,rcgh->rgqc', query_heads, keys_whole, preferred_element_...]
  transfers between devices with their start and end apart: 5 -> 47, of which waited for: 5 -> 16; matrix products, arithmetic and copies ran while one was open for 1% -> 6% of each run, Pallas kernels for 0% -> 3%
where the time goes in v1:
time: 124 us
  starting transfers between devices  57.5 us (46%)
  waiting for transfers between devices  28.7 us (23%)
  Pallas kernels  16.8 us (14%)
  matrix products  8.68 us (7%)
  local copies, waits for them, and re-layouts  7.12 us (6%)
  other arithmetic  4.46 us (4%)
    ppermute x34, starting transfers between devices, rotate(): return lax.ppermute(value, 'dev', pairs)  50.4 us
    ppermute x34, waiting for transfers between devices, rotate(): return lax.ppermute(value, 'dev', pairs)  24.8 us
    pallas_call x1, Pallas kernels, experts(): pl.pallas_call(functools.partial(expert_kernel, dims, keys, rows, 1e-06),...  13 us
    all_to_all x1, starting transfers between devices, local(): lax.all_to_all(outgoing, 'dev', split_axis=0, concat_axis=0, tiled=True)  5.36 us
    dot_general x1, matrix products, attention(): jnp.einsum('rgqh,rcgh->rgqc', query_heads, keys_whole, preferred_element_...  4.62 us
    dot_general x1, matrix products, attention(): jnp.einsum('rgqc,rcgh->rgqh', weights_bf, values_whole, preferred_element...  3.89 us
    pallas_call x1, Pallas kernels, project(): pl.pallas_call(functools.partial(project_kernel, dims, keys, rows), out_s...  3.79 us
    unnamed x48, local copies, waits for them, and re-layouts  3.25 us
  transfers between devices with their start and end apart: 47, of which 16 were waited for; matrix products, arithmetic and copies ran while one was open for 6% of the time, Pallas kernels for 3%

profile of v1, /device:TPU:0, one launch (start us, length us, event | category | flops | bytes accessed | tf_op | source)
XLA Modules:
  0.0 123.8 jit_solution(8765623042569133590)
XLA Ops:
  0.0 0.9 copy.29
  0.9 0.7 iota_compare_fusion.1
  1.7 0.7 reshape.108
  2.6 4.6 %fusion.33 = (f32[16,2,16]{2,1,0:T(2,128)S(1)}, f32[16,2,16,768]{3,2,1,0:T(8,128)S(1)}) fusion(bf16[16,2,16,128]{3,2,1,0:T(8,128)(2,1)S(1)} %bitcast.46, pred[16,768]{1,0:T(8,128)(4,1)S(1)} %iota_compare_fusion.1, bf16[16,768,256]{2,1,0:T(8,128)(2,1)} %param.15), kind=kOutput, calls=%fused_computation.59 | convolution fusion | flops 101842432 | bytes 8009728 | tf_op jit(solution)/shard_map/rgqh,rcgh->rgqc/dot_general | solution.py:365
  7.2 0.5 fusion.8
  7.8 3.9 %fusion.12 = bf16[16,2,16,128]{3,2,1,0:T(8,128)(2,1)S(1)} fusion(f32[16,2,16,768]{3,2,1,0:T(8,128)S(1)} %get-tuple-element.38, f32[16,2,16]{2,1,0:T(2,128)S(1)} %get-tuple-element.36, f32[16,2,16]{2,1,0:T(2,128)S(1)} %multiply_maximum_fusion, f32[16,2,128]{2,1,0:T(2,128)S(1)} %reshape.104, f32[16,2,16]{2,1,0:T(2,128)S(1)} %get-tuple-element.35, ...), kind=kOutput, calls=%fused_computation.11 | convolution fusion | flops 102039552 | bytes 8017920 | tf_op jit(solution)/shard_map/rgqc,rcgh->rgqh/dot_general | solution.py:376
  11.8 3.1 %collective-permute-start.6 = (bf16[16,2048]{1,0:T(8,128)(2,1)S(1)}, bf16[16,2048]{1,0:T(8,128)(2,1)S(1)}, u32[]{:S(2)}, u32[]{:S(2)}) collective-permute-start(bf16[16,2048]{1,0:T(8,128)(2,1)S(1)} %get-tuple-element.31), channel_id=1, source_target_pairs={{0,4},{1,5},{2,6},{3,7},{4,8},{5,9},{6,10},{7,11},{8,12},{9,13},{1... | collective-permute-start | bytes 196616 | tf_op jit(solution)/shard_map/ppermute | solution.py:41
  14.8 2.6 %collective-permute-start.7 = (bf16[16,2048]{1,0:T(8,128)(2,1)S(1)}, bf16[16,2048]{1,0:T(8,128)(2,1)S(1)}, u32[]{:S(2)}, u32[]{:S(2)}) collective-permute-start(bf16[16,2048]{1,0:T(8,128)(2,1)S(1)} %get-tuple-element.31), channel_id=1, source_target_pairs={{0,8},{1,9},{2,10},{3,11},{4,12},{5,13},{6,14},{7,15},{8,0},{9,1},... | collective-permute-start | bytes 196616 | tf_op jit(solution)/shard_map/ppermute | solution.py:41
  17.4 1.3 %collective-permute-start.8 = (bf16[16,2048]{1,0:T(8,128)(2,1)S(1)}, bf16[16,2048]{1,0:T(8,128)(2,1)S(1)}, u32[]{:S(2)}, u32[]{:S(2)}) collective-permute-start(bf16[16,2048]{1,0:T(8,128)(2,1)S(1)} %get-tuple-element.31), channel_id=1, source_target_pairs={{0,12},{1,13},{2,14},{3,15},{4,0},{5,1},{6,2},{7,3},{8,4},{9,5},{1... | collective-permute-start | bytes 196616 | tf_op jit(solution)/shard_map/ppermute | solution.py:41
  18.8 0.7 collective-permute-start
  19.8 2.8 %collective-permute-start.2 = (bf16[16,2048]{1,0:T(8,128)(2,1)S(1)}, bf16[16,2048]{1,0:T(8,128)(2,1)S(1)}, u32[]{:S(2)}, u32[]{:S(2)}) collective-permute-start(bf16[16,2048]{1,0:T(8,128)(2,1)S(1)} %get-tuple-element.32), channel_id=1, source_target_pairs={{0,12},{1,13},{2,14},{3,15},{4,0},{5,1},{6,2},{7,3},{8,4},{9,5},{1... | collective-permute-start | bytes 196616 | tf_op jit(solution)/shard_map/ppermute | solution.py:41
  22.6 1.6 %collective-permute-start.10 = (bf16[64,2048]{1,0:T(8,128)(2,1)S(1)}, bf16[64,2048]{1,0:T(8,128)(2,1)S(1)}, u32[]{:S(2)}, u32[]{:S(2)}) collective-permute-start(bf16[64,2048]{1,0:T(8,128)(2,1)S(1)} %pad_maximum_fusion.1.refs_4_), channel_id=1, source_target_pairs={{0,2},{1,3},{2,0},{3,1},{4,6},{5,7},{6,4},{7,5},{8,10},{9,11},{10,... | collective-permute-start | bytes 786440 | tf_op jit(solution)/shard_map/ppermute | solution.py:41
  24.2 0.9 collective-permute-done
  25.2 2.4 %collective-permute-done.1 = bf16[16,2048]{1,0:T(8,128)(2,1)S(1)} collective-permute-done((bf16[16,2048]{1,0:T(8,128)(2,1)S(1)}, bf16[16,2048]{1,0:T(8,128)(2,1)S(1)}, u32[]{:S(2)}, u32[]{:S(2)}) %collective-permute-start.1) | collective-permute-done | bytes 65568 | tf_op jit(solution)/shard_map/ppermute | solution.py:41
  27.5 1.8 %collective-permute-start.3 = (bf16[64,2048]{1,0:T(8,128)(2,1)S(1)}, bf16[64,2048]{1,0:T(8,128)(2,1)S(1)}, u32[]{:S(2)}, u32[]{:S(2)}) collective-permute-start(bf16[64,2048]{1,0:T(8,128)(2,1)S(1)} %pad_maximum_fusion.refs_0_), channel_id=1, source_target_pairs={{0,1},{1,0},{2,3},{3,2},{4,5},{5,4},{6,7},{7,6},{8,9},{9,8},{10,11... | collective-permute-start | bytes 786440 | tf_op jit(solution)/shard_map/ppermute | solution.py:41
  30.2 1.8 %collective-permute-start.4 = (bf16[64,2048]{1,0:T(8,128)(2,1)S(1)}, bf16[64,2048]{1,0:T(8,128)(2,1)}, u32[]{:S(2)}, u32[]{:S(2)}) collective-permute-start(bf16[64,2048]{1,0:T(8,128)(2,1)S(1)} %pad_maximum_fusion.refs_0_), channel_id=1, source_target_pairs={{0,2},{1,3},{2,0},{3,1},{4,6},{5,7},{6,4},{7,5},{8,10},{9,11},{10,... | collective-permute-start | bytes 786440 | tf_op jit(solution)/shard_map/ppermute | solution.py:41
  32.0 1.5 %collective-permute-start.11 = (bf16[64,2048]{1,0:T(8,128)(2,1)S(1)}, bf16[64,2048]{1,0:T(8,128)(2,1)}, u32[]{:S(2)}, u32[]{:S(2)}) collective-permute-start(bf16[64,2048]{1,0:T(8,128)(2,1)S(1)} %collective-permute-done.10.refs_6_), channel_id=1, source_target_pairs={{0,1},{1,0},{2,3},{3,2},{4,5},{5,4},{6,7},{7,6},{8,9},{9,8},{10,11... | collective-permute-start | bytes 786440 | tf_op jit(solution)/shard_map/ppermute | solution.py:41
  33.5 3.3 %collective-permute-done.3.refs_1_ = bf16[64,2048]{1,0:T(8,128)(2,1)S(1)} collective-permute-done((bf16[64,2048]{1,0:T(8,128)(2,1)S(1)}, bf16[64,2048]{1,0:T(8,128)(2,1)S(1)}, u32[]{:S(2)}, u32[]{:S(2)}) %collective-permute-start.3) | collective-permute-done | bytes 262176 | tf_op jit(solution)/shard_map/ppermute | solution.py:41
  36.8 1.8 %collective-permute-start.5 = (bf16[64,2048]{1,0:T(8,128)(2,1)S(1)}, bf16[64,2048]{1,0:T(8,128)(2,1)}, u32[]{:S(2)}, u32[]{:S(2)}) collective-permute-start(bf16[64,2048]{1,0:T(8,128)(2,1)S(1)} %collective-permute-done.3.refs_1_), channel_id=1, source_target_pairs={{0,2},{1,3},{2,0},{3,1},{4,6},{5,7},{6,4},{7,5},{8,10},{9,11},{10,... | collective-permute-start | bytes 786440 | tf_op jit(solution)/shard_map/ppermute | solution.py:41
  38.7 0.7 pad_maximum_fusion.2
  39.3 5.4 %all-to-all-start = ((bf16[16,16,256]{2,1,0:T(8,128)(2,1)}), bf16[16,16,256]{2,1,0:T(8,128)(2,1)}, u32[]{:S(2)}, u32[]{:S(2)}) async-start(bf16[16,16,256]{2,1,0:T(8,128)(2,1)} %pad_maximum_fusion.2), calls=%async_computation | async-start | bytes 262144 | tf_op jit(solution)/shard_map/all_to_all | solution.py:418
  44.7 2.9 %collective-permute-done.11.refs_7_ = bf16[64,2048]{1,0:T(8,128)(2,1)} collective-permute-done((bf16[64,2048]{1,0:T(8,128)(2,1)S(1)}, bf16[64,2048]{1,0:T(8,128)(2,1)}, u32[]{:S(2)}, u32[]{:S(2)}) %collective-permute-start.11) | collective-permute-done | bytes 262176 | tf_op jit(solution)/shard_map/ppermute | solution.py:41
  47.7 3.8 %project.1 = (f32[256,128]{1,0:T(8,128)S(1)}, f32[256,128]{1,0:T(8,128)}) custom-call(bf16[64,2048]{1,0:T(8,128)(2,1)S(1)} %pad_maximum_fusion.refs_0_, bf16[64,2048]{1,0:T(8,128)(2,1)S(1)} %collective-permute-done.3.refs_1_, bf16[64,2048]{1,0:T(8,128)(2,1)} %collective-permute-done.4.refs_2_, bf16[64,2048]{1,0:T(8,128)(2,1)} %collective-permute-done.5.refs_3_, ...), custom_call_target="tpu_custom_call" | custom-call | flops 536870912 | bytes 4194304 | tf_op jit(solution)/shard_map/project/pallas_call | solution.py:126
  51.6 1.0 all-to-all-done
  52.6 1.5 %fusion.30 = (bf16[16,16,128]{2,1,0:T(8,128)(2,1)}, bf16[16,16,128]{2,1,0:T(8,128)(2,1)S(1)}) fusion(bf16[16,16,256]{2,1,0:T(8,128)(2,1)} %all-to-all-done), kind=kLoop, calls=%fused_computation.56 | loop fusion | bytes 262144 | tf_op jit(solution)/shard_map/slice | solution.py:420
  54.1 1.1 collective-permute-start.19
  55.2 1.1 collective-permute-start.20
  56.3 1.7 %collective-permute-start.21 = (bf16[128,128]{1,0:T(8,128)(2,1)S(1)}, bf16[128,128]{1,0:T(8,128)(2,1)S(1)}, u32[]{:S(2)}, u32[]{:S(2)}) collective-permute-start(bf16[128,128]{1,0:T(8,128)(2,1)S(1)} %get-tuple-element.33), channel_id=1, source_target_pairs={{0,12},{1,13},{2,14},{3,15},{4,0},{5,1},{6,2},{7,3},{8,4},{9,5},{1... | collective-permute-start | bytes 98312 | tf_op jit(solution)/shard_map/ppermute | solution.py:41
  58.0 0.6 collective-permute-start.13
  58.6 1.6 %collective-permute-start.14 = (bf16[128,128]{1,0:T(8,128)(2,1)S(1)}, bf16[128,128]{1,0:T(8,128)(2,1)S(1)}, u32[]{:S(2)}, u32[]{:S(2)}) collective-permute-start(bf16[128,128]{1,0:T(8,128)(2,1)S(1)} %get-tuple-element.34), channel_id=1, source_target_pairs={{0,8},{1,9},{2,10},{3,11},{4,12},{5,13},{6,14},{7,15},{8,0},{9,1},... | collective-permute-start | bytes 98312 | tf_op jit(solution)/shard_map/ppermute | solution.py:41
  60.1 2.8 %collective-permute-start.15 = (bf16[128,128]{1,0:T(8,128)(2,1)S(1)}, bf16[128,128]{1,0:T(8,128)(2,1)S(1)}, u32[]{:S(2)}, u32[]{:S(2)}) collective-permute-start(bf16[128,128]{1,0:T(8,128)(2,1)S(1)} %get-tuple-element.34), channel_id=1, source_target_pairs={{0,12},{1,13},{2,14},{3,15},{4,0},{5,1},{6,2},{7,3},{8,4},{9,5},{1... | collective-permute-start | bytes 98312 | tf_op jit(solution)/shard_map/ppermute | solution.py:41
  63.0 0.8 collective-permute-start.23
  63.8 1.0 collective-permute-start.22
  64.9 1.1 collective-permute-start.16
  65.9 1.3 %collective-permute-start.17 = (bf16[512,128]{1,0:T(8,128)(2,1)S(1)}, bf16[512,128]{1,0:T(8,128)(2,1)S(1)}, u32[]{:S(2)}, u32[]{:S(2)}) collective-permute-start(bf16[512,128]{1,0:T(8,128)(2,1)S(1)} %pad_maximum_fusion.3.refs_0_), channel_id=1, source_target_pairs={{0,2},{1,3},{2,0},{3,1},{4,6},{5,7},{6,4},{7,5},{8,10},{9,11},{10,... | collective-permute-start | bytes 393224 | tf_op jit(solution)/shard_map/ppermute | solution.py:41
  67.2 0.8 collective-permute-done.23.refs_6_
  68.0 1.5 %collective-permute-done.22.refs_5_ = bf16[512,128]{1,0:T(8,128)(2,1)S(1)} collective-permute-done((bf16[512,128]{1,0:T(8,128)(2,1)S(1)}, bf16[512,128]{1,0:T(8,128)(2,1)S(1)}, u32[]{:S(2)}, u32[]{:S(2)}) %collective-permute-start.22) | collective-permute-done | bytes 131104 | tf_op jit(solution)/shard_map/ppermute | solution.py:41
  69.5 1.1 collective-permute-start.24
  70.6 1.3 %collective-permute-done.16.refs_1_ = bf16[512,128]{1,0:T(8,128)(2,1)S(1)} collective-permute-done((bf16[512,128]{1,0:T(8,128)(2,1)S(1)}, bf16[512,128]{1,0:T(8,128)(2,1)S(1)}, u32[]{:S(2)}, u32[]{:S(2)}) %collective-permute-start.16) | collective-permute-done | bytes 131104 | tf_op jit(solution)/shard_map/ppermute | solution.py:41
  71.9 1.6 %collective-permute-start.18 = (bf16[512,128]{1,0:T(8,128)(2,1)S(1)}, bf16[512,128]{1,0:T(8,128)(2,1)S(1)}, u32[]{:S(2)}, u32[]{:S(2)}) collective-permute-start(bf16[512,128]{1,0:T(8,128)(2,1)S(1)} %collective-permute-done.16.refs_1_), channel_id=1, source_target_pairs={{0,2},{1,3},{2,0},{3,1},{4,6},{5,7},{6,4},{7,5},{8,10},{9,11},{10,... | collective-permute-start | bytes 393224 | tf_op jit(solution)/shard_map/ppermute | solution.py:41
  73.6 0.5 collective-permute-start.26
  74.5 0.5 collective-permute-start.32
  75.0 1.9 %collective-permute-done.18.refs_3_ = bf16[512,128]{1,0:T(8,128)(2,1)S(1)} collective-permute-done((bf16[512,128]{1,0:T(8,128)(2,1)S(1)}, bf16[512,128]{1,0:T(8,128)(2,1)S(1)}, u32[]{:S(2)}, u32[]{:S(2)}) %collective-permute-start.18) | collective-permute-done | bytes 131104 | tf_op jit(solution)/shard_map/ppermute | solution.py:41
  76.9 1.4 %copy.24 = bf16[4096,16]{1,0:T(8,128)(2,1)S(1)} copy(bf16[4096,16]{0,1:T(8,128)(2,1)} %param.23) | data formatting | bytes 262144 | tf_op args[9]
  78.3 1.2 pad.4.refs_18_
  79.8 0.5 copy-done.13
  80.5 13.0 %experts.1 = (bf16[256,1024]{1,0:T(8,128)(2,1)}, bf16[256,1024]{1,0:T(8,128)(2,1)}, bf16[256,1024]{1,0:T(8,128)(2,1)}, bf16[256,1024]{1,0:T(8,128)(2,1)}, bf16[16,4096]{1,0:T(8,128)(2,1)}) custom-call(bf16[512,128]{1,0:T(8,128)(2,1)} %copy-done.2, bf16[512,128]{1,0:T(8,128)(2,1)} %copy-done.7, bf16[512,128]{1,0:T(8,128)(2,1)} %copy-done.8, ...), custom_call_target="tpu_custom_call" | custom-call | flops 2415919104 | bytes 15728640 | tf_op jit(solution)/shard_map/experts/pallas_call | solution.py:318
  93.5 0.5 collective-permute-start.33
  94.1 1.7 %collective-permute-done.33 = bf16[256,1024]{1,0:T(8,128)(2,1)S(1)} collective-permute-done((bf16[256,1024]{1,0:T(8,128)(2,1)}, bf16[256,1024]{1,0:T(8,128)(2,1)S(1)}, u32[]{:S(2)}, u32[]{:S(2)}) %collective-permute-start.33) | collective-permute-done | bytes 524320 | tf_op jit(solution)/shard_map/ppermute | solution.py:45
  95.7 1.2 convert_add_fusion.1
  97.0 1.1 collective-permute-start.34
  98.3 2.0 %collective-permute-start.40 = (bf16[128,1024]{1,0:T(8,128)(2,1)S(1)}, bf16[128,1024]{1,0:T(8,128)(2,1)S(1)}, u32[]{:S(2)}, u32[]{:S(2)}) collective-permute-start(bf16[128,1024]{1,0:T(8,128)(2,1)S(1)} %slice.154), channel_id=1, source_target_pairs={{0,2},{1,3},{2,0},{3,1},{4,6},{5,7},{6,4},{7,5},{8,10},{9,11},{10,... | collective-permute-start | bytes 786440 | tf_op jit(solution)/shard_map/ppermute | solution.py:41
  100.3 5.4 %collective-permute-done.34 = bf16[128,1024]{1,0:T(8,128)(2,1)S(1)} collective-permute-done((bf16[128,1024]{1,0:T(8,128)(2,1)S(1)}, bf16[128,1024]{1,0:T(8,128)(2,1)S(1)}, u32[]{:S(2)}, u32[]{:S(2)}) %collective-permute-start.34) | collective-permute-done | bytes 262176 | tf_op jit(solution)/shard_map/ppermute | solution.py:41
  105.7 1.7 %collective-permute-start.35 = (bf16[64,1024]{1,0:T(8,128)(2,1)S(1)}, bf16[64,1024]{1,0:T(8,128)(2,1)S(1)}, u32[]{:S(2)}, u32[]{:S(2)}) collective-permute-start(bf16[64,1024]{1,0:T(8,128)(2,1)S(1)} %slice.157), channel_id=1, source_target_pairs={{0,2},{1,3},{2,0},{3,1},{4,6},{5,7},{6,4},{7,5},{8,10},{9,11},{10,... | collective-permute-start | bytes 393224 | tf_op jit(solution)/shard_map/ppermute | solution.py:41
  107.5 1.3 %collective-permute-start.41 = (bf16[64,1024]{1,0:T(8,128)(2,1)S(1)}, bf16[64,1024]{1,0:T(8,128)(2,1)S(1)}, u32[]{:S(2)}, u32[]{:S(2)}) collective-permute-start(bf16[64,1024]{1,0:T(8,128)(2,1)S(1)} %slice.156), channel_id=1, source_target_pairs={{0,1},{1,0},{2,3},{3,2},{4,5},{5,4},{6,7},{7,6},{8,9},{9,8},{10,11... | collective-permute-start | bytes 393224 | tf_op jit(solution)/shard_map/ppermute | solution.py:41
  108.9 1.9 %collective-permute-done.35 = bf16[64,1024]{1,0:T(8,128)(2,1)S(1)} collective-permute-done((bf16[64,1024]{1,0:T(8,128)(2,1)S(1)}, bf16[64,1024]{1,0:T(8,128)(2,1)S(1)}, u32[]{:S(2)}, u32[]{:S(2)}) %collective-permute-start.35) | collective-permute-done | bytes 131104 | tf_op jit(solution)/shard_map/ppermute | solution.py:41
  111.1 2.2 %collective-permute-start.37 = (bf16[16,1024]{1,0:T(8,128)(2,1)S(1)}, bf16[16,1024]{1,0:T(8,128)(2,1)S(1)}, u32[]{:S(2)}, u32[]{:S(2)}) collective-permute-start(bf16[16,1024]{1,0:T(8,128)(2,1)S(1)} %get-tuple-element.25), channel_id=1, source_target_pairs={{0,8},{1,9},{2,10},{3,11},{4,12},{5,13},{6,14},{7,15},{8,0},{9,1},... | collective-permute-start | bytes 98312 | tf_op jit(solution)/shard_map/ppermute | solution.py:41
  113.3 2.1 %collective-permute-start.38 = (bf16[16,1024]{1,0:T(8,128)(2,1)S(1)}, bf16[16,1024]{1,0:T(8,128)(2,1)S(1)}, u32[]{:S(2)}, u32[]{:S(2)}) collective-permute-start(bf16[16,1024]{1,0:T(8,128)(2,1)S(1)} %get-tuple-element.24), channel_id=1, source_target_pairs={{0,12},{1,13},{2,14},{3,15},{4,0},{5,1},{6,2},{7,3},{8,4},{9,5},{1... | collective-permute-start | bytes 98312 | tf_op jit(solution)/shard_map/ppermute | solution.py:41
  115.5 1.5 %collective-permute-start.43 = (bf16[16,1024]{1,0:T(8,128)(2,1)S(1)}, bf16[16,1024]{1,0:T(8,128)(2,1)S(1)}, u32[]{:S(2)}, u32[]{:S(2)}) collective-permute-start(bf16[16,1024]{1,0:T(8,128)(2,1)S(1)} %get-tuple-element.28), channel_id=1, source_target_pairs={{0,8},{1,9},{2,10},{3,11},{4,12},{5,13},{6,14},{7,15},{8,0},{9,1},... | collective-permute-start | bytes 98312 | tf_op jit(solution)/shard_map/ppermute | solution.py:41
  116.9 2.8 %collective-permute-start.44 = (bf16[16,1024]{1,0:T(8,128)(2,1)S(1)}, bf16[16,1024]{1,0:T(8,128)(2,1)S(1)}, u32[]{:S(2)}, u32[]{:S(2)}) collective-permute-start(bf16[16,1024]{1,0:T(8,128)(2,1)S(1)} %get-tuple-element.27), channel_id=1, source_target_pairs={{0,12},{1,13},{2,14},{3,15},{4,0},{5,1},{6,2},{7,3},{8,4},{9,5},{1... | collective-permute-start | bytes 98312 | tf_op jit(solution)/shard_map/ppermute | solution.py:41
  119.8 1.4 %collective-permute-done.42 = bf16[16,1024]{1,0:T(8,128)(2,1)S(1)} collective-permute-done((bf16[16,1024]{1,0:T(8,128)(2,1)S(1)}, bf16[16,1024]{1,0:T(8,128)(2,1)S(1)}, u32[]{:S(2)}, u32[]{:S(2)}) %collective-permute-start.42) | collective-permute-done | bytes 32800 | tf_op jit(solution)/shard_map/ppermute | solution.py:41
  121.2 0.6 collective-permute-done.44
  121.9 1.2 collective-permute-done.45
  123.1 0.7 maximum_select_fusion
  (121 shorter events, 3.4 us)
Async XLA Ops:
  2.5 5.2 %copy-start.20 = (bf16[16,256]{1,0:T(8,128)(2,1)S(1)}, bf16[16,256]{1,0:T(8,128)(2,1)}, u32[]{:S(2)}) copy-start(bf16[16,256]{1,0:T(8,128)(2,1)} %param.18) | copy-start | bytes 24580
  7.7 21.6 %copy-start.18 = (bf16[16,4096]{1,0:T(8,128)(2,1)S(1)}, bf16[16,4096]{1,0:T(8,128)(2,1)}, u32[]{:S(2)}) copy-start(bf16[16,4096]{1,0:T(8,128)(2,1)} %param.20) | copy-start | bytes 393220
  11.6 18.0 %copy-start.21 = (s32[16,8]{0,1:T(8,128)S(1)}, s32[16,8]{0,1:T(8,128)}, u32[]{:S(2)}) copy-start(s32[16,8]{0,1:T(8,128)} %param.24) | copy-start | bytes 1540
  11.7 36.0 %copy-start = (bf16[4096,256]{1,0:T(8,128)(2,1)S(1)}, bf16[4096,256]{1,0:T(8,128)(2,1)}, u32[]{:S(2)}) copy-start(bf16[4096,256]{1,0:T(8,128)(2,1)} %refs_8_.1) | copy-start | bytes 6291460
  11.8 8.0 %collective-permute-start.6 = (bf16[16,2048]{1,0:T(8,128)(2,1)S(1)}, bf16[16,2048]{1,0:T(8,128)(2,1)S(1)}, u32[]{:S(2)}, u32[]{:S(2)}) collective-permute-start(bf16[16,2048]{1,0:T(8,128)(2,1)S(1)} %get-tuple-element.31), channel_id=1, source_target_pairs={{0,4},{1,5},{2,6},{3,7},{4,8},{5,9},{6,10},{7,11},{8,12},{9,13},{1... | collective-permute-start | bytes 196616 | tf_op jit(solution)/shard_map/ppermute | solution.py:41
  14.8 7.8 %collective-permute-start.7 = (bf16[16,2048]{1,0:T(8,128)(2,1)S(1)}, bf16[16,2048]{1,0:T(8,128)(2,1)S(1)}, u32[]{:S(2)}, u32[]{:S(2)}) collective-permute-start(bf16[16,2048]{1,0:T(8,128)(2,1)S(1)} %get-tuple-element.31), channel_id=1, source_target_pairs={{0,8},{1,9},{2,10},{3,11},{4,12},{5,13},{6,14},{7,15},{8,0},{9,1},... | collective-permute-start | bytes 196616 | tf_op jit(solution)/shard_map/ppermute | solution.py:41
  17.4 5.2 %collective-permute-start.8 = (bf16[16,2048]{1,0:T(8,128)(2,1)S(1)}, bf16[16,2048]{1,0:T(8,128)(2,1)S(1)}, u32[]{:S(2)}, u32[]{:S(2)}) collective-permute-start(bf16[16,2048]{1,0:T(8,128)(2,1)S(1)} %get-tuple-element.31), channel_id=1, source_target_pairs={{0,12},{1,13},{2,14},{3,15},{4,0},{5,1},{6,2},{7,3},{8,4},{9,5},{1... | collective-permute-start | bytes 196616 | tf_op jit(solution)/shard_map/ppermute | solution.py:41
  18.8 6.4 %collective-permute-start = (bf16[16,2048]{1,0:T(8,128)(2,1)S(1)}, bf16[16,2048]{1,0:T(8,128)(2,1)S(1)}, u32[]{:S(2)}, u32[]{:S(2)}) collective-permute-start(bf16[16,2048]{1,0:T(8,128)(2,1)S(1)} %get-tuple-element.32), channel_id=1, source_target_pairs={{0,4},{1,5},{2,6},{3,7},{4,8},{5,9},{6,10},{7,11},{8,12},{9,13},{1... | collective-permute-start | bytes 196616 | tf_op jit(solution)/shard_map/ppermute | solution.py:41
  19.4 8.1 %collective-permute-start.1 = (bf16[16,2048]{1,0:T(8,128)(2,1)S(1)}, bf16[16,2048]{1,0:T(8,128)(2,1)S(1)}, u32[]{:S(2)}, u32[]{:S(2)}) collective-permute-start(bf16[16,2048]{1,0:T(8,128)(2,1)S(1)} %get-tuple-element.32), channel_id=1, source_target_pairs={{0,8},{1,9},{2,10},{3,11},{4,12},{5,13},{6,14},{7,15},{8,0},{9,1},... | collective-permute-start | bytes 196616 | tf_op jit(solution)/shard_map/ppermute | solution.py:41
  19.8 7.7 %collective-permute-start.2 = (bf16[16,2048]{1,0:T(8,128)(2,1)S(1)}, bf16[16,2048]{1,0:T(8,128)(2,1)S(1)}, u32[]{:S(2)}, u32[]{:S(2)}) collective-permute-start(bf16[16,2048]{1,0:T(8,128)(2,1)S(1)} %get-tuple-element.32), channel_id=1, source_target_pairs={{0,12},{1,13},{2,14},{3,15},{4,0},{5,1},{6,2},{7,3},{8,4},{9,5},{1... | collective-permute-start | bytes 196616 | tf_op jit(solution)/shard_map/ppermute | solution.py:41
  22.6 9.4 %collective-permute-start.10 = (bf16[64,2048]{1,0:T(8,128)(2,1)S(1)}, bf16[64,2048]{1,0:T(8,128)(2,1)S(1)}, u32[]{:S(2)}, u32[]{:S(2)}) collective-permute-start(bf16[64,2048]{1,0:T(8,128)(2,1)S(1)} %pad_maximum_fusion.1.refs_4_), channel_id=1, source_target_pairs={{0,2},{1,3},{2,0},{3,1},{4,6},{5,7},{6,4},{7,5},{8,10},{9,11},{10,... | collective-permute-start | bytes 786440 | tf_op jit(solution)/shard_map/ppermute | solution.py:41
  27.5 9.3 %collective-permute-start.3 = (bf16[64,2048]{1,0:T(8,128)(2,1)S(1)}, bf16[64,2048]{1,0:T(8,128)(2,1)S(1)}, u32[]{:S(2)}, u32[]{:S(2)}) collective-permute-start(bf16[64,2048]{1,0:T(8,128)(2,1)S(1)} %pad_maximum_fusion.refs_0_), channel_id=1, source_target_pairs={{0,1},{1,0},{2,3},{3,2},{4,5},{5,4},{6,7},{7,6},{8,9},{9,8},{10,11... | collective-permute-start | bytes 786440 | tf_op jit(solution)/shard_map/ppermute | solution.py:41
  29.9 14.9 %collective-permute-start.9 = (bf16[64,2048]{1,0:T(8,128)(2,1)S(1)}, bf16[64,2048]{1,0:T(8,128)(2,1)S(1)}, u32[]{:S(2)}, u32[]{:S(2)}) collective-permute-start(bf16[64,2048]{1,0:T(8,128)(2,1)S(1)} %pad_maximum_fusion.1.refs_4_), channel_id=1, source_target_pairs={{0,1},{1,0},{2,3},{3,2},{4,5},{5,4},{6,7},{7,6},{8,9},{9,8},{10,11... | collective-permute-start | bytes 786440 | tf_op jit(solution)/shard_map/ppermute | solution.py:41
  30.2 14.5 %collective-permute-start.4 = (bf16[64,2048]{1,0:T(8,128)(2,1)S(1)}, bf16[64,2048]{1,0:T(8,128)(2,1)}, u32[]{:S(2)}, u32[]{:S(2)}) collective-permute-start(bf16[64,2048]{1,0:T(8,128)(2,1)S(1)} %pad_maximum_fusion.refs_0_), channel_id=1, source_target_pairs={{0,2},{1,3},{2,0},{3,1},{4,6},{5,7},{6,4},{7,5},{8,10},{9,11},{10,... | collective-permute-start | bytes 786440 | tf_op jit(solution)/shard_map/ppermute | solution.py:41
  32.0 15.7 %collective-permute-start.11 = (bf16[64,2048]{1,0:T(8,128)(2,1)S(1)}, bf16[64,2048]{1,0:T(8,128)(2,1)}, u32[]{:S(2)}, u32[]{:S(2)}) collective-permute-start(bf16[64,2048]{1,0:T(8,128)(2,1)S(1)} %collective-permute-done.10.refs_6_), channel_id=1, source_target_pairs={{0,1},{1,0},{2,3},{3,2},{4,5},{5,4},{6,7},{7,6},{8,9},{9,8},{10,11... | collective-permute-start | bytes 786440 | tf_op jit(solution)/shard_map/ppermute | solution.py:41
  36.8 10.9 %collective-permute-start.5 = (bf16[64,2048]{1,0:T(8,128)(2,1)S(1)}, bf16[64,2048]{1,0:T(8,128)(2,1)}, u32[]{:S(2)}, u32[]{:S(2)}) collective-permute-start(bf16[64,2048]{1,0:T(8,128)(2,1)S(1)} %collective-permute-done.3.refs_1_), channel_id=1, source_target_pairs={{0,2},{1,3},{2,0},{3,1},{4,6},{5,7},{6,4},{7,5},{8,10},{9,11},{10,... | collective-permute-start | bytes 786440 | tf_op jit(solution)/shard_map/ppermute | solution.py:41
  39.3 13.2 %all-to-all-start = ((bf16[16,16,256]{2,1,0:T(8,128)(2,1)}), bf16[16,16,256]{2,1,0:T(8,128)(2,1)}, u32[]{:S(2)}, u32[]{:S(2)}) async-start(bf16[16,16,256]{2,1,0:T(8,128)(2,1)} %pad_maximum_fusion.2), calls=%async_computation | async-start | bytes 262144 | tf_op jit(solution)/shard_map/all_to_all | solution.py:418
  51.5 2.6 %collective-permute-start.12 = (f32[256,128]{1,0:T(8,128)}, f32[256,128]{1,0:T(8,128)S(1)}, u32[]{:S(2)}, u32[]{:S(2)}) collective-permute-start(f32[256,128]{1,0:T(8,128)} %get-tuple-element.13), channel_id=1, source_target_pairs={{0,16},{16,0},{1,17},{17,1},{2,18},{18,2},{3,19},{19,3},{4,20},{20... | collective-permute-start | bytes 393224 | tf_op jit(solution)/shard_map/ppermute | solution.py:45
  54.1 6.0 %collective-permute-start.19 = (bf16[128,128]{1,0:T(8,128)(2,1)S(1)}, bf16[128,128]{1,0:T(8,128)(2,1)S(1)}, u32[]{:S(2)}, u32[]{:S(2)}) collective-permute-start(bf16[128,128]{1,0:T(8,128)(2,1)S(1)} %get-tuple-element.33), channel_id=1, source_target_pairs={{0,4},{1,5},{2,6},{3,7},{4,8},{5,9},{6,10},{7,11},{8,12},{9,13},{1... | collective-permute-start | bytes 98312 | tf_op jit(solution)/shard_map/ppermute | solution.py:41
  55.2 7.8 %collective-permute-start.20 = (bf16[128,128]{1,0:T(8,128)(2,1)S(1)}, bf16[128,128]{1,0:T(8,128)(2,1)S(1)}, u32[]{:S(2)}, u32[]{:S(2)}) collective-permute-start(bf16[128,128]{1,0:T(8,128)(2,1)S(1)} %get-tuple-element.33), channel_id=1, source_target_pairs={{0,8},{1,9},{2,10},{3,11},{4,12},{5,13},{6,14},{7,15},{8,0},{9,1},... | collective-permute-start | bytes 98312 | tf_op jit(solution)/shard_map/ppermute | solution.py:41
  56.3 6.7 %collective-permute-start.21 = (bf16[128,128]{1,0:T(8,128)(2,1)S(1)}, bf16[128,128]{1,0:T(8,128)(2,1)S(1)}, u32[]{:S(2)}, u32[]{:S(2)}) collective-permute-start(bf16[128,128]{1,0:T(8,128)(2,1)S(1)} %get-tuple-element.33), channel_id=1, source_target_pairs={{0,12},{1,13},{2,14},{3,15},{4,0},{5,1},{6,2},{7,3},{8,4},{9,5},{1... | collective-permute-start | bytes 98312 | tf_op jit(solution)/shard_map/ppermute | solution.py:41
  58.0 6.8 %collective-permute-start.13 = (bf16[128,128]{1,0:T(8,128)(2,1)S(1)}, bf16[128,128]{1,0:T(8,128)(2,1)S(1)}, u32[]{:S(2)}, u32[]{:S(2)}) collective-permute-start(bf16[128,128]{1,0:T(8,128)(2,1)S(1)} %get-tuple-element.34), channel_id=1, source_target_pairs={{0,4},{1,5},{2,6},{3,7},{4,8},{5,9},{6,10},{7,11},{8,12},{9,13},{1... | collective-permute-start | bytes 98312 | tf_op jit(solution)/shard_map/ppermute | solution.py:41
  58.6 6.3 %collective-permute-start.14 = (bf16[128,128]{1,0:T(8,128)(2,1)S(1)}, bf16[128,128]{1,0:T(8,128)(2,1)S(1)}, u32[]{:S(2)}, u32[]{:S(2)}) collective-permute-start(bf16[128,128]{1,0:T(8,128)(2,1)S(1)} %get-tuple-element.34), channel_id=1, source_target_pairs={{0,8},{1,9},{2,10},{3,11},{4,12},{5,13},{6,14},{7,15},{8,0},{9,1},... | collective-permute-start | bytes 98312 | tf_op jit(solution)/shard_map/ppermute | solution.py:41
  60.1 4.7 %collective-permute-start.15 = (bf16[128,128]{1,0:T(8,128)(2,1)S(1)}, bf16[128,128]{1,0:T(8,128)(2,1)S(1)}, u32[]{:S(2)}, u32[]{:S(2)}) collective-permute-start(bf16[128,128]{1,0:T(8,128)(2,1)S(1)} %get-tuple-element.34), channel_id=1, source_target_pairs={{0,12},{1,13},{2,14},{3,15},{4,0},{5,1},{6,2},{7,3},{8,4},{9,5},{1... | collective-permute-start | bytes 98312 | tf_op jit(solution)/shard_map/ppermute | solution.py:41
  63.0 16.7 %copy-start.1 = (bf16[512,128]{1,0:T(8,128)(2,1)}, bf16[512,128]{1,0:T(8,128)(2,1)S(1)}, u32[]{:S(2)}) copy-start(bf16[512,128]{1,0:T(8,128)(2,1)S(1)} %pad_maximum_fusion.4.refs_4_) | copy-start | bytes 393220
  63.0 5.0 %collective-permute-start.23 = (bf16[512,128]{1,0:T(8,128)(2,1)S(1)}, bf16[512,128]{1,0:T(8,128)(2,1)S(1)}, u32[]{:S(2)}, u32[]{:S(2)}) collective-permute-start(bf16[512,128]{1,0:T(8,128)(2,1)S(1)} %pad_maximum_fusion.4.refs_4_), channel_id=1, source_target_pairs={{0,2},{1,3},{2,0},{3,1},{4,6},{5,7},{6,4},{7,5},{8,10},{9,11},{10,... | collective-permute-start | bytes 393224 | tf_op jit(solution)/shard_map/ppermute | solution.py:41
  63.8 5.7 %collective-permute-start.22 = (bf16[512,128]{1,0:T(8,128)(2,1)S(1)}, bf16[512,128]{1,0:T(8,128)(2,1)S(1)}, u32[]{:S(2)}, u32[]{:S(2)}) collective-permute-start(bf16[512,128]{1,0:T(8,128)(2,1)S(1)} %pad_maximum_fusion.4.refs_4_), channel_id=1, source_target_pairs={{0,1},{1,0},{2,3},{3,2},{4,5},{5,4},{6,7},{7,6},{8,9},{9,8},{10,11... | collective-permute-start | bytes 393224 | tf_op jit(solution)/shard_map/ppermute | solution.py:41
  64.8 5.8 %collective-permute-start.29 = (bf16[512,128]{1,0:T(8,128)(2,1)S(1)}, bf16[512,128]{1,0:T(8,128)(2,1)S(1)}, u32[]{:S(2)}, u32[]{:S(2)}) collective-permute-start(bf16[512,128]{1,0:T(8,128)(2,1)S(1)} %pad_maximum_fusion.4.refs_4_), channel_id=1, source_target_pairs={{0,16},{16,0},{1,17},{17,1},{2,18},{18,2},{3,19},{19,3},{4,20},{20... | collective-permute-start | bytes 393224 | tf_op jit(solution)/shard_map/ppermute | solution.py:45
  64.9 14.8 %copy-start.2 = (bf16[512,128]{1,0:T(8,128)(2,1)}, bf16[512,128]{1,0:T(8,128)(2,1)S(1)}, u32[]{:S(2)}) copy-start(bf16[512,128]{1,0:T(8,128)(2,1)S(1)} %pad_maximum_fusion.3.refs_0_) | copy-start | bytes 393220
  64.9 7.1 %collective-permute-start.16 = (bf16[512,128]{1,0:T(8,128)(2,1)S(1)}, bf16[512,128]{1,0:T(8,128)(2,1)S(1)}, u32[]{:S(2)}, u32[]{:S(2)}) collective-permute-start(bf16[512,128]{1,0:T(8,128)(2,1)S(1)} %pad_maximum_fusion.3.refs_0_), channel_id=1, source_target_pairs={{0,1},{1,0},{2,3},{3,2},{4,5},{5,4},{6,7},{7,6},{8,9},{9,8},{10,11... | collective-permute-start | bytes 393224 | tf_op jit(solution)/shard_map/ppermute | solution.py:41
  65.9 7.6 %collective-permute-start.17 = (bf16[512,128]{1,0:T(8,128)(2,1)S(1)}, bf16[512,128]{1,0:T(8,128)(2,1)S(1)}, u32[]{:S(2)}, u32[]{:S(2)}) collective-permute-start(bf16[512,128]{1,0:T(8,128)(2,1)S(1)} %pad_maximum_fusion.3.refs_0_), channel_id=1, source_target_pairs={{0,2},{1,3},{2,0},{3,1},{4,6},{5,7},{6,4},{7,5},{8,10},{9,11},{10,... | collective-permute-start | bytes 393224 | tf_op jit(solution)/shard_map/ppermute | solution.py:41
  68.0 11.7 %copy-start.4 = (bf16[512,128]{1,0:T(8,128)(2,1)}, bf16[512,128]{1,0:T(8,128)(2,1)S(1)}, u32[]{:S(2)}) copy-start(bf16[512,128]{1,0:T(8,128)(2,1)S(1)} %collective-permute-done.23.refs_6_) | copy-start | bytes 393220
  68.0 5.6 %collective-permute-start.25 = (bf16[512,128]{1,0:T(8,128)(2,1)S(1)}, bf16[512,128]{1,0:T(8,128)(2,1)S(1)}, u32[]{:S(2)}, u32[]{:S(2)}) collective-permute-start(bf16[512,128]{1,0:T(8,128)(2,1)S(1)} %pad_maximum_fusion.3.refs_0_), channel_id=1, source_target_pairs={{0,16},{16,0},{1,17},{17,1},{2,18},{18,2},{3,19},{19,3},{4,20},{20... | collective-permute-start | bytes 393224 | tf_op jit(solution)/shard_map/ppermute | solution.py:45
  69.5 10.2 %copy-start.5 = (bf16[512,128]{1,0:T(8,128)(2,1)}, bf16[512,128]{1,0:T(8,128)(2,1)S(1)}, u32[]{:S(2)}) copy-start(bf16[512,128]{1,0:T(8,128)(2,1)S(1)} %collective-permute-done.22.refs_5_) | copy-start | bytes 393220
  69.5 5.0 %collective-permute-start.24 = (bf16[512,128]{1,0:T(8,128)(2,1)S(1)}, bf16[512,128]{1,0:T(8,128)(2,1)S(1)}, u32[]{:S(2)}, u32[]{:S(2)}) collective-permute-start(bf16[512,128]{1,0:T(8,128)(2,1)S(1)} %collective-permute-done.23.refs_6_), channel_id=1, source_target_pairs={{0,1},{1,0},{2,3},{3,2},{4,5},{5,4},{6,7},{7,6},{8,9},{9,8},{10,11... | collective-permute-start | bytes 393224 | tf_op jit(solution)/shard_map/ppermute | solution.py:41
  70.6 9.1 %copy-start.6 = (bf16[512,128]{1,0:T(8,128)(2,1)}, bf16[512,128]{1,0:T(8,128)(2,1)S(1)}, u32[]{:S(2)}) copy-start(bf16[512,128]{1,0:T(8,128)(2,1)S(1)} %collective-permute-done.29.refs_12_) | copy-start | bytes 393220
  70.6 3.9 %collective-permute-start.30 = (bf16[512,128]{1,0:T(8,128)(2,1)S(1)}, bf16[512,128]{1,0:T(8,128)(2,1)S(1)}, u32[]{:S(2)}, u32[]{:S(2)}) collective-permute-start(bf16[512,128]{1,0:T(8,128)(2,1)S(1)} %collective-permute-done.22.refs_5_), channel_id=1, source_target_pairs={{0,16},{16,0},{1,17},{17,1},{2,18},{18,2},{3,19},{19,3},{4,20},{20... | collective-permute-start | bytes 393224 | tf_op jit(solution)/shard_map/ppermute | solution.py:45
  71.9 7.8 %copy-start.7 = (bf16[512,128]{1,0:T(8,128)(2,1)}, bf16[512,128]{1,0:T(8,128)(2,1)S(1)}, u32[]{:S(2)}) copy-start(bf16[512,128]{1,0:T(8,128)(2,1)S(1)} %collective-permute-done.16.refs_1_) | copy-start | bytes 393220
  71.9 5.0 %collective-permute-start.18 = (bf16[512,128]{1,0:T(8,128)(2,1)S(1)}, bf16[512,128]{1,0:T(8,128)(2,1)S(1)}, u32[]{:S(2)}, u32[]{:S(2)}) collective-permute-start(bf16[512,128]{1,0:T(8,128)(2,1)S(1)} %collective-permute-done.16.refs_1_), channel_id=1, source_target_pairs={{0,2},{1,3},{2,0},{3,1},{4,6},{5,7},{6,4},{7,5},{8,10},{9,11},{10,... | collective-permute-start | bytes 393224 | tf_op jit(solution)/shard_map/ppermute | solution.py:41
  73.6 6.2 %copy-start.8 = (bf16[512,128]{1,0:T(8,128)(2,1)}, bf16[512,128]{1,0:T(8,128)(2,1)S(1)}, u32[]{:S(2)}) copy-start(bf16[512,128]{1,0:T(8,128)(2,1)S(1)} %collective-permute-done.17.refs_2_) | copy-start | bytes 393220
  73.6 6.0 %collective-permute-start.31 = (bf16[512,128]{1,0:T(8,128)(2,1)S(1)}, bf16[512,128]{1,0:T(8,128)(2,1)S(1)}, u32[]{:S(2)}, u32[]{:S(2)}) collective-permute-start(bf16[512,128]{1,0:T(8,128)(2,1)S(1)} %collective-permute-done.23.refs_6_), channel_id=1, source_target_pairs={{0,16},{16,0},{1,17},{17,1},{2,18},{18,2},{3,19},{19,3},{4,20},{20... | collective-permute-start | bytes 393224 | tf_op jit(solution)/shard_map/ppermute | solution.py:45
  73.6 6.1 %copy-start.9 = (bf16[512,128]{1,0:T(8,128)(2,1)}, bf16[512,128]{1,0:T(8,128)(2,1)S(1)}, u32[]{:S(2)}) copy-start(bf16[512,128]{1,0:T(8,128)(2,1)S(1)} %collective-permute-done.25.refs_8_) | copy-start | bytes 393220
  73.6 6.0 %collective-permute-start.26 = (bf16[512,128]{1,0:T(8,128)(2,1)S(1)}, bf16[512,128]{1,0:T(8,128)(2,1)S(1)}, u32[]{:S(2)}, u32[]{:S(2)}) collective-permute-start(bf16[512,128]{1,0:T(8,128)(2,1)S(1)} %collective-permute-done.16.refs_1_), channel_id=1, source_target_pairs={{0,16},{16,0},{1,17},{17,1},{2,18},{18,2},{3,19},{19,3},{4,20},{20... | collective-permute-start | bytes 393224 | tf_op jit(solution)/shard_map/ppermute | solution.py:45
  74.5 5.2 %copy-start.10 = (bf16[512,128]{1,0:T(8,128)(2,1)}, bf16[512,128]{1,0:T(8,128)(2,1)S(1)}, u32[]{:S(2)}) copy-start(bf16[512,128]{1,0:T(8,128)(2,1)S(1)} %collective-permute-done.24.refs_7_) | copy-start | bytes 393220
  74.5 5.1 %collective-permute-start.27 = (bf16[512,128]{1,0:T(8,128)(2,1)S(1)}, bf16[512,128]{1,0:T(8,128)(2,1)S(1)}, u32[]{:S(2)}, u32[]{:S(2)}) collective-permute-start(bf16[512,128]{1,0:T(8,128)(2,1)S(1)} %collective-permute-done.17.refs_2_), channel_id=1, source_target_pairs={{0,16},{16,0},{1,17},{17,1},{2,18},{18,2},{3,19},{19,3},{4,20},{20... | collective-permute-start | bytes 393224 | tf_op jit(solution)/shard_map/ppermute | solution.py:45
  74.5 5.2 %copy-start.11 = (bf16[512,128]{1,0:T(8,128)(2,1)}, bf16[512,128]{1,0:T(8,128)(2,1)S(1)}, u32[]{:S(2)}) copy-start(bf16[512,128]{1,0:T(8,128)(2,1)S(1)} %collective-permute-done.30.refs_13_) | copy-start | bytes 393220
  74.5 5.1 %collective-permute-start.32 = (bf16[512,128]{1,0:T(8,128)(2,1)S(1)}, bf16[512,128]{1,0:T(8,128)(2,1)S(1)}, u32[]{:S(2)}, u32[]{:S(2)}) collective-permute-start(bf16[512,128]{1,0:T(8,128)(2,1)S(1)} %collective-permute-done.24.refs_7_), channel_id=1, source_target_pairs={{0,16},{16,0},{1,17},{17,1},{2,18},{18,2},{3,19},{19,3},{4,20},{20... | collective-permute-start | bytes 393224 | tf_op jit(solution)/shard_map/ppermute | solution.py:45
  76.9 2.9 %copy-start.12 = (bf16[512,128]{1,0:T(8,128)(2,1)}, bf16[512,128]{1,0:T(8,128)(2,1)S(1)}, u32[]{:S(2)}) copy-start(bf16[512,128]{1,0:T(8,128)(2,1)S(1)} %collective-permute-done.18.refs_3_) | copy-start | bytes 393220
  76.9 2.7 %collective-permute-start.28 = (bf16[512,128]{1,0:T(8,128)(2,1)S(1)}, bf16[512,128]{1,0:T(8,128)(2,1)S(1)}, u32[]{:S(2)}, u32[]{:S(2)}) collective-permute-start(bf16[512,128]{1,0:T(8,128)(2,1)S(1)} %collective-permute-done.18.refs_3_), channel_id=1, source_target_pairs={{0,16},{16,0},{1,17},{17,1},{2,18},{18,2},{3,19},{19,3},{4,20},{20... | collective-permute-start | bytes 393224 | tf_op jit(solution)/shard_map/ppermute | solution.py:45
  93.4 4.6 %copy-start.3 = (bf16[256,1024]{1,0:T(8,128)(2,1)S(1)}, bf16[256,1024]{1,0:T(8,128)(2,1)}, u32[]{:S(2)}) copy-start(bf16[256,1024]{1,0:T(8,128)(2,1)} %get-tuple-element.17) | copy-start | bytes 1572868
  93.5 2.3 %collective-permute-start.33 = (bf16[256,1024]{1,0:T(8,128)(2,1)}, bf16[256,1024]{1,0:T(8,128)(2,1)S(1)}, u32[]{:S(2)}, u32[]{:S(2)}) collective-permute-start(bf16[256,1024]{1,0:T(8,128)(2,1)} %get-tuple-element.16), channel_id=1, source_target_pairs={{0,16},{16,0},{1,17},{17,1},{2,18},{18,2},{3,19},{19,3},{4,20},{20... | collective-permute-start | bytes 1572872 | tf_op jit(solution)/shard_map/ppermute | solution.py:45
  94.0 4.1 %collective-permute-start.39 = (bf16[256,1024]{1,0:T(8,128)(2,1)}, bf16[256,1024]{1,0:T(8,128)(2,1)S(1)}, u32[]{:S(2)}, u32[]{:S(2)}) collective-permute-start(bf16[256,1024]{1,0:T(8,128)(2,1)} %get-tuple-element.18), channel_id=1, source_target_pairs={{0,16},{16,0},{1,17},{17,1},{2,18},{18,2},{3,19},{19,3},{4,20},{20... | collective-permute-start | bytes 1572872 | tf_op jit(solution)/shard_map/ppermute | solution.py:45
  97.0 8.7 %collective-permute-start.34 = (bf16[128,1024]{1,0:T(8,128)(2,1)S(1)}, bf16[128,1024]{1,0:T(8,128)(2,1)S(1)}, u32[]{:S(2)}, u32[]{:S(2)}) collective-permute-start(bf16[128,1024]{1,0:T(8,128)(2,1)S(1)} %slice.155), channel_id=1, source_target_pairs={{0,1},{1,0},{2,3},{3,2},{4,5},{5,4},{6,7},{7,6},{8,9},{9,8},{10,11... | collective-permute-start | bytes 786440 | tf_op jit(solution)/shard_map/ppermute | solution.py:41
  98.3 9.2 %collective-permute-start.40 = (bf16[128,1024]{1,0:T(8,128)(2,1)S(1)}, bf16[128,1024]{1,0:T(8,128)(2,1)S(1)}, u32[]{:S(2)}, u32[]{:S(2)}) collective-permute-start(bf16[128,1024]{1,0:T(8,128)(2,1)S(1)} %slice.154), channel_id=1, source_target_pairs={{0,2},{1,3},{2,0},{3,1},{4,6},{5,7},{6,4},{7,5},{8,10},{9,11},{10,... | collective-permute-start | bytes 786440 | tf_op jit(solution)/shard_map/ppermute | solution.py:41
  105.7 16.1 %copy-start.19 = (bf16[16,4096]{1,0:T(8,128)(2,1)S(1)}, bf16[16,4096]{1,0:T(8,128)(2,1)}, u32[]{:S(2)}) copy-start(bf16[16,4096]{1,0:T(8,128)(2,1)} %get-tuple-element.14) | copy-start | bytes 393220
  105.7 5.0 %collective-permute-start.35 = (bf16[64,1024]{1,0:T(8,128)(2,1)S(1)}, bf16[64,1024]{1,0:T(8,128)(2,1)S(1)}, u32[]{:S(2)}, u32[]{:S(2)}) collective-permute-start(bf16[64,1024]{1,0:T(8,128)(2,1)S(1)} %slice.157), channel_id=1, source_target_pairs={{0,2},{1,3},{2,0},{3,1},{4,6},{5,7},{6,4},{7,5},{8,10},{9,11},{10,... | collective-permute-start | bytes 393224 | tf_op jit(solution)/shard_map/ppermute | solution.py:41
  107.5 7.8 %collective-permute-start.41 = (bf16[64,1024]{1,0:T(8,128)(2,1)S(1)}, bf16[64,1024]{1,0:T(8,128)(2,1)S(1)}, u32[]{:S(2)}, u32[]{:S(2)}) collective-permute-start(bf16[64,1024]{1,0:T(8,128)(2,1)S(1)} %slice.156), channel_id=1, source_target_pairs={{0,1},{1,0},{2,3},{3,2},{4,5},{5,4},{6,7},{7,6},{8,9},{9,8},{10,11... | collective-permute-start | bytes 393224 | tf_op jit(solution)/shard_map/ppermute | solution.py:41
  110.8 6.1 %collective-permute-start.36 = (bf16[16,1024]{1,0:T(8,128)(2,1)S(1)}, bf16[16,1024]{1,0:T(8,128)(2,1)S(1)}, u32[]{:S(2)}, u32[]{:S(2)}) collective-permute-start(bf16[16,1024]{1,0:T(8,128)(2,1)S(1)} %get-tuple-element.23), channel_id=1, source_target_pairs={{0,4},{1,5},{2,6},{3,7},{4,8},{5,9},{6,10},{7,11},{8,12},{9,13},{1... | collective-permute-start | bytes 98312 | tf_op jit(solution)/shard_map/ppermute | solution.py:41
  111.1 8.7 %collective-permute-start.37 = (bf16[16,1024]{1,0:T(8,128)(2,1)S(1)}, bf16[16,1024]{1,0:T(8,128)(2,1)S(1)}, u32[]{:S(2)}, u32[]{:S(2)}) collective-permute-start(bf16[16,1024]{1,0:T(8,128)(2,1)S(1)} %get-tuple-element.25), channel_id=1, source_target_pairs={{0,8},{1,9},{2,10},{3,11},{4,12},{5,13},{6,14},{7,15},{8,0},{9,1},... | collective-permute-start | bytes 98312 | tf_op jit(solution)/shard_map/ppermute | solution.py:41
  113.3 6.5 %collective-permute-start.38 = (bf16[16,1024]{1,0:T(8,128)(2,1)S(1)}, bf16[16,1024]{1,0:T(8,128)(2,1)S(1)}, u32[]{:S(2)}, u32[]{:S(2)}) collective-permute-start(bf16[16,1024]{1,0:T(8,128)(2,1)S(1)} %get-tuple-element.24), channel_id=1, source_target_pairs={{0,12},{1,13},{2,14},{3,15},{4,0},{5,1},{6,2},{7,3},{8,4},{9,5},{1... | collective-permute-start | bytes 98312 | tf_op jit(solution)/shard_map/ppermute | solution.py:41
  115.4 5.8 %collective-permute-start.42 = (bf16[16,1024]{1,0:T(8,128)(2,1)S(1)}, bf16[16,1024]{1,0:T(8,128)(2,1)S(1)}, u32[]{:S(2)}, u32[]{:S(2)}) collective-permute-start(bf16[16,1024]{1,0:T(8,128)(2,1)S(1)} %get-tuple-element.26), channel_id=1, source_target_pairs={{0,4},{1,5},{2,6},{3,7},{4,8},{5,9},{6,10},{7,11},{8,12},{9,13},{1... | collective-permute-start | bytes 98312 | tf_op jit(solution)/shard_map/ppermute | solution.py:41
  115.5 5.7 %collective-permute-start.43 = (bf16[16,1024]{1,0:T(8,128)(2,1)S(1)}, bf16[16,1024]{1,0:T(8,128)(2,1)S(1)}, u32[]{:S(2)}, u32[]{:S(2)}) collective-permute-start(bf16[16,1024]{1,0:T(8,128)(2,1)S(1)} %get-tuple-element.28), channel_id=1, source_target_pairs={{0,8},{1,9},{2,10},{3,11},{4,12},{5,13},{6,14},{7,15},{8,0},{9,1},... | collective-permute-start | bytes 98312 | tf_op jit(solution)/shard_map/ppermute | solution.py:41
  116.9 4.8 %collective-permute-start.44 = (bf16[16,1024]{1,0:T(8,128)(2,1)S(1)}, bf16[16,1024]{1,0:T(8,128)(2,1)S(1)}, u32[]{:S(2)}, u32[]{:S(2)}) collective-permute-start(bf16[16,1024]{1,0:T(8,128)(2,1)S(1)} %get-tuple-element.27), channel_id=1, source_target_pairs={{0,12},{1,13},{2,14},{3,15},{4,0},{5,1},{6,2},{7,3},{8,4},{9,5},{1... | collective-permute-start | bytes 98312 | tf_op jit(solution)/shard_map/ppermute | solution.py:41
  121.8 1.3 %collective-permute-start.45 = (bf16[16,2048]{1,0:T(8,128)(2,1)S(1)}, bf16[16,2048]{1,0:T(8,128)(2,1)S(1)}, u32[]{:S(2)}, u32[]{:S(2)}) collective-permute-start(bf16[16,2048]{1,0:T(8,128)(2,1)S(1)} %fusion.17), channel_id=1, source_target_pairs={{0,16},{16,0},{1,17},{17,1},{2,18},{18,2},{3,19},{19,3},{4,20},{20... | collective-permute-start | bytes 196616 | tf_op jit(solution)/shard_map/ppermute | solution.py:45
  (5 other events, 3.7 us)

commit v2 on v0

v2 whole, which is shorter than its diff:
```python
import functools
import math

import jax
import jax.numpy as jnp
from jax import lax
from jax.experimental import pallas as pl
from jax.experimental.pallas import tpu as pltpu
from jax.sharding import PartitionSpec as P

HEAD = 128
masked_score = -1e30
BF = jnp.bfloat16
F32 = jnp.float32


def grid_of(n):
    known = {16: (4, 2, 2), 64: (4, 4, 4)}
    return known.get(n, (n, 1, 1))


def code_of(dims, kz, ky, kx):
    return (kz * dims[1] + ky) * dims[2] + kx


def trade(value, dims, kz=0, ky=0, kx=0):
    code = code_of(dims, kz, ky, kx)
    n = dims[0] * dims[1] * dims[2]
    return lax.ppermute(value, "dev", [(d, d ^ code) for d in range(n)])


def along_z(dims):
    return sorted(range(1, dims[0]), key=lambda k: (k == 1, k))


def swap_sec(value):
    return lax.ppermute(value, "sec", [(0, 1), (1, 0)])


def planes(a, b, dims):
    _, ny, nx = dims
    first, second, third = [], [], []
    near_a = {kx: trade(a, dims, kx=kx) for kx in range(1, nx)}
    near_b = {ky: trade(b, dims, ky=ky) for ky in range(1, ny)}
    first += [((0, kx), 0, v) for kx, v in near_a.items()]
    first += [((ky, 0), 1, v) for ky, v in near_b.items()]
    second += [((ky, 0), 0, trade(a, dims, ky=ky)) for ky in range(1, ny)]
    second += [((0, kx), 1, trade(b, dims, kx=kx)) for kx in range(1, nx)]
    third += [
        ((ky, kx), 0, trade(v, dims, ky=ky)) for kx, v in near_a.items() for ky in range(1, ny)
    ]
    third += [
        ((ky, kx), 1, trade(v, dims, kx=kx)) for ky, v in near_b.items() for kx in range(1, nx)
    ]
    return first, second, third


ANY = pl.BlockSpec(memory_space=pl.ANY)
VM = pl.BlockSpec(memory_space=pltpu.VMEM)
HBM = pl.BlockSpec(memory_space=pltpu.HBM)
MIB = 1024 * 1024


def project_kernel(pieces, rows, count, *refs):
    arrays = refs[:count]
    w_ref, keep_ref, send_ref, held, sems = refs[count:]
    half = held.shape[1] // 2
    me = lax.axis_index("dev")
    sec = lax.axis_index("sec")
    copies = []
    for i, (which, offset, code, column) in enumerate(pieces):
        place = pl.multiple_of((me ^ code) * rows, rows)
        copies.append(
            pltpu.make_async_copy(
                arrays[which].at[pl.ds(offset, rows), pl.ds(0, half)],
                held.at[pl.ds(place, rows), pl.ds(column * half, half)],
                sems.at[i],
            )
        )
    for c in copies:
        c.start()
    for c in copies:
        c.wait()
    total = jnp.dot(held[...], w_ref[...], preferred_element_type=F32)
    part = total.shape[1] // 2
    low, high = total[:, :part], total[:, part:]
    keep_ref[...] = jnp.where(sec == 0, low, high)
    send_ref[...] = jnp.where(sec == 0, high, low)


def project(arrays, pieces, weight, n, rows):
    depth, cols = weight.shape
    out = jax.ShapeDtypeStruct((n * rows, cols // 2), F32)
    return pl.pallas_call(
        functools.partial(project_kernel, pieces, rows, len(arrays)),
        out_shape=(out, out),
        in_specs=[ANY] * len(arrays) + [VM],
        out_specs=(VM, VM),
        scratch_shapes=[
            pltpu.VMEM((n * rows, depth), BF),
            pltpu.SemaphoreType.DMA((len(pieces),)),
        ],
        compiler_params=pltpu.CompilerParams(vmem_limit_bytes=(4 + n // 2) * MIB),
        cost_estimate=pl.CostEstimate(
            flops=2 * n * rows * depth * cols,
            bytes_accessed=2 * depth * (cols + n * rows),
            transcendentals=0,
        ),
        name="project",
    )(*arrays, weight)


STEPS = 8


def expert_kernel(dims, pieces, rows, eps, count, *refs):
    nz, ny, nx = dims
    arrays = refs[:count]
    (
        mask_ref,
        gain_ref,
        router_ref,
        gate_ref,
        up_ref,
        down_ref,
        keep_near,
        keep_far,
        send_near,
        send_far,
        own_ref,
        held,
        acc,
        route_acc,
        square,
        hidden,
        hidden_a,
        hidden_b,
        xsems,
    ) = refs[count:]
    width = held.shape[1]
    units = down_ref.shape[1]
    part = width // (nz * ny * nx) // 2
    me = lax.axis_index("dev")
    sec = lax.axis_index("sec")
    step = width // STEPS

    copies = []
    if not pieces:
        copies.append(pltpu.make_async_copy(arrays[0], held, xsems.at[0]))
    for i, (which, offset, length, code, side, start) in enumerate(pieces):
        whose = sec if side == 0 else 1 - sec
        column = pl.multiple_of(((me ^ code) * 2 + whose) * part, part)
        copies.append(
            pltpu.make_async_copy(
                arrays[which].at[pl.ds(offset, length)],
                held.at[pl.ds(start, length), pl.ds(column, part)],
                xsems.at[i],
            )
        )
    for c in copies:
        c.start()
    for c in copies:
        c.wait()
    acc[...] = jnp.zeros_like(acc)
    route_acc[...] = jnp.zeros_like(route_acc)
    square[...] = jnp.zeros_like(square)

    def body(c, carry):
        span = pl.ds(pl.multiple_of(c * step, step), step)
        x = held[:, span].astype(F32)
        total = square[...]
        for t in range(step // 128):
            piece = x[:, t * 128 : (t + 1) * 128]
            total = total + piece * piece
        square[...] = total
        scaled = (x * gain_ref[:, span]).astype(BF)
        both = jnp.concatenate([gate_ref[0, span], up_ref[0, span]], axis=1)
        acc[...] += jnp.dot(scaled, both, preferred_element_type=F32)
        route_acc[...] += lax.dot_general(
            scaled, router_ref[:, span], (((1,), (1,)), ((), ())), preferred_element_type=F32
        )
        return carry

    lax.fori_loop(0, STEPS, body, 0)
    mean = jnp.sum(square[...], axis=1, keepdims=True) * (1.0 / width)
    inverse = lax.rsqrt(mean + eps)
    live = mask_ref[:, : route_acc.shape[1]].astype(F32) > 0.5
    logits = jnp.where(live, route_acc[...] * inverse, masked_score)
    top = jnp.max(logits, axis=1, keepdims=True)
    powers = jnp.where(live, jnp.exp(logits - top), 0.0)
    lane = lax.broadcasted_iota(jnp.int32, powers.shape, 1)
    mine = jnp.sum(jnp.where(lane == me, powers, 0.0), axis=1, keepdims=True)
    weight = mine / jnp.sum(powers, axis=1, keepdims=True)
    gate = acc[:, :units] * inverse
    up = acc[:, units:] * inverse
    hidden[...] = (gate / (1.0 + jnp.exp(-gate)) * up * weight).astype(BF)
    own_ref[...] = held[pl.ds(pl.multiple_of(me * rows, rows), rows)]
    for kz in range(nz):
        for ky in range(ny):
            for kx in range(nx):
                place = pl.multiple_of((me ^ code_of(dims, kz, ky, kx)) * rows, rows)
                block = hidden[pl.ds(place, rows)]
                hidden_a[pl.ds(((kx * ny + ky) * nz + kz) * rows, rows)] = block
                hidden_b[pl.ds(((ky * nx + kx) * nz + kz) * rows, rows)] = block
    quarter = width // 4
    wide = quarter // 2
    for h, near, far in ((1, send_near, send_far), (0, keep_near, keep_far)):
        near_cut = hidden.shape[0] // nx
        far_cut = hidden.shape[0] - near_cut
        for q, (source, first) in enumerate(((hidden_a, nx), (hidden_b, ny))):
            cut = source.shape[0] // first
            rest = source.shape[0] - cut
            for t in range(2):
                whose = sec if h == 0 else 1 - sec
                place = pl.multiple_of(whose * 2 * quarter + q * quarter + t * wide, wide)
                found = jnp.dot(
                    source[...],
                    down_ref[0, :, pl.ds(place, wide)],
                    preferred_element_type=F32,
                ).astype(BF)
                span = slice(t * wide, (t + 1) * wide)
                near[q * near_cut : q * near_cut + cut, span] = found[:cut]
                far[q * far_cut : q * far_cut + rest, span] = found[cut:]


def in_order(arrays, pieces, n, total_rows, part):
    me = lax.axis_index("dev")
    sec = lax.axis_index("sec")
    held = jnp.zeros((total_rows, n * 2 * part), BF)
    for which, offset, length, code, side, start in pieces:
        whose = sec if side == 0 else 1 - sec
        column = ((me ^ code) * 2 + whose) * part
        held = lax.dynamic_update_slice(
            held, arrays[which][offset : offset + length], (start, column)
        )
    return held


def experts(arrays, pieces, mask, gain, router, gate, up, down, dims, rows):
    nz, ny, nx = dims
    n = nz * ny * nx
    total_rows = n * rows
    _, width, units = gate.shape
    quarter = width // 4
    lanes = router.shape[0]
    near = total_rows // nx + total_rows // ny
    far = 2 * total_rows - near
    part = width // n // 2
    if part % 128:
        arrays = [in_order(arrays, pieces, n, total_rows, part)]
        pieces = ()
    shapes = [jax.ShapeDtypeStruct((r, quarter), BF) for r in (near, far, near, far)]
    return pl.pallas_call(
        functools.partial(expert_kernel, dims, pieces, rows, 1e-6, len(arrays)),
        out_shape=(*shapes, jax.ShapeDtypeStruct((rows, width), BF)),
        in_specs=[ANY] * len(arrays) + [VM] * 6,
        out_specs=(VM,) * 5,
        scratch_shapes=[
            pltpu.VMEM((total_rows, width), BF),
            pltpu.VMEM((total_rows, 2 * units), F32),
            pltpu.VMEM((total_rows, lanes), F32),
            pltpu.VMEM((total_rows, 128), F32),
            pltpu.VMEM((total_rows, units), BF),
            pltpu.VMEM((total_rows, units), BF),
            pltpu.VMEM((total_rows, units), BF),
            pltpu.SemaphoreType.DMA((max(1, len(pieces)),)),
        ],
        compiler_params=pltpu.CompilerParams(vmem_limit_bytes=(6 + n // 2) * MIB),
        cost_estimate=pl.CostEstimate(
            flops=6 * total_rows * width * units,
            bytes_accessed=6 * width * units + 6 * total_rows * width,
            transcendentals=0,
        ),
        name="experts",
    )(*arrays, mask, gain, router, gate, up, down)


GROUP = 4
CHUNK = 128


def attend_kernel(dims, lanes, *refs):
    (
        len_ref,
        ids_ref,
        q_ref,
        nk_ref,
        nv_ref,
        extra_ref,
        k_ref,
        v_ref,
        *outs,
        keys,
        values,
        apart,
        joined,
        ksems,
        vsems,
    ) = refs
    b_ref, sends = outs[0], outs[1:]
    rows, span, cols = keys.shape
    heads = q_ref.shape[1] // HEAD
    half = b_ref.shape[1]
    groups = cols // HEAD
    per = heads // groups
    me = lax.axis_index("dev")
    sec = lax.axis_index("sec")

    def fetch(r, source, target, sem):
        live = (len_ref[r] + CHUNK - 1) // CHUNK * CHUNK
        part = pl.ds(0, pl.multiple_of(live, CHUNK))
        return pltpu.make_async_copy(source.at[r, part], target.at[r, part], sem.at[r])

    for start in range(0, rows, GROUP):
        for r in range(start, start + GROUP):
            fetch(r, k_ref, keys, ksems).start()
        values[pl.ds(start, GROUP)] = jnp.zeros((GROUP, span, cols), BF)
        for r in range(start, start + GROUP):
            fetch(r, v_ref, values, vsems).start()

    lane_ids = lax.broadcasted_iota(jnp.int32, (lanes, rows), 0)
    chosen = jnp.zeros((lanes, rows), F32)
    for k in range(ids_ref.shape[0]):
        chosen = jnp.where(lane_ids == ids_ref[k : k + 1, :], 1.0, chosen)
    chosen = chosen.T.astype(BF)
    plane = dims[1] * dims[2]
    for kz in range(dims[0]):
        target = sends[kz]
        for c in range(plane):
            owner = me ^ (kz * plane + c)
            if len(extra_ref.shape) == 3:
                block = extra_ref[owner]
            else:
                place = pl.multiple_of((owner * 2 + sec) * 128, 128)
                block = extra_ref[:, pl.ds(place, 128)]
            target[:, half + c * 128 : half + (c + 1) * 128] = block
        target[:, half + plane * 128 :] = chosen

    for h in range(heads):
        apart[pl.ds(h * rows, rows)] = q_ref[:, h * HEAD : (h + 1) * HEAD].astype(F32)
    fresh_k = nk_ref[...].astype(F32)
    fresh_v = nv_ref[...].astype(F32)
    head = lax.broadcasted_iota(jnp.int32, (heads, HEAD), 0)
    belongs = [(head >= g * per) & (head < (g + 1) * per) for g in range(groups)]
    place = lax.broadcasted_iota(jnp.int32, (heads, span), 1)
    scale = 1.0 / math.sqrt(HEAD)

    def of_group(wide):
        found = jnp.broadcast_to(wide[:, :HEAD], (heads, HEAD))
        for g in range(1, groups):
            piece = wide[:, g * HEAD : (g + 1) * HEAD]
            found = jnp.where(belongs[g], jnp.broadcast_to(piece, (heads, HEAD)), found)
        return found

    for start in range(0, rows, GROUP):
        group = range(start, start + GROUP)
        for r in group:
            fetch(r, k_ref, keys, ksems).wait()
            fetch(r, v_ref, values, vsems).wait()
        queries, scores = {}, {}
        for r in group:
            q = apart[pl.ds(r, heads, stride=rows), :]
            queries[r] = q
            wide = jnp.concatenate([jnp.where(m, q, 0.0) for m in belongs], axis=1)
            scores[r] = lax.dot_general(
                wide.astype(BF), keys[r], (((1,), (1,)), ((), ())), preferred_element_type=F32
            )
        for r in group:
            s = jnp.where(place < len_ref[r], scores[r] * scale, masked_score)
            own = jnp.sum(queries[r] * of_group(fresh_k[r : r + 1]), axis=1, keepdims=True) * scale
            top = jnp.maximum(jnp.max(s, axis=1, keepdims=True), own)
            power = jnp.exp(s - top)
            own_power = jnp.exp(own - top)
            total = jnp.sum(power, axis=1, keepdims=True) + own_power
            mixed = jnp.dot(power.astype(BF), values[r], preferred_element_type=F32)
            picked = mixed[:, :HEAD]
            for g in range(1, groups):
                picked = jnp.where(belongs[g], mixed[:, g * HEAD : (g + 1) * HEAD], picked)
            picked = (picked + own_power * of_group(fresh_v[r : r + 1])) / total
            joined[pl.ds(r, heads, stride=rows), :] = picked
    for h in range(heads):
        block = joined[pl.ds(h * rows, rows)].astype(BF)
        at = h * HEAD
        for target in sends if at < half else (b_ref,):
            target[:, at % half : at % half + HEAD] = block


def attention(
    queries, key_cache, value_cache, new_key, new_value, cache_lengths, ids, extra, lanes, dims
):
    rows, span, cols = key_cache.shape
    width = queries.shape[1]
    heads = width // HEAD
    half = width // 2
    side = dims[1] * dims[2] * 128 + lanes
    outs = [(rows, half)] + [(rows, half + side)] * dims[0]
    return pl.pallas_call(
        functools.partial(attend_kernel, dims, lanes),
        out_shape=tuple(jax.ShapeDtypeStruct(o, BF) for o in outs),
        in_specs=[pl.BlockSpec(memory_space=pltpu.SMEM)] + [VM] * 5 + [HBM, HBM],
        out_specs=(VM,) * len(outs),
        scratch_shapes=[
            pltpu.VMEM((rows, span, cols), BF),
            pltpu.VMEM((rows, span, cols), BF),
            pltpu.VMEM((rows * heads, HEAD), F32),
            pltpu.VMEM((rows * heads, HEAD), F32),
            pltpu.SemaphoreType.DMA((rows,)),
            pltpu.SemaphoreType.DMA((rows,)),
        ],
        compiler_params=pltpu.CompilerParams(vmem_limit_bytes=60 * MIB),
        cost_estimate=pl.CostEstimate(
            flops=4 * rows * heads * span * cols,
            bytes_accessed=4 * rows * span * cols,
            transcendentals=rows * heads * span,
        ),
        name="attend",
    )(cache_lengths, ids, queries, new_key, new_value, extra, key_cache, value_cache)


def pack_kernel(dims, lanes, *refs):
    nz, ny, nx = dims
    lines, outs = refs[:nz], refs[nz:]
    mine_ref, xa, ya = outs[0], outs[1 : nx], outs[nx:]
    rows = lines[0].shape[0]
    plane = ny * nx * 128
    half = lines[0].shape[1] - plane - lanes
    for kz in range(nz):
        span = slice(kz * rows, (kz + 1) * rows)
        source = lines[kz]

        def block(ky, kx):
            at = half + (ky * nx + kx) * 128
            return source[:, at : at + 128]

        a, mask = source[:, :half], source[:, half + plane :]
        mine_ref[span, :half] = a
        mine_ref[span, half : half + 128] = block(0, 0)
        mine_ref[span, half + 128 :] = mask
        for kx in range(1, nx):
            xa[kx - 1][span, :half] = a
            for ky in range(ny):
                xa[kx - 1][span, half + ky * 128 : half + (ky + 1) * 128] = block(ky, kx)
            xa[kx - 1][span, half + ny * 128 :] = mask
        for ky in range(1, ny):
            ya[ky - 1][span, :half] = a
            ya[ky - 1][span, half : half + 128] = block(ky, 0)
            ya[ky - 1][span, half + 128 :] = mask


def pack(lines, lanes, dims):
    nz, ny, nx = dims
    rows, width = lines[0].shape
    half = width - ny * nx * 128 - lanes
    widths = [half + 128 + lanes]
    widths += [half + ny * 128 + lanes] * (nx - 1)
    widths += [half + 128 + lanes] * (ny - 1)
    outs = pl.pallas_call(
        functools.partial(pack_kernel, dims, lanes),
        out_shape=tuple(jax.ShapeDtypeStruct((nz * rows, w), BF) for w in widths),
        in_specs=[VM] * nz,
        out_specs=(VM,) * len(widths),
        compiler_params=pltpu.CompilerParams(vmem_limit_bytes=16 * MIB),
        name="pack",
    )(*lines)
    return outs[0], outs[1:nx], outs[nx:]


def arrange_kernel(pieces, rows, count, *refs):
    arrays, outs, sems = refs[:count], refs[count : count + 2], refs[count + 2]
    me = lax.axis_index("dev")
    copies = []
    for i, (which, offset, code, column, target) in enumerate(pieces):
        place = pl.multiple_of((me ^ code) * rows, rows)
        out = outs[target]
        copies.append(
            pltpu.make_async_copy(
                arrays[which].at[pl.ds(offset, rows), pl.ds(column, out.shape[1])],
                out.at[pl.ds(place, rows)],
                sems.at[i],
            )
        )
    for c in copies:
        c.start()
    for c in copies:
        c.wait()


def arrange(arrays, pieces, lanes, n, rows):
    return pl.pallas_call(
        functools.partial(arrange_kernel, pieces, rows, len(arrays)),
        out_shape=tuple(jax.ShapeDtypeStruct((n * rows, w), BF) for w in (128, lanes)),
        in_specs=[ANY] * len(arrays),
        out_specs=(VM, VM),
        scratch_shapes=[pltpu.SemaphoreType.DMA((len(pieces),))],
        compiler_params=pltpu.CompilerParams(vmem_limit_bytes=8 * MIB),
        name="arrange",
    )(*arrays)


def local(
    dims,
    queries,
    key_cache,
    value_cache,
    new_key,
    new_value,
    cache_lengths,
    residual_in,
    out_weight,
    norm_gain,
    router_weight,
    expert_ids,
    gate_weight,
    up_weight,
    down_weight,
):
    nz, ny, nx = dims
    n = nz * ny * nx
    rows, width = residual_in.shape
    total_rows = n * rows
    expert_total = router_weight.shape[1]
    sec = lax.axis_index("sec")
    lanes = -(-expert_total // 128) * 128
    part = width // n // 2

    if part % 128:
        extra = lax.dynamic_index_in_dim(
            residual_in.reshape(rows, n, 2, part), sec, axis=2, keepdims=False
        )
        extra = jnp.pad(jnp.swapaxes(extra, 0, 1), ((0, 0), (0, 0), (0, 128 - part)))
    else:
        extra = residual_in
    b_own, *a_own = attention(
        queries,
        key_cache,
        value_cache,
        new_key,
        new_value,
        cache_lengths,
        expert_ids.T,
        extra,
        lanes,
        dims,
    )
    middle = b_own.shape[1]

    steps = along_z(dims)
    a_lines = {kz: trade(a_own[kz], dims, kz=kz) for kz in steps}
    b_own, a_lines[steps[-1]] = lax.optimization_barrier((b_own, a_lines[steps[-1]]))
    b_lines = {kz: trade(b_own, dims, kz=kz) for kz in steps}
    mine, xa, ya = pack([a_own[0]] + [a_lines[kz] for kz in range(1, nz)], lanes, dims)
    arrays, pieces, places = [], [], []

    def add(array, ky, kx, column, block=None, mask=None):
        arrays.append(array)
        for kz in range(nz):
            code = code_of(dims, kz, ky, kx)
            pieces.append((len(arrays) - 1, kz * rows, code, column))
            if block is not None:
                places.append((len(arrays) - 1, kz * rows, code, block, 0))
                places.append((len(arrays) - 1, kz * rows, code, mask, 1))

    add(mine, 0, 0, 0, middle, middle + 128)
    near_a = {kx: trade(xa[kx - 1], dims, kx=kx) for kx in range(1, nx)}
    for kx, v in near_a.items():
        add(v, 0, kx, 0, middle, middle + ny * 128)
    for ky in range(1, ny):
        add(trade(ya[ky - 1], dims, ky=ky), ky, 0, 0, middle, middle + 128)
    b = jnp.concatenate([b_own] + [b_lines[kz] for kz in range(1, nz)], axis=0)
    add(b, 0, 0, 1)
    near_b = {ky: trade(b, dims, ky=ky) for ky in range(1, ny)}
    for ky, v in near_b.items():
        add(v, ky, 0, 1)
    for kx in range(1, nx):
        add(trade(b, dims, kx=kx), 0, kx, 1)
    for kx, v in near_a.items():
        for ky in range(1, ny):
            add(trade(v, dims, ky=ky), ky, kx, 0, middle + ky * 128, middle + ny * 128)
    for ky, v in near_b.items():
        for kx in range(1, nx):
            add(trade(v, dims, kx=kx), ky, kx, 1)
    keep, send = project(arrays, tuple(pieces), out_weight, n, rows)
    residual, mask = arrange(arrays, tuple(places), lanes, n, rows)
    residual = residual[:, :part]
    projected = (keep + swap_sec(send)).astype(BF)
    mixed = (residual.astype(F32) + projected.astype(F32)).astype(BF)

    half_rows = total_rows // 2
    lines = {kz: trade(mixed, dims, kz=kz) for kz in steps}
    stacked = jnp.concatenate([mixed] + [lines[kz] for kz in range(1, nz)], axis=0)
    arrays, pieces = [stacked, swap_sec(stacked)], []
    for side in range(2):
        for kz in range(nz):
            pieces.append((side, kz * total_rows, total_rows, code_of(dims, kz, 0, 0), side, 0))
    parted = stacked.reshape(nz, 2, half_rows, part)
    a, b = (parted[:, h].reshape(nz * half_rows, part) for h in range(2))
    for wave in planes(a, b, dims):
        whole = swap_sec(jnp.concatenate([array for _, _, array in wave], axis=0))
        for i, ((ky, kx), half, array) in enumerate(wave):
            for which, base, side in ((len(arrays), 0, 0), (None, i * nz * half_rows, 1)):
                for kz in range(nz):
                    pieces.append(
                        (
                            which if side == 0 else -1,
                            base + kz * half_rows,
                            half_rows,
                            code_of(dims, kz, ky, kx),
                            side,
                            half * half_rows,
                        )
                    )
            arrays.append(array)
        arrays.append(whole)
        pieces = [
            (len(arrays) - 1 if p[0] == -1 else p[0],) + tuple(p[1:]) for p in pieces
        ]
    keep_near, keep_far, send_near, send_far, own_mixed = experts(
        arrays,
        tuple(pieces),
        mask,
        norm_gain.reshape(1, width),
        router_weight.T,
        gate_weight,
        up_weight,
        down_weight,
        dims,
        rows,
    )

    quarter = width // 4
    far = keep_far.astype(F32) + swap_sec(send_far).astype(F32)
    near = keep_near.astype(F32) + swap_sec(send_near).astype(F32)
    cut_far = total_rows - total_rows // nx
    cut_near = total_rows // nx
    sums = []
    for h, (nf, ns) in enumerate(((nx, ny), (ny, nx))):
        away = (far[:cut_far] if h == 0 else far[cut_far:]).astype(BF)
        total = near[:cut_near] if h == 0 else near[cut_near:]
        size = total_rows // nf
        for k in range(1, nf):
            came = trade(
                away[(k - 1) * size : k * size], dims, **({"kx": k} if h == 0 else {"ky": k})
            )
            total = total + came.astype(F32)
        total = total.reshape(ns, nz * rows, quarter)
        inner = total[0]
        for k in range(1, ns):
            came = trade(total[k].astype(BF), dims, **({"ky": k} if h == 0 else {"kx": k}))
            inner = inner + came.astype(F32)
        sums.append(inner)
    joined = jnp.concatenate(sums, axis=1).reshape(nz, rows, width // 2)
    last = joined[0]
    came = [trade(joined[k].astype(BF), dims, kz=k) for k in steps]
    for v in came:
        last = last + v.astype(F32)
    own_half = lax.dynamic_slice_in_dim(own_mixed, sec * (width // 2), width // 2, 1)
    done = (own_half.astype(F32) + last).astype(BF)
    other = swap_sec(done)
    return jnp.where(
        sec == 0, jnp.concatenate([done, other], axis=1), jnp.concatenate([other, done], axis=1)
    )


def solution(mesh):
    dims = grid_of(mesh.shape["dev"])
    placed = (
        P("dev", "sec"),
        P("dev", None, "sec"),
        P("dev", None, "sec"),
        P("dev", "sec"),
        P("dev", "sec"),
        P("dev"),
        P("dev", None),
        P("sec", "dev"),
        P(),
        P(),
        P("dev", None),
        P("dev", None, "sec"),
        P("dev", None, "sec"),
        P("dev", "sec", None),
    )
    return jax.shard_map(
        functools.partial(local, dims),
        mesh=mesh,
        in_specs=placed,
        out_specs=P("dev", None),
        check_vma=False,
    )
```

time: 236 us -> 110 us (0.47)
  waiting for transfers between devices: 145 us -> 48.1 us
  blocking collectives: 34 us -> 0 us
  starting transfers between devices: 11.3 us -> 40.8 us
  matrix products: 24.2 us -> 0 us
  Pallas kernels: 0 us -> 17.3 us
  between operations: 13.3 us -> 0.32 us
  other arithmetic: 5.03 us -> 1.45 us
    all_gather x2 -> x0, waiting for transfers between devices: 71.9 us -> none  [the longest x1 62.9 us: local(): lax.all_gather(attended, 'dev', axis=0, tiled=True)]
    all_to_all x2 -> x0, waiting for transfers between devices: 49.7 us -> none  [the longest x1 42.1 us: local(): lax.all_to_all(result, 'dev', split_axis=0, concat_axis=0, tiled=True)]
    ppermute x0 -> x36, waiting for transfers between devices: none -> 48.1 us  [the longest x28 43 us: trade(): return lax.ppermute(value, 'dev', [(d, d ^ code) for d in range(n)])]
    ppermute x0 -> x36, starting transfers between devices: none -> 40.8 us  [the longest x28 39.4 us: trade(): return lax.ppermute(value, 'dev', [(d, d ^ code) for d in range(n)])]
    all_to_all x1 -> x0, blocking collectives: 29.3 us -> none  [local(): lax.all_to_all(outgoing, 'dev', split_axis=0, concat_axis=0, tiled=True)]
    dot_general x11 -> x0, matrix products: 24.2 us -> none  [the longest x1 6.37 us: local(): jnp.dot(hidden, down_weight[0], preferred_element_type=jnp.float32)]
    psum x1 -> x0, waiting for transfers between devices: 22.9 us -> none  [local(): lax.psum(combined.astype(jnp.bfloat16), 'sec').astype(jnp.float32)]
    pallas_call x0 -> x5, Pallas kernels: none -> 17.3 us  [the longest x1 7.52 us: attention(): pl.pallas_call(functools.partial(attend_kernel, dims, lanes), out_shape=t...]
  transfers between devices with their start and end apart: 5 -> 36, of which waited for: 5 -> 23; matrix products, arithmetic and copies ran while one was open for 1% -> 1% of each run, Pallas kernels for 0% -> 0%
where the time goes in v2:
time: 110 us
  waiting for transfers between devices  48.1 us (44%)
  starting transfers between devices  40.8 us (37%)
  Pallas kernels  17.3 us (16%)
  local copies, waits for them, and re-layouts  1.92 us (2%)
  other arithmetic  1.45 us (1%)
    ppermute x28, waiting for transfers between devices, trade(): return lax.ppermute(value, 'dev', [(d, d ^ code) for d in range(n)])  43 us
    ppermute x28, starting transfers between devices, trade(): return lax.ppermute(value, 'dev', [(d, d ^ code) for d in range(n)])  39.4 us
    pallas_call x1, Pallas kernels, attention(): pl.pallas_call(functools.partial(attend_kernel, dims, lanes), out_shape=t...  7.52 us
    pallas_call x1, Pallas kernels, experts(): pl.pallas_call(functools.partial(expert_kernel, dims, pieces, rows, 1e-06...  6.61 us
    ppermute x8, waiting for transfers between devices, swap_sec(): return lax.ppermute(value, 'sec', [(0, 1), (1, 0)])  5.05 us
    pallas_call x1, Pallas kernels, project(): pl.pallas_call(functools.partial(project_kernel, pieces, rows, len(arrays...  2.65 us
  transfers between devices with their start and end apart: 36, of which 23 were waited for; matrix products, arithmetic and copies ran while one was open for 1% of the time, Pallas kernels for 0%

profile of v2, /device:TPU:0, one launch (start us, length us, event | category | flops | bytes accessed | tf_op | source)
XLA Modules:
  0.0 109.8 jit_solution(6389782563495094863)
XLA Ops:
  0.0 7.5 %attend.1 = (bf16[16,2048]{1,0:T(8,128)(2,1)}, bf16[16,2688]{1,0:T(8,128)(2,1)}, bf16[16,2688]{1,0:T(8,128)(2,1)}, bf16[16,2688]{1,0:T(8,128)(2,1)}, bf16[16,2688]{1,0:T(8,128)(2,1)}) custom-call(s32[16]{0:T(128)} %refs_0_.1, s32[8,16]{1,0:T(8,128)} %bitcast.17, bf16[16,4096]{1,0:T(8,128)(2,1)} %refs_2_.1, bf16[16,256]{1,0:T(8,128)(2,1)} %refs_3_.1, ...), custom_call_target="tpu_custom_call" | custom-call | flops 402653184 | bytes 12582912 | tf_op jit(solution)/shard_map/attend/pallas_call | solution.py:397
  7.5 3.2 %collective-permute-start = (bf16[16,2688]{1,0:T(8,128)(2,1)}, bf16[16,2688]{1,0:T(8,128)(2,1)S(1)}, u32[]{:S(2)}, u32[]{:S(2)}) collective-permute-start(bf16[16,2688]{1,0:T(8,128)(2,1)} %get-tuple-element.26), channel_id=1, source_target_pairs={{0,4},{1,5},{2,6},{3,7},{4,0},{5,1},{6,2},{7,3},{8,12},{9,13},{10,... | collective-permute-start | bytes 258056 | tf_op jit(solution)/shard_map/ppermute | solution.py:29
  10.7 2.4 %collective-permute-start.1 = (bf16[16,2688]{1,0:T(8,128)(2,1)}, bf16[16,2688]{1,0:T(8,128)(2,1)S(1)}, u32[]{:S(2)}, u32[]{:S(2)}) collective-permute-start(bf16[16,2688]{1,0:T(8,128)(2,1)} %get-tuple-element.28), channel_id=1, source_target_pairs={{0,8},{1,9},{2,10},{3,11},{4,12},{5,13},{6,14},{7,15},{8,0},{9,1},... | collective-permute-start | bytes 258056 | tf_op jit(solution)/shard_map/ppermute | solution.py:29
  13.1 0.3 collective-permute-done.refs_1_
  13.4 2.0 %collective-permute-start.5 = (bf16[16,2048]{1,0:T(8,128)(2,1)}, bf16[16,2048]{1,0:T(8,128)(2,1)S(1)}, u32[]{:S(2)}, u32[]{:S(2)}) collective-permute-start(bf16[16,2048]{1,0:T(8,128)(2,1)} %get-tuple-element.33), channel_id=1, source_target_pairs={{0,4},{1,5},{2,6},{3,7},{4,0},{5,1},{6,2},{7,3},{8,12},{9,13},{10,... | collective-permute-start | bytes 196616 | tf_op jit(solution)/shard_map/ppermute | solution.py:29
  15.4 0.9 constant_dynamic-update-slice_fusion.3
  16.3 3.2 %collective-permute-start.6 = (bf16[16,2048]{1,0:T(8,128)(2,1)}, bf16[16,2048]{1,0:T(8,128)(2,1)S(1)}, u32[]{:S(2)}, u32[]{:S(2)}) collective-permute-start(bf16[16,2048]{1,0:T(8,128)(2,1)} %get-tuple-element.33), channel_id=1, source_target_pairs={{0,8},{1,9},{2,10},{3,11},{4,12},{5,13},{6,14},{7,15},{8,0},{9,1},... | collective-permute-start | bytes 196616 | tf_op jit(solution)/shard_map/ppermute | solution.py:29
  19.5 1.6 %collective-permute-done.1.refs_2_ = bf16[16,2688]{1,0:T(8,128)(2,1)S(1)} collective-permute-done((bf16[16,2688]{1,0:T(8,128)(2,1)}, bf16[16,2688]{1,0:T(8,128)(2,1)S(1)}, u32[]{:S(2)}, u32[]{:S(2)}) %collective-permute-start.1) | collective-permute-done | bytes 86048 | tf_op jit(solution)/shard_map/ppermute | solution.py:29
  21.1 0.9 copy-done.5
  22.0 1.3 %collective-permute-start.3 = (bf16[64,2432]{1,0:T(8,128)(2,1)S(1)}, bf16[64,2432]{1,0:T(8,128)(2,1)S(1)}, u32[]{:S(2)}, u32[]{:S(2)}) collective-permute-start(bf16[64,2432]{1,0:T(8,128)(2,1)S(1)} %get-tuple-element.31), channel_id=1, source_target_pairs={{0,1},{1,0},{2,3},{3,2},{4,5},{5,4},{6,7},{7,6},{8,9},{9,8},{10,11... | collective-permute-start | bytes 933896 | tf_op jit(solution)/shard_map/ppermute | solution.py:29
  23.4 2.9 %collective-permute-done.6 = bf16[16,2048]{1,0:T(8,128)(2,1)S(1)} collective-permute-done((bf16[16,2048]{1,0:T(8,128)(2,1)}, bf16[16,2048]{1,0:T(8,128)(2,1)S(1)}, u32[]{:S(2)}, u32[]{:S(2)}) %collective-permute-start.6) | collective-permute-done | bytes 65568 | tf_op jit(solution)/shard_map/ppermute | solution.py:29
  26.3 1.5 %collective-permute-start.8 = (bf16[64,2048]{1,0:T(8,128)(2,1)S(1)}, bf16[64,2048]{1,0:T(8,128)(2,1)S(1)}, u32[]{:S(2)}, u32[]{:S(2)}) collective-permute-start(bf16[64,2048]{1,0:T(8,128)(2,1)S(1)} %constant_dynamic-update-slice_fusion.refs_3_), channel_id=1, source_target_pairs={{0,2},{1,3},{2,0},{3,1},{4,6},{5,7},{6,4},{7,5},{8,10},{9,11},{10,... | collective-permute-start | bytes 786440 | tf_op jit(solution)/shard_map/ppermute | solution.py:29
  27.8 1.2 %collective-permute-done.3.refs_1_ = bf16[64,2432]{1,0:T(8,128)(2,1)S(1)} collective-permute-done((bf16[64,2432]{1,0:T(8,128)(2,1)S(1)}, bf16[64,2432]{1,0:T(8,128)(2,1)S(1)}, u32[]{:S(2)}, u32[]{:S(2)}) %collective-permute-start.3) | collective-permute-done | bytes 311328 | tf_op jit(solution)/shard_map/ppermute | solution.py:29
  29.0 1.5 %collective-permute-start.10 = (bf16[64,2432]{1,0:T(8,128)(2,1)S(1)}, bf16[64,2432]{1,0:T(8,128)(2,1)S(1)}, u32[]{:S(2)}, u32[]{:S(2)}) collective-permute-start(bf16[64,2432]{1,0:T(8,128)(2,1)S(1)} %collective-permute-done.3.refs_1_), channel_id=1, source_target_pairs={{0,2},{1,3},{2,0},{3,1},{4,6},{5,7},{6,4},{7,5},{8,10},{9,11},{10,... | collective-permute-start | bytes 933896 | tf_op jit(solution)/shard_map/ppermute | solution.py:29
  30.6 0.5 collective-permute-start.4
  31.0 1.3 %collective-permute-start.9 = (bf16[64,2048]{1,0:T(8,128)(2,1)S(1)}, bf16[64,2048]{1,0:T(8,128)(2,1)S(1)}, u32[]{:S(2)}, u32[]{:S(2)}) collective-permute-start(bf16[64,2048]{1,0:T(8,128)(2,1)S(1)} %constant_dynamic-update-slice_fusion.refs_3_), channel_id=1, source_target_pairs={{0,1},{1,0},{2,3},{3,2},{4,5},{5,4},{6,7},{7,6},{8,9},{9,8},{10,11... | collective-permute-start | bytes 786440 | tf_op jit(solution)/shard_map/ppermute | solution.py:29
  32.3 3.3 %collective-permute-done.8.refs_4_ = bf16[64,2048]{1,0:T(8,128)(2,1)S(1)} collective-permute-done((bf16[64,2048]{1,0:T(8,128)(2,1)S(1)}, bf16[64,2048]{1,0:T(8,128)(2,1)S(1)}, u32[]{:S(2)}, u32[]{:S(2)}) %collective-permute-start.8) | collective-permute-done | bytes 262176 | tf_op jit(solution)/shard_map/ppermute | solution.py:29
  35.6 1.3 %collective-permute-start.11 = (bf16[64,2048]{1,0:T(8,128)(2,1)S(1)}, bf16[64,2048]{1,0:T(8,128)(2,1)S(1)}, u32[]{:S(2)}, u32[]{:S(2)}) collective-permute-start(bf16[64,2048]{1,0:T(8,128)(2,1)S(1)} %collective-permute-done.8.refs_4_), channel_id=1, source_target_pairs={{0,1},{1,0},{2,3},{3,2},{4,5},{5,4},{6,7},{7,6},{8,9},{9,8},{10,11... | collective-permute-start | bytes 786440 | tf_op jit(solution)/shard_map/ppermute | solution.py:29
  36.9 8.1 %collective-permute-done.4.refs_2_ = bf16[64,2304]{1,0:T(8,128)(2,1)S(1)} collective-permute-done((bf16[64,2304]{1,0:T(8,128)(2,1)S(1)}, bf16[64,2304]{1,0:T(8,128)(2,1)S(1)}, u32[]{:S(2)}, u32[]{:S(2)}) %collective-permute-start.4) | collective-permute-done | bytes 294944 | tf_op jit(solution)/shard_map/ppermute | solution.py:29
  45.1 2.6 %project.1 = (f32[256,128]{1,0:T(8,128)S(1)}, f32[256,128]{1,0:T(8,128)S(1)}) custom-call(bf16[64,2304]{1,0:T(8,128)(2,1)S(1)} %get-tuple-element.30.refs_0_, bf16[64,2432]{1,0:T(8,128)(2,1)S(1)} %collective-permute-done.3.refs_1_, bf16[64,2304]{1,0:T(8,128)(2,1)S(1)} %collective-permute-done.4.refs_2_, ...), custom_call_target="tpu_custom_call" | custom-call | flops 536870912 | bytes 4194304 | tf_op jit(solution)/shard_map/project/pallas_call | solution.py:94
  47.8 0.1 collective-permute-start.12
  47.9 0.4 arrange.1
  48.3 0.9 collective-permute-done.12
  49.2 2.6 %collective-permute-start.13 = (bf16[256,128]{1,0:T(8,128)(2,1)S(1)}, bf16[256,128]{1,0:T(8,128)(2,1)S(1)}, u32[]{:S(2)}, u32[]{:S(2)}) collective-permute-start(bf16[256,128]{1,0:T(8,128)(2,1)S(1)} %add_convert_fusion.1), channel_id=1, source_target_pairs={{0,4},{1,5},{2,6},{3,7},{4,0},{5,1},{6,2},{7,3},{8,12},{9,13},{10,... | collective-permute-start | bytes 196616 | tf_op jit(solution)/shard_map/ppermute | solution.py:29
  51.9 0.5 collective-permute-start.14
  52.4 1.9 %collective-permute-start.15 = (bf16[256,128]{1,0:T(8,128)(2,1)S(1)}, bf16[256,128]{1,0:T(8,128)(2,1)S(1)}, u32[]{:S(2)}, u32[]{:S(2)}) collective-permute-start(bf16[256,128]{1,0:T(8,128)(2,1)S(1)} %add_convert_fusion.1), channel_id=1, source_target_pairs={{0,12},{1,13},{2,14},{3,15},{4,8},{5,9},{6,10},{7,11},{8,4},{9,5},... | collective-permute-start | bytes 196616 | tf_op jit(solution)/shard_map/ppermute | solution.py:29
  54.3 5.6 %collective-permute-done.14 = bf16[256,128]{1,0:T(8,128)(2,1)S(1)} collective-permute-done((bf16[256,128]{1,0:T(8,128)(2,1)S(1)}, bf16[256,128]{1,0:T(8,128)(2,1)S(1)}, u32[]{:S(2)}, u32[]{:S(2)}) %collective-permute-start.14) | collective-permute-done | bytes 65568 | tf_op jit(solution)/shard_map/ppermute | solution.py:29
  60.0 1.6 %collective-permute-start.17 = (bf16[512,128]{1,0:T(8,128)(2,1)S(1)}, bf16[512,128]{1,0:T(8,128)(2,1)S(1)}, u32[]{:S(2)}, u32[]{:S(2)}) collective-permute-start(bf16[512,128]{1,0:T(8,128)(2,1)S(1)} %bitcast.15), channel_id=1, source_target_pairs={{0,1},{1,0},{2,3},{3,2},{4,5},{5,4},{6,7},{7,6},{8,9},{9,8},{10,11... | collective-permute-start | bytes 393224 | tf_op jit(solution)/shard_map/ppermute | solution.py:29
  61.6 1.5 %collective-permute-start.18 = (bf16[512,128]{1,0:T(8,128)(2,1)S(1)}, bf16[512,128]{1,0:T(8,128)(2,1)S(1)}, u32[]{:S(2)}, u32[]{:S(2)}) collective-permute-start(bf16[512,128]{1,0:T(8,128)(2,1)S(1)} %bitcast.13), channel_id=1, source_target_pairs={{0,2},{1,3},{2,0},{3,1},{4,6},{5,7},{6,4},{7,5},{8,10},{9,11},{10,... | collective-permute-start | bytes 393224 | tf_op jit(solution)/shard_map/ppermute | solution.py:29
  63.2 0.5 collective-permute-start.20
  63.6 0.5 collective-permute-start.21
  64.1 1.7 %collective-permute-done.17.refs_2_ = bf16[512,128]{1,0:T(8,128)(2,1)S(1)} collective-permute-done((bf16[512,128]{1,0:T(8,128)(2,1)S(1)}, bf16[512,128]{1,0:T(8,128)(2,1)S(1)}, u32[]{:S(2)}, u32[]{:S(2)}) %collective-permute-start.17) | collective-permute-done | bytes 131104 | tf_op jit(solution)/shard_map/ppermute | solution.py:29
  65.8 0.9 collective-permute-start.23
  66.7 0.4 collective-permute-done.18.refs_3_
  67.1 2.1 %collective-permute-start.24 = (bf16[512,128]{1,0:T(8,128)(2,1)S(1)}, bf16[512,128]{1,0:T(8,128)(2,1)S(1)}, u32[]{:S(2)}, u32[]{:S(2)}) collective-permute-start(bf16[512,128]{1,0:T(8,128)(2,1)S(1)} %collective-permute-done.18.refs_3_), channel_id=1, source_target_pairs={{0,1},{1,0},{2,3},{3,2},{4,5},{5,4},{6,7},{7,6},{8,9},{9,8},{10,11... | collective-permute-start | bytes 393224 | tf_op jit(solution)/shard_map/ppermute | solution.py:29
  69.2 0.5 collective-permute-done.20.refs_5_
  69.7 0.1 collective-permute-start.22
  69.8 0.6 collective-permute-start.19
  70.3 0.9 collective-permute-done.23.refs_8_
  71.3 0.8 collective-permute-done.24.refs_9_
  72.1 0.1 collective-permute-start.25
  72.3 1.5 %collective-permute-done.25.refs_10_ = bf16[1024,128]{1,0:T(8,128)(2,1)S(1)} collective-permute-done((bf16[1024,128]{1,0:T(8,128)(2,1)S(1)}, bf16[1024,128]{1,0:T(8,128)(2,1)S(1)}, u32[]{:S(2)}, u32[]{:S(2)}) %collective-permute-start.25) | collective-permute-done | bytes 262176 | tf_op jit(solution)/shard_map/ppermute | solution.py:37
  73.8 6.6 %experts.1 = (bf16[256,1024]{1,0:T(8,128)(2,1)S(1)}, bf16[256,1024]{1,0:T(8,128)(2,1)S(1)}, bf16[256,1024]{1,0:T(8,128)(2,1)S(1)}, bf16[256,1024]{1,0:T(8,128)(2,1)S(1)}, bf16[16,4096]{1,0:T(8,128)(2,1)S(1)}) custom-call(bf16[1024,128]{1,0:T(8,128)(2,1)S(1)} %pad_maximum_fusion.1.refs_0_, bf16[1024,128]{1,0:T(8,128)(2,1)S(1)} %collective-permute-done.16.refs_1_, ...), custom_call_target="tpu_custom_call" | custom-call | flops 2415919104 | bytes 15728640 | tf_op jit(solution)/shard_map/experts/pallas_call | solution.py:253
  80.4 0.2 collective-permute-start.27
  80.6 0.4 collective-permute-start.26
  81.0 1.4 %collective-permute-done.27 = bf16[256,1024]{1,0:T(8,128)(2,1)S(1)} collective-permute-done((bf16[256,1024]{1,0:T(8,128)(2,1)S(1)}, bf16[256,1024]{1,0:T(8,128)(2,1)S(1)}, u32[]{:S(2)}, u32[]{:S(2)}) %collective-permute-start.27) | collective-permute-done | bytes 524320 | tf_op jit(solution)/shard_map/ppermute | solution.py:37
  82.4 0.2 add_convert_fusion
  82.6 2.1 %collective-permute-start.28 = (bf16[128,1024]{1,0:T(8,128)(2,1)S(1)}, bf16[128,1024]{1,0:T(8,128)(2,1)S(1)}, u32[]{:S(2)}, u32[]{:S(2)}) collective-permute-start(bf16[128,1024]{1,0:T(8,128)(2,1)S(1)} %get-tuple-element.46), channel_id=1, source_target_pairs={{0,1},{1,0},{2,3},{3,2},{4,5},{5,4},{6,7},{7,6},{8,9},{9,8},{10,11... | collective-permute-start | bytes 786440 | tf_op jit(solution)/shard_map/ppermute | solution.py:29
  84.7 0.6 collective-permute-start.30
  85.3 0.2 convert_add_fusion
  85.5 5.8 %collective-permute-done.28 = bf16[128,1024]{1,0:T(8,128)(2,1)S(1)} collective-permute-done((bf16[128,1024]{1,0:T(8,128)(2,1)S(1)}, bf16[128,1024]{1,0:T(8,128)(2,1)S(1)}, u32[]{:S(2)}, u32[]{:S(2)}) %collective-permute-start.28) | collective-permute-done | bytes 262176 | tf_op jit(solution)/shard_map/ppermute | solution.py:29
  91.3 1.5 %collective-permute-done.30 = bf16[128,1024]{1,0:T(8,128)(2,1)S(1)} collective-permute-done((bf16[128,1024]{1,0:T(8,128)(2,1)S(1)}, bf16[128,1024]{1,0:T(8,128)(2,1)S(1)}, u32[]{:S(2)}, u32[]{:S(2)}) %collective-permute-start.30) | collective-permute-done | bytes 262176 | tf_op jit(solution)/shard_map/ppermute | solution.py:29
  92.8 0.2 slice_add_fusion
  93.0 0.4 collective-permute-start.31
  93.4 1.6 %collective-permute-start.29 = (bf16[64,1024]{1,0:T(8,128)(2,1)S(1)}, bf16[64,1024]{1,0:T(8,128)(2,1)S(1)}, u32[]{:S(2)}, u32[]{:S(2)}) collective-permute-start(bf16[64,1024]{1,0:T(8,128)(2,1)S(1)} %slice.109), channel_id=1, source_target_pairs={{0,2},{1,3},{2,0},{3,1},{4,6},{5,7},{6,4},{7,5},{8,10},{9,11},{10,... | collective-permute-start | bytes 393224 | tf_op jit(solution)/shard_map/ppermute | solution.py:29
  95.0 3.0 %collective-permute-done.31 = bf16[64,1024]{1,0:T(8,128)(2,1)S(1)} collective-permute-done((bf16[64,1024]{1,0:T(8,128)(2,1)S(1)}, bf16[64,1024]{1,0:T(8,128)(2,1)S(1)}, u32[]{:S(2)}, u32[]{:S(2)}) %collective-permute-start.31) | collective-permute-done | bytes 131104 | tf_op jit(solution)/shard_map/ppermute | solution.py:29
  98.0 0.4 collective-permute-done.29
  98.5 2.8 %collective-permute-start.32 = (bf16[16,2048]{1,0:T(8,128)(2,1)S(1)}, bf16[16,2048]{1,0:T(8,128)(2,1)S(1)}, u32[]{:S(2)}, u32[]{:S(2)}) collective-permute-start(bf16[16,2048]{1,0:T(8,128)(2,1)S(1)} %get-tuple-element.47), channel_id=1, source_target_pairs={{0,8},{1,9},{2,10},{3,11},{4,12},{5,13},{6,14},{7,15},{8,0},{9,1},... | collective-permute-start | bytes 196616 | tf_op jit(solution)/shard_map/ppermute | solution.py:29
  101.4 1.5 %collective-permute-start.33 = (bf16[16,2048]{1,0:T(8,128)(2,1)S(1)}, bf16[16,2048]{1,0:T(8,128)(2,1)S(1)}, u32[]{:S(2)}, u32[]{:S(2)}) collective-permute-start(bf16[16,2048]{1,0:T(8,128)(2,1)S(1)} %get-tuple-element.49), channel_id=1, source_target_pairs={{0,12},{1,13},{2,14},{3,15},{4,8},{5,9},{6,10},{7,11},{8,4},{9,5},... | collective-permute-start | bytes 196616 | tf_op jit(solution)/shard_map/ppermute | solution.py:29
  102.8 1.9 %collective-permute-done.32 = bf16[16,2048]{1,0:T(8,128)(2,1)S(1)} collective-permute-done((bf16[16,2048]{1,0:T(8,128)(2,1)S(1)}, bf16[16,2048]{1,0:T(8,128)(2,1)S(1)}, u32[]{:S(2)}, u32[]{:S(2)}) %collective-permute-start.32) | collective-permute-done | bytes 65568 | tf_op jit(solution)/shard_map/ppermute | solution.py:29
  104.7 2.9 %collective-permute-done.33 = bf16[16,2048]{1,0:T(8,128)(2,1)S(1)} collective-permute-done((bf16[16,2048]{1,0:T(8,128)(2,1)S(1)}, bf16[16,2048]{1,0:T(8,128)(2,1)S(1)}, u32[]{:S(2)}, u32[]{:S(2)}) %collective-permute-start.33) | collective-permute-done | bytes 65568 | tf_op jit(solution)/shard_map/ppermute | solution.py:29
  107.5 0.3 collective-permute-done.34
  107.9 1.2 %collective-permute-done.35 = bf16[16,2048]{1,0:T(8,128)(2,1)S(1)} collective-permute-done((bf16[16,2048]{1,0:T(8,128)(2,1)S(1)}, bf16[16,2048]{1,0:T(8,128)(2,1)S(1)}, u32[]{:S(2)}, u32[]{:S(2)}) %collective-permute-start.35) | collective-permute-done | bytes 65568 | tf_op jit(solution)/shard_map/ppermute | solution.py:37
  109.1 0.7 maximum_select_fusion
  (49 shorter events, 0.6 us)
Async XLA Ops:
  0.0 45.1 %copy-start.3 = (bf16[4096,256]{1,0:T(8,128)(2,1)S(1)}, bf16[4096,256]{1,0:T(8,128)(2,1)}, u32[]{:S(2)}) copy-start(bf16[4096,256]{1,0:T(8,128)(2,1)} %refs_8_.1) | copy-start | bytes 6291460
  7.5 5.9 %collective-permute-start = (bf16[16,2688]{1,0:T(8,128)(2,1)}, bf16[16,2688]{1,0:T(8,128)(2,1)S(1)}, u32[]{:S(2)}, u32[]{:S(2)}) collective-permute-start(bf16[16,2688]{1,0:T(8,128)(2,1)} %get-tuple-element.26), channel_id=1, source_target_pairs={{0,4},{1,5},{2,6},{3,7},{4,0},{5,1},{6,2},{7,3},{8,12},{9,13},{10,... | collective-permute-start | bytes 258056 | tf_op jit(solution)/shard_map/ppermute | solution.py:29
  10.7 10.4 %collective-permute-start.1 = (bf16[16,2688]{1,0:T(8,128)(2,1)}, bf16[16,2688]{1,0:T(8,128)(2,1)S(1)}, u32[]{:S(2)}, u32[]{:S(2)}) collective-permute-start(bf16[16,2688]{1,0:T(8,128)(2,1)} %get-tuple-element.28), channel_id=1, source_target_pairs={{0,8},{1,9},{2,10},{3,11},{4,12},{5,13},{6,14},{7,15},{8,0},{9,1},... | collective-permute-start | bytes 258056 | tf_op jit(solution)/shard_map/ppermute | solution.py:29
  13.1 8.0 %collective-permute-start.2 = (bf16[16,2688]{1,0:T(8,128)(2,1)}, bf16[16,2688]{1,0:T(8,128)(2,1)S(1)}, u32[]{:S(2)}, u32[]{:S(2)}) collective-permute-start(bf16[16,2688]{1,0:T(8,128)(2,1)} %get-tuple-element.29), channel_id=1, source_target_pairs={{0,12},{1,13},{2,14},{3,15},{4,8},{5,9},{6,10},{7,11},{8,4},{9,5},... | collective-permute-start | bytes 258056 | tf_op jit(solution)/shard_map/ppermute | solution.py:29
  13.4 9.9 %collective-permute-start.5 = (bf16[16,2048]{1,0:T(8,128)(2,1)}, bf16[16,2048]{1,0:T(8,128)(2,1)S(1)}, u32[]{:S(2)}, u32[]{:S(2)}) collective-permute-start(bf16[16,2048]{1,0:T(8,128)(2,1)} %get-tuple-element.33), channel_id=1, source_target_pairs={{0,4},{1,5},{2,6},{3,7},{4,0},{5,1},{6,2},{7,3},{8,12},{9,13},{10,... | collective-permute-start | bytes 196616 | tf_op jit(solution)/shard_map/ppermute | solution.py:29
  16.3 10.0 %collective-permute-start.6 = (bf16[16,2048]{1,0:T(8,128)(2,1)}, bf16[16,2048]{1,0:T(8,128)(2,1)S(1)}, u32[]{:S(2)}, u32[]{:S(2)}) collective-permute-start(bf16[16,2048]{1,0:T(8,128)(2,1)} %get-tuple-element.33), channel_id=1, source_target_pairs={{0,8},{1,9},{2,10},{3,11},{4,12},{5,13},{6,14},{7,15},{8,0},{9,1},... | collective-permute-start | bytes 196616 | tf_op jit(solution)/shard_map/ppermute | solution.py:29
  19.5 6.8 %collective-permute-start.7 = (bf16[16,2048]{1,0:T(8,128)(2,1)}, bf16[16,2048]{1,0:T(8,128)(2,1)S(1)}, u32[]{:S(2)}, u32[]{:S(2)}) collective-permute-start(bf16[16,2048]{1,0:T(8,128)(2,1)} %get-tuple-element.33), channel_id=1, source_target_pairs={{0,12},{1,13},{2,14},{3,15},{4,8},{5,9},{6,10},{7,11},{8,4},{9,5},... | collective-permute-start | bytes 196616 | tf_op jit(solution)/shard_map/ppermute | solution.py:29
  21.1 0.9 copy-start.5
  22.0 7.0 %collective-permute-start.3 = (bf16[64,2432]{1,0:T(8,128)(2,1)S(1)}, bf16[64,2432]{1,0:T(8,128)(2,1)S(1)}, u32[]{:S(2)}, u32[]{:S(2)}) collective-permute-start(bf16[64,2432]{1,0:T(8,128)(2,1)S(1)} %get-tuple-element.31), channel_id=1, source_target_pairs={{0,1},{1,0},{2,3},{3,2},{4,5},{5,4},{6,7},{7,6},{8,9},{9,8},{10,11... | collective-permute-start | bytes 933896 | tf_op jit(solution)/shard_map/ppermute | solution.py:29
  26.3 9.3 %collective-permute-start.8 = (bf16[64,2048]{1,0:T(8,128)(2,1)S(1)}, bf16[64,2048]{1,0:T(8,128)(2,1)S(1)}, u32[]{:S(2)}, u32[]{:S(2)}) collective-permute-start(bf16[64,2048]{1,0:T(8,128)(2,1)S(1)} %constant_dynamic-update-slice_fusion.refs_3_), channel_id=1, source_target_pairs={{0,2},{1,3},{2,0},{3,1},{4,6},{5,7},{6,4},{7,5},{8,10},{9,11},{10,... | collective-permute-start | bytes 786440 | tf_op jit(solution)/shard_map/ppermute | solution.py:29
  29.0 16.0 %collective-permute-start.10 = (bf16[64,2432]{1,0:T(8,128)(2,1)S(1)}, bf16[64,2432]{1,0:T(8,128)(2,1)S(1)}, u32[]{:S(2)}, u32[]{:S(2)}) collective-permute-start(bf16[64,2432]{1,0:T(8,128)(2,1)S(1)} %collective-permute-done.3.refs_1_), channel_id=1, source_target_pairs={{0,2},{1,3},{2,0},{3,1},{4,6},{5,7},{6,4},{7,5},{8,10},{9,11},{10,... | collective-permute-start | bytes 933896 | tf_op jit(solution)/shard_map/ppermute | solution.py:29
  30.6 14.5 %collective-permute-start.4 = (bf16[64,2304]{1,0:T(8,128)(2,1)S(1)}, bf16[64,2304]{1,0:T(8,128)(2,1)S(1)}, u32[]{:S(2)}, u32[]{:S(2)}) collective-permute-start(bf16[64,2304]{1,0:T(8,128)(2,1)S(1)} %get-tuple-element.32), channel_id=1, source_target_pairs={{0,2},{1,3},{2,0},{3,1},{4,6},{5,7},{6,4},{7,5},{8,10},{9,11},{10,... | collective-permute-start | bytes 884744 | tf_op jit(solution)/shard_map/ppermute | solution.py:29
  31.0 14.0 %collective-permute-start.9 = (bf16[64,2048]{1,0:T(8,128)(2,1)S(1)}, bf16[64,2048]{1,0:T(8,128)(2,1)S(1)}, u32[]{:S(2)}, u32[]{:S(2)}) collective-permute-start(bf16[64,2048]{1,0:T(8,128)(2,1)S(1)} %constant_dynamic-update-slice_fusion.refs_3_), channel_id=1, source_target_pairs={{0,1},{1,0},{2,3},{3,2},{4,5},{5,4},{6,7},{7,6},{8,9},{9,8},{10,11... | collective-permute-start | bytes 786440 | tf_op jit(solution)/shard_map/ppermute | solution.py:29
  35.6 9.5 %collective-permute-start.11 = (bf16[64,2048]{1,0:T(8,128)(2,1)S(1)}, bf16[64,2048]{1,0:T(8,128)(2,1)S(1)}, u32[]{:S(2)}, u32[]{:S(2)}) collective-permute-start(bf16[64,2048]{1,0:T(8,128)(2,1)S(1)} %collective-permute-done.8.refs_4_), channel_id=1, source_target_pairs={{0,1},{1,0},{2,3},{3,2},{4,5},{5,4},{6,7},{7,6},{8,9},{9,8},{10,11... | collective-permute-start | bytes 786440 | tf_op jit(solution)/shard_map/ppermute | solution.py:29
  45.1 28.7 %copy-start.1 = (bf16[1,4096,384]{2,1,0:T(8,128)(2,1)S(1)}, bf16[1,4096,384]{2,1,0:T(8,128)(2,1)}, u32[]{:S(2)}) copy-start(bf16[1,4096,384]{2,1,0:T(8,128)(2,1)} %refs_15_.1) | copy-start | bytes 9437188
  45.1 28.7 %copy-start.2 = (bf16[1,384,4096]{2,1,0:T(8,128)(2,1)S(1)}, bf16[1,384,4096]{2,1,0:T(8,128)(2,1)}, u32[]{:S(2)}) copy-start(bf16[1,384,4096]{2,1,0:T(8,128)(2,1)} %refs_16_.1) | copy-start | bytes 9437188
  47.7 26.0 %copy-start = (bf16[1,4096,384]{2,1,0:T(8,128)(2,1)S(1)}, bf16[1,4096,384]{2,1,0:T(8,128)(2,1)}, u32[]{:S(2)}) copy-start(bf16[1,4096,384]{2,1,0:T(8,128)(2,1)} %refs_14_.1) | copy-start | bytes 9437188
  47.8 26.0 %copy-start.4 = (bf16[4096,16]{0,1:T(8,128)(2,1)S(1)}, bf16[4096,16]{0,1:T(8,128)(2,1)}, u32[]{:S(2)}) copy-start(bf16[4096,16]{0,1:T(8,128)(2,1)} %param.23) | copy-start | bytes 393220
  47.8 26.0 %copy-start.6 = (f32[4096]{0:T(1024)S(1)}, f32[4096]{0:T(1024)}, u32[]{:S(2)}) copy-start(f32[4096]{0:T(1024)} %param.22) | copy-start | bytes 49156
  47.8 1.4 %collective-permute-start.12 = (f32[256,128]{1,0:T(8,128)S(1)}, f32[256,128]{1,0:T(8,128)S(1)}, u32[]{:S(2)}, u32[]{:S(2)}) collective-permute-start(f32[256,128]{1,0:T(8,128)S(1)} %get-tuple-element.36), channel_id=1, source_target_pairs={{0,16},{16,0},{1,17},{17,1},{2,18},{18,2},{3,19},{19,3},{4,20},{20... | collective-permute-start | bytes 393224 | tf_op jit(solution)/shard_map/ppermute | solution.py:37
  49.2 5.1 %collective-permute-start.13 = (bf16[256,128]{1,0:T(8,128)(2,1)S(1)}, bf16[256,128]{1,0:T(8,128)(2,1)S(1)}, u32[]{:S(2)}, u32[]{:S(2)}) collective-permute-start(bf16[256,128]{1,0:T(8,128)(2,1)S(1)} %add_convert_fusion.1), channel_id=1, source_target_pairs={{0,4},{1,5},{2,6},{3,7},{4,0},{5,1},{6,2},{7,3},{8,12},{9,13},{10,... | collective-permute-start | bytes 196616 | tf_op jit(solution)/shard_map/ppermute | solution.py:29
  51.9 8.1 %collective-permute-start.14 = (bf16[256,128]{1,0:T(8,128)(2,1)S(1)}, bf16[256,128]{1,0:T(8,128)(2,1)S(1)}, u32[]{:S(2)}, u32[]{:S(2)}) collective-permute-start(bf16[256,128]{1,0:T(8,128)(2,1)S(1)} %add_convert_fusion.1), channel_id=1, source_target_pairs={{0,8},{1,9},{2,10},{3,11},{4,12},{5,13},{6,14},{7,15},{8,0},{9,1},... | collective-permute-start | bytes 196616 | tf_op jit(solution)/shard_map/ppermute | solution.py:29
  52.4 7.5 %collective-permute-start.15 = (bf16[256,128]{1,0:T(8,128)(2,1)S(1)}, bf16[256,128]{1,0:T(8,128)(2,1)S(1)}, u32[]{:S(2)}, u32[]{:S(2)}) collective-permute-start(bf16[256,128]{1,0:T(8,128)(2,1)S(1)} %add_convert_fusion.1), channel_id=1, source_target_pairs={{0,12},{1,13},{2,14},{3,15},{4,8},{5,9},{6,10},{7,11},{8,4},{9,5},... | collective-permute-start | bytes 196616 | tf_op jit(solution)/shard_map/ppermute | solution.py:29
  60.0 5.8 %collective-permute-start.17 = (bf16[512,128]{1,0:T(8,128)(2,1)S(1)}, bf16[512,128]{1,0:T(8,128)(2,1)S(1)}, u32[]{:S(2)}, u32[]{:S(2)}) collective-permute-start(bf16[512,128]{1,0:T(8,128)(2,1)S(1)} %bitcast.15), channel_id=1, source_target_pairs={{0,1},{1,0},{2,3},{3,2},{4,5},{5,4},{6,7},{7,6},{8,9},{9,8},{10,11... | collective-permute-start | bytes 393224 | tf_op jit(solution)/shard_map/ppermute | solution.py:29
  61.6 5.4 %collective-permute-start.18 = (bf16[512,128]{1,0:T(8,128)(2,1)S(1)}, bf16[512,128]{1,0:T(8,128)(2,1)S(1)}, u32[]{:S(2)}, u32[]{:S(2)}) collective-permute-start(bf16[512,128]{1,0:T(8,128)(2,1)S(1)} %bitcast.13), channel_id=1, source_target_pairs={{0,2},{1,3},{2,0},{3,1},{4,6},{5,7},{6,4},{7,5},{8,10},{9,11},{10,... | collective-permute-start | bytes 393224 | tf_op jit(solution)/shard_map/ppermute | solution.py:29
  63.2 6.5 %collective-permute-start.20 = (bf16[512,128]{1,0:T(8,128)(2,1)S(1)}, bf16[512,128]{1,0:T(8,128)(2,1)S(1)}, u32[]{:S(2)}, u32[]{:S(2)}) collective-permute-start(bf16[512,128]{1,0:T(8,128)(2,1)S(1)} %bitcast.16), channel_id=1, source_target_pairs={{0,2},{1,3},{2,0},{3,1},{4,6},{5,7},{6,4},{7,5},{8,10},{9,11},{10,... | collective-permute-start | bytes 393224 | tf_op jit(solution)/shard_map/ppermute | solution.py:29
  63.6 6.0 %collective-permute-start.21 = (bf16[512,128]{1,0:T(8,128)(2,1)S(1)}, bf16[512,128]{1,0:T(8,128)(2,1)S(1)}, u32[]{:S(2)}, u32[]{:S(2)}) collective-permute-start(bf16[512,128]{1,0:T(8,128)(2,1)S(1)} %bitcast.14), channel_id=1, source_target_pairs={{0,1},{1,0},{2,3},{3,2},{4,5},{5,4},{6,7},{7,6},{8,9},{9,8},{10,11... | collective-permute-start | bytes 393224 | tf_op jit(solution)/shard_map/ppermute | solution.py:29
  64.1 8.1 %collective-permute-start.16 = (bf16[1024,128]{1,0:T(8,128)(2,1)S(1)}, bf16[1024,128]{1,0:T(8,128)(2,1)S(1)}, u32[]{:S(2)}, u32[]{:S(2)}) collective-permute-start(bf16[1024,128]{1,0:T(8,128)(2,1)S(1)} %pad_maximum_fusion.1.refs_0_), channel_id=1, source_target_pairs={{0,16},{16,0},{1,17},{17,1},{2,18},{18,2},{3,19},{19,3},{4,20},{20... | collective-permute-start | bytes 786440 | tf_op jit(solution)/shard_map/ppermute | solution.py:37
  65.8 5.5 %collective-permute-start.23 = (bf16[512,128]{1,0:T(8,128)(2,1)S(1)}, bf16[512,128]{1,0:T(8,128)(2,1)S(1)}, u32[]{:S(2)}, u32[]{:S(2)}) collective-permute-start(bf16[512,128]{1,0:T(8,128)(2,1)S(1)} %collective-permute-done.17.refs_2_), channel_id=1, source_target_pairs={{0,2},{1,3},{2,0},{3,1},{4,6},{5,7},{6,4},{7,5},{8,10},{9,11},{10,... | collective-permute-start | bytes 393224 | tf_op jit(solution)/shard_map/ppermute | solution.py:29
  67.1 5.1 %collective-permute-start.24 = (bf16[512,128]{1,0:T(8,128)(2,1)S(1)}, bf16[512,128]{1,0:T(8,128)(2,1)S(1)}, u32[]{:S(2)}, u32[]{:S(2)}) collective-permute-start(bf16[512,128]{1,0:T(8,128)(2,1)S(1)} %collective-permute-done.18.refs_3_), channel_id=1, source_target_pairs={{0,1},{1,0},{2,3},{3,2},{4,5},{5,4},{6,7},{7,6},{8,9},{9,8},{10,11... | collective-permute-start | bytes 393224 | tf_op jit(solution)/shard_map/ppermute | solution.py:29
  69.7 2.6 %collective-permute-start.22 = (bf16[1024,128]{1,0:T(8,128)(2,1)S(1)}, bf16[1024,128]{1,0:T(8,128)(2,1)S(1)}, u32[]{:S(2)}, u32[]{:S(2)}) collective-permute-start(bf16[1024,128]{1,0:T(8,128)(2,1)S(1)} %pad_maximum_fusion.3), channel_id=1, source_target_pairs={{0,16},{16,0},{1,17},{17,1},{2,18},{18,2},{3,19},{19,3},{4,20},{20... | collective-permute-start | bytes 786440 | tf_op jit(solution)/shard_map/ppermute | solution.py:37
  69.8 2.5 %collective-permute-start.19 = (bf16[1024,128]{1,0:T(8,128)(2,1)S(1)}, bf16[1024,128]{1,0:T(8,128)(2,1)S(1)}, u32[]{:S(2)}, u32[]{:S(2)}) collective-permute-start(bf16[1024,128]{1,0:T(8,128)(2,1)S(1)} %pad_maximum_fusion.2), channel_id=1, source_target_pairs={{0,16},{16,0},{1,17},{17,1},{2,18},{18,2},{3,19},{19,3},{4,20},{20... | collective-permute-start | bytes 786440 | tf_op jit(solution)/shard_map/ppermute | solution.py:37
  72.1 1.6 %collective-permute-start.25 = (bf16[1024,128]{1,0:T(8,128)(2,1)S(1)}, bf16[1024,128]{1,0:T(8,128)(2,1)S(1)}, u32[]{:S(2)}, u32[]{:S(2)}) collective-permute-start(bf16[1024,128]{1,0:T(8,128)(2,1)S(1)} %pad_maximum_fusion.4), channel_id=1, source_target_pairs={{0,16},{16,0},{1,17},{17,1},{2,18},{18,2},{3,19},{19,3},{4,20},{20... | collective-permute-start | bytes 786440 | tf_op jit(solution)/shard_map/ppermute | solution.py:37
  80.4 2.0 %collective-permute-start.27 = (bf16[256,1024]{1,0:T(8,128)(2,1)S(1)}, bf16[256,1024]{1,0:T(8,128)(2,1)S(1)}, u32[]{:S(2)}, u32[]{:S(2)}) collective-permute-start(bf16[256,1024]{1,0:T(8,128)(2,1)S(1)} %get-tuple-element.42), channel_id=1, source_target_pairs={{0,16},{16,0},{1,17},{17,1},{2,18},{18,2},{3,19},{19,3},{4,20},{20... | collective-permute-start | bytes 1572872 | tf_op jit(solution)/shard_map/ppermute | solution.py:37
  80.6 4.7 %collective-permute-start.26 = (bf16[256,1024]{1,0:T(8,128)(2,1)S(1)}, bf16[256,1024]{1,0:T(8,128)(2,1)S(1)}, u32[]{:S(2)}, u32[]{:S(2)}) collective-permute-start(bf16[256,1024]{1,0:T(8,128)(2,1)S(1)} %get-tuple-element.40), channel_id=1, source_target_pairs={{0,16},{16,0},{1,17},{17,1},{2,18},{18,2},{3,19},{19,3},{4,20},{20... | collective-permute-start | bytes 1572872 | tf_op jit(solution)/shard_map/ppermute | solution.py:37
  82.6 8.7 %collective-permute-start.28 = (bf16[128,1024]{1,0:T(8,128)(2,1)S(1)}, bf16[128,1024]{1,0:T(8,128)(2,1)S(1)}, u32[]{:S(2)}, u32[]{:S(2)}) collective-permute-start(bf16[128,1024]{1,0:T(8,128)(2,1)S(1)} %get-tuple-element.46), channel_id=1, source_target_pairs={{0,1},{1,0},{2,3},{3,2},{4,5},{5,4},{6,7},{7,6},{8,9},{9,8},{10,11... | collective-permute-start | bytes 786440 | tf_op jit(solution)/shard_map/ppermute | solution.py:29
  84.7 8.1 %collective-permute-start.30 = (bf16[128,1024]{1,0:T(8,128)(2,1)S(1)}, bf16[128,1024]{1,0:T(8,128)(2,1)S(1)}, u32[]{:S(2)}, u32[]{:S(2)}) collective-permute-start(bf16[128,1024]{1,0:T(8,128)(2,1)S(1)} %get-tuple-element.45), channel_id=1, source_target_pairs={{0,2},{1,3},{2,0},{3,1},{4,6},{5,7},{6,4},{7,5},{8,10},{9,11},{10,... | collective-permute-start | bytes 786440 | tf_op jit(solution)/shard_map/ppermute | solution.py:29
  93.0 5.0 %collective-permute-start.31 = (bf16[64,1024]{1,0:T(8,128)(2,1)S(1)}, bf16[64,1024]{1,0:T(8,128)(2,1)S(1)}, u32[]{:S(2)}, u32[]{:S(2)}) collective-permute-start(bf16[64,1024]{1,0:T(8,128)(2,1)S(1)} %slice.108), channel_id=1, source_target_pairs={{0,1},{1,0},{2,3},{3,2},{4,5},{5,4},{6,7},{7,6},{8,9},{9,8},{10,11... | collective-permute-start | bytes 393224 | tf_op jit(solution)/shard_map/ppermute | solution.py:29
  93.4 5.0 %collective-permute-start.29 = (bf16[64,1024]{1,0:T(8,128)(2,1)S(1)}, bf16[64,1024]{1,0:T(8,128)(2,1)S(1)}, u32[]{:S(2)}, u32[]{:S(2)}) collective-permute-start(bf16[64,1024]{1,0:T(8,128)(2,1)S(1)} %slice.109), channel_id=1, source_target_pairs={{0,2},{1,3},{2,0},{3,1},{4,6},{5,7},{6,4},{7,5},{8,10},{9,11},{10,... | collective-permute-start | bytes 393224 | tf_op jit(solution)/shard_map/ppermute | solution.py:29
  98.5 6.1 %collective-permute-start.32 = (bf16[16,2048]{1,0:T(8,128)(2,1)S(1)}, bf16[16,2048]{1,0:T(8,128)(2,1)S(1)}, u32[]{:S(2)}, u32[]{:S(2)}) collective-permute-start(bf16[16,2048]{1,0:T(8,128)(2,1)S(1)} %get-tuple-element.47), channel_id=1, source_target_pairs={{0,8},{1,9},{2,10},{3,11},{4,12},{5,13},{6,14},{7,15},{8,0},{9,1},... | collective-permute-start | bytes 196616 | tf_op jit(solution)/shard_map/ppermute | solution.py:29
  101.4 6.2 %collective-permute-start.33 = (bf16[16,2048]{1,0:T(8,128)(2,1)S(1)}, bf16[16,2048]{1,0:T(8,128)(2,1)S(1)}, u32[]{:S(2)}, u32[]{:S(2)}) collective-permute-start(bf16[16,2048]{1,0:T(8,128)(2,1)S(1)} %get-tuple-element.49), channel_id=1, source_target_pairs={{0,12},{1,13},{2,14},{3,15},{4,8},{5,9},{6,10},{7,11},{8,4},{9,5},... | collective-permute-start | bytes 196616 | tf_op jit(solution)/shard_map/ppermute | solution.py:29
  102.8 5.0 %collective-permute-start.34 = (bf16[16,2048]{1,0:T(8,128)(2,1)S(1)}, bf16[16,2048]{1,0:T(8,128)(2,1)S(1)}, u32[]{:S(2)}, u32[]{:S(2)}) collective-permute-start(bf16[16,2048]{1,0:T(8,128)(2,1)S(1)} %get-tuple-element.48), channel_id=1, source_target_pairs={{0,4},{1,5},{2,6},{3,7},{4,0},{5,1},{6,2},{7,3},{8,12},{9,13},{10,... | collective-permute-start | bytes 196616 | tf_op jit(solution)/shard_map/ppermute | solution.py:29
  107.8 1.3 %collective-permute-start.35 = (bf16[16,2048]{1,0:T(8,128)(2,1)S(1)}, bf16[16,2048]{1,0:T(8,128)(2,1)S(1)}, u32[]{:S(2)}, u32[]{:S(2)}) collective-permute-start(bf16[16,2048]{1,0:T(8,128)(2,1)S(1)} %fusion.6), channel_id=1, source_target_pairs={{0,16},{16,0},{1,17},{17,1},{2,18},{18,2},{3,19},{19,3},{4,20},{20... | collective-permute-start | bytes 196616 | tf_op jit(solution)/shard_map/ppermute | solution.py:37

commit v3 on v2

--- a/solution.py
+++ b/solution.py
@@ -21,6 +21,11 @@
 
 def code_of(dims, kz, ky, kx):
     return (kz * dims[1] + ky) * dims[2] + kx
+
+
+def row_of(dims, chip):
+    plane = dims[1] * dims[2]
+    return (chip % plane) * dims[0] + chip // plane
 
 
 def trade(value, dims, kz=0, ky=0, kx=0):
@@ -61,22 +66,31 @@
 MIB = 1024 * 1024
 
 
-def project_kernel(pieces, rows, count, *refs):
+def project_kernel(nz, plane, pieces, rows, *refs):
+    count = len(pieces)
     arrays = refs[:count]
     w_ref, keep_ref, send_ref, held, sems = refs[count:]
     half = held.shape[1] // 2
-    me = lax.axis_index("dev")
     sec = lax.axis_index("sec")
+    z = lax.axis_index("dev") // plane
     copies = []
-    for i, (which, offset, code, column) in enumerate(pieces):
-        place = pl.multiple_of((me ^ code) * rows, rows)
+
+    def move(i, source, place, size, column):
         copies.append(
             pltpu.make_async_copy(
-                arrays[which].at[pl.ds(offset, rows), pl.ds(0, half)],
-                held.at[pl.ds(place, rows), pl.ds(column * half, half)],
-                sems.at[i],
+                arrays[i].at[pl.ds(source, size), pl.ds(0, half)],
+                held.at[pl.ds(place, size), pl.ds(column * half, half)],
+                sems.at[len(copies)],
             )
         )
+
+    for i, (slot, column, ordered) in enumerate(pieces):
+        if ordered:
+            move(i, 0, slot * nz * rows, nz * rows, column)
+            continue
+        for kz in range(nz):
+            place = pl.multiple_of((slot * nz + (z ^ kz)) * rows, rows)
+            move(i, kz * rows, place, rows, column)
     for c in copies:
         c.start()
     for c in copies:
@@ -88,104 +102,128 @@
     send_ref[...] = jnp.where(sec == 0, high, low)
 
 
-def project(arrays, pieces, weight, n, rows):
+def project(arrays, pieces, weight, dims, rows):
     depth, cols = weight.shape
-    out = jax.ShapeDtypeStruct((n * rows, cols // 2), F32)
+    nz, ny, nx = dims
+    tall = nz * ny * nx * rows
+    out = jax.ShapeDtypeStruct((tall, cols // 2), F32)
     return pl.pallas_call(
-        functools.partial(project_kernel, pieces, rows, len(arrays)),
+        functools.partial(project_kernel, nz, ny * nx, pieces, rows),
         out_shape=(out, out),
         in_specs=[ANY] * len(arrays) + [VM],
         out_specs=(VM, VM),
         scratch_shapes=[
-            pltpu.VMEM((n * rows, depth), BF),
-            pltpu.SemaphoreType.DMA((len(pieces),)),
+            pltpu.VMEM((tall, depth), BF),
+            pltpu.SemaphoreType.DMA((sum(1 if p[2] else nz for p in pieces),)),
         ],
-        compiler_params=pltpu.CompilerParams(vmem_limit_bytes=(4 + n // 2) * MIB),
+        compiler_params=pltpu.CompilerParams(vmem_limit_bytes=(4 + tall // 32) * MIB),
         cost_estimate=pl.CostEstimate(
-            flops=2 * n * rows * depth * cols,
-            bytes_accessed=2 * depth * (cols + n * rows),
+            flops=2 * tall * depth * cols,
+            bytes_accessed=2 * depth * (cols + tall),
             transcendentals=0,
         ),
         name="project",
     )(*arrays, weight)
 
 
-STEPS = 8
-
-
-def expert_kernel(dims, pieces, rows, eps, count, *refs):
+def gather_products(dims, codes, arrays, gain_ref, router_ref, gate_ref, up_ref, sums, own_ref):
+    acc, route, square = sums
+    nz, ny, nx = dims
+    plane = ny * nx
+    me = lax.axis_index("dev")
+    sec = lax.axis_index("sec")
+    total = acc.shape[0]
+    rows = own_ref.shape[0]
+    part = arrays[0].shape[1]
+    place = pl.multiple_of(row_of(dims, me) * rows, rows)
+
+    def add_products(x, at):
+        power = x * x
+        for t in range(0, power.shape[1], 128):
+            square[...] += power[:, t : t + 128]
+        scaled = (x * gain_ref[:, at]).astype(BF)
+        weights = jnp.concatenate([gate_ref[0, at], up_ref[0, at]], axis=1)
+        acc[...] += jnp.dot(scaled, weights, preferred_element_type=F32)
+        route[...] += lax.dot_general(
+            scaled, router_ref[:, at], (((1,), (1,)), ((), ())), preferred_element_type=F32
+        )
+
+    if codes is None:
+        for t in range(0, gain_ref.shape[1], 256):
+            add_products(arrays[0][:, t : t + 256].astype(F32), pl.ds(t, 256))
+        own_ref[...] = arrays[0][pl.ds(place, rows), :]
+        return
+    for i, code in enumerate(codes):
+        here, there = arrays[2 * i : 2 * i + 2]
+        for kz in range(nz):
+            span = slice(kz * total, (kz + 1) * total)
+            low = jnp.where(sec == 0, here[span, :], there[span, :])
+            high = jnp.where(sec == 0, there[span, :], here[span, :])
+            block = jnp.concatenate([low, high], axis=1)
+            owner = me ^ (kz * plane + code)
+            at = pl.ds(pl.multiple_of(owner * 2 * part, 2 * part), 2 * part)
+            add_products(block.astype(F32), at)
+        for kz in range(nz):
+            owner = me ^ (kz * plane + code)
+            spot = pl.ds(pl.multiple_of(kz * total + place, rows), rows)
+            mine = [here[spot, :], there[spot, :]]
+            first = jnp.where(sec == 0, mine[0], mine[1])
+            second = jnp.where(sec == 0, mine[1], mine[0])
+            at = pl.ds(pl.multiple_of(owner * 2 * part, 2 * part), 2 * part)
+            own_ref[:, at] = jnp.concatenate([first, second], axis=1)
+
+
+def early_kernel(dims, codes, count, *refs):
+    arrays = refs[:count]
+    gain_ref, router_ref, gate_ref, up_ref, acc, route, square, own_ref = refs[count:]
+    acc[...] = jnp.zeros_like(acc)
+    route[...] = jnp.zeros_like(route)
+    square[...] = jnp.zeros_like(square)
+    own_ref[...] = jnp.zeros_like(own_ref)
+    gather_products(
+        dims, codes, arrays, gain_ref, router_ref, gate_ref, up_ref, (acc, route, square), own_ref
+    )
+
+
+def late_kernel(dims, codes, eps, count, *refs):
     nz, ny, nx = dims
     arrays = refs[:count]
     (
-        mask_ref,
         gain_ref,
         router_ref,
         gate_ref,
         up_ref,
+        acc_in,
+        route_in,
+        square_in,
+        own_in,
         down_ref,
-        keep_near,
-        keep_far,
-        send_near,
-        send_far,
+        mask_ref,
+        *outs,
         own_ref,
-        held,
         acc,
-        route_acc,
+        route,
         square,
         hidden,
         hidden_a,
         hidden_b,
-        xsems,
     ) = refs[count:]
-    width = held.shape[1]
+    acc[...] = acc_in[...]
+    route[...] = route_in[...]
+    square[...] = square_in[...]
+    own_ref[...] = own_in[...]
+    gather_products(
+        dims, codes, arrays, gain_ref, router_ref, gate_ref, up_ref, (acc, route, square), own_ref
+    )
+    width = gain_ref.shape[1]
     units = down_ref.shape[1]
-    part = width // (nz * ny * nx) // 2
+    rows = own_ref.shape[0]
     me = lax.axis_index("dev")
     sec = lax.axis_index("sec")
-    step = width // STEPS
-
-    copies = []
-    if not pieces:
-        copies.append(pltpu.make_async_copy(arrays[0], held, xsems.at[0]))
-    for i, (which, offset, length, code, side, start) in enumerate(pieces):
-        whose = sec if side == 0 else 1 - sec
-        column = pl.multiple_of(((me ^ code) * 2 + whose) * part, part)
-        copies.append(
-            pltpu.make_async_copy(
-                arrays[which].at[pl.ds(offset, length)],
-                held.at[pl.ds(start, length), pl.ds(column, part)],
-                xsems.at[i],
-            )
-        )
-    for c in copies:
-        c.start()
-    for c in copies:
-        c.wait()
-    acc[...] = jnp.zeros_like(acc)
-    route_acc[...] = jnp.zeros_like(route_acc)
-    square[...] = jnp.zeros_like(square)
-
-    def body(c, carry):
-        span = pl.ds(pl.multiple_of(c * step, step), step)
-        x = held[:, span].astype(F32)
-        total = square[...]
-        for t in range(step // 128):
-            piece = x[:, t * 128 : (t + 1) * 128]
-            total = total + piece * piece
-        square[...] = total
-        scaled = (x * gain_ref[:, span]).astype(BF)
-        both = jnp.concatenate([gate_ref[0, span], up_ref[0, span]], axis=1)
-        acc[...] += jnp.dot(scaled, both, preferred_element_type=F32)
-        route_acc[...] += lax.dot_general(
-            scaled, router_ref[:, span], (((1,), (1,)), ((), ())), preferred_element_type=F32
-        )
-        return carry
-
-    lax.fori_loop(0, STEPS, body, 0)
     mean = jnp.sum(square[...], axis=1, keepdims=True) * (1.0 / width)
     inverse = lax.rsqrt(mean + eps)
-    live = mask_ref[:, : route_acc.shape[1]].astype(F32) > 0.5
-    logits = jnp.where(live, route_acc[...] * inverse, masked_score)
+    live = mask_ref[:, : route.shape[1]].astype(F32) > 0.5
+    logits = jnp.where(live, route[...] * inverse, masked_score)
     top = jnp.max(logits, axis=1, keepdims=True)
     powers = jnp.where(live, jnp.exp(logits - top), 0.0)
     lane = lax.broadcasted_iota(jnp.int32, powers.shape, 1)
@@ -194,85 +232,106 @@
     gate = acc[:, :units] * inverse
     up = acc[:, units:] * inverse
     hidden[...] = (gate / (1.0 + jnp.exp(-gate)) * up * weight).astype(BF)
-    own_ref[...] = held[pl.ds(pl.multiple_of(me * rows, rows), rows)]
     for kz in range(nz):
         for ky in range(ny):
             for kx in range(nx):
-                place = pl.multiple_of((me ^ code_of(dims, kz, ky, kx)) * rows, rows)
+                chip = me ^ code_of(dims, kz, ky, kx)
+                place = pl.multiple_of(row_of(dims, chip) * rows, rows)
                 block = hidden[pl.ds(place, rows)]
                 hidden_a[pl.ds(((kx * ny + ky) * nz + kz) * rows, rows)] = block
                 hidden_b[pl.ds(((ky * nx + kx) * nz + kz) * rows, rows)] = block
-    quarter = width // 4
+    finish(dims, sec, hidden_a, hidden_b, down_ref, outs)
+
+
+def finish(dims, sec, hidden_a, hidden_b, down_ref, outs):
+    _, ny, nx = dims
+    keep_near, keep_far, send_near, send_far = outs
+    quarter = keep_near.shape[1]
     wide = quarter // 2
+    near_cut = hidden_a.shape[0] // nx
+    far_cut = hidden_a.shape[0] - near_cut
     for h, near, far in ((1, send_near, send_far), (0, keep_near, keep_far)):
-        near_cut = hidden.shape[0] // nx
-        far_cut = hidden.shape[0] - near_cut
+        whose = sec if h == 0 else 1 - sec
         for q, (source, first) in enumerate(((hidden_a, nx), (hidden_b, ny))):
             cut = source.shape[0] // first
             rest = source.shape[0] - cut
             for t in range(2):
-                whose = sec if h == 0 else 1 - sec
                 place = pl.multiple_of(whose * 2 * quarter + q * quarter + t * wide, wide)
                 found = jnp.dot(
-                    source[...],
-                    down_ref[0, :, pl.ds(place, wide)],
-                    preferred_element_type=F32,
+                    source[...], down_ref[0, :, pl.ds(place, wide)], preferred_element_type=F32
                 ).astype(BF)
                 span = slice(t * wide, (t + 1) * wide)
                 near[q * near_cut : q * near_cut + cut, span] = found[:cut]
                 far[q * far_cut : q * far_cut + rest, span] = found[cut:]
 
 
-def in_order(arrays, pieces, n, total_rows, part):
+def in_order(pairs, n, total_rows, part, dims):
     me = lax.axis_index("dev")
     sec = lax.axis_index("sec")
     held = jnp.zeros((total_rows, n * 2 * part), BF)
-    for which, offset, length, code, side, start in pieces:
-        whose = sec if side == 0 else 1 - sec
-        column = ((me ^ code) * 2 + whose) * part
-        held = lax.dynamic_update_slice(
-            held, arrays[which][offset : offset + length], (start, column)
+    for code, *both in pairs:
+        for side, array in enumerate(both):
+            for kz in range(dims[0]):
+                owner = me ^ (kz * dims[1] * dims[2] + code)
+                whose = sec if side == 0 else 1 - sec
+                block = array[kz * total_rows : (kz + 1) * total_rows]
+                held = lax.dynamic_update_slice(held, block, (0, (owner * 2 + whose) * part))
+    return held
+
+
+def experts(pairs, mask, gain, router, gate, up, down, dims, rows):
+    nz, ny, nx = dims
+    total_rows = nz * ny * nx * rows
+    _, width, units = gate.shape
+    count = max(1, len(pairs) // 2)
+    sums = [
+        jax.ShapeDtypeStruct((total_rows, 2 * units), F32),
+        jax.ShapeDtypeStruct((total_rows, router.shape[0]), F32),
+        jax.ShapeDtypeStruct((total_rows, 128), F32),
+        jax.ShapeDtypeStruct((rows, width), BF),
+    ]
+    params = pltpu.CompilerParams(vmem_limit_bytes=(4 + total_rows // 64) * MIB)
+
+    def cost(share):
+        return pl.CostEstimate(
+            flops=int(6 * total_rows * width * units * share),
+            bytes_accessed=int(6 * width * units * share),
+            transcendentals=0,
         )
-    return held
-
-
-def experts(arrays, pieces, mask, gain, router, gate, up, down, dims, rows):
-    nz, ny, nx = dims
-    n = nz * ny * nx
-    total_rows = n * rows
-    _, width, units = gate.shape
-    quarter = width // 4
-    lanes = router.shape[0]
+
+    early = [v for _, *both in pairs[:count] for v in both]
+    late = [v for _, *both in pairs[count:] for v in both]
+    codes = [p[0] for p in pairs]
+    part = pairs[0][1].shape[1]
+    found = None
+    if part % 128:
+        late, codes = [in_order(pairs, nz * ny * nx, total_rows, part, dims)], None
+        found = [jnp.zeros(v.shape, v.dtype) for v in sums]
+    found = found or pl.pallas_call(
+        functools.partial(early_kernel, dims, codes and codes[:count], len(early)),
+        out_shape=tuple(sums),
+        in_specs=[VM] * (len(early) + 4),
+        out_specs=(VM,) * 4,
+        compiler_params=params,
+        cost_estimate=cost(0.33),
+        name="experts_early",
+    )(*early, gain, router, gate, up)
     near = total_rows // nx + total_rows // ny
-    far = 2 * total_rows - near
-    part = width // n // 2
-    if part % 128:
-        arrays = [in_order(arrays, pieces, n, total_rows, part)]
-        pieces = ()
-    shapes = [jax.ShapeDtypeStruct((r, quarter), BF) for r in (near, far, near, far)]
+    shapes = [
+        jax.ShapeDtypeStruct((r, width // 4), BF)
+        for r in (near, 2 * total_rows - near, near, 2 * total_rows - near)
+    ]
     return pl.pallas_call(
-        functools.partial(expert_kernel, dims, pieces, rows, 1e-6, len(arrays)),
-        out_shape=(*shapes, jax.ShapeDtypeStruct((rows, width), BF)),
-        in_specs=[ANY] * len(arrays) + [VM] * 6,
+        functools.partial(late_kernel, dims, codes and codes[count:], 1e-6, len(late)),
+        out_shape=(*shapes, sums[3]),
+        in_specs=[VM] * (len(late) + 10),
         out_specs=(VM,) * 5,
-        scratch_shapes=[
-            pltpu.VMEM((total_rows, width), BF),
-            pltpu.VMEM((total_rows, 2 * units), F32),
-            pltpu.VMEM((total_rows, lanes), F32),
-            pltpu.VMEM((total_rows, 128), F32),
-            pltpu.VMEM((total_rows, units), BF),
-            pltpu.VMEM((total_rows, units), BF),
-            pltpu.VMEM((total_rows, units), BF),
-            pltpu.SemaphoreType.DMA((max(1, len(pieces)),)),
-        ],
-        compiler_params=pltpu.CompilerParams(vmem_limit_bytes=(6 + n // 2) * MIB),
-        cost_estimate=pl.CostEstimate(
-            flops=6 * total_rows * width * units,
-            bytes_accessed=6 * width * units + 6 * total_rows * width,
-            transcendentals=0,
-        ),
-        name="experts",
-    )(*arrays, mask, gain, router, gate, up, down)
+        scratch_shapes=[pltpu.VMEM(v.shape, v.dtype) for v in sums[:3]]
+        + [pltpu.VMEM((total_rows, units), BF)] * 3,
+        compiler_params=params,
+        cost_estimate=cost(0.67),
+        name="experts_late",
+    )(*late, gain, router, gate, up, *found, down, mask)
 
 
 GROUP = 4
@@ -417,16 +476,18 @@
     )(cache_lengths, ids, queries, new_key, new_value, extra, key_cache, value_cache)
 
 
-def pack_kernel(dims, lanes, *refs):
-    nz, ny, nx = dims
-    lines, outs = refs[:nz], refs[nz:]
-    mine_ref, xa, ya = outs[0], outs[1 : nx], outs[nx:]
+def pack_kernel(ny, nx, lanes, extras, count, *refs):
+    lines, outs = refs[:count], refs[count:]
     rows = lines[0].shape[0]
-    plane = ny * nx * 128
-    half = lines[0].shape[1] - plane - lanes
-    for kz in range(nz):
-        span = slice(kz * rows, (kz + 1) * rows)
-        source = lines[kz]
+    z = lax.axis_index("dev") // (ny * nx)
+    for kz, source in enumerate(lines):
+        span = pl.ds(pl.multiple_of((z ^ kz) * rows, rows), rows)
+        if not extras:
+            outs[0][span, :] = source[...]
+            continue
+        mine_ref, xa, ya = outs[0], outs[1:nx], outs[nx:]
+        plane = ny * nx * 128
+        half = source.shape[1] - plane - lanes
 
         def block(ky, kx):
             at = half + (ky * nx + kx) * 128
@@ -447,17 +508,19 @@
             ya[ky - 1][span, half + 128 :] = mask
 
 
-def pack(lines, lanes, dims):
-    nz, ny, nx = dims
+def pack(lines, lanes, dims, extras):
+    _, ny, nx = dims
     rows, width = lines[0].shape
-    half = width - ny * nx * 128 - lanes
-    widths = [half + 128 + lanes]
-    widths += [half + ny * 128 + lanes] * (nx - 1)
-    widths += [half + 128 + lanes] * (ny - 1)
+    widths = [width]
+    if extras:
+        half = width - ny * nx * 128 - lanes
+        widths = [half + 128 + lanes]
+        widths += [half + ny * 128 + lanes] * (nx - 1)
+        widths += [half + 128 + lanes] * (ny - 1)
     outs = pl.pallas_call(
-        functools.partial(pack_kernel, dims, lanes),
-        out_shape=tuple(jax.ShapeDtypeStruct((nz * rows, w), BF) for w in widths),
-        in_specs=[VM] * nz,
+        functools.partial(pack_kernel, ny, nx, lanes, extras, len(lines)),
+        out_shape=tuple(jax.ShapeDtypeStruct((len(lines) * rows, w), BF) for w in widths),
+        in_specs=[VM] * len(lines),
         out_specs=(VM,) * len(widths),
         compiler_params=pltpu.CompilerParams(vmem_limit_bytes=16 * MIB),
         name="pack",
@@ -465,36 +528,65 @@
     return outs[0], outs[1:nx], outs[nx:]
 
 
-def arrange_kernel(pieces, rows, count, *refs):
+def arrange_kernel(places, size, *refs):
+    count = len(places)
     arrays, outs, sems = refs[:count], refs[count : count + 2], refs[count + 2]
-    me = lax.axis_index("dev")
     copies = []
-    for i, (which, offset, code, column, target) in enumerate(pieces):
-        place = pl.multiple_of((me ^ code) * rows, rows)
-        out = outs[target]
-        copies.append(
-            pltpu.make_async_copy(
-                arrays[which].at[pl.ds(offset, rows), pl.ds(column, out.shape[1])],
-                out.at[pl.ds(place, rows)],
-                sems.at[i],
+    for i, (slot, *columns) in enumerate(places):
+        for j, out in enumerate(outs):
+            copies.append(
+                pltpu.make_async_copy(
+                    arrays[i].at[:, pl.ds(columns[j], out.shape[1])],
+                    out.at[pl.ds(slot * size, size)],
+                    sems.at[2 * i + j],
+                )
             )
-        )
     for c in copies:
         c.start()
     for c in copies:
         c.wait()
 
 
-def arrange(arrays, pieces, lanes, n, rows):
+def arrange(arrays, places, lanes, size):
+    tall = len(places) * size
     return pl.pallas_call(
-        functools.partial(arrange_kernel, pieces, rows, len(arrays)),
-        out_shape=tuple(jax.ShapeDtypeStruct((n * rows, w), BF) for w in (128, lanes)),
+        functools.partial(arrange_kernel, places, size),
+        out_shape=tuple(jax.ShapeDtypeStruct((tall, w), BF) for w in (128, lanes)),
         in_specs=[ANY] * len(arrays),
         out_specs=(VM, VM),
-        scratch_shapes=[pltpu.SemaphoreType.DMA((len(pieces),))],
+        scratch_shapes=[pltpu.SemaphoreType.DMA((2 * len(places),))],
         compiler_params=pltpu.CompilerParams(vmem_limit_bytes=8 * MIB),
         name="arrange",
     )(*arrays)
+
+
+def merge_kernel(dims, rows, *refs):
+    nz, ny, nx = dims
+    parts, mask, (stacked, mask_out) = refs[:nz], refs[nz], refs[nz + 1 :]
+    here = lax.axis_index("dev") % (ny * nx)
+    size = nz * rows
+    total = ny * nx * size
+    for code in range(ny * nx):
+        place = (here ^ code) * size
+        span = slice(code * size, (code + 1) * size)
+        mask_out[pl.ds(pl.multiple_of(place, size), size), :] = mask[span, :]
+        for kz in range(nz):
+            spot = pl.ds(pl.multiple_of(kz * total + place, size), size)
+            stacked[spot, :] = parts[kz][span, :]
+
+
+def merge(parts, mask, dims, rows):
+    nz, ny, nx = dims
+    total = nz * ny * nx * rows
+    shapes = [(nz * total, parts[0].shape[1]), (total, mask.shape[1])]
+    return pl.pallas_call(
+        functools.partial(merge_kernel, dims, rows),
+        out_shape=tuple(jax.ShapeDtypeStruct(t, BF) for t in shapes),
+        in_specs=[VM] * (nz + 1),
+        out_specs=(VM, VM),
+        compiler_params=pltpu.CompilerParams(vmem_limit_bytes=16 * MIB),
+        name="merge",
+    )(*parts, mask)
 
 
 def local(
@@ -548,75 +640,47 @@
     a_lines = {kz: trade(a_own[kz], dims, kz=kz) for kz in steps}
     b_own, a_lines[steps[-1]] = lax.optimization_barrier((b_own, a_lines[steps[-1]]))
     b_lines = {kz: trade(b_own, dims, kz=kz) for kz in steps}
-    mine, xa, ya = pack([a_own[0]] + [a_lines[kz] for kz in range(1, nz)], lanes, dims)
-    arrays, pieces, places = [], [], []
-
-    def add(array, ky, kx, column, block=None, mask=None):
-        arrays.append(array)
-        for kz in range(nz):
-            code = code_of(dims, kz, ky, kx)
-            pieces.append((len(arrays) - 1, kz * rows, code, column))
-            if block is not None:
-                places.append((len(arrays) - 1, kz * rows, code, block, 0))
-                places.append((len(arrays) - 1, kz * rows, code, mask, 1))
-
-    add(mine, 0, 0, 0, middle, middle + 128)
+    mine, xa, ya = pack([a_own[0]] + [a_lines[kz] for kz in range(1, nz)], lanes, dims, True)
+    found = [(mine, 0, 0, 0, True, middle, middle + 128)]
     near_a = {kx: trade(xa[kx - 1], dims, kx=kx) for kx in range(1, nx)}
     for kx, v in near_a.items():
-        add(v, 0, kx, 0, middle, middle + ny * 128)
+        found.append((v, 0, kx, 0, True, middle, middle + ny * 128))
     for ky in range(1, ny):
-        add(trade(ya[ky - 1], dims, ky=ky), ky, 0, 0, middle, middle + 128)
+        v = trade(ya[ky - 1], dims, ky=ky)
+        found.append((v, ky, 0, 0, True, middle, middle + 128))
     b = jnp.concatenate([b_own] + [b_lines[kz] for kz in range(1, nz)], axis=0)
-    add(b, 0, 0, 1)
+    found.append((b, 0, 0, 1, False))
     near_b = {ky: trade(b, dims, ky=ky) for ky in range(1, ny)}
     for ky, v in near_b.items():
-        add(v, ky, 0, 1)
+        found.append((v, ky, 0, 1, False))
     for kx in range(1, nx):
-        add(trade(b, dims, kx=kx), 0, kx, 1)
+        found.append((trade(b, dims, kx=kx), 0, kx, 1, False))
     for kx, v in near_a.items():
         for ky in range(1, ny):
-            add(trade(v, dims, ky=ky), ky, kx, 0, middle + ky * 128, middle + ny * 128)
+            third = trade(v, dims, ky=ky)
+            found.append((third, ky, kx, 0, True, middle + ky * 128, middle + ny * 128))
     for ky, v in near_b.items():
         for kx in range(1, nx):
-            add(trade(v, dims, kx=kx), ky, kx, 1)
-    keep, send = project(arrays, tuple(pieces), out_weight, n, rows)
-    residual, mask = arrange(arrays, tuple(places), lanes, n, rows)
-    residual = residual[:, :part]
+            found.append((trade(v, dims, kx=kx), ky, kx, 1, False))
+
+    size = nz * rows
+    pieces = tuple((f[1] * nx + f[2], f[3], f[4]) for f in found)
+    keep, send = project([f[0] for f in found], pieces, out_weight, dims, rows)
+    carriers = [f for f in found if len(f) > 5]
+    places = tuple((f[1] * nx + f[2], f[5], f[6]) for f in carriers)
+    residual, mask = arrange([f[0] for f in carriers], places, lanes, size)
     projected = (keep + swap_sec(send)).astype(BF)
-    mixed = (residual.astype(F32) + projected.astype(F32)).astype(BF)
-
-    half_rows = total_rows // 2
+    mixed = (residual[:, :part].astype(F32) + projected.astype(F32)).astype(BF)
+
     lines = {kz: trade(mixed, dims, kz=kz) for kz in steps}
-    stacked = jnp.concatenate([mixed] + [lines[kz] for kz in range(1, nz)], axis=0)
-    arrays, pieces = [stacked, swap_sec(stacked)], []
-    for side in range(2):
-        for kz in range(nz):
-            pieces.append((side, kz * total_rows, total_rows, code_of(dims, kz, 0, 0), side, 0))
-    parted = stacked.reshape(nz, 2, half_rows, part)
-    a, b = (parted[:, h].reshape(nz * half_rows, part) for h in range(2))
-    for wave in planes(a, b, dims):
-        whole = swap_sec(jnp.concatenate([array for _, _, array in wave], axis=0))
-        for i, ((ky, kx), half, array) in enumerate(wave):
-            for which, base, side in ((len(arrays), 0, 0), (None, i * nz * half_rows, 1)):
-                for kz in range(nz):
-                    pieces.append(
-                        (
-                            which if side == 0 else -1,
-                            base + kz * half_rows,
-                            half_rows,
-                            code_of(dims, kz, ky, kx),
-                            side,
-                            half * half_rows,
-                        )
-                    )
-            arrays.append(array)
-        arrays.append(whole)
-        pieces = [
-            (len(arrays) - 1 if p[0] == -1 else p[0],) + tuple(p[1:]) for p in pieces
-        ]
+    stacked, mask = merge([mixed] + [lines[kz] for kz in range(1, nz)], mask, dims, rows)
+    pairs = []
+    for ky in range(ny):
+        for kx in range(nx):
+            got = stacked if ky + kx == 0 else trade(stacked, dims, ky=ky, kx=kx)
+            pairs.append((ky * nx + kx, got, swap_sec(got)))
     keep_near, keep_far, send_near, send_far, own_mixed = experts(
-        arrays,
-        tuple(pieces),
+        pairs,
         mask,
         norm_gain.reshape(1, width),
         router_weight.T,

time: 110 us -> 108 us (0.982)
  Pallas kernels: 17.3 us -> 13.5 us
  waiting for transfers between devices: 48.1 us -> 51.2 us
  starting transfers between devices: 40.8 us -> 38.6 us
    ppermute x28 -> x25, waiting for transfers between devices: 43 us -> 47.1 us  [trade(): return lax.ppermute(value, 'dev', [(d, d ^ code) for d in range(n)])]
    pallas_call x4 -> x6, Pallas kernels: 9.73 us -> 5.99 us  [the longest x1 2.76 us: experts(): pl.pallas_call(functools.partial(late_kernel, dims, codes and codes[count...]
    ppermute x28 -> x25, starting transfers between devices: 39.4 us -> 37.8 us  [trade(): return lax.ppermute(value, 'dev', [(d, d ^ code) for d in range(n)])]
  transfers between devices with their start and end apart: 36 -> 33, of which waited for: 23 -> 20; matrix products, arithmetic and copies ran while one was open for 1% -> 1% of each run, Pallas kernels for 0% -> 1%
where the time goes in v3:
time: 108 us; the launch traced here: 107 us
  waiting for transfers between devices  51.2 us (47%)
  starting transfers between devices  38.6 us (36%)
  Pallas kernels  13.5 us (12%)
  local copies, waits for them, and re-layouts  2.3 us (2%)
  other arithmetic  1.37 us (1%)
    ppermute x25, waiting for transfers between devices, trade(): return lax.ppermute(value, 'dev', [(d, d ^ code) for d in range(n)])  47.1 us
    ppermute x25, starting transfers between devices, trade(): return lax.ppermute(value, 'dev', [(d, d ^ code) for d in range(n)])  37.8 us
    pallas_call x1, Pallas kernels, attention(): pl.pallas_call(functools.partial(attend_kernel, dims, lanes), out_shape=t...  7.47 us
    ppermute x8, waiting for transfers between devices, swap_sec(): return lax.ppermute(value, 'sec', [(0, 1), (1, 0)])  4.1 us
    pallas_call x1, Pallas kernels, experts(): pl.pallas_call(functools.partial(late_kernel, dims, codes and codes[count...  2.76 us
    unnamed x17, local copies, waits for them, and re-layouts  2.21 us
  transfers between devices with their start and end apart: 33, of which 20 were waited for; matrix products, arithmetic and copies ran while one was open for 1% of the time, Pallas kernels for 1%

profile of v3, /device:TPU:0, one launch (start us, length us, event | category | flops | bytes accessed | tf_op | source)
XLA Modules:
  0.0 107.2 jit_solution(3492262203230911527)
XLA Ops:
  0.0 7.5 %attend.1 = (bf16[16,2048]{1,0:T(8,128)(2,1)}, bf16[16,2688]{1,0:T(8,128)(2,1)}, bf16[16,2688]{1,0:T(8,128)(2,1)}, bf16[16,2688]{1,0:T(8,128)(2,1)}, bf16[16,2688]{1,0:T(8,128)(2,1)}) custom-call(s32[16]{0:T(128)} %refs_0_.1, s32[8,16]{1,0:T(8,128)} %bitcast.7, bf16[16,4096]{1,0:T(8,128)(2,1)} %refs_2_.1, bf16[16,256]{1,0:T(8,128)(2,1)} %refs_3_.1, ...), custom_call_target="tpu_custom_call" | custom-call | flops 402653184 | bytes 12582912 | tf_op jit(solution)/shard_map/attend/pallas_call | solution.py:456
  7.5 3.1 %collective-permute-start = (bf16[16,2688]{1,0:T(8,128)(2,1)}, bf16[16,2688]{1,0:T(8,128)(2,1)S(1)}, u32[]{:S(2)}, u32[]{:S(2)}) collective-permute-start(bf16[16,2688]{1,0:T(8,128)(2,1)} %get-tuple-element.32), channel_id=1, source_target_pairs={{0,4},{1,5},{2,6},{3,7},{4,0},{5,1},{6,2},{7,3},{8,12},{9,13},{10,... | collective-permute-start | bytes 258056 | tf_op jit(solution)/shard_map/ppermute | solution.py:34
  10.6 2.4 %collective-permute-start.1 = (bf16[16,2688]{1,0:T(8,128)(2,1)}, bf16[16,2688]{1,0:T(8,128)(2,1)S(1)}, u32[]{:S(2)}, u32[]{:S(2)}) collective-permute-start(bf16[16,2688]{1,0:T(8,128)(2,1)} %get-tuple-element.34), channel_id=1, source_target_pairs={{0,8},{1,9},{2,10},{3,11},{4,12},{5,13},{6,14},{7,15},{8,0},{9,1},... | collective-permute-start | bytes 258056 | tf_op jit(solution)/shard_map/ppermute | solution.py:34
  13.0 0.0 collective-permute-start.2
  13.0 0.3 collective-permute-done.refs_1_
  13.3 2.0 %collective-permute-start.6 = (bf16[16,2048]{1,0:T(8,128)(2,1)}, bf16[16,2048]{1,0:T(8,128)(2,1)S(1)}, u32[]{:S(2)}, u32[]{:S(2)}) collective-permute-start(bf16[16,2048]{1,0:T(8,128)(2,1)} %get-tuple-element.40), channel_id=1, source_target_pairs={{0,4},{1,5},{2,6},{3,7},{4,0},{5,1},{6,2},{7,3},{8,12},{9,13},{10,... | collective-permute-start | bytes 196616 | tf_op jit(solution)/shard_map/ppermute | solution.py:34
  15.3 0.9 constant_dynamic-update-slice_fusion.3
  16.2 3.3 %collective-permute-start.7 = (bf16[16,2048]{1,0:T(8,128)(2,1)}, bf16[16,2048]{1,0:T(8,128)(2,1)S(1)}, u32[]{:S(2)}, u32[]{:S(2)}) collective-permute-start(bf16[16,2048]{1,0:T(8,128)(2,1)} %get-tuple-element.40), channel_id=1, source_target_pairs={{0,8},{1,9},{2,10},{3,11},{4,12},{5,13},{6,14},{7,15},{8,0},{9,1},... | collective-permute-start | bytes 196616 | tf_op jit(solution)/shard_map/ppermute | solution.py:34
  19.4 1.6 %collective-permute-done.1.refs_2_ = bf16[16,2688]{1,0:T(8,128)(2,1)S(1)} collective-permute-done((bf16[16,2688]{1,0:T(8,128)(2,1)}, bf16[16,2688]{1,0:T(8,128)(2,1)S(1)}, u32[]{:S(2)}, u32[]{:S(2)}) %collective-permute-start.1) | collective-permute-done | bytes 86048 | tf_op jit(solution)/shard_map/ppermute | solution.py:34
  21.0 0.9 copy-done.5
  21.9 0.1 pack.1
  22.0 1.7 %collective-permute-start.3 = (bf16[64,2432]{1,0:T(8,128)(2,1)S(1)}, bf16[64,2432]{1,0:T(8,128)(2,1)S(1)}, u32[]{:S(2)}, u32[]{:S(2)}) collective-permute-start(bf16[64,2432]{1,0:T(8,128)(2,1)S(1)} %get-tuple-element.37), channel_id=1, source_target_pairs={{0,1},{1,0},{2,3},{3,2},{4,5},{5,4},{6,7},{7,6},{8,9},{9,8},{10,11... | collective-permute-start | bytes 933896 | tf_op jit(solution)/shard_map/ppermute | solution.py:34
  23.7 2.4 %collective-permute-done.7 = bf16[16,2048]{1,0:T(8,128)(2,1)S(1)} collective-permute-done((bf16[16,2048]{1,0:T(8,128)(2,1)}, bf16[16,2048]{1,0:T(8,128)(2,1)S(1)}, u32[]{:S(2)}, u32[]{:S(2)}) %collective-permute-start.7) | collective-permute-done | bytes 65568 | tf_op jit(solution)/shard_map/ppermute | solution.py:34
  26.2 1.6 %collective-permute-start.9 = (bf16[64,2048]{1,0:T(8,128)(2,1)S(1)}, bf16[64,2048]{1,0:T(8,128)(2,1)S(1)}, u32[]{:S(2)}, u32[]{:S(2)}) collective-permute-start(bf16[64,2048]{1,0:T(8,128)(2,1)S(1)} %constant_dynamic-update-slice_fusion.refs_3_), channel_id=1, source_target_pairs={{0,2},{1,3},{2,0},{3,1},{4,6},{5,7},{6,4},{7,5},{8,10},{9,11},{10,... | collective-permute-start | bytes 786440 | tf_op jit(solution)/shard_map/ppermute | solution.py:34
  27.7 1.2 %collective-permute-done.3.refs_1_ = bf16[64,2432]{1,0:T(8,128)(2,1)S(1)} collective-permute-done((bf16[64,2432]{1,0:T(8,128)(2,1)S(1)}, bf16[64,2432]{1,0:T(8,128)(2,1)S(1)}, u32[]{:S(2)}, u32[]{:S(2)}) %collective-permute-start.3) | collective-permute-done | bytes 311328 | tf_op jit(solution)/shard_map/ppermute | solution.py:34
  29.0 1.5 %collective-permute-start.5 = (bf16[64,2432]{1,0:T(8,128)(2,1)S(1)}, bf16[64,2432]{1,0:T(8,128)(2,1)S(1)}, u32[]{:S(2)}, u32[]{:S(2)}) collective-permute-start(bf16[64,2432]{1,0:T(8,128)(2,1)S(1)} %collective-permute-done.3.refs_1_), channel_id=1, source_target_pairs={{0,2},{1,3},{2,0},{3,1},{4,6},{5,7},{6,4},{7,5},{8,10},{9,11},{10,... | collective-permute-start | bytes 933896 | tf_op jit(solution)/shard_map/ppermute | solution.py:34
  30.4 0.6 collective-permute-start.4
  31.0 1.6 %collective-permute-start.10 = (bf16[64,2048]{1,0:T(8,128)(2,1)S(1)}, bf16[64,2048]{1,0:T(8,128)(2,1)S(1)}, u32[]{:S(2)}, u32[]{:S(2)}) collective-permute-start(bf16[64,2048]{1,0:T(8,128)(2,1)S(1)} %constant_dynamic-update-slice_fusion.refs_3_), channel_id=1, source_target_pairs={{0,1},{1,0},{2,3},{3,2},{4,5},{5,4},{6,7},{7,6},{8,9},{9,8},{10,11... | collective-permute-start | bytes 786440 | tf_op jit(solution)/shard_map/ppermute | solution.py:34
  32.6 2.9 %collective-permute-done.9.refs_4_ = bf16[64,2048]{1,0:T(8,128)(2,1)S(1)} collective-permute-done((bf16[64,2048]{1,0:T(8,128)(2,1)S(1)}, bf16[64,2048]{1,0:T(8,128)(2,1)S(1)}, u32[]{:S(2)}, u32[]{:S(2)}) %collective-permute-start.9) | collective-permute-done | bytes 262176 | tf_op jit(solution)/shard_map/ppermute | solution.py:34
  35.5 1.6 %collective-permute-start.11 = (bf16[64,2048]{1,0:T(8,128)(2,1)S(1)}, bf16[64,2048]{1,0:T(8,128)(2,1)S(1)}, u32[]{:S(2)}, u32[]{:S(2)}) collective-permute-start(bf16[64,2048]{1,0:T(8,128)(2,1)S(1)} %collective-permute-done.9.refs_4_), channel_id=1, source_target_pairs={{0,1},{1,0},{2,3},{3,2},{4,5},{5,4},{6,7},{7,6},{8,9},{9,8},{10,11... | collective-permute-start | bytes 786440 | tf_op jit(solution)/shard_map/ppermute | solution.py:34
  37.1 7.9 %collective-permute-done.4.refs_2_ = bf16[64,2304]{1,0:T(8,128)(2,1)S(1)} collective-permute-done((bf16[64,2304]{1,0:T(8,128)(2,1)S(1)}, bf16[64,2304]{1,0:T(8,128)(2,1)S(1)}, u32[]{:S(2)}, u32[]{:S(2)}) %collective-permute-start.4) | collective-permute-done | bytes 294944 | tf_op jit(solution)/shard_map/ppermute | solution.py:34
  45.0 0.0 copy-start
  45.0 0.0 copy-start.1
  45.0 1.7 %project.1 = (f32[256,128]{1,0:T(8,128)S(1)}, f32[256,128]{1,0:T(8,128)S(1)}) custom-call(bf16[64,2304]{1,0:T(8,128)(2,1)S(1)} %get-tuple-element.36.refs_0_, bf16[64,2432]{1,0:T(8,128)(2,1)S(1)} %collective-permute-done.3.refs_1_, bf16[64,2304]{1,0:T(8,128)(2,1)S(1)} %collective-permute-done.4.refs_2_, ...), custom_call_target="tpu_custom_call" | custom-call | flops 536870912 | bytes 4194304 | tf_op jit(solution)/shard_map/project/pallas_call | solution.py:110
  46.7 0.1 collective-permute-start.12
  46.8 0.1 arrange.1
  46.9 1.2 %collective-permute-done.12 = f32[256,128]{1,0:T(8,128)S(1)} collective-permute-done((f32[256,128]{1,0:T(8,128)S(1)}, f32[256,128]{1,0:T(8,128)S(1)}, u32[]{:S(2)}, u32[]{:S(2)}) %collective-permute-start.12) | collective-permute-done | bytes 131104 | tf_op jit(solution)/shard_map/ppermute | solution.py:42
  48.1 2.6 %collective-permute-start.13 = (bf16[256,128]{1,0:T(8,128)(2,1)S(1)}, bf16[256,128]{1,0:T(8,128)(2,1)S(1)}, u32[]{:S(2)}, u32[]{:S(2)}) collective-permute-start(bf16[256,128]{1,0:T(8,128)(2,1)S(1)} %add_convert_fusion.1.refs_0_), channel_id=1, source_target_pairs={{0,4},{1,5},{2,6},{3,7},{4,0},{5,1},{6,2},{7,3},{8,12},{9,13},{10,... | collective-permute-start | bytes 196616 | tf_op jit(solution)/shard_map/ppermute | solution.py:34
  50.8 0.9 collective-permute-start.14
  51.7 1.5 %collective-permute-start.15 = (bf16[256,128]{1,0:T(8,128)(2,1)S(1)}, bf16[256,128]{1,0:T(8,128)(2,1)S(1)}, u32[]{:S(2)}, u32[]{:S(2)}) collective-permute-start(bf16[256,128]{1,0:T(8,128)(2,1)S(1)} %add_convert_fusion.1.refs_0_), channel_id=1, source_target_pairs={{0,12},{1,13},{2,14},{3,15},{4,8},{5,9},{6,10},{7,11},{8,4},{9,5},... | collective-permute-start | bytes 196616 | tf_op jit(solution)/shard_map/ppermute | solution.py:34
  53.2 0.0 collective-permute-done.13.refs_1_
  53.3 5.7 %collective-permute-done.14.refs_2_ = bf16[256,128]{1,0:T(8,128)(2,1)S(1)} collective-permute-done((bf16[256,128]{1,0:T(8,128)(2,1)S(1)}, bf16[256,128]{1,0:T(8,128)(2,1)S(1)}, u32[]{:S(2)}, u32[]{:S(2)}) %collective-permute-start.14) | collective-permute-done | bytes 65568 | tf_op jit(solution)/shard_map/ppermute | solution.py:34
  59.1 0.9 collective-permute-start.21
  60.0 1.5 %collective-permute-start.16 = (bf16[1024,128]{1,0:T(8,128)(2,1)S(1)}, bf16[1024,128]{1,0:T(8,128)(2,1)S(1)}, u32[]{:S(2)}, u32[]{:S(2)}) collective-permute-start(bf16[1024,128]{1,0:T(8,128)(2,1)S(1)} %get-tuple-element.44.refs_0_), channel_id=1, source_target_pairs={{0,2},{1,3},{2,0},{3,1},{4,6},{5,7},{6,4},{7,5},{8,10},{9,11},{10,... | collective-permute-start | bytes 786440 | tf_op jit(solution)/shard_map/ppermute | solution.py:34
  61.5 1.1 %collective-permute-start.18 = (bf16[1024,128]{1,0:T(8,128)(2,1)S(1)}, bf16[1024,128]{1,0:T(8,128)(2,1)S(1)}, u32[]{:S(2)}, u32[]{:S(2)}) collective-permute-start(bf16[1024,128]{1,0:T(8,128)(2,1)S(1)} %get-tuple-element.44.refs_0_), channel_id=1, source_target_pairs={{0,3},{1,2},{2,1},{3,0},{4,7},{5,6},{6,5},{7,4},{8,11},{9,10},{10,... | collective-permute-start | bytes 786440 | tf_op jit(solution)/shard_map/ppermute | solution.py:34
  62.6 5.8 %collective-permute-done.21.refs_2_ = bf16[1024,128]{1,0:T(8,128)(2,1)S(1)} collective-permute-done((bf16[1024,128]{1,0:T(8,128)(2,1)S(1)}, bf16[1024,128]{1,0:T(8,128)(2,1)S(1)}, u32[]{:S(2)}, u32[]{:S(2)}) %collective-permute-start.21) | collective-permute-done | bytes 262176 | tf_op jit(solution)/shard_map/ppermute | solution.py:34
  68.4 3.3 %collective-permute-done.16.refs_0_ = bf16[1024,128]{1,0:T(8,128)(2,1)S(1)} collective-permute-done((bf16[1024,128]{1,0:T(8,128)(2,1)S(1)}, bf16[1024,128]{1,0:T(8,128)(2,1)S(1)}, u32[]{:S(2)}, u32[]{:S(2)}) %collective-permute-start.16) | collective-permute-done | bytes 262176 | tf_op jit(solution)/shard_map/ppermute | solution.py:34
  71.7 0.9 collective-permute-done.18.refs_2_
  72.6 0.0 copy-start.2
  72.6 1.3 %experts_early.1 = (f32[256,768]{1,0:T(8,128)S(1)}, f32[256,16]{1,0:T(8,128)S(1)}, f32[256,128]{1,0:T(8,128)S(1)}, bf16[16,4096]{1,0:T(8,128)(2,1)S(1)}) custom-call(bf16[1024,128]{1,0:T(8,128)(2,1)S(1)} %get-tuple-element.44.refs_0_, bf16[1024,128]{1,0:T(8,128)(2,1)S(1)} %collective-permute-done.20.refs_1_, ...), custom_call_target="tpu_custom_call" | custom-call | flops 797253312 | bytes 3114270 | tf_op jit(solution)/shard_map/experts_early/pallas_call | solution.py:310
  73.9 0.2 collective-permute-done.19.refs_3_
  74.1 0.4 copy-done.2
  74.5 2.8 %experts_late.1 = (bf16[256,1024]{1,0:T(8,128)(2,1)S(1)}, bf16[256,1024]{1,0:T(8,128)(2,1)S(1)}, bf16[256,1024]{1,0:T(8,128)(2,1)S(1)}, bf16[256,1024]{1,0:T(8,128)(2,1)S(1)}, bf16[16,4096]{1,0:T(8,128)(2,1)S(1)}) custom-call(bf16[1024,128]{1,0:T(8,128)(2,1)S(1)} %collective-permute-done.16.refs_0_, bf16[1024,128]{1,0:T(8,128)(2,1)S(1)} %collective-permute-done.17.refs_1_, ...), custom_call_target="tpu_custom_call" | custom-call | flops 1618665856 | bytes 6322913 | tf_op jit(solution)/shard_map/experts_late/pallas_call | solution.py:324
  77.3 0.6 collective-permute-start.24
  77.9 0.1 collective-permute-start.23
  77.9 1.5 %collective-permute-done.24 = bf16[256,1024]{1,0:T(8,128)(2,1)S(1)} collective-permute-done((bf16[256,1024]{1,0:T(8,128)(2,1)S(1)}, bf16[256,1024]{1,0:T(8,128)(2,1)S(1)}, u32[]{:S(2)}, u32[]{:S(2)}) %collective-permute-start.24) | collective-permute-done | bytes 524320 | tf_op jit(solution)/shard_map/ppermute | solution.py:42
  79.4 0.2 add_convert_fusion
  79.6 1.4 %collective-permute-start.25 = (bf16[128,1024]{1,0:T(8,128)(2,1)S(1)}, bf16[128,1024]{1,0:T(8,128)(2,1)S(1)}, u32[]{:S(2)}, u32[]{:S(2)}) collective-permute-start(bf16[128,1024]{1,0:T(8,128)(2,1)S(1)} %get-tuple-element.58), channel_id=1, source_target_pairs={{0,1},{1,0},{2,3},{3,2},{4,5},{5,4},{6,7},{7,6},{8,9},{9,8},{10,11... | collective-permute-start | bytes 786440 | tf_op jit(solution)/shard_map/ppermute | solution.py:34
  81.1 1.3 %collective-permute-start.27 = (bf16[128,1024]{1,0:T(8,128)(2,1)S(1)}, bf16[128,1024]{1,0:T(8,128)(2,1)S(1)}, u32[]{:S(2)}, u32[]{:S(2)}) collective-permute-start(bf16[128,1024]{1,0:T(8,128)(2,1)S(1)} %get-tuple-element.57), channel_id=1, source_target_pairs={{0,2},{1,3},{2,0},{3,1},{4,6},{5,7},{6,4},{7,5},{8,10},{9,11},{10,... | collective-permute-start | bytes 786440 | tf_op jit(solution)/shard_map/ppermute | solution.py:34
  82.4 0.2 convert_add_fusion
  82.5 5.7 %collective-permute-done.25 = bf16[128,1024]{1,0:T(8,128)(2,1)S(1)} collective-permute-done((bf16[128,1024]{1,0:T(8,128)(2,1)S(1)}, bf16[128,1024]{1,0:T(8,128)(2,1)S(1)}, u32[]{:S(2)}, u32[]{:S(2)}) %collective-permute-start.25) | collective-permute-done | bytes 262176 | tf_op jit(solution)/shard_map/ppermute | solution.py:34
  88.3 1.1 collective-permute-done.27
  89.3 0.2 slice_add_fusion
  89.6 0.8 collective-permute-start.28
  90.3 1.8 %collective-permute-start.26 = (bf16[64,1024]{1,0:T(8,128)(2,1)S(1)}, bf16[64,1024]{1,0:T(8,128)(2,1)S(1)}, u32[]{:S(2)}, u32[]{:S(2)}) collective-permute-start(bf16[64,1024]{1,0:T(8,128)(2,1)S(1)} %slice.99), channel_id=1, source_target_pairs={{0,2},{1,3},{2,0},{3,1},{4,6},{5,7},{6,4},{7,5},{8,10},{9,11},{10,... | collective-permute-start | bytes 393224 | tf_op jit(solution)/shard_map/ppermute | solution.py:34
  92.1 2.4 %collective-permute-done.28 = bf16[64,1024]{1,0:T(8,128)(2,1)S(1)} collective-permute-done((bf16[64,1024]{1,0:T(8,128)(2,1)S(1)}, bf16[64,1024]{1,0:T(8,128)(2,1)S(1)}, u32[]{:S(2)}, u32[]{:S(2)}) %collective-permute-start.28) | collective-permute-done | bytes 131104 | tf_op jit(solution)/shard_map/ppermute | solution.py:34
  94.6 0.8 collective-permute-done.26
  95.5 3.6 %collective-permute-start.29 = (bf16[16,2048]{1,0:T(8,128)(2,1)S(1)}, bf16[16,2048]{1,0:T(8,128)(2,1)S(1)}, u32[]{:S(2)}, u32[]{:S(2)}) collective-permute-start(bf16[16,2048]{1,0:T(8,128)(2,1)S(1)} %get-tuple-element.59), channel_id=1, source_target_pairs={{0,8},{1,9},{2,10},{3,11},{4,12},{5,13},{6,14},{7,15},{8,0},{9,1},... | collective-permute-start | bytes 196616 | tf_op jit(solution)/shard_map/ppermute | solution.py:34
  99.1 1.0 collective-permute-start.30
  100.1 2.5 %collective-permute-done.29 = bf16[16,2048]{1,0:T(8,128)(2,1)S(1)} collective-permute-done((bf16[16,2048]{1,0:T(8,128)(2,1)S(1)}, bf16[16,2048]{1,0:T(8,128)(2,1)S(1)}, u32[]{:S(2)}, u32[]{:S(2)}) %collective-permute-start.29) | collective-permute-done | bytes 65568 | tf_op jit(solution)/shard_map/ppermute | solution.py:34
  102.6 2.6 %collective-permute-done.30 = bf16[16,2048]{1,0:T(8,128)(2,1)S(1)} collective-permute-done((bf16[16,2048]{1,0:T(8,128)(2,1)S(1)}, bf16[16,2048]{1,0:T(8,128)(2,1)S(1)}, u32[]{:S(2)}, u32[]{:S(2)}) %collective-permute-start.30) | collective-permute-done | bytes 65568 | tf_op jit(solution)/shard_map/ppermute | solution.py:34
  105.2 0.1 collective-permute-start.32
  105.3 1.2 %collective-permute-done.32 = bf16[16,2048]{1,0:T(8,128)(2,1)S(1)} collective-permute-done((bf16[16,2048]{1,0:T(8,128)(2,1)S(1)}, bf16[16,2048]{1,0:T(8,128)(2,1)S(1)}, u32[]{:S(2)}, u32[]{:S(2)}) %collective-permute-start.32) | collective-permute-done | bytes 65568 | tf_op jit(solution)/shard_map/ppermute | solution.py:42
  106.5 0.7 maximum_select_fusion
  (40 shorter events, 0.4 us)
Async XLA Ops:
  0.0 44.9 %copy-start.3 = (bf16[4096,256]{1,0:T(8,128)(2,1)S(1)}, bf16[4096,256]{1,0:T(8,128)(2,1)}, u32[]{:S(2)}) copy-start(bf16[4096,256]{1,0:T(8,128)(2,1)} %refs_8_.1) | copy-start | bytes 6291460
  7.5 5.9 %collective-permute-start = (bf16[16,2688]{1,0:T(8,128)(2,1)}, bf16[16,2688]{1,0:T(8,128)(2,1)S(1)}, u32[]{:S(2)}, u32[]{:S(2)}) collective-permute-start(bf16[16,2688]{1,0:T(8,128)(2,1)} %get-tuple-element.32), channel_id=1, source_target_pairs={{0,4},{1,5},{2,6},{3,7},{4,0},{5,1},{6,2},{7,3},{8,12},{9,13},{10,... | collective-permute-start | bytes 258056 | tf_op jit(solution)/shard_map/ppermute | solution.py:34
  10.6 10.4 %collective-permute-start.1 = (bf16[16,2688]{1,0:T(8,128)(2,1)}, bf16[16,2688]{1,0:T(8,128)(2,1)S(1)}, u32[]{:S(2)}, u32[]{:S(2)}) collective-permute-start(bf16[16,2688]{1,0:T(8,128)(2,1)} %get-tuple-element.34), channel_id=1, source_target_pairs={{0,8},{1,9},{2,10},{3,11},{4,12},{5,13},{6,14},{7,15},{8,0},{9,1},... | collective-permute-start | bytes 258056 | tf_op jit(solution)/shard_map/ppermute | solution.py:34
  13.0 8.0 %collective-permute-start.2 = (bf16[16,2688]{1,0:T(8,128)(2,1)}, bf16[16,2688]{1,0:T(8,128)(2,1)S(1)}, u32[]{:S(2)}, u32[]{:S(2)}) collective-permute-start(bf16[16,2688]{1,0:T(8,128)(2,1)} %get-tuple-element.35), channel_id=1, source_target_pairs={{0,12},{1,13},{2,14},{3,15},{4,8},{5,9},{6,10},{7,11},{8,4},{9,5},... | collective-permute-start | bytes 258056 | tf_op jit(solution)/shard_map/ppermute | solution.py:34
  13.3 10.4 %collective-permute-start.6 = (bf16[16,2048]{1,0:T(8,128)(2,1)}, bf16[16,2048]{1,0:T(8,128)(2,1)S(1)}, u32[]{:S(2)}, u32[]{:S(2)}) collective-permute-start(bf16[16,2048]{1,0:T(8,128)(2,1)} %get-tuple-element.40), channel_id=1, source_target_pairs={{0,4},{1,5},{2,6},{3,7},{4,0},{5,1},{6,2},{7,3},{8,12},{9,13},{10,... | collective-permute-start | bytes 196616 | tf_op jit(solution)/shard_map/ppermute | solution.py:34
  16.2 10.0 %collective-permute-start.7 = (bf16[16,2048]{1,0:T(8,128)(2,1)}, bf16[16,2048]{1,0:T(8,128)(2,1)S(1)}, u32[]{:S(2)}, u32[]{:S(2)}) collective-permute-start(bf16[16,2048]{1,0:T(8,128)(2,1)} %get-tuple-element.40), channel_id=1, source_target_pairs={{0,8},{1,9},{2,10},{3,11},{4,12},{5,13},{6,14},{7,15},{8,0},{9,1},... | collective-permute-start | bytes 196616 | tf_op jit(solution)/shard_map/ppermute | solution.py:34
  19.4 6.7 %collective-permute-start.8 = (bf16[16,2048]{1,0:T(8,128)(2,1)}, bf16[16,2048]{1,0:T(8,128)(2,1)S(1)}, u32[]{:S(2)}, u32[]{:S(2)}) collective-permute-start(bf16[16,2048]{1,0:T(8,128)(2,1)} %get-tuple-element.40), channel_id=1, source_target_pairs={{0,12},{1,13},{2,14},{3,15},{4,8},{5,9},{6,10},{7,11},{8,4},{9,5},... | collective-permute-start | bytes 196616 | tf_op jit(solution)/shard_map/ppermute | solution.py:34
  21.0 0.9 copy-start.5
  22.0 7.0 %collective-permute-start.3 = (bf16[64,2432]{1,0:T(8,128)(2,1)S(1)}, bf16[64,2432]{1,0:T(8,128)(2,1)S(1)}, u32[]{:S(2)}, u32[]{:S(2)}) collective-permute-start(bf16[64,2432]{1,0:T(8,128)(2,1)S(1)} %get-tuple-element.37), channel_id=1, source_target_pairs={{0,1},{1,0},{2,3},{3,2},{4,5},{5,4},{6,7},{7,6},{8,9},{9,8},{10,11... | collective-permute-start | bytes 933896 | tf_op jit(solution)/shard_map/ppermute | solution.py:34
  26.1 46.4 %copy-start.4 = (bf16[4096,16]{0,1:T(8,128)(2,1)S(1)}, bf16[4096,16]{0,1:T(8,128)(2,1)}, u32[]{:S(2)}) copy-start(bf16[4096,16]{0,1:T(8,128)(2,1)} %param.23) | copy-start | bytes 393220
  26.1 46.5 %copy-start.6 = (f32[4096]{0:T(1024)S(1)}, f32[4096]{0:T(1024)}, u32[]{:S(2)}) copy-start(f32[4096]{0:T(1024)} %param.22) | copy-start | bytes 49156
  26.2 9.3 %collective-permute-start.9 = (bf16[64,2048]{1,0:T(8,128)(2,1)S(1)}, bf16[64,2048]{1,0:T(8,128)(2,1)S(1)}, u32[]{:S(2)}, u32[]{:S(2)}) collective-permute-start(bf16[64,2048]{1,0:T(8,128)(2,1)S(1)} %constant_dynamic-update-slice_fusion.refs_3_), channel_id=1, source_target_pairs={{0,2},{1,3},{2,0},{3,1},{4,6},{5,7},{6,4},{7,5},{8,10},{9,11},{10,... | collective-permute-start | bytes 786440 | tf_op jit(solution)/shard_map/ppermute | solution.py:34
  29.0 16.0 %collective-permute-start.5 = (bf16[64,2432]{1,0:T(8,128)(2,1)S(1)}, bf16[64,2432]{1,0:T(8,128)(2,1)S(1)}, u32[]{:S(2)}, u32[]{:S(2)}) collective-permute-start(bf16[64,2432]{1,0:T(8,128)(2,1)S(1)} %collective-permute-done.3.refs_1_), channel_id=1, source_target_pairs={{0,2},{1,3},{2,0},{3,1},{4,6},{5,7},{6,4},{7,5},{8,10},{9,11},{10,... | collective-permute-start | bytes 933896 | tf_op jit(solution)/shard_map/ppermute | solution.py:34
  30.4 14.5 %collective-permute-start.4 = (bf16[64,2304]{1,0:T(8,128)(2,1)S(1)}, bf16[64,2304]{1,0:T(8,128)(2,1)S(1)}, u32[]{:S(2)}, u32[]{:S(2)}) collective-permute-start(bf16[64,2304]{1,0:T(8,128)(2,1)S(1)} %get-tuple-element.38), channel_id=1, source_target_pairs={{0,2},{1,3},{2,0},{3,1},{4,6},{5,7},{6,4},{7,5},{8,10},{9,11},{10,... | collective-permute-start | bytes 884744 | tf_op jit(solution)/shard_map/ppermute | solution.py:34
  31.0 14.0 %collective-permute-start.10 = (bf16[64,2048]{1,0:T(8,128)(2,1)S(1)}, bf16[64,2048]{1,0:T(8,128)(2,1)S(1)}, u32[]{:S(2)}, u32[]{:S(2)}) collective-permute-start(bf16[64,2048]{1,0:T(8,128)(2,1)S(1)} %constant_dynamic-update-slice_fusion.refs_3_), channel_id=1, source_target_pairs={{0,1},{1,0},{2,3},{3,2},{4,5},{5,4},{6,7},{7,6},{8,9},{9,8},{10,11... | collective-permute-start | bytes 786440 | tf_op jit(solution)/shard_map/ppermute | solution.py:34
  35.5 9.5 %collective-permute-start.11 = (bf16[64,2048]{1,0:T(8,128)(2,1)S(1)}, bf16[64,2048]{1,0:T(8,128)(2,1)S(1)}, u32[]{:S(2)}, u32[]{:S(2)}) collective-permute-start(bf16[64,2048]{1,0:T(8,128)(2,1)S(1)} %collective-permute-done.9.refs_4_), channel_id=1, source_target_pairs={{0,1},{1,0},{2,3},{3,2},{4,5},{5,4},{6,7},{7,6},{8,9},{9,8},{10,11... | collective-permute-start | bytes 786440 | tf_op jit(solution)/shard_map/ppermute | solution.py:34
  45.0 27.6 %copy-start = (bf16[1,4096,384]{2,1,0:T(8,128)(2,1)S(1)}, bf16[1,4096,384]{2,1,0:T(8,128)(2,1)}, u32[]{:S(2)}) copy-start(bf16[1,4096,384]{2,1,0:T(8,128)(2,1)} %refs_6_.5) | copy-start | bytes 9437188
  45.0 27.6 %copy-start.1 = (bf16[1,4096,384]{2,1,0:T(8,128)(2,1)S(1)}, bf16[1,4096,384]{2,1,0:T(8,128)(2,1)}, u32[]{:S(2)}) copy-start(bf16[1,4096,384]{2,1,0:T(8,128)(2,1)} %refs_7_.5) | copy-start | bytes 9437188
  46.7 1.4 %collective-permute-start.12 = (f32[256,128]{1,0:T(8,128)S(1)}, f32[256,128]{1,0:T(8,128)S(1)}, u32[]{:S(2)}, u32[]{:S(2)}) collective-permute-start(f32[256,128]{1,0:T(8,128)S(1)} %get-tuple-element.42), channel_id=1, source_target_pairs={{0,16},{16,0},{1,17},{17,1},{2,18},{18,2},{3,19},{19,3},{4,20},{20... | collective-permute-start | bytes 393224 | tf_op jit(solution)/shard_map/ppermute | solution.py:42
  48.1 5.1 %collective-permute-start.13 = (bf16[256,128]{1,0:T(8,128)(2,1)S(1)}, bf16[256,128]{1,0:T(8,128)(2,1)S(1)}, u32[]{:S(2)}, u32[]{:S(2)}) collective-permute-start(bf16[256,128]{1,0:T(8,128)(2,1)S(1)} %add_convert_fusion.1.refs_0_), channel_id=1, source_target_pairs={{0,4},{1,5},{2,6},{3,7},{4,0},{5,1},{6,2},{7,3},{8,12},{9,13},{10,... | collective-permute-start | bytes 196616 | tf_op jit(solution)/shard_map/ppermute | solution.py:34
  50.8 8.2 %collective-permute-start.14 = (bf16[256,128]{1,0:T(8,128)(2,1)S(1)}, bf16[256,128]{1,0:T(8,128)(2,1)S(1)}, u32[]{:S(2)}, u32[]{:S(2)}) collective-permute-start(bf16[256,128]{1,0:T(8,128)(2,1)S(1)} %add_convert_fusion.1.refs_0_), channel_id=1, source_target_pairs={{0,8},{1,9},{2,10},{3,11},{4,12},{5,13},{6,14},{7,15},{8,0},{9,1},... | collective-permute-start | bytes 196616 | tf_op jit(solution)/shard_map/ppermute | solution.py:34
  51.7 7.3 %collective-permute-start.15 = (bf16[256,128]{1,0:T(8,128)(2,1)S(1)}, bf16[256,128]{1,0:T(8,128)(2,1)S(1)}, u32[]{:S(2)}, u32[]{:S(2)}) collective-permute-start(bf16[256,128]{1,0:T(8,128)(2,1)S(1)} %add_convert_fusion.1.refs_0_), channel_id=1, source_target_pairs={{0,12},{1,13},{2,14},{3,15},{4,8},{5,9},{6,10},{7,11},{8,4},{9,5},... | collective-permute-start | bytes 196616 | tf_op jit(solution)/shard_map/ppermute | solution.py:34
  59.1 9.3 %collective-permute-start.21 = (bf16[1024,128]{1,0:T(8,128)(2,1)S(1)}, bf16[1024,128]{1,0:T(8,128)(2,1)S(1)}, u32[]{:S(2)}, u32[]{:S(2)}) collective-permute-start(bf16[1024,128]{1,0:T(8,128)(2,1)S(1)} %get-tuple-element.44.refs_0_), channel_id=1, source_target_pairs={{0,1},{1,0},{2,3},{3,2},{4,5},{5,4},{6,7},{7,6},{8,9},{9,8},{10,11... | collective-permute-start | bytes 786440 | tf_op jit(solution)/shard_map/ppermute | solution.py:34
  60.0 11.7 %collective-permute-start.16 = (bf16[1024,128]{1,0:T(8,128)(2,1)S(1)}, bf16[1024,128]{1,0:T(8,128)(2,1)S(1)}, u32[]{:S(2)}, u32[]{:S(2)}) collective-permute-start(bf16[1024,128]{1,0:T(8,128)(2,1)S(1)} %get-tuple-element.44.refs_0_), channel_id=1, source_target_pairs={{0,2},{1,3},{2,0},{3,1},{4,6},{5,7},{6,4},{7,5},{8,10},{9,11},{10,... | collective-permute-start | bytes 786440 | tf_op jit(solution)/shard_map/ppermute | solution.py:34
  61.5 11.1 %collective-permute-start.18 = (bf16[1024,128]{1,0:T(8,128)(2,1)S(1)}, bf16[1024,128]{1,0:T(8,128)(2,1)S(1)}, u32[]{:S(2)}, u32[]{:S(2)}) collective-permute-start(bf16[1024,128]{1,0:T(8,128)(2,1)S(1)} %get-tuple-element.44.refs_0_), channel_id=1, source_target_pairs={{0,3},{1,2},{2,1},{3,0},{4,7},{5,6},{6,5},{7,4},{8,11},{9,10},{10,... | collective-permute-start | bytes 786440 | tf_op jit(solution)/shard_map/ppermute | solution.py:34
  62.6 10.0 %collective-permute-start.20 = (bf16[1024,128]{1,0:T(8,128)(2,1)S(1)}, bf16[1024,128]{1,0:T(8,128)(2,1)S(1)}, u32[]{:S(2)}, u32[]{:S(2)}) collective-permute-start(bf16[1024,128]{1,0:T(8,128)(2,1)S(1)} %get-tuple-element.44.refs_0_), channel_id=1, source_target_pairs={{0,16},{16,0},{1,17},{17,1},{2,18},{18,2},{3,19},{19,3},{4,20},{20... | collective-permute-start | bytes 786440 | tf_op jit(solution)/shard_map/ppermute | solution.py:42
  68.4 4.2 %collective-permute-start.22 = (bf16[1024,128]{1,0:T(8,128)(2,1)S(1)}, bf16[1024,128]{1,0:T(8,128)(2,1)S(1)}, u32[]{:S(2)}, u32[]{:S(2)}) collective-permute-start(bf16[1024,128]{1,0:T(8,128)(2,1)S(1)} %collective-permute-done.21.refs_2_), channel_id=1, source_target_pairs={{0,16},{16,0},{1,17},{17,1},{2,18},{18,2},{3,19},{19,3},{4,20},{20... | collective-permute-start | bytes 786440 | tf_op jit(solution)/shard_map/ppermute | solution.py:42
  71.7 2.2 %collective-permute-start.17 = (bf16[1024,128]{1,0:T(8,128)(2,1)S(1)}, bf16[1024,128]{1,0:T(8,128)(2,1)S(1)}, u32[]{:S(2)}, u32[]{:S(2)}) collective-permute-start(bf16[1024,128]{1,0:T(8,128)(2,1)S(1)} %collective-permute-done.16.refs_0_), channel_id=1, source_target_pairs={{0,16},{16,0},{1,17},{17,1},{2,18},{18,2},{3,19},{19,3},{4,20},{20... | collective-permute-start | bytes 786440 | tf_op jit(solution)/shard_map/ppermute | solution.py:42
  72.6 1.5 %collective-permute-start.19 = (bf16[1024,128]{1,0:T(8,128)(2,1)S(1)}, bf16[1024,128]{1,0:T(8,128)(2,1)S(1)}, u32[]{:S(2)}, u32[]{:S(2)}) collective-permute-start(bf16[1024,128]{1,0:T(8,128)(2,1)S(1)} %collective-permute-done.18.refs_2_), channel_id=1, source_target_pairs={{0,16},{16,0},{1,17},{17,1},{2,18},{18,2},{3,19},{19,3},{4,20},{20... | collective-permute-start | bytes 786440 | tf_op jit(solution)/shard_map/ppermute | solution.py:42
  72.6 1.9 %copy-start.2 = (bf16[1,384,4096]{2,1,0:T(8,128)(2,1)S(1)}, bf16[1,384,4096]{2,1,0:T(8,128)(2,1)}, u32[]{:S(2)}) copy-start(bf16[1,384,4096]{2,1,0:T(8,128)(2,1)} %refs_12_.1) | copy-start | bytes 9437188
  77.3 2.1 %collective-permute-start.24 = (bf16[256,1024]{1,0:T(8,128)(2,1)S(1)}, bf16[256,1024]{1,0:T(8,128)(2,1)S(1)}, u32[]{:S(2)}, u32[]{:S(2)}) collective-permute-start(bf16[256,1024]{1,0:T(8,128)(2,1)S(1)} %get-tuple-element.54), channel_id=1, source_target_pairs={{0,16},{16,0},{1,17},{17,1},{2,18},{18,2},{3,19},{19,3},{4,20},{20... | collective-permute-start | bytes 1572872 | tf_op jit(solution)/shard_map/ppermute | solution.py:42
  77.9 4.5 %collective-permute-start.23 = (bf16[256,1024]{1,0:T(8,128)(2,1)S(1)}, bf16[256,1024]{1,0:T(8,128)(2,1)S(1)}, u32[]{:S(2)}, u32[]{:S(2)}) collective-permute-start(bf16[256,1024]{1,0:T(8,128)(2,1)S(1)} %get-tuple-element.52), channel_id=1, source_target_pairs={{0,16},{16,0},{1,17},{17,1},{2,18},{18,2},{3,19},{19,3},{4,20},{20... | collective-permute-start | bytes 1572872 | tf_op jit(solution)/shard_map/ppermute | solution.py:42
  79.6 8.7 %collective-permute-start.25 = (bf16[128,1024]{1,0:T(8,128)(2,1)S(1)}, bf16[128,1024]{1,0:T(8,128)(2,1)S(1)}, u32[]{:S(2)}, u32[]{:S(2)}) collective-permute-start(bf16[128,1024]{1,0:T(8,128)(2,1)S(1)} %get-tuple-element.58), channel_id=1, source_target_pairs={{0,1},{1,0},{2,3},{3,2},{4,5},{5,4},{6,7},{7,6},{8,9},{9,8},{10,11... | collective-permute-start | bytes 786440 | tf_op jit(solution)/shard_map/ppermute | solution.py:34
  81.1 8.3 %collective-permute-start.27 = (bf16[128,1024]{1,0:T(8,128)(2,1)S(1)}, bf16[128,1024]{1,0:T(8,128)(2,1)S(1)}, u32[]{:S(2)}, u32[]{:S(2)}) collective-permute-start(bf16[128,1024]{1,0:T(8,128)(2,1)S(1)} %get-tuple-element.57), channel_id=1, source_target_pairs={{0,2},{1,3},{2,0},{3,1},{4,6},{5,7},{6,4},{7,5},{8,10},{9,11},{10,... | collective-permute-start | bytes 786440 | tf_op jit(solution)/shard_map/ppermute | solution.py:34
  89.6 5.0 %collective-permute-start.28 = (bf16[64,1024]{1,0:T(8,128)(2,1)S(1)}, bf16[64,1024]{1,0:T(8,128)(2,1)S(1)}, u32[]{:S(2)}, u32[]{:S(2)}) collective-permute-start(bf16[64,1024]{1,0:T(8,128)(2,1)S(1)} %slice.98), channel_id=1, source_target_pairs={{0,1},{1,0},{2,3},{3,2},{4,5},{5,4},{6,7},{7,6},{8,9},{9,8},{10,11... | collective-permute-start | bytes 393224 | tf_op jit(solution)/shard_map/ppermute | solution.py:34
  90.3 5.0 %collective-permute-start.26 = (bf16[64,1024]{1,0:T(8,128)(2,1)S(1)}, bf16[64,1024]{1,0:T(8,128)(2,1)S(1)}, u32[]{:S(2)}, u32[]{:S(2)}) collective-permute-start(bf16[64,1024]{1,0:T(8,128)(2,1)S(1)} %slice.99), channel_id=1, source_target_pairs={{0,2},{1,3},{2,0},{3,1},{4,6},{5,7},{6,4},{7,5},{8,10},{9,11},{10,... | collective-permute-start | bytes 393224 | tf_op jit(solution)/shard_map/ppermute | solution.py:34
  95.5 7.1 %collective-permute-start.29 = (bf16[16,2048]{1,0:T(8,128)(2,1)S(1)}, bf16[16,2048]{1,0:T(8,128)(2,1)S(1)}, u32[]{:S(2)}, u32[]{:S(2)}) collective-permute-start(bf16[16,2048]{1,0:T(8,128)(2,1)S(1)} %get-tuple-element.59), channel_id=1, source_target_pairs={{0,8},{1,9},{2,10},{3,11},{4,12},{5,13},{6,14},{7,15},{8,0},{9,1},... | collective-permute-start | bytes 196616 | tf_op jit(solution)/shard_map/ppermute | solution.py:34
  99.1 6.1 %collective-permute-start.30 = (bf16[16,2048]{1,0:T(8,128)(2,1)S(1)}, bf16[16,2048]{1,0:T(8,128)(2,1)S(1)}, u32[]{:S(2)}, u32[]{:S(2)}) collective-permute-start(bf16[16,2048]{1,0:T(8,128)(2,1)S(1)} %get-tuple-element.61), channel_id=1, source_target_pairs={{0,12},{1,13},{2,14},{3,15},{4,8},{5,9},{6,10},{7,11},{8,4},{9,5},... | collective-permute-start | bytes 196616 | tf_op jit(solution)/shard_map/ppermute | solution.py:34
  100.1 5.0 %collective-permute-start.31 = (bf16[16,2048]{1,0:T(8,128)(2,1)S(1)}, bf16[16,2048]{1,0:T(8,128)(2,1)S(1)}, u32[]{:S(2)}, u32[]{:S(2)}) collective-permute-start(bf16[16,2048]{1,0:T(8,128)(2,1)S(1)} %get-tuple-element.60), channel_id=1, source_target_pairs={{0,4},{1,5},{2,6},{3,7},{4,0},{5,1},{6,2},{7,3},{8,12},{9,13},{10,... | collective-permute-start | bytes 196616 | tf_op jit(solution)/shard_map/ppermute | solution.py:34
  105.2 1.3 %collective-permute-start.32 = (bf16[16,2048]{1,0:T(8,128)(2,1)S(1)}, bf16[16,2048]{1,0:T(8,128)(2,1)S(1)}, u32[]{:S(2)}, u32[]{:S(2)}) collective-permute-start(bf16[16,2048]{1,0:T(8,128)(2,1)S(1)} %fusion.6), channel_id=1, source_target_pairs={{0,16},{16,0},{1,17},{17,1},{2,18},{18,2},{3,19},{19,3},{4,20},{20... | collective-permute-start | bytes 196616 | tf_op jit(solution)/shard_map/ppermute | solution.py:42

commit v4 on v3

--- a/solution.py
+++ b/solution.py
@@ -334,6 +334,7 @@
     )(*late, gain, router, gate, up, *found, down, mask)
 
 
+LINE_HEADS = 24
 GROUP = 4
 CHUNK = 128
 
@@ -356,10 +357,11 @@
         ksems,
         vsems,
     ) = refs
-    b_ref, sends = outs[0], outs[1:]
+    a_ref, sends = outs[0], outs[1:]
     rows, span, cols = keys.shape
     heads = q_ref.shape[1] // HEAD
-    half = b_ref.shape[1]
+    wide = a_ref.shape[1]
+    rest = heads * HEAD - wide
     groups = cols // HEAD
     per = heads // groups
     me = lax.axis_index("dev")
@@ -383,17 +385,17 @@
         chosen = jnp.where(lane_ids == ids_ref[k : k + 1, :], 1.0, chosen)
     chosen = chosen.T.astype(BF)
     plane = dims[1] * dims[2]
-    for kz in range(dims[0]):
-        target = sends[kz]
-        for c in range(plane):
-            owner = me ^ (kz * plane + c)
+    for code, target in enumerate(sends):
+        for kz in range(dims[0]):
+            owner = me ^ (kz * plane + code)
             if len(extra_ref.shape) == 3:
                 block = extra_ref[owner]
             else:
                 place = pl.multiple_of((owner * 2 + sec) * 128, 128)
                 block = extra_ref[:, pl.ds(place, 128)]
-            target[:, half + c * 128 : half + (c + 1) * 128] = block
-        target[:, half + plane * 128 :] = chosen
+            at = rest + kz * 128
+            target[:, at : at + 128] = block
+        target[:, rest + dims[0] * 128 :] = chosen
 
     for h in range(heads):
         apart[pl.ds(h * rows, rows)] = q_ref[:, h * HEAD : (h + 1) * HEAD].astype(F32)
@@ -420,9 +422,9 @@
         for r in group:
             q = apart[pl.ds(r, heads, stride=rows), :]
             queries[r] = q
-            wide = jnp.concatenate([jnp.where(m, q, 0.0) for m in belongs], axis=1)
+            apart_q = jnp.concatenate([jnp.where(m, q, 0.0) for m in belongs], axis=1)
             scores[r] = lax.dot_general(
-                wide.astype(BF), keys[r], (((1,), (1,)), ((), ())), preferred_element_type=F32
+                apart_q.astype(BF), keys[r], (((1,), (1,)), ((), ())), preferred_element_type=F32
             )
         for r in group:
             s = jnp.where(place < len_ref[r], scores[r] * scale, masked_score)
@@ -440,8 +442,11 @@
     for h in range(heads):
         block = joined[pl.ds(h * rows, rows)].astype(BF)
         at = h * HEAD
-        for target in sends if at < half else (b_ref,):
-            target[:, at % half : at % half + HEAD] = block
+        if at < wide:
+            a_ref[:, at : at + HEAD] = block
+        else:
+            for target in sends:
+                target[:, at - wide : at - wide + HEAD] = block
 
 
 def attention(
@@ -450,9 +455,9 @@
     rows, span, cols = key_cache.shape
     width = queries.shape[1]
     heads = width // HEAD
-    half = width // 2
-    side = dims[1] * dims[2] * 128 + lanes
-    outs = [(rows, half)] + [(rows, half + side)] * dims[0]
+    wide = LINE_HEADS * HEAD
+    side = width - wide + dims[0] * 128 + lanes
+    outs = [(rows, wide)] + [(rows, side)] * (dims[1] * dims[2])
     return pl.pallas_call(
         functools.partial(attend_kernel, dims, lanes),
         out_shape=tuple(jax.ShapeDtypeStruct(o, BF) for o in outs),
@@ -476,117 +481,158 @@
     )(cache_lengths, ids, queries, new_key, new_value, extra, key_cache, value_cache)
 
 
-def pack_kernel(ny, nx, lanes, extras, count, *refs):
-    lines, outs = refs[:count], refs[count:]
+def pack_line_kernel(plane, *refs):
+    lines, (a_ref, b_ref) = refs[:-2], refs[-2:]
     rows = lines[0].shape[0]
-    z = lax.axis_index("dev") // (ny * nx)
+    half = a_ref.shape[1]
+    z = lax.axis_index("dev") // plane
     for kz, source in enumerate(lines):
         span = pl.ds(pl.multiple_of((z ^ kz) * rows, rows), rows)
-        if not extras:
-            outs[0][span, :] = source[...]
-            continue
-        mine_ref, xa, ya = outs[0], outs[1:nx], outs[nx:]
-        plane = ny * nx * 128
-        half = source.shape[1] - plane - lanes
-
-        def block(ky, kx):
-            at = half + (ky * nx + kx) * 128
-            return source[:, at : at + 128]
-
-        a, mask = source[:, :half], source[:, half + plane :]
-        mine_ref[span, :half] = a
-        mine_ref[span, half : half + 128] = block(0, 0)
-        mine_ref[span, half + 128 :] = mask
-        for kx in range(1, nx):
-            xa[kx - 1][span, :half] = a
-            for ky in range(ny):
-                xa[kx - 1][span, half + ky * 128 : half + (ky + 1) * 128] = block(ky, kx)
-            xa[kx - 1][span, half + ny * 128 :] = mask
-        for ky in range(1, ny):
-            ya[ky - 1][span, :half] = a
-            ya[ky - 1][span, half : half + 128] = block(ky, 0)
-            ya[ky - 1][span, half + 128 :] = mask
-
-
-def pack(lines, lanes, dims, extras):
-    _, ny, nx = dims
+        a_ref[span, :] = source[:, :half]
+        b_ref[span, :] = source[:, half:]
+
+
+def pack_line(lines, plane):
     rows, width = lines[0].shape
-    widths = [width]
-    if extras:
-        half = width - ny * nx * 128 - lanes
-        widths = [half + 128 + lanes]
-        widths += [half + ny * 128 + lanes] * (nx - 1)
-        widths += [half + 128 + lanes] * (ny - 1)
-    outs = pl.pallas_call(
-        functools.partial(pack_kernel, ny, nx, lanes, extras, len(lines)),
-        out_shape=tuple(jax.ShapeDtypeStruct((len(lines) * rows, w), BF) for w in widths),
+    out = jax.ShapeDtypeStruct((len(lines) * rows, width // 2), BF)
+    return pl.pallas_call(
+        functools.partial(pack_line_kernel, plane),
+        out_shape=(out, out),
         in_specs=[VM] * len(lines),
-        out_specs=(VM,) * len(widths),
+        out_specs=(VM, VM),
         compiler_params=pltpu.CompilerParams(vmem_limit_bytes=16 * MIB),
-        name="pack",
+        name="pack_line",
     )(*lines)
-    return outs[0], outs[1:nx], outs[nx:]
-
-
-def arrange_kernel(places, size, *refs):
-    count = len(places)
-    arrays, outs, sems = refs[:count], refs[count : count + 2], refs[count + 2]
+
+
+def pack_plane_kernel(nz, lanes, count, *refs):
+    blocks, outs = refs[:count], refs[count:]
+    rows = blocks[0].shape[0]
+    share = blocks[0].shape[1] - nz * 128 - lanes
+    here = lax.axis_index("dev") % count
+    for code, source in enumerate(blocks):
+        span = pl.ds(pl.multiple_of((here ^ code) * rows, rows), rows)
+        for kz in range(nz):
+            outs[kz][span, :share] = source[:, :share]
+            at = share + kz * 128
+            outs[kz][span, share : share + 128] = source[:, at : at + 128]
+            outs[kz][span, share + 128 :] = source[:, share + nz * 128 :]
+
+
+def pack_plane(blocks, lanes, nz):
+    count = len(blocks)
+    rows, width = blocks[0].shape
+    out = jax.ShapeDtypeStruct((count * rows, width - (nz - 1) * 128), BF)
+    return pl.pallas_call(
+        functools.partial(pack_plane_kernel, nz, lanes, count),
+        out_shape=(out,) * nz,
+        in_specs=[VM] * count,
+        out_specs=(VM,) * nz,
+        compiler_params=pltpu.CompilerParams(vmem_limit_bytes=16 * MIB),
+        name="pack_plane",
+    )(*blocks)
+
+
+def scatter_rows(dims, kz, rows):
+    nz, ny, nx = dims
+    z = lax.axis_index("dev") // (ny * nx)
+    for q in range(ny * nx):
+        yield q * rows, pl.multiple_of((q * nz + (z ^ kz)) * rows, rows)
+
+
+def project_kernel(dims, rows, codes, *refs):
+    nz, ny, nx = dims
+    count = len(codes)
+    firsts, seconds = refs[:count], refs[count : 2 * count]
+    rest = refs[2 * count : 2 * count + nz]
+    w_ref, keep_ref, send_ref, held, sems = refs[2 * count + nz :]
+    sec = lax.axis_index("sec")
+    here = lax.axis_index("dev") % (ny * nx)
+    half = firsts[0].shape[1]
+    share = held.shape[1] - 2 * half
+    size = nz * rows
     copies = []
-    for i, (slot, *columns) in enumerate(places):
-        for j, out in enumerate(outs):
-            copies.append(
-                pltpu.make_async_copy(
-                    arrays[i].at[:, pl.ds(columns[j], out.shape[1])],
-                    out.at[pl.ds(slot * size, size)],
-                    sems.at[2 * i + j],
-                )
+
+    def move(source, target):
+        copies.append(pltpu.make_async_copy(source, target, sems.at[len(copies)]))
+
+    for i, code in enumerate(codes):
+        span = pl.ds(pl.multiple_of((here ^ code) * size, size), size)
+        move(firsts[i], held.at[span, pl.ds(0, half)])
+        move(seconds[i], held.at[span, pl.ds(half, half)])
+    for kz in range(nz):
+        for source, target in scatter_rows(dims, kz, rows):
+            move(
+                rest[kz].at[pl.ds(source, rows), pl.ds(0, share)],
+                held.at[pl.ds(target, rows), pl.ds(2 * half, share)],
             )
     for c in copies:
         c.start()
     for c in copies:
         c.wait()
-
-
-def arrange(arrays, places, lanes, size):
-    tall = len(places) * size
+    total = jnp.dot(held[...], w_ref[...], preferred_element_type=F32)
+    part = total.shape[1] // 2
+    low, high = total[:, :part], total[:, part:]
+    keep_ref[...] = jnp.where(sec == 0, low, high)
+    send_ref[...] = jnp.where(sec == 0, high, low)
+
+
+def project(firsts, seconds, codes, rest, weight, dims, rows):
+    depth, cols = weight.shape
+    tall = dims[0] * dims[1] * dims[2] * rows
+    out = jax.ShapeDtypeStruct((tall, cols // 2), F32)
+    arrays = [*firsts, *seconds, *rest]
     return pl.pallas_call(
-        functools.partial(arrange_kernel, places, size),
+        functools.partial(project_kernel, dims, rows, codes),
+        out_shape=(out, out),
+        in_specs=[ANY] * len(arrays) + [VM],
+        out_specs=(VM, VM),
+        scratch_shapes=[
+            pltpu.VMEM((tall, depth), BF),
+            pltpu.SemaphoreType.DMA((2 * len(codes) + tall // rows,)),
+        ],
+        compiler_params=pltpu.CompilerParams(vmem_limit_bytes=(4 + tall // 32) * MIB),
+        cost_estimate=pl.CostEstimate(
+            flops=2 * tall * depth * cols,
+            bytes_accessed=2 * depth * (cols + tall),
+            transcendentals=0,
+        ),
+        name="project",
+    )(*arrays, weight)
+
+
+def arrange_kernel(dims, rows, *refs):
+    nz = dims[0]
+    rest, (residual, mask, sems) = refs[:nz], refs[nz:]
+    share = rest[0].shape[1] - 128 - mask.shape[1]
+    copies = []
+    for kz in range(nz):
+        for source, target in scatter_rows(dims, kz, rows):
+            for start, out in ((share, residual), (share + 128, mask)):
+                copies.append(
+                    pltpu.make_async_copy(
+                        rest[kz].at[pl.ds(source, rows), pl.ds(start, out.shape[1])],
+                        out.at[pl.ds(target, rows)],
+                        sems.at[len(copies)],
+                    )
+                )
+    for c in copies:
+        c.start()
+    for c in copies:
+        c.wait()
+
+
+def arrange(rest, lanes, dims, rows):
+    tall = dims[0] * dims[1] * dims[2] * rows
+    return pl.pallas_call(
+        functools.partial(arrange_kernel, dims, rows),
         out_shape=tuple(jax.ShapeDtypeStruct((tall, w), BF) for w in (128, lanes)),
-        in_specs=[ANY] * len(arrays),
+        in_specs=[ANY] * len(rest),
         out_specs=(VM, VM),
-        scratch_shapes=[pltpu.SemaphoreType.DMA((2 * len(places),))],
+        scratch_shapes=[pltpu.SemaphoreType.DMA((2 * tall // rows,))],
         compiler_params=pltpu.CompilerParams(vmem_limit_bytes=8 * MIB),
         name="arrange",
-    )(*arrays)
-
-
-def merge_kernel(dims, rows, *refs):
-    nz, ny, nx = dims
-    parts, mask, (stacked, mask_out) = refs[:nz], refs[nz], refs[nz + 1 :]
-    here = lax.axis_index("dev") % (ny * nx)
-    size = nz * rows
-    total = ny * nx * size
-    for code in range(ny * nx):
-        place = (here ^ code) * size
-        span = slice(code * size, (code + 1) * size)
-        mask_out[pl.ds(pl.multiple_of(place, size), size), :] = mask[span, :]
-        for kz in range(nz):
-            spot = pl.ds(pl.multiple_of(kz * total + place, size), size)
-            stacked[spot, :] = parts[kz][span, :]
-
-
-def merge(parts, mask, dims, rows):
-    nz, ny, nx = dims
-    total = nz * ny * nx * rows
-    shapes = [(nz * total, parts[0].shape[1]), (total, mask.shape[1])]
-    return pl.pallas_call(
-        functools.partial(merge_kernel, dims, rows),
-        out_shape=tuple(jax.ShapeDtypeStruct(t, BF) for t in shapes),
-        in_specs=[VM] * (nz + 1),
-        out_specs=(VM, VM),
-        compiler_params=pltpu.CompilerParams(vmem_limit_bytes=16 * MIB),
-        name="merge",
-    )(*parts, mask)
+    )(*rest)
 
 
 def local(
@@ -622,7 +668,7 @@
         extra = jnp.pad(jnp.swapaxes(extra, 0, 1), ((0, 0), (0, 0), (0, 128 - part)))
     else:
         extra = residual_in
-    b_own, *a_own = attention(
+    a_own, *blocks = attention(
         queries,
         key_cache,
         value_cache,
@@ -634,46 +680,32 @@
         lanes,
         dims,
     )
-    middle = b_own.shape[1]
-
+
+    plane = ny * nx
     steps = along_z(dims)
-    a_lines = {kz: trade(a_own[kz], dims, kz=kz) for kz in steps}
-    b_own, a_lines[steps[-1]] = lax.optimization_barrier((b_own, a_lines[steps[-1]]))
-    b_lines = {kz: trade(b_own, dims, kz=kz) for kz in steps}
-    mine, xa, ya = pack([a_own[0]] + [a_lines[kz] for kz in range(1, nz)], lanes, dims, True)
-    found = [(mine, 0, 0, 0, True, middle, middle + 128)]
-    near_a = {kx: trade(xa[kx - 1], dims, kx=kx) for kx in range(1, nx)}
-    for kx, v in near_a.items():
-        found.append((v, 0, kx, 0, True, middle, middle + ny * 128))
-    for ky in range(1, ny):
-        v = trade(ya[ky - 1], dims, ky=ky)
-        found.append((v, ky, 0, 0, True, middle, middle + 128))
-    b = jnp.concatenate([b_own] + [b_lines[kz] for kz in range(1, nz)], axis=0)
-    found.append((b, 0, 0, 1, False))
-    near_b = {ky: trade(b, dims, ky=ky) for ky in range(1, ny)}
-    for ky, v in near_b.items():
-        found.append((v, ky, 0, 1, False))
-    for kx in range(1, nx):
-        found.append((trade(b, dims, kx=kx), 0, kx, 1, False))
-    for kx, v in near_a.items():
-        for ky in range(1, ny):
-            third = trade(v, dims, ky=ky)
-            found.append((third, ky, kx, 0, True, middle + ky * 128, middle + ny * 128))
-    for ky, v in near_b.items():
-        for kx in range(1, nx):
-            found.append((trade(v, dims, kx=kx), ky, kx, 1, False))
-
-    size = nz * rows
-    pieces = tuple((f[1] * nx + f[2], f[3], f[4]) for f in found)
-    keep, send = project([f[0] for f in found], pieces, out_weight, dims, rows)
-    carriers = [f for f in found if len(f) > 5]
-    places = tuple((f[1] * nx + f[2], f[5], f[6]) for f in carriers)
-    residual, mask = arrange([f[0] for f in carriers], places, lanes, size)
+    lines = {kz: trade(a_own, dims, kz=kz) for kz in steps}
+    blocks = [blocks[0]] + [
+        trade(blocks[c], dims, ky=c // nx, kx=c % nx) for c in range(1, plane)
+    ]
+    rest = pack_plane(blocks, lanes, nz)
+    lines, rest = lax.optimization_barrier((lines, rest))
+    rest = [rest[0]] + [trade(rest[kz], dims, kz=kz) for kz in range(1, nz)]
+    a, b = pack_line([a_own] + [lines[kz] for kz in range(1, nz)], plane)
+    firsts, seconds = {0: a}, {0: b}
+    for wave in planes(a, b, dims):
+        for (ky, kx), half, array in wave:
+            (firsts, seconds)[half][ky * nx + kx] = array
+    codes = sorted(firsts)
+
+    keep, send = project(
+        [firsts[c] for c in codes], [seconds[c] for c in codes], codes, rest, out_weight, dims, rows
+    )
+    residual, mask = arrange(rest, lanes, dims, rows)
     projected = (keep + swap_sec(send)).astype(BF)
     mixed = (residual[:, :part].astype(F32) + projected.astype(F32)).astype(BF)
 
     lines = {kz: trade(mixed, dims, kz=kz) for kz in steps}
-    stacked, mask = merge([mixed] + [lines[kz] for kz in range(1, nz)], mask, dims, rows)
+    stacked = jnp.concatenate([mixed] + [lines[kz] for kz in range(1, nz)], axis=0)
     pairs = []
     for ky in range(ny):
         for kx in range(nx):

time: 108 us -> 104 us (0.963)
  waiting for transfers between devices: 51.2 us -> 46.7 us
    ppermute x25 -> x28, waiting for transfers between devices: 47.1 us -> 43.1 us  [trade(): return lax.ppermute(value, 'dev', [(d, d ^ code) for d in range(n)])]
    ppermute x25 -> x28, starting transfers between devices: 37.8 us -> 37.7 us  [trade(): return lax.ppermute(value, 'dev', [(d, d ^ code) for d in range(n)])]
    unnamed x17 -> x16, local copies, waits for them, and re-layouts: 2.21 us -> 2.26 us
  transfers between devices with their start and end apart: 33 -> 36, of which waited for: 20 -> 20; matrix products, arithmetic and copies ran while one was open for 1% -> 0% of each run, Pallas kernels for 1% -> 2%
where the time goes in v4:
time: 104 us; the launch traced here: 103 us
  waiting for transfers between devices  46.7 us (45%)
  starting transfers between devices  38.9 us (37%)
  Pallas kernels  13.7 us (13%)
  local copies, waits for them, and re-layouts  2.34 us (2%)
  other arithmetic  1.39 us (1%)
    ppermute x28, waiting for transfers between devices, trade(): return lax.ppermute(value, 'dev', [(d, d ^ code) for d in range(n)])  43.1 us
    ppermute x28, starting transfers between devices, trade(): return lax.ppermute(value, 'dev', [(d, d ^ code) for d in range(n)])  37.7 us
    pallas_call x1, Pallas kernels, attention(): pl.pallas_call(functools.partial(attend_kernel, dims, lanes), out_shape=t...  7.56 us
    ppermute x8, waiting for transfers between devices, swap_sec(): return lax.ppermute(value, 'sec', [(0, 1), (1, 0)])  3.62 us
    pallas_call x1, Pallas kernels, experts(): pl.pallas_call(functools.partial(late_kernel, dims, codes and codes[count...  2.77 us
    unnamed x16, local copies, waits for them, and re-layouts  2.26 us
  transfers between devices with their start and end apart: 36, of which 20 were waited for; matrix products, arithmetic and copies ran while one was open for 0% of the time, Pallas kernels for 2%

profile of v4, /device:TPU:0, one launch (start us, length us, event | category | flops | bytes accessed | tf_op | source)
XLA Modules:
  0.0 103.3 jit_solution(14302328926512566101)
XLA Ops:
  0.0 7.6 %attend.1 = (bf16[16,3072]{1,0:T(8,128)(2,1)}, bf16[16,1664]{1,0:T(8,128)(2,1)}, bf16[16,1664]{1,0:T(8,128)(2,1)}, bf16[16,1664]{1,0:T(8,128)(2,1)}, bf16[16,1664]{1,0:T(8,128)(2,1)}) custom-call(s32[16]{0:T(128)} %refs_0_.1, s32[8,16]{1,0:T(8,128)} %bitcast.7, bf16[16,4096]{1,0:T(8,128)(2,1)} %refs_2_.1, bf16[16,256]{1,0:T(8,128)(2,1)} %refs_3_.1, ...), custom_call_target="tpu_custom_call" | custom-call | flops 402653184 | bytes 12582912 | tf_op jit(solution)/shard_map/attend/pallas_call | solution.py:461
  7.6 3.0 %collective-permute-start.3 = (bf16[16,1664]{1,0:T(8,128)(2,1)}, bf16[16,1664]{1,0:T(8,128)(2,1)S(1)}, u32[]{:S(2)}, u32[]{:S(2)}) collective-permute-start(bf16[16,1664]{1,0:T(8,128)(2,1)} %get-tuple-element.38), channel_id=1, source_target_pairs={{0,1},{1,0},{2,3},{3,2},{4,5},{5,4},{6,7},{7,6},{8,9},{9,8},{10,11... | collective-permute-start | bytes 159752 | tf_op jit(solution)/shard_map/ppermute | solution.py:34
  10.6 1.3 %collective-permute-start = (bf16[16,3072]{1,0:T(8,128)(2,1)}, bf16[16,3072]{1,0:T(8,128)(2,1)S(1)}, u32[]{:S(2)}, u32[]{:S(2)}) collective-permute-start(bf16[16,3072]{1,0:T(8,128)(2,1)} %get-tuple-element.36.refs_0_), channel_id=1, source_target_pairs={{0,4},{1,5},{2,6},{3,7},{4,0},{5,1},{6,2},{7,3},{8,12},{9,13},{10,... | collective-permute-start | bytes 294920 | tf_op jit(solution)/shard_map/ppermute | solution.py:34
  11.9 2.5 %collective-permute-start.1 = (bf16[16,3072]{1,0:T(8,128)(2,1)}, bf16[16,3072]{1,0:T(8,128)(2,1)S(1)}, u32[]{:S(2)}, u32[]{:S(2)}) collective-permute-start(bf16[16,3072]{1,0:T(8,128)(2,1)} %get-tuple-element.36.refs_0_), channel_id=1, source_target_pairs={{0,8},{1,9},{2,10},{3,11},{4,12},{5,13},{6,14},{7,15},{8,0},{9,1},... | collective-permute-start | bytes 294920 | tf_op jit(solution)/shard_map/ppermute | solution.py:34
  14.4 0.6 collective-permute-start.2
  15.0 1.2 %collective-permute-start.4 = (bf16[16,1664]{1,0:T(8,128)(2,1)}, bf16[16,1664]{1,0:T(8,128)(2,1)S(1)}, u32[]{:S(2)}, u32[]{:S(2)}) collective-permute-start(bf16[16,1664]{1,0:T(8,128)(2,1)} %get-tuple-element.39), channel_id=1, source_target_pairs={{0,2},{1,3},{2,0},{3,1},{4,6},{5,7},{6,4},{7,5},{8,10},{9,11},{10,... | collective-permute-start | bytes 159752 | tf_op jit(solution)/shard_map/ppermute | solution.py:34
  16.2 0.5 collective-permute-start.5
  16.6 3.1 %collective-permute-done.4.refs_2_ = bf16[16,1664]{1,0:T(8,128)(2,1)S(1)} collective-permute-done((bf16[16,1664]{1,0:T(8,128)(2,1)}, bf16[16,1664]{1,0:T(8,128)(2,1)S(1)}, u32[]{:S(2)}, u32[]{:S(2)}) %collective-permute-start.4) | collective-permute-done | bytes 53280 | tf_op jit(solution)/shard_map/ppermute | solution.py:34
  19.7 1.7 %collective-permute-done.5.refs_3_ = bf16[16,1664]{1,0:T(8,128)(2,1)S(1)} collective-permute-done((bf16[16,1664]{1,0:T(8,128)(2,1)}, bf16[16,1664]{1,0:T(8,128)(2,1)S(1)}, u32[]{:S(2)}, u32[]{:S(2)}) %collective-permute-start.5) | collective-permute-done | bytes 53280 | tf_op jit(solution)/shard_map/ppermute | solution.py:34
  21.4 0.8 copy-done.7
  22.2 0.1 pack_plane.1
  22.4 0.9 copy-done.5
  23.3 0.7 collective-permute-start.9
  24.0 1.5 %collective-permute-start.13 = (bf16[64,1536]{1,0:T(8,128)(2,1)S(1)}, bf16[64,1536]{1,0:T(8,128)(2,1)S(1)}, u32[]{:S(2)}, u32[]{:S(2)}) collective-permute-start(bf16[64,1536]{1,0:T(8,128)(2,1)S(1)} %get-tuple-element.54.refs_4_), channel_id=1, source_target_pairs={{0,2},{1,3},{2,0},{3,1},{4,6},{5,7},{6,4},{7,5},{8,10},{9,11},{10,... | collective-permute-start | bytes 589832 | tf_op jit(solution)/shard_map/ppermute | solution.py:34
  25.5 1.7 %collective-permute-start.6 = (bf16[64,1280]{1,0:T(8,128)(2,1)S(1)}, bf16[64,1280]{1,0:T(8,128)(2,1)S(1)}, u32[]{:S(2)}, u32[]{:S(2)}) collective-permute-start(bf16[64,1280]{1,0:T(8,128)(2,1)S(1)} %get-tuple-element.46), channel_id=1, source_target_pairs={{0,4},{1,5},{2,6},{3,7},{4,0},{5,1},{6,2},{7,3},{8,12},{9,13},{10,... | collective-permute-start | bytes 491528 | tf_op jit(solution)/shard_map/ppermute | solution.py:34
  27.2 1.6 %collective-permute-start.7 = (bf16[64,1280]{1,0:T(8,128)(2,1)S(1)}, bf16[64,1280]{1,0:T(8,128)(2,1)S(1)}, u32[]{:S(2)}, u32[]{:S(2)}) collective-permute-start(bf16[64,1280]{1,0:T(8,128)(2,1)S(1)} %get-tuple-element.47), channel_id=1, source_target_pairs={{0,8},{1,9},{2,10},{3,11},{4,12},{5,13},{6,14},{7,15},{8,0},{9,1},... | collective-permute-start | bytes 491528 | tf_op jit(solution)/shard_map/ppermute | solution.py:34
  28.8 1.6 %collective-permute-start.10 = (bf16[64,1536]{1,0:T(8,128)(2,1)S(1)}, bf16[64,1536]{1,0:T(8,128)(2,1)S(1)}, u32[]{:S(2)}, u32[]{:S(2)}) collective-permute-start(bf16[64,1536]{1,0:T(8,128)(2,1)S(1)} %get-tuple-element.53.refs_0_), channel_id=1, source_target_pairs={{0,2},{1,3},{2,0},{3,1},{4,6},{5,7},{6,4},{7,5},{8,10},{9,11},{10,... | collective-permute-start | bytes 589832 | tf_op jit(solution)/shard_map/ppermute | solution.py:34
  30.4 1.7 %collective-permute-done.6.refs_1_.refs_9_ = bf16[64,1280]{1,0:T(8,128)(2,1)S(1)} collective-permute-done((bf16[64,1280]{1,0:T(8,128)(2,1)S(1)}, bf16[64,1280]{1,0:T(8,128)(2,1)S(1)}, u32[]{:S(2)}, u32[]{:S(2)}) %collective-permute-start.6) | collective-permute-done | bytes 163872 | tf_op jit(solution)/shard_map/ppermute | solution.py:34
  32.1 1.5 %collective-permute-start.12 = (bf16[64,1536]{1,0:T(8,128)(2,1)S(1)}, bf16[64,1536]{1,0:T(8,128)(2,1)S(1)}, u32[]{:S(2)}, u32[]{:S(2)}) collective-permute-start(bf16[64,1536]{1,0:T(8,128)(2,1)S(1)} %get-tuple-element.54.refs_4_), channel_id=1, source_target_pairs={{0,1},{1,0},{2,3},{3,2},{4,5},{5,4},{6,7},{7,6},{8,9},{9,8},{10,11... | collective-permute-start | bytes 589832 | tf_op jit(solution)/shard_map/ppermute | solution.py:34
  33.6 0.6 collective-permute-start.11
  34.2 0.5 collective-permute-start.14
  34.7 2.0 %collective-permute-done.7.refs_2_.refs_10_ = bf16[64,1280]{1,0:T(8,128)(2,1)S(1)} collective-permute-done((bf16[64,1280]{1,0:T(8,128)(2,1)S(1)}, bf16[64,1280]{1,0:T(8,128)(2,1)S(1)}, u32[]{:S(2)}, u32[]{:S(2)}) %collective-permute-start.7) | collective-permute-done | bytes 163872 | tf_op jit(solution)/shard_map/ppermute | solution.py:34
  36.7 3.5 %collective-permute-start.8 = (bf16[64,1280]{1,0:T(8,128)(2,1)S(1)}, bf16[64,1280]{1,0:T(8,128)(2,1)S(1)}, u32[]{:S(2)}, u32[]{:S(2)}) collective-permute-start(bf16[64,1280]{1,0:T(8,128)(2,1)S(1)} %get-tuple-element.48), channel_id=1, source_target_pairs={{0,12},{1,13},{2,14},{3,15},{4,8},{5,9},{6,10},{7,11},{8,4},{9,5},... | collective-permute-start | bytes 491528 | tf_op jit(solution)/shard_map/ppermute | solution.py:34
  40.2 3.6 %collective-permute-done.8.refs_3_.refs_11_ = bf16[64,1280]{1,0:T(8,128)(2,1)S(1)} collective-permute-done((bf16[64,1280]{1,0:T(8,128)(2,1)S(1)}, bf16[64,1280]{1,0:T(8,128)(2,1)S(1)}, u32[]{:S(2)}, u32[]{:S(2)}) %collective-permute-start.8) | collective-permute-done | bytes 163872 | tf_op jit(solution)/shard_map/ppermute | solution.py:34
  43.8 1.6 %project.1 = (f32[256,128]{1,0:T(8,128)S(1)}, f32[256,128]{1,0:T(8,128)S(1)}) custom-call(bf16[64,1536]{1,0:T(8,128)(2,1)S(1)} %get-tuple-element.53.refs_0_, bf16[64,1536]{1,0:T(8,128)(2,1)S(1)} %collective-permute-done.9.refs_1_, bf16[64,1536]{1,0:T(8,128)(2,1)S(1)} %collective-permute-done.10.refs_2_, ...), custom_call_target="tpu_custom_call" | custom-call | flops 536870912 | bytes 4194304 | tf_op jit(solution)/shard_map/project/pallas_call | solution.py:585
  45.4 0.1 collective-permute-start.15
  45.5 0.4 arrange.1
  45.9 0.9 collective-permute-done.15
  46.9 0.1 collective-permute-start.16
  47.0 4.0 %collective-permute-start.17 = (bf16[256,128]{1,0:T(8,128)(2,1)S(1)}, bf16[256,128]{1,0:T(8,128)(2,1)S(1)}, u32[]{:S(2)}, u32[]{:S(2)}) collective-permute-start(bf16[256,128]{1,0:T(8,128)(2,1)S(1)} %add_convert_fusion.1), channel_id=1, source_target_pairs={{0,8},{1,9},{2,10},{3,11},{4,12},{5,13},{6,14},{7,15},{8,0},{9,1},... | collective-permute-start | bytes 196616 | tf_op jit(solution)/shard_map/ppermute | solution.py:34
  51.0 0.3 collective-permute-start.18
  51.3 3.7 %collective-permute-done.17 = bf16[256,128]{1,0:T(8,128)(2,1)S(1)} collective-permute-done((bf16[256,128]{1,0:T(8,128)(2,1)S(1)}, bf16[256,128]{1,0:T(8,128)(2,1)S(1)}, u32[]{:S(2)}, u32[]{:S(2)}) %collective-permute-start.17) | collective-permute-done | bytes 65568 | tf_op jit(solution)/shard_map/ppermute | solution.py:34
  55.1 2.1 %collective-permute-done.18 = bf16[256,128]{1,0:T(8,128)(2,1)S(1)} collective-permute-done((bf16[256,128]{1,0:T(8,128)(2,1)S(1)}, bf16[256,128]{1,0:T(8,128)(2,1)S(1)}, u32[]{:S(2)}, u32[]{:S(2)}) %collective-permute-start.18) | collective-permute-done | bytes 65568 | tf_op jit(solution)/shard_map/ppermute | solution.py:34
  57.2 0.4 collective-permute-start.24
  57.6 0.2 collective-permute-start.19
  57.8 2.9 %collective-permute-start.21 = (bf16[1024,128]{1,0:T(8,128)(2,1)S(1)}, bf16[1024,128]{1,0:T(8,128)(2,1)S(1)}, u32[]{:S(2)}, u32[]{:S(2)}) collective-permute-start(bf16[1024,128]{1,0:T(8,128)(2,1)S(1)} %pad_maximum_fusion.1.refs_0_), channel_id=1, source_target_pairs={{0,3},{1,2},{2,1},{3,0},{4,7},{5,6},{6,5},{7,4},{8,11},{9,10},{10,... | collective-permute-start | bytes 786440 | tf_op jit(solution)/shard_map/ppermute | solution.py:34
  60.8 5.8 %collective-permute-done.24.refs_2_ = bf16[1024,128]{1,0:T(8,128)(2,1)S(1)} collective-permute-done((bf16[1024,128]{1,0:T(8,128)(2,1)S(1)}, bf16[1024,128]{1,0:T(8,128)(2,1)S(1)}, u32[]{:S(2)}, u32[]{:S(2)}) %collective-permute-start.24) | collective-permute-done | bytes 262176 | tf_op jit(solution)/shard_map/ppermute | solution.py:34
  66.5 3.1 %collective-permute-done.19.refs_0_ = bf16[1024,128]{1,0:T(8,128)(2,1)S(1)} collective-permute-done((bf16[1024,128]{1,0:T(8,128)(2,1)S(1)}, bf16[1024,128]{1,0:T(8,128)(2,1)S(1)}, u32[]{:S(2)}, u32[]{:S(2)}) %collective-permute-start.19) | collective-permute-done | bytes 262176 | tf_op jit(solution)/shard_map/ppermute | solution.py:34
  69.6 0.5 collective-permute-start.22
  70.2 1.3 %experts_early.1 = (f32[256,768]{1,0:T(8,128)S(1)}, f32[256,16]{1,0:T(8,128)S(1)}, f32[256,128]{1,0:T(8,128)S(1)}, bf16[16,4096]{1,0:T(8,128)(2,1)S(1)}) custom-call(bf16[1024,128]{1,0:T(8,128)(2,1)S(1)} %pad_maximum_fusion.1.refs_0_, bf16[1024,128]{1,0:T(8,128)(2,1)S(1)} %collective-permute-done.23.refs_1_, ...), custom_call_target="tpu_custom_call" | custom-call | flops 797253312 | bytes 3114270 | tf_op jit(solution)/shard_map/experts_early/pallas_call | solution.py:310
  71.5 0.5 copy-done.2
  72.1 2.8 %experts_late.1 = (bf16[256,1024]{1,0:T(8,128)(2,1)S(1)}, bf16[256,1024]{1,0:T(8,128)(2,1)S(1)}, bf16[256,1024]{1,0:T(8,128)(2,1)S(1)}, bf16[256,1024]{1,0:T(8,128)(2,1)S(1)}, bf16[16,4096]{1,0:T(8,128)(2,1)S(1)}) custom-call(bf16[1024,128]{1,0:T(8,128)(2,1)S(1)} %collective-permute-done.19.refs_0_, bf16[1024,128]{1,0:T(8,128)(2,1)S(1)} %collective-permute-done.20.refs_1_, ...), custom_call_target="tpu_custom_call" | custom-call | flops 1618665856 | bytes 6322913 | tf_op jit(solution)/shard_map/experts_late/pallas_call | solution.py:324
  74.9 0.1 collective-permute-start.27
  74.9 0.5 collective-permute-start.26
  75.4 1.4 %collective-permute-done.27 = bf16[256,1024]{1,0:T(8,128)(2,1)S(1)} collective-permute-done((bf16[256,1024]{1,0:T(8,128)(2,1)S(1)}, bf16[256,1024]{1,0:T(8,128)(2,1)S(1)}, u32[]{:S(2)}, u32[]{:S(2)}) %collective-permute-start.27) | collective-permute-done | bytes 524320 | tf_op jit(solution)/shard_map/ppermute | solution.py:42
  76.8 0.2 add_convert_fusion
  77.1 1.7 %collective-permute-start.28 = (bf16[128,1024]{1,0:T(8,128)(2,1)S(1)}, bf16[128,1024]{1,0:T(8,128)(2,1)S(1)}, u32[]{:S(2)}, u32[]{:S(2)}) collective-permute-start(bf16[128,1024]{1,0:T(8,128)(2,1)S(1)} %get-tuple-element.70), channel_id=1, source_target_pairs={{0,1},{1,0},{2,3},{3,2},{4,5},{5,4},{6,7},{7,6},{8,9},{9,8},{10,11... | collective-permute-start | bytes 786440 | tf_op jit(solution)/shard_map/ppermute | solution.py:34
  78.8 0.3 collective-permute-start.30
  79.1 0.2 convert_add_fusion
  79.3 6.2 %collective-permute-done.28 = bf16[128,1024]{1,0:T(8,128)(2,1)S(1)} collective-permute-done((bf16[128,1024]{1,0:T(8,128)(2,1)S(1)}, bf16[128,1024]{1,0:T(8,128)(2,1)S(1)}, u32[]{:S(2)}, u32[]{:S(2)}) %collective-permute-start.28) | collective-permute-done | bytes 262176 | tf_op jit(solution)/shard_map/ppermute | solution.py:34
  85.5 1.4 %collective-permute-done.30 = bf16[128,1024]{1,0:T(8,128)(2,1)S(1)} collective-permute-done((bf16[128,1024]{1,0:T(8,128)(2,1)S(1)}, bf16[128,1024]{1,0:T(8,128)(2,1)S(1)}, u32[]{:S(2)}, u32[]{:S(2)}) %collective-permute-start.30) | collective-permute-done | bytes 262176 | tf_op jit(solution)/shard_map/ppermute | solution.py:34
  86.9 0.2 slice_add_fusion
  87.1 0.4 collective-permute-start.31
  87.5 1.3 %collective-permute-start.29 = (bf16[64,1024]{1,0:T(8,128)(2,1)S(1)}, bf16[64,1024]{1,0:T(8,128)(2,1)S(1)}, u32[]{:S(2)}, u32[]{:S(2)}) collective-permute-start(bf16[64,1024]{1,0:T(8,128)(2,1)S(1)} %slice.99), channel_id=1, source_target_pairs={{0,2},{1,3},{2,0},{3,1},{4,6},{5,7},{6,4},{7,5},{8,10},{9,11},{10,... | collective-permute-start | bytes 393224 | tf_op jit(solution)/shard_map/ppermute | solution.py:34
  88.8 3.3 %collective-permute-done.31 = bf16[64,1024]{1,0:T(8,128)(2,1)S(1)} collective-permute-done((bf16[64,1024]{1,0:T(8,128)(2,1)S(1)}, bf16[64,1024]{1,0:T(8,128)(2,1)S(1)}, u32[]{:S(2)}, u32[]{:S(2)}) %collective-permute-start.31) | collective-permute-done | bytes 131104 | tf_op jit(solution)/shard_map/ppermute | solution.py:34
  92.1 0.4 collective-permute-done.29
  92.7 2.4 %collective-permute-start.32 = (bf16[16,2048]{1,0:T(8,128)(2,1)S(1)}, bf16[16,2048]{1,0:T(8,128)(2,1)S(1)}, u32[]{:S(2)}, u32[]{:S(2)}) collective-permute-start(bf16[16,2048]{1,0:T(8,128)(2,1)S(1)} %get-tuple-element.71), channel_id=1, source_target_pairs={{0,8},{1,9},{2,10},{3,11},{4,12},{5,13},{6,14},{7,15},{8,0},{9,1},... | collective-permute-start | bytes 196616 | tf_op jit(solution)/shard_map/ppermute | solution.py:34
  95.0 1.3 %collective-permute-start.33 = (bf16[16,2048]{1,0:T(8,128)(2,1)S(1)}, bf16[16,2048]{1,0:T(8,128)(2,1)S(1)}, u32[]{:S(2)}, u32[]{:S(2)}) collective-permute-start(bf16[16,2048]{1,0:T(8,128)(2,1)S(1)} %get-tuple-element.73), channel_id=1, source_target_pairs={{0,12},{1,13},{2,14},{3,15},{4,8},{5,9},{6,10},{7,11},{8,4},{9,5},... | collective-permute-start | bytes 196616 | tf_op jit(solution)/shard_map/ppermute | solution.py:34
  96.3 2.4 %collective-permute-done.32 = bf16[16,2048]{1,0:T(8,128)(2,1)S(1)} collective-permute-done((bf16[16,2048]{1,0:T(8,128)(2,1)S(1)}, bf16[16,2048]{1,0:T(8,128)(2,1)S(1)}, u32[]{:S(2)}, u32[]{:S(2)}) %collective-permute-start.32) | collective-permute-done | bytes 65568 | tf_op jit(solution)/shard_map/ppermute | solution.py:34
  98.8 2.4 %collective-permute-done.33 = bf16[16,2048]{1,0:T(8,128)(2,1)S(1)} collective-permute-done((bf16[16,2048]{1,0:T(8,128)(2,1)S(1)}, bf16[16,2048]{1,0:T(8,128)(2,1)S(1)}, u32[]{:S(2)}, u32[]{:S(2)}) %collective-permute-start.33) | collective-permute-done | bytes 65568 | tf_op jit(solution)/shard_map/ppermute | solution.py:34
  101.2 0.1 collective-permute-done.34
  101.3 0.1 collective-permute-start.35
  101.4 1.2 %collective-permute-done.35 = bf16[16,2048]{1,0:T(8,128)(2,1)S(1)} collective-permute-done((bf16[16,2048]{1,0:T(8,128)(2,1)S(1)}, bf16[16,2048]{1,0:T(8,128)(2,1)S(1)}, u32[]{:S(2)}, u32[]{:S(2)}) %collective-permute-start.35) | collective-permute-done | bytes 65568 | tf_op jit(solution)/shard_map/ppermute | solution.py:42
  102.7 0.7 maximum_select_fusion
  (45 shorter events, 0.4 us)
Async XLA Ops:
  0.0 43.8 %copy-start.3 = (bf16[4096,256]{1,0:T(8,128)(2,1)S(1)}, bf16[4096,256]{1,0:T(8,128)(2,1)}, u32[]{:S(2)}) copy-start(bf16[4096,256]{1,0:T(8,128)(2,1)} %refs_12_.2) | copy-start | bytes 6291460
  7.6 8.6 %collective-permute-start.3 = (bf16[16,1664]{1,0:T(8,128)(2,1)}, bf16[16,1664]{1,0:T(8,128)(2,1)S(1)}, u32[]{:S(2)}, u32[]{:S(2)}) collective-permute-start(bf16[16,1664]{1,0:T(8,128)(2,1)} %get-tuple-element.38), channel_id=1, source_target_pairs={{0,1},{1,0},{2,3},{3,2},{4,5},{5,4},{6,7},{7,6},{8,9},{9,8},{10,11... | collective-permute-start | bytes 159752 | tf_op jit(solution)/shard_map/ppermute | solution.py:34
  10.6 11.7 %collective-permute-start = (bf16[16,3072]{1,0:T(8,128)(2,1)}, bf16[16,3072]{1,0:T(8,128)(2,1)S(1)}, u32[]{:S(2)}, u32[]{:S(2)}) collective-permute-start(bf16[16,3072]{1,0:T(8,128)(2,1)} %get-tuple-element.36.refs_0_), channel_id=1, source_target_pairs={{0,4},{1,5},{2,6},{3,7},{4,0},{5,1},{6,2},{7,3},{8,12},{9,13},{10,... | collective-permute-start | bytes 294920 | tf_op jit(solution)/shard_map/ppermute | solution.py:34
  11.9 10.4 %collective-permute-start.1 = (bf16[16,3072]{1,0:T(8,128)(2,1)}, bf16[16,3072]{1,0:T(8,128)(2,1)S(1)}, u32[]{:S(2)}, u32[]{:S(2)}) collective-permute-start(bf16[16,3072]{1,0:T(8,128)(2,1)} %get-tuple-element.36.refs_0_), channel_id=1, source_target_pairs={{0,8},{1,9},{2,10},{3,11},{4,12},{5,13},{6,14},{7,15},{8,0},{9,1},... | collective-permute-start | bytes 294920 | tf_op jit(solution)/shard_map/ppermute | solution.py:34
  14.4 8.0 %collective-permute-start.2 = (bf16[16,3072]{1,0:T(8,128)(2,1)}, bf16[16,3072]{1,0:T(8,128)(2,1)S(1)}, u32[]{:S(2)}, u32[]{:S(2)}) collective-permute-start(bf16[16,3072]{1,0:T(8,128)(2,1)} %get-tuple-element.36.refs_0_), channel_id=1, source_target_pairs={{0,12},{1,13},{2,14},{3,15},{4,8},{5,9},{6,10},{7,11},{8,4},{9,5},... | collective-permute-start | bytes 294920 | tf_op jit(solution)/shard_map/ppermute | solution.py:34
  15.0 4.7 %collective-permute-start.4 = (bf16[16,1664]{1,0:T(8,128)(2,1)}, bf16[16,1664]{1,0:T(8,128)(2,1)S(1)}, u32[]{:S(2)}, u32[]{:S(2)}) collective-permute-start(bf16[16,1664]{1,0:T(8,128)(2,1)} %get-tuple-element.39), channel_id=1, source_target_pairs={{0,2},{1,3},{2,0},{3,1},{4,6},{5,7},{6,4},{7,5},{8,10},{9,11},{10,... | collective-permute-start | bytes 159752 | tf_op jit(solution)/shard_map/ppermute | solution.py:34
  16.2 5.2 %collective-permute-start.5 = (bf16[16,1664]{1,0:T(8,128)(2,1)}, bf16[16,1664]{1,0:T(8,128)(2,1)S(1)}, u32[]{:S(2)}, u32[]{:S(2)}) collective-permute-start(bf16[16,1664]{1,0:T(8,128)(2,1)} %get-tuple-element.40), channel_id=1, source_target_pairs={{0,3},{1,2},{2,1},{3,0},{4,7},{5,6},{6,5},{7,4},{8,11},{9,10},{10,... | collective-permute-start | bytes 159752 | tf_op jit(solution)/shard_map/ppermute | solution.py:34
  21.4 0.8 copy-start.7
  22.2 47.9 %copy-start.4 = (bf16[4096,16]{0,1:T(8,128)(2,1)S(1)}, bf16[4096,16]{0,1:T(8,128)(2,1)}, u32[]{:S(2)}) copy-start(bf16[4096,16]{0,1:T(8,128)(2,1)} %param.23) | copy-start | bytes 393220
  22.2 47.9 %copy-start.6 = (f32[4096]{0:T(1024)S(1)}, f32[4096]{0:T(1024)}, u32[]{:S(2)}) copy-start(f32[4096]{0:T(1024)} %param.22) | copy-start | bytes 49156
  22.3 0.9 copy-start.5
  23.2 46.9 %copy-start = (bf16[1,4096,384]{2,1,0:T(8,128)(2,1)S(1)}, bf16[1,4096,384]{2,1,0:T(8,128)(2,1)}, u32[]{:S(2)}) copy-start(bf16[1,4096,384]{2,1,0:T(8,128)(2,1)} %refs_6_.5) | copy-start | bytes 9437188
  23.2 46.9 %copy-start.1 = (bf16[1,4096,384]{2,1,0:T(8,128)(2,1)S(1)}, bf16[1,4096,384]{2,1,0:T(8,128)(2,1)}, u32[]{:S(2)}) copy-start(bf16[1,4096,384]{2,1,0:T(8,128)(2,1)} %refs_7_.5) | copy-start | bytes 9437188
  23.3 10.4 %collective-permute-start.9 = (bf16[64,1536]{1,0:T(8,128)(2,1)S(1)}, bf16[64,1536]{1,0:T(8,128)(2,1)S(1)}, u32[]{:S(2)}, u32[]{:S(2)}) collective-permute-start(bf16[64,1536]{1,0:T(8,128)(2,1)S(1)} %get-tuple-element.53.refs_0_), channel_id=1, source_target_pairs={{0,1},{1,0},{2,3},{3,2},{4,5},{5,4},{6,7},{7,6},{8,9},{9,8},{10,11... | collective-permute-start | bytes 589832 | tf_op jit(solution)/shard_map/ppermute | solution.py:34
  24.0 10.3 %collective-permute-start.13 = (bf16[64,1536]{1,0:T(8,128)(2,1)S(1)}, bf16[64,1536]{1,0:T(8,128)(2,1)S(1)}, u32[]{:S(2)}, u32[]{:S(2)}) collective-permute-start(bf16[64,1536]{1,0:T(8,128)(2,1)S(1)} %get-tuple-element.54.refs_4_), channel_id=1, source_target_pairs={{0,2},{1,3},{2,0},{3,1},{4,6},{5,7},{6,4},{7,5},{8,10},{9,11},{10,... | collective-permute-start | bytes 589832 | tf_op jit(solution)/shard_map/ppermute | solution.py:34
  25.5 6.6 %collective-permute-start.6 = (bf16[64,1280]{1,0:T(8,128)(2,1)S(1)}, bf16[64,1280]{1,0:T(8,128)(2,1)S(1)}, u32[]{:S(2)}, u32[]{:S(2)}) collective-permute-start(bf16[64,1280]{1,0:T(8,128)(2,1)S(1)} %get-tuple-element.46), channel_id=1, source_target_pairs={{0,4},{1,5},{2,6},{3,7},{4,0},{5,1},{6,2},{7,3},{8,12},{9,13},{10,... | collective-permute-start | bytes 491528 | tf_op jit(solution)/shard_map/ppermute | solution.py:34
  27.2 9.5 %collective-permute-start.7 = (bf16[64,1280]{1,0:T(8,128)(2,1)S(1)}, bf16[64,1280]{1,0:T(8,128)(2,1)S(1)}, u32[]{:S(2)}, u32[]{:S(2)}) collective-permute-start(bf16[64,1280]{1,0:T(8,128)(2,1)S(1)} %get-tuple-element.47), channel_id=1, source_target_pairs={{0,8},{1,9},{2,10},{3,11},{4,12},{5,13},{6,14},{7,15},{8,0},{9,1},... | collective-permute-start | bytes 491528 | tf_op jit(solution)/shard_map/ppermute | solution.py:34
  28.8 15.0 %collective-permute-start.10 = (bf16[64,1536]{1,0:T(8,128)(2,1)S(1)}, bf16[64,1536]{1,0:T(8,128)(2,1)S(1)}, u32[]{:S(2)}, u32[]{:S(2)}) collective-permute-start(bf16[64,1536]{1,0:T(8,128)(2,1)S(1)} %get-tuple-element.53.refs_0_), channel_id=1, source_target_pairs={{0,2},{1,3},{2,0},{3,1},{4,6},{5,7},{6,4},{7,5},{8,10},{9,11},{10,... | collective-permute-start | bytes 589832 | tf_op jit(solution)/shard_map/ppermute | solution.py:34
  32.1 11.7 %collective-permute-start.12 = (bf16[64,1536]{1,0:T(8,128)(2,1)S(1)}, bf16[64,1536]{1,0:T(8,128)(2,1)S(1)}, u32[]{:S(2)}, u32[]{:S(2)}) collective-permute-start(bf16[64,1536]{1,0:T(8,128)(2,1)S(1)} %get-tuple-element.54.refs_4_), channel_id=1, source_target_pairs={{0,1},{1,0},{2,3},{3,2},{4,5},{5,4},{6,7},{7,6},{8,9},{9,8},{10,11... | collective-permute-start | bytes 589832 | tf_op jit(solution)/shard_map/ppermute | solution.py:34
  33.6 10.2 %collective-permute-start.11 = (bf16[64,1536]{1,0:T(8,128)(2,1)S(1)}, bf16[64,1536]{1,0:T(8,128)(2,1)S(1)}, u32[]{:S(2)}, u32[]{:S(2)}) collective-permute-start(bf16[64,1536]{1,0:T(8,128)(2,1)S(1)} %collective-permute-done.9.refs_1_), channel_id=1, source_target_pairs={{0,2},{1,3},{2,0},{3,1},{4,6},{5,7},{6,4},{7,5},{8,10},{9,11},{10,... | collective-permute-start | bytes 589832 | tf_op jit(solution)/shard_map/ppermute | solution.py:34
  34.2 9.6 %collective-permute-start.14 = (bf16[64,1536]{1,0:T(8,128)(2,1)S(1)}, bf16[64,1536]{1,0:T(8,128)(2,1)S(1)}, u32[]{:S(2)}, u32[]{:S(2)}) collective-permute-start(bf16[64,1536]{1,0:T(8,128)(2,1)S(1)} %collective-permute-done.13.refs_6_), channel_id=1, source_target_pairs={{0,1},{1,0},{2,3},{3,2},{4,5},{5,4},{6,7},{7,6},{8,9},{9,8},{10,11... | collective-permute-start | bytes 589832 | tf_op jit(solution)/shard_map/ppermute | solution.py:34
  36.7 7.1 %collective-permute-start.8 = (bf16[64,1280]{1,0:T(8,128)(2,1)S(1)}, bf16[64,1280]{1,0:T(8,128)(2,1)S(1)}, u32[]{:S(2)}, u32[]{:S(2)}) collective-permute-start(bf16[64,1280]{1,0:T(8,128)(2,1)S(1)} %get-tuple-element.48), channel_id=1, source_target_pairs={{0,12},{1,13},{2,14},{3,15},{4,8},{5,9},{6,10},{7,11},{8,4},{9,5},... | collective-permute-start | bytes 491528 | tf_op jit(solution)/shard_map/ppermute | solution.py:34
  45.4 1.4 %collective-permute-start.15 = (f32[256,128]{1,0:T(8,128)S(1)}, f32[256,128]{1,0:T(8,128)S(1)}, u32[]{:S(2)}, u32[]{:S(2)}) collective-permute-start(f32[256,128]{1,0:T(8,128)S(1)} %get-tuple-element.56), channel_id=1, source_target_pairs={{0,16},{16,0},{1,17},{17,1},{2,18},{18,2},{3,19},{19,3},{4,20},{20... | collective-permute-start | bytes 393224 | tf_op jit(solution)/shard_map/ppermute | solution.py:42
  46.9 4.5 %collective-permute-start.16 = (bf16[256,128]{1,0:T(8,128)(2,1)S(1)}, bf16[256,128]{1,0:T(8,128)(2,1)S(1)}, u32[]{:S(2)}, u32[]{:S(2)}) collective-permute-start(bf16[256,128]{1,0:T(8,128)(2,1)S(1)} %add_convert_fusion.1), channel_id=1, source_target_pairs={{0,4},{1,5},{2,6},{3,7},{4,0},{5,1},{6,2},{7,3},{8,12},{9,13},{10,... | collective-permute-start | bytes 196616 | tf_op jit(solution)/shard_map/ppermute | solution.py:34
  47.0 8.1 %collective-permute-start.17 = (bf16[256,128]{1,0:T(8,128)(2,1)S(1)}, bf16[256,128]{1,0:T(8,128)(2,1)S(1)}, u32[]{:S(2)}, u32[]{:S(2)}) collective-permute-start(bf16[256,128]{1,0:T(8,128)(2,1)S(1)} %add_convert_fusion.1), channel_id=1, source_target_pairs={{0,8},{1,9},{2,10},{3,11},{4,12},{5,13},{6,14},{7,15},{8,0},{9,1},... | collective-permute-start | bytes 196616 | tf_op jit(solution)/shard_map/ppermute | solution.py:34
  51.0 6.2 %collective-permute-start.18 = (bf16[256,128]{1,0:T(8,128)(2,1)S(1)}, bf16[256,128]{1,0:T(8,128)(2,1)S(1)}, u32[]{:S(2)}, u32[]{:S(2)}) collective-permute-start(bf16[256,128]{1,0:T(8,128)(2,1)S(1)} %add_convert_fusion.1), channel_id=1, source_target_pairs={{0,12},{1,13},{2,14},{3,15},{4,8},{5,9},{6,10},{7,11},{8,4},{9,5},... | collective-permute-start | bytes 196616 | tf_op jit(solution)/shard_map/ppermute | solution.py:34
  57.2 9.3 %collective-permute-start.24 = (bf16[1024,128]{1,0:T(8,128)(2,1)S(1)}, bf16[1024,128]{1,0:T(8,128)(2,1)S(1)}, u32[]{:S(2)}, u32[]{:S(2)}) collective-permute-start(bf16[1024,128]{1,0:T(8,128)(2,1)S(1)} %pad_maximum_fusion.1.refs_0_), channel_id=1, source_target_pairs={{0,1},{1,0},{2,3},{3,2},{4,5},{5,4},{6,7},{7,6},{8,9},{9,8},{10,11... | collective-permute-start | bytes 786440 | tf_op jit(solution)/shard_map/ppermute | solution.py:34
  57.6 12.0 %collective-permute-start.19 = (bf16[1024,128]{1,0:T(8,128)(2,1)S(1)}, bf16[1024,128]{1,0:T(8,128)(2,1)S(1)}, u32[]{:S(2)}, u32[]{:S(2)}) collective-permute-start(bf16[1024,128]{1,0:T(8,128)(2,1)S(1)} %pad_maximum_fusion.1.refs_0_), channel_id=1, source_target_pairs={{0,2},{1,3},{2,0},{3,1},{4,6},{5,7},{6,4},{7,5},{8,10},{9,11},{10,... | collective-permute-start | bytes 786440 | tf_op jit(solution)/shard_map/ppermute | solution.py:34
  57.8 11.8 %collective-permute-start.21 = (bf16[1024,128]{1,0:T(8,128)(2,1)S(1)}, bf16[1024,128]{1,0:T(8,128)(2,1)S(1)}, u32[]{:S(2)}, u32[]{:S(2)}) collective-permute-start(bf16[1024,128]{1,0:T(8,128)(2,1)S(1)} %pad_maximum_fusion.1.refs_0_), channel_id=1, source_target_pairs={{0,3},{1,2},{2,1},{3,0},{4,7},{5,6},{6,5},{7,4},{8,11},{9,10},{10,... | collective-permute-start | bytes 786440 | tf_op jit(solution)/shard_map/ppermute | solution.py:34
  60.8 9.4 %collective-permute-start.23 = (bf16[1024,128]{1,0:T(8,128)(2,1)S(1)}, bf16[1024,128]{1,0:T(8,128)(2,1)S(1)}, u32[]{:S(2)}, u32[]{:S(2)}) collective-permute-start(bf16[1024,128]{1,0:T(8,128)(2,1)S(1)} %pad_maximum_fusion.1.refs_0_), channel_id=1, source_target_pairs={{0,16},{16,0},{1,17},{17,1},{2,18},{18,2},{3,19},{19,3},{4,20},{20... | collective-permute-start | bytes 786440 | tf_op jit(solution)/shard_map/ppermute | solution.py:42
  66.5 3.6 %collective-permute-start.25 = (bf16[1024,128]{1,0:T(8,128)(2,1)S(1)}, bf16[1024,128]{1,0:T(8,128)(2,1)S(1)}, u32[]{:S(2)}, u32[]{:S(2)}) collective-permute-start(bf16[1024,128]{1,0:T(8,128)(2,1)S(1)} %collective-permute-done.24.refs_2_), channel_id=1, source_target_pairs={{0,16},{16,0},{1,17},{17,1},{2,18},{18,2},{3,19},{19,3},{4,20},{20... | collective-permute-start | bytes 786440 | tf_op jit(solution)/shard_map/ppermute | solution.py:42
  69.6 1.8 %collective-permute-start.20 = (bf16[1024,128]{1,0:T(8,128)(2,1)S(1)}, bf16[1024,128]{1,0:T(8,128)(2,1)S(1)}, u32[]{:S(2)}, u32[]{:S(2)}) collective-permute-start(bf16[1024,128]{1,0:T(8,128)(2,1)S(1)} %collective-permute-done.19.refs_0_), channel_id=1, source_target_pairs={{0,16},{16,0},{1,17},{17,1},{2,18},{18,2},{3,19},{19,3},{4,20},{20... | collective-permute-start | bytes 786440 | tf_op jit(solution)/shard_map/ppermute | solution.py:42
  69.6 1.9 %collective-permute-start.22 = (bf16[1024,128]{1,0:T(8,128)(2,1)S(1)}, bf16[1024,128]{1,0:T(8,128)(2,1)S(1)}, u32[]{:S(2)}, u32[]{:S(2)}) collective-permute-start(bf16[1024,128]{1,0:T(8,128)(2,1)S(1)} %collective-permute-done.21.refs_2_), channel_id=1, source_target_pairs={{0,16},{16,0},{1,17},{17,1},{2,18},{18,2},{3,19},{19,3},{4,20},{20... | collective-permute-start | bytes 786440 | tf_op jit(solution)/shard_map/ppermute | solution.py:42
  70.2 1.9 %copy-start.2 = (bf16[1,384,4096]{2,1,0:T(8,128)(2,1)S(1)}, bf16[1,384,4096]{2,1,0:T(8,128)(2,1)}, u32[]{:S(2)}) copy-start(bf16[1,384,4096]{2,1,0:T(8,128)(2,1)} %refs_12_.3) | copy-start | bytes 9437188
  74.9 2.0 %collective-permute-start.27 = (bf16[256,1024]{1,0:T(8,128)(2,1)S(1)}, bf16[256,1024]{1,0:T(8,128)(2,1)S(1)}, u32[]{:S(2)}, u32[]{:S(2)}) collective-permute-start(bf16[256,1024]{1,0:T(8,128)(2,1)S(1)} %get-tuple-element.66), channel_id=1, source_target_pairs={{0,16},{16,0},{1,17},{17,1},{2,18},{18,2},{3,19},{19,3},{4,20},{20... | collective-permute-start | bytes 1572872 | tf_op jit(solution)/shard_map/ppermute | solution.py:42
  74.9 4.1 %collective-permute-start.26 = (bf16[256,1024]{1,0:T(8,128)(2,1)S(1)}, bf16[256,1024]{1,0:T(8,128)(2,1)S(1)}, u32[]{:S(2)}, u32[]{:S(2)}) collective-permute-start(bf16[256,1024]{1,0:T(8,128)(2,1)S(1)} %get-tuple-element.64), channel_id=1, source_target_pairs={{0,16},{16,0},{1,17},{17,1},{2,18},{18,2},{3,19},{19,3},{4,20},{20... | collective-permute-start | bytes 1572872 | tf_op jit(solution)/shard_map/ppermute | solution.py:42
  77.1 8.4 %collective-permute-start.28 = (bf16[128,1024]{1,0:T(8,128)(2,1)S(1)}, bf16[128,1024]{1,0:T(8,128)(2,1)S(1)}, u32[]{:S(2)}, u32[]{:S(2)}) collective-permute-start(bf16[128,1024]{1,0:T(8,128)(2,1)S(1)} %get-tuple-element.70), channel_id=1, source_target_pairs={{0,1},{1,0},{2,3},{3,2},{4,5},{5,4},{6,7},{7,6},{8,9},{9,8},{10,11... | collective-permute-start | bytes 786440 | tf_op jit(solution)/shard_map/ppermute | solution.py:34
  78.8 8.1 %collective-permute-start.30 = (bf16[128,1024]{1,0:T(8,128)(2,1)S(1)}, bf16[128,1024]{1,0:T(8,128)(2,1)S(1)}, u32[]{:S(2)}, u32[]{:S(2)}) collective-permute-start(bf16[128,1024]{1,0:T(8,128)(2,1)S(1)} %get-tuple-element.69), channel_id=1, source_target_pairs={{0,2},{1,3},{2,0},{3,1},{4,6},{5,7},{6,4},{7,5},{8,10},{9,11},{10,... | collective-permute-start | bytes 786440 | tf_op jit(solution)/shard_map/ppermute | solution.py:34
  87.1 5.0 %collective-permute-start.31 = (bf16[64,1024]{1,0:T(8,128)(2,1)S(1)}, bf16[64,1024]{1,0:T(8,128)(2,1)S(1)}, u32[]{:S(2)}, u32[]{:S(2)}) collective-permute-start(bf16[64,1024]{1,0:T(8,128)(2,1)S(1)} %slice.98), channel_id=1, source_target_pairs={{0,1},{1,0},{2,3},{3,2},{4,5},{5,4},{6,7},{7,6},{8,9},{9,8},{10,11... | collective-permute-start | bytes 393224 | tf_op jit(solution)/shard_map/ppermute | solution.py:34
  87.5 5.0 %collective-permute-start.29 = (bf16[64,1024]{1,0:T(8,128)(2,1)S(1)}, bf16[64,1024]{1,0:T(8,128)(2,1)S(1)}, u32[]{:S(2)}, u32[]{:S(2)}) collective-permute-start(bf16[64,1024]{1,0:T(8,128)(2,1)S(1)} %slice.99), channel_id=1, source_target_pairs={{0,2},{1,3},{2,0},{3,1},{4,6},{5,7},{6,4},{7,5},{8,10},{9,11},{10,... | collective-permute-start | bytes 393224 | tf_op jit(solution)/shard_map/ppermute | solution.py:34
  92.7 6.1 %collective-permute-start.32 = (bf16[16,2048]{1,0:T(8,128)(2,1)S(1)}, bf16[16,2048]{1,0:T(8,128)(2,1)S(1)}, u32[]{:S(2)}, u32[]{:S(2)}) collective-permute-start(bf16[16,2048]{1,0:T(8,128)(2,1)S(1)} %get-tuple-element.71), channel_id=1, source_target_pairs={{0,8},{1,9},{2,10},{3,11},{4,12},{5,13},{6,14},{7,15},{8,0},{9,1},... | collective-permute-start | bytes 196616 | tf_op jit(solution)/shard_map/ppermute | solution.py:34
  95.0 6.2 %collective-permute-start.33 = (bf16[16,2048]{1,0:T(8,128)(2,1)S(1)}, bf16[16,2048]{1,0:T(8,128)(2,1)S(1)}, u32[]{:S(2)}, u32[]{:S(2)}) collective-permute-start(bf16[16,2048]{1,0:T(8,128)(2,1)S(1)} %get-tuple-element.73), channel_id=1, source_target_pairs={{0,12},{1,13},{2,14},{3,15},{4,8},{5,9},{6,10},{7,11},{8,4},{9,5},... | collective-permute-start | bytes 196616 | tf_op jit(solution)/shard_map/ppermute | solution.py:34
  96.3 5.0 %collective-permute-start.34 = (bf16[16,2048]{1,0:T(8,128)(2,1)S(1)}, bf16[16,2048]{1,0:T(8,128)(2,1)S(1)}, u32[]{:S(2)}, u32[]{:S(2)}) collective-permute-start(bf16[16,2048]{1,0:T(8,128)(2,1)S(1)} %get-tuple-element.72), channel_id=1, source_target_pairs={{0,4},{1,5},{2,6},{3,7},{4,0},{5,1},{6,2},{7,3},{8,12},{9,13},{10,... | collective-permute-start | bytes 196616 | tf_op jit(solution)/shard_map/ppermute | solution.py:34
  101.3 1.3 %collective-permute-start.35 = (bf16[16,2048]{1,0:T(8,128)(2,1)S(1)}, bf16[16,2048]{1,0:T(8,128)(2,1)S(1)}, u32[]{:S(2)}, u32[]{:S(2)}) collective-permute-start(bf16[16,2048]{1,0:T(8,128)(2,1)S(1)} %fusion.6), channel_id=1, source_target_pairs={{0,16},{16,0},{1,17},{17,1},{2,18},{18,2},{3,19},{19,3},{4,20},{20... | collective-permute-start | bytes 196616 | tf_op jit(solution)/shard_map/ppermute | solution.py:42

commit v5 on v4

--- a/solution.py
+++ b/solution.py
@@ -42,88 +42,30 @@
     return lax.ppermute(value, "sec", [(0, 1), (1, 0)])
 
 
-def planes(a, b, dims):
+def over_plane(block, dims):
     _, ny, nx = dims
-    first, second, third = [], [], []
-    near_a = {kx: trade(a, dims, kx=kx) for kx in range(1, nx)}
-    near_b = {ky: trade(b, dims, ky=ky) for ky in range(1, ny)}
-    first += [((0, kx), 0, v) for kx, v in near_a.items()]
-    first += [((ky, 0), 1, v) for ky, v in near_b.items()]
-    second += [((ky, 0), 0, trade(a, dims, ky=ky)) for ky in range(1, ny)]
-    second += [((0, kx), 1, trade(b, dims, kx=kx)) for kx in range(1, nx)]
-    third += [
-        ((ky, kx), 0, trade(v, dims, ky=ky)) for kx, v in near_a.items() for ky in range(1, ny)
-    ]
-    third += [
-        ((ky, kx), 1, trade(v, dims, kx=kx)) for ky, v in near_b.items() for kx in range(1, nx)
-    ]
-    return first, second, third
+    heads = block.shape[1] // HEAD
+    cuts = [i * heads // 3 * HEAD for i in range(4)]
+    along_x = {kx: trade(block, dims, kx=kx) for kx in range(1, nx)}
+    along_y = {ky: trade(block, dims, ky=ky) for ky in range(1, ny)}
+    found = [(0, 0, block)]
+    found += [(kx, 0, v) for kx, v in along_x.items()]
+    found += [(ky * nx, 0, v) for ky, v in along_y.items()]
+    for ky in range(1, ny):
+        for kx in range(1, nx):
+            for i, (start, stop) in enumerate(zip(cuts, cuts[1:])):
+                if i < 2:
+                    piece = trade(along_x[kx][:, start:stop], dims, ky=ky)
+                else:
+                    piece = trade(along_y[ky][:, start:stop], dims, kx=kx)
+                found.append((ky * nx + kx, start, piece))
+    return found
 
 
 ANY = pl.BlockSpec(memory_space=pl.ANY)
 VM = pl.BlockSpec(memory_space=pltpu.VMEM)
 HBM = pl.BlockSpec(memory_space=pltpu.HBM)
 MIB = 1024 * 1024
-
-
-def project_kernel(nz, plane, pieces, rows, *refs):
-    count = len(pieces)
-    arrays = refs[:count]
-    w_ref, keep_ref, send_ref, held, sems = refs[count:]
-    half = held.shape[1] // 2
-    sec = lax.axis_index("sec")
-    z = lax.axis_index("dev") // plane
-    copies = []
-
-    def move(i, source, place, size, column):
-        copies.append(
-            pltpu.make_async_copy(
-                arrays[i].at[pl.ds(source, size), pl.ds(0, half)],
-                held.at[pl.ds(place, size), pl.ds(column * half, half)],
-                sems.at[len(copies)],
-            )
-        )
-
-    for i, (slot, column, ordered) in enumerate(pieces):
-        if ordered:
-            move(i, 0, slot * nz * rows, nz * rows, column)
-            continue
-        for kz in range(nz):
-            place = pl.multiple_of((slot * nz + (z ^ kz)) * rows, rows)
-            move(i, kz * rows, place, rows, column)
-    for c in copies:
-        c.start()
-    for c in copies:
-        c.wait()
-    total = jnp.dot(held[...], w_ref[...], preferred_element_type=F32)
-    part = total.shape[1] // 2
-    low, high = total[:, :part], total[:, part:]
-    keep_ref[...] = jnp.where(sec == 0, low, high)
-    send_ref[...] = jnp.where(sec == 0, high, low)
-
-
-def project(arrays, pieces, weight, dims, rows):
-    depth, cols = weight.shape
-    nz, ny, nx = dims
-    tall = nz * ny * nx * rows
-    out = jax.ShapeDtypeStruct((tall, cols // 2), F32)
-    return pl.pallas_call(
-        functools.partial(project_kernel, nz, ny * nx, pieces, rows),
-        out_shape=(out, out),
-        in_specs=[ANY] * len(arrays) + [VM],
-        out_specs=(VM, VM),
-        scratch_shapes=[
-            pltpu.VMEM((tall, depth), BF),
-            pltpu.SemaphoreType.DMA((sum(1 if p[2] else nz for p in pieces),)),
-        ],
-        compiler_params=pltpu.CompilerParams(vmem_limit_bytes=(4 + tall // 32) * MIB),
-        cost_estimate=pl.CostEstimate(
-            flops=2 * tall * depth * cols,
-            bytes_accessed=2 * depth * (cols + tall),
-            transcendentals=0,
-        ),
-        name="project",
-    )(*arrays, weight)
 
 
 def gather_products(dims, codes, arrays, gain_ref, router_ref, gate_ref, up_ref, sums, own_ref):
@@ -334,7 +276,6 @@
     )(*late, gain, router, gate, up, *found, down, mask)
 
 
-LINE_HEADS = 24
 GROUP = 4
 CHUNK = 128
 
@@ -455,7 +396,7 @@
     rows, span, cols = key_cache.shape
     width = queries.shape[1]
     heads = width // HEAD
-    wide = LINE_HEADS * HEAD
+    wide = heads * 3 // 4 * HEAD
     side = width - wide + dims[0] * 128 + lanes
     outs = [(rows, wide)] + [(rows, side)] * (dims[1] * dims[2])
     return pl.pallas_call(
@@ -482,24 +423,20 @@
 
 
 def pack_line_kernel(plane, *refs):
-    lines, (a_ref, b_ref) = refs[:-2], refs[-2:]
+    lines, out = refs[:-1], refs[-1]
     rows = lines[0].shape[0]
-    half = a_ref.shape[1]
     z = lax.axis_index("dev") // plane
     for kz, source in enumerate(lines):
-        span = pl.ds(pl.multiple_of((z ^ kz) * rows, rows), rows)
-        a_ref[span, :] = source[:, :half]
-        b_ref[span, :] = source[:, half:]
+        out[pl.ds(pl.multiple_of((z ^ kz) * rows, rows), rows), :] = source[...]
 
 
 def pack_line(lines, plane):
     rows, width = lines[0].shape
-    out = jax.ShapeDtypeStruct((len(lines) * rows, width // 2), BF)
     return pl.pallas_call(
         functools.partial(pack_line_kernel, plane),
-        out_shape=(out, out),
+        out_shape=jax.ShapeDtypeStruct((len(lines) * rows, width), BF),
         in_specs=[VM] * len(lines),
-        out_specs=(VM, VM),
+        out_specs=VM,
         compiler_params=pltpu.CompilerParams(vmem_limit_bytes=16 * MIB),
         name="pack_line",
     )(*lines)
@@ -540,32 +477,23 @@
         yield q * rows, pl.multiple_of((q * nz + (z ^ kz)) * rows, rows)
 
 
-def project_kernel(dims, rows, codes, *refs):
+def project_kernel(dims, rows, wide, spots, *refs):
     nz, ny, nx = dims
-    count = len(codes)
-    firsts, seconds = refs[:count], refs[count : 2 * count]
-    rest = refs[2 * count : 2 * count + nz]
-    w_ref, keep_ref, send_ref, held, sems = refs[2 * count + nz :]
+    count = len(spots)
+    arrays = refs[:count]
+    rest, w_ref, keep_ref, send_ref, held, sems = refs[count:]
     sec = lax.axis_index("sec")
     here = lax.axis_index("dev") % (ny * nx)
-    half = firsts[0].shape[1]
-    share = held.shape[1] - 2 * half
     size = nz * rows
     copies = []
 
     def move(source, target):
         copies.append(pltpu.make_async_copy(source, target, sems.at[len(copies)]))
 
-    for i, code in enumerate(codes):
+    for source, (code, column) in zip(arrays, spots):
         span = pl.ds(pl.multiple_of((here ^ code) * size, size), size)
-        move(firsts[i], held.at[span, pl.ds(0, half)])
-        move(seconds[i], held.at[span, pl.ds(half, half)])
-    for kz in range(nz):
-        for source, target in scatter_rows(dims, kz, rows):
-            move(
-                rest[kz].at[pl.ds(source, rows), pl.ds(0, share)],
-                held.at[pl.ds(target, rows), pl.ds(2 * half, share)],
-            )
+        move(source, held.at[span, pl.ds(column, source.shape[1])])
+    move(rest, held.at[:, pl.ds(wide, rest.shape[1])])
     for c in copies:
         c.start()
     for c in copies:
@@ -577,19 +505,21 @@
     send_ref[...] = jnp.where(sec == 0, high, low)
 
 
-def project(firsts, seconds, codes, rest, weight, dims, rows):
+def project(found, rest, weight, dims, rows):
     depth, cols = weight.shape
     tall = dims[0] * dims[1] * dims[2] * rows
     out = jax.ShapeDtypeStruct((tall, cols // 2), F32)
-    arrays = [*firsts, *seconds, *rest]
+    arrays = [*(f[2] for f in found), rest]
+    spots = tuple(f[:2] for f in found)
+    wide = found[0][2].shape[1]
     return pl.pallas_call(
-        functools.partial(project_kernel, dims, rows, codes),
+        functools.partial(project_kernel, dims, rows, wide, spots),
         out_shape=(out, out),
         in_specs=[ANY] * len(arrays) + [VM],
         out_specs=(VM, VM),
         scratch_shapes=[
             pltpu.VMEM((tall, depth), BF),
-            pltpu.SemaphoreType.DMA((2 * len(codes) + tall // rows,)),
+            pltpu.SemaphoreType.DMA((len(arrays),)),
         ],
         compiler_params=pltpu.CompilerParams(vmem_limit_bytes=(4 + tall // 32) * MIB),
         cost_estimate=pl.CostEstimate(
@@ -601,37 +531,31 @@
     )(*arrays, weight)
 
 
-def arrange_kernel(dims, rows, *refs):
+def settle_kernel(dims, rows, *refs):
     nz = dims[0]
-    rest, (residual, mask, sems) = refs[:nz], refs[nz:]
-    share = rest[0].shape[1] - 128 - mask.shape[1]
-    copies = []
+    rest, outs = refs[:nz], refs[nz:]
     for kz in range(nz):
         for source, target in scatter_rows(dims, kz, rows):
-            for start, out in ((share, residual), (share + 128, mask)):
-                copies.append(
-                    pltpu.make_async_copy(
-                        rest[kz].at[pl.ds(source, rows), pl.ds(start, out.shape[1])],
-                        out.at[pl.ds(target, rows)],
-                        sems.at[len(copies)],
-                    )
-                )
-    for c in copies:
-        c.start()
-    for c in copies:
-        c.wait()
-
-
-def arrange(rest, lanes, dims, rows):
+            at = 0
+            for out in outs:
+                cols = out.shape[1]
+                out[pl.ds(target, rows), :] = rest[kz][source : source + rows, at : at + cols]
+                at += cols
+
+
+def settle(rest, lanes, dims, rows):
     tall = dims[0] * dims[1] * dims[2] * rows
+    share = rest[0].shape[1] - 128 - lanes
     return pl.pallas_call(
-        functools.partial(arrange_kernel, dims, rows),
-        out_shape=tuple(jax.ShapeDtypeStruct((tall, w), BF) for w in (128, lanes)),
-        in_specs=[ANY] * len(rest),
-        out_specs=(VM, VM),
-        scratch_shapes=[pltpu.SemaphoreType.DMA((2 * tall // rows,))],
-        compiler_params=pltpu.CompilerParams(vmem_limit_bytes=8 * MIB),
-        name="arrange",
+        functools.partial(settle_kernel, dims, rows),
+        out_shape=tuple(jax.ShapeDtypeStruct((tall, w), BF) for w in (share, 128, lanes)),
+        in_specs=[VM] * len(rest),
+        out_specs=(VM,) * 3,
+        compiler_params=pltpu.CompilerParams(vmem_limit_bytes=(6 + tall // 64) * MIB),
+        cost_estimate=pl.CostEstimate(
+            flops=0, bytes_accessed=3 * MIB, transcendentals=0
+        ),
+        name="settle",
     )(*rest)
 
 
@@ -690,17 +614,11 @@
     rest = pack_plane(blocks, lanes, nz)
     lines, rest = lax.optimization_barrier((lines, rest))
     rest = [rest[0]] + [trade(rest[kz], dims, kz=kz) for kz in range(1, nz)]
-    a, b = pack_line([a_own] + [lines[kz] for kz in range(1, nz)], plane)
-    firsts, seconds = {0: a}, {0: b}
-    for wave in planes(a, b, dims):
-        for (ky, kx), half, array in wave:
-            (firsts, seconds)[half][ky * nx + kx] = array
-    codes = sorted(firsts)
-
-    keep, send = project(
-        [firsts[c] for c in codes], [seconds[c] for c in codes], codes, rest, out_weight, dims, rows
-    )
-    residual, mask = arrange(rest, lanes, dims, rows)
+    block = pack_line([a_own] + [lines[kz] for kz in range(1, nz)], plane)
+    found = over_plane(block, dims)
+
+    rest, residual, mask = settle(rest, lanes, dims, rows)
+    keep, send = project(found, rest, out_weight, dims, rows)
     projected = (keep + swap_sec(send)).astype(BF)
     mixed = (residual[:, :part].astype(F32) + projected.astype(F32)).astype(BF)
 

time: 104 us -> 103 us (level)
  Pallas kernels: 13.7 us -> 12.5 us
    ppermute x28 -> x27, starting transfers between devices: 37.7 us -> 37.3 us  [trade(): return lax.ppermute(value, 'dev', [(d, d ^ code) for d in range(n)])]
    ppermute x28 -> x27, waiting for transfers between devices: 43.1 us -> 43.1 us  [trade(): return lax.ppermute(value, 'dev', [(d, d ^ code) for d in range(n)])]
  transfers between devices with their start and end apart: 36 -> 35, of which waited for: 20 -> 19; matrix products, arithmetic and copies ran while one was open for 0% -> 0% of each run, Pallas kernels for 2% -> 1%
where the time goes in v5:
time: 103 us; the launch traced here: 102 us
  waiting for transfers between devices  47.1 us (46%)
  starting transfers between devices  38.5 us (37%)
  Pallas kernels  12.5 us (12%)
  local copies, waits for them, and re-layouts  2.38 us (2%)
  other arithmetic  1.39 us (1%)
    ppermute x27, waiting for transfers between devices, trade(): return lax.ppermute(value, 'dev', [(d, d ^ code) for d in range(n)])  43.1 us
    ppermute x27, starting transfers between devices, trade(): return lax.ppermute(value, 'dev', [(d, d ^ code) for d in range(n)])  37.3 us
    pallas_call x1, Pallas kernels, attention(): pl.pallas_call(functools.partial(attend_kernel, dims, lanes), out_shape=t...  7.29 us
    ppermute x8, waiting for transfers between devices, swap_sec(): return lax.ppermute(value, 'sec', [(0, 1), (1, 0)])  4.04 us
    pallas_call x1, Pallas kernels, experts(): pl.pallas_call(functools.partial(late_kernel, dims, codes and codes[count...  2.77 us
    unnamed x16, local copies, waits for them, and re-layouts  2.27 us
  transfers between devices with their start and end apart: 35, of which 19 were waited for; matrix products, arithmetic and copies ran while one was open for 0% of the time, Pallas kernels for 1%

profile of v5, /device:TPU:0, one launch (start us, length us, event | category | flops | bytes accessed | tf_op | source)
XLA Modules:
  0.0 102.3 jit_solution(4580920103795978105)
XLA Ops:
  0.0 7.3 %attend.1 = (bf16[16,3072]{1,0:T(8,128)(2,1)}, bf16[16,1664]{1,0:T(8,128)(2,1)}, bf16[16,1664]{1,0:T(8,128)(2,1)}, bf16[16,1664]{1,0:T(8,128)(2,1)}, bf16[16,1664]{1,0:T(8,128)(2,1)}) custom-call(s32[16]{0:T(128)} %refs_0_.1, s32[8,16]{1,0:T(8,128)} %bitcast.7, bf16[16,4096]{1,0:T(8,128)(2,1)} %refs_2_.1, bf16[16,256]{1,0:T(8,128)(2,1)} %refs_3_.1, ...), custom_call_target="tpu_custom_call" | custom-call | flops 402653184 | bytes 12582912 | tf_op jit(solution)/shard_map/attend/pallas_call | solution.py:402
  7.3 2.9 %collective-permute-start.3 = (bf16[16,1664]{1,0:T(8,128)(2,1)}, bf16[16,1664]{1,0:T(8,128)(2,1)S(1)}, u32[]{:S(2)}, u32[]{:S(2)}) collective-permute-start(bf16[16,1664]{1,0:T(8,128)(2,1)} %get-tuple-element.37), channel_id=1, source_target_pairs={{0,1},{1,0},{2,3},{3,2},{4,5},{5,4},{6,7},{7,6},{8,9},{9,8},{10,11... | collective-permute-start | bytes 159752 | tf_op jit(solution)/shard_map/ppermute | solution.py:34
  10.2 1.9 %collective-permute-start = (bf16[16,3072]{1,0:T(8,128)(2,1)}, bf16[16,3072]{1,0:T(8,128)(2,1)S(1)}, u32[]{:S(2)}, u32[]{:S(2)}) collective-permute-start(bf16[16,3072]{1,0:T(8,128)(2,1)} %get-tuple-element.35.refs_0_), channel_id=1, source_target_pairs={{0,4},{1,5},{2,6},{3,7},{4,0},{5,1},{6,2},{7,3},{8,12},{9,13},{10,... | collective-permute-start | bytes 294920 | tf_op jit(solution)/shard_map/ppermute | solution.py:34
  12.1 2.3 %collective-permute-start.1 = (bf16[16,3072]{1,0:T(8,128)(2,1)}, bf16[16,3072]{1,0:T(8,128)(2,1)S(1)}, u32[]{:S(2)}, u32[]{:S(2)}) collective-permute-start(bf16[16,3072]{1,0:T(8,128)(2,1)} %get-tuple-element.35.refs_0_), channel_id=1, source_target_pairs={{0,8},{1,9},{2,10},{3,11},{4,12},{5,13},{6,14},{7,15},{8,0},{9,1},... | collective-permute-start | bytes 294920 | tf_op jit(solution)/shard_map/ppermute | solution.py:34
  14.5 0.1 collective-permute-start.2
  14.6 1.6 %collective-permute-start.4 = (bf16[16,1664]{1,0:T(8,128)(2,1)}, bf16[16,1664]{1,0:T(8,128)(2,1)S(1)}, u32[]{:S(2)}, u32[]{:S(2)}) collective-permute-start(bf16[16,1664]{1,0:T(8,128)(2,1)} %get-tuple-element.38), channel_id=1, source_target_pairs={{0,2},{1,3},{2,0},{3,1},{4,6},{5,7},{6,4},{7,5},{8,10},{9,11},{10,... | collective-permute-start | bytes 159752 | tf_op jit(solution)/shard_map/ppermute | solution.py:34
  16.2 0.5 collective-permute-start.5
  16.7 2.8 %collective-permute-done.4.refs_2_ = bf16[16,1664]{1,0:T(8,128)(2,1)S(1)} collective-permute-done((bf16[16,1664]{1,0:T(8,128)(2,1)}, bf16[16,1664]{1,0:T(8,128)(2,1)S(1)}, u32[]{:S(2)}, u32[]{:S(2)}) %collective-permute-start.4) | collective-permute-done | bytes 53280 | tf_op jit(solution)/shard_map/ppermute | solution.py:34
  19.5 2.0 %collective-permute-done.5.refs_3_ = bf16[16,1664]{1,0:T(8,128)(2,1)S(1)} collective-permute-done((bf16[16,1664]{1,0:T(8,128)(2,1)}, bf16[16,1664]{1,0:T(8,128)(2,1)S(1)}, u32[]{:S(2)}, u32[]{:S(2)}) %collective-permute-start.5) | collective-permute-done | bytes 53280 | tf_op jit(solution)/shard_map/ppermute | solution.py:34
  21.5 0.8 copy-done.7
  22.3 0.1 pack_plane.1
  22.3 0.1 collective-permute-done.1.refs_2_
  22.5 0.9 copy-done.5
  23.4 0.8 collective-permute-start.9
  24.3 1.3 %collective-permute-start.10 = (bf16[64,3072]{1,0:T(8,128)(2,1)S(1)}, bf16[64,3072]{1,0:T(8,128)(2,1)S(1)}, u32[]{:S(2)}, u32[]{:S(2)}) collective-permute-start(bf16[64,3072]{1,0:T(8,128)(2,1)S(1)} %pack_line.1.refs_0_), channel_id=1, source_target_pairs={{0,2},{1,3},{2,0},{3,1},{4,6},{5,7},{6,4},{7,5},{8,10},{9,11},{10,... | collective-permute-start | bytes 1179656 | tf_op jit(solution)/shard_map/ppermute | solution.py:34
  25.6 1.7 %collective-permute-start.6 = (bf16[64,1280]{1,0:T(8,128)(2,1)S(1)}, bf16[64,1280]{1,0:T(8,128)(2,1)S(1)}, u32[]{:S(2)}, u32[]{:S(2)}) collective-permute-start(bf16[64,1280]{1,0:T(8,128)(2,1)S(1)} %get-tuple-element.45), channel_id=1, source_target_pairs={{0,4},{1,5},{2,6},{3,7},{4,0},{5,1},{6,2},{7,3},{8,12},{9,13},{10,... | collective-permute-start | bytes 491528 | tf_op jit(solution)/shard_map/ppermute | solution.py:34
  27.3 1.5 %collective-permute-start.7 = (bf16[64,1280]{1,0:T(8,128)(2,1)S(1)}, bf16[64,1280]{1,0:T(8,128)(2,1)S(1)}, u32[]{:S(2)}, u32[]{:S(2)}) collective-permute-start(bf16[64,1280]{1,0:T(8,128)(2,1)S(1)} %get-tuple-element.46), channel_id=1, source_target_pairs={{0,8},{1,9},{2,10},{3,11},{4,12},{5,13},{6,14},{7,15},{8,0},{9,1},... | collective-permute-start | bytes 491528 | tf_op jit(solution)/shard_map/ppermute | solution.py:34
  28.8 1.2 %collective-permute-start.8 = (bf16[64,1280]{1,0:T(8,128)(2,1)S(1)}, bf16[64,1280]{1,0:T(8,128)(2,1)S(1)}, u32[]{:S(2)}, u32[]{:S(2)}) collective-permute-start(bf16[64,1280]{1,0:T(8,128)(2,1)S(1)} %get-tuple-element.47), channel_id=1, source_target_pairs={{0,12},{1,13},{2,14},{3,15},{4,8},{5,9},{6,10},{7,11},{8,4},{9,5},... | collective-permute-start | bytes 491528 | tf_op jit(solution)/shard_map/ppermute | solution.py:34
  30.0 2.3 %collective-permute-done.9.refs_1_ = bf16[64,3072]{1,0:T(8,128)(2,1)S(1)} collective-permute-done((bf16[64,3072]{1,0:T(8,128)(2,1)S(1)}, bf16[64,3072]{1,0:T(8,128)(2,1)S(1)}, u32[]{:S(2)}, u32[]{:S(2)}) %collective-permute-start.9) | collective-permute-done | bytes 393248 | tf_op jit(solution)/shard_map/ppermute | solution.py:34
  32.3 0.0 copy-start.6
  32.3 1.1 %collective-permute-start.11 = (bf16[64,1024]{1,0:T(8,128)(2,1)S(1)}, bf16[64,1024]{1,0:T(8,128)(2,1)S(1)}, u32[]{:S(2)}, u32[]{:S(2)}) collective-permute-start(bf16[64,1024]{1,0:T(8,128)(2,1)S(1)} %get-tuple-element.70), channel_id=1, source_target_pairs={{0,2},{1,3},{2,0},{3,1},{4,6},{5,7},{6,4},{7,5},{8,10},{9,11},{10,... | collective-permute-start | bytes 393224 | tf_op jit(solution)/shard_map/ppermute | solution.py:34
  33.5 1.5 %collective-permute-start.12 = (bf16[64,1024]{1,0:T(8,128)(2,1)S(1)}, bf16[64,1024]{1,0:T(8,128)(2,1)S(1)}, u32[]{:S(2)}, u32[]{:S(2)}) collective-permute-start(bf16[64,1024]{1,0:T(8,128)(2,1)S(1)} %get-tuple-element.69), channel_id=1, source_target_pairs={{0,2},{1,3},{2,0},{3,1},{4,6},{5,7},{6,4},{7,5},{8,10},{9,11},{10,... | collective-permute-start | bytes 393224 | tf_op jit(solution)/shard_map/ppermute | solution.py:34
  34.9 1.9 %collective-permute-start.13 = (bf16[64,1024]{1,0:T(8,128)(2,1)S(1)}, bf16[64,1024]{1,0:T(8,128)(2,1)S(1)}, u32[]{:S(2)}, u32[]{:S(2)}) collective-permute-start(bf16[64,1024]{1,0:T(8,128)(2,1)S(1)} %slice.77), channel_id=1, source_target_pairs={{0,1},{1,0},{2,3},{3,2},{4,5},{5,4},{6,7},{7,6},{8,9},{9,8},{10,11... | collective-permute-start | bytes 393224 | tf_op jit(solution)/shard_map/ppermute | solution.py:34
  36.9 3.9 %collective-permute-done.7.refs_2_ = bf16[64,1280]{1,0:T(8,128)(2,1)S(1)} collective-permute-done((bf16[64,1280]{1,0:T(8,128)(2,1)S(1)}, bf16[64,1280]{1,0:T(8,128)(2,1)S(1)}, u32[]{:S(2)}, u32[]{:S(2)}) %collective-permute-start.7) | collective-permute-done | bytes 163872 | tf_op jit(solution)/shard_map/ppermute | solution.py:34
  40.8 0.1 settle.1
  40.9 1.0 %project.1 = (f32[256,128]{1,0:T(8,128)S(1)}, f32[256,128]{1,0:T(8,128)S(1)}) custom-call(bf16[64,3072]{1,0:T(8,128)(2,1)S(1)} %pack_line.1.refs_0_, bf16[64,3072]{1,0:T(8,128)(2,1)S(1)} %collective-permute-done.9.refs_1_, bf16[64,3072]{1,0:T(8,128)(2,1)S(1)} %collective-permute-done.10.refs_2_, bf16[64,1024]{1,0:T(8,128)(2,1)S(1)} %collective-permute-done.11.refs_3_, ...), custom_call_target="tpu_custom_call" | custom-call | flops 536870912 | bytes 4194304 | tf_op jit(solution)/shard_map/project/pallas_call | solution.py:515
  42.0 0.1 collective-permute-start.14
  42.1 1.3 %collective-permute-done.14 = f32[256,128]{1,0:T(8,128)S(1)} collective-permute-done((f32[256,128]{1,0:T(8,128)S(1)}, f32[256,128]{1,0:T(8,128)S(1)}, u32[]{:S(2)}, u32[]{:S(2)}) %collective-permute-start.14) | collective-permute-done | bytes 131104 | tf_op jit(solution)/shard_map/ppermute | solution.py:42
  43.4 2.9 %collective-permute-start.15 = (bf16[256,128]{1,0:T(8,128)(2,1)S(1)}, bf16[256,128]{1,0:T(8,128)(2,1)S(1)}, u32[]{:S(2)}, u32[]{:S(2)}) collective-permute-start(bf16[256,128]{1,0:T(8,128)(2,1)S(1)} %add_convert_fusion.1), channel_id=1, source_target_pairs={{0,4},{1,5},{2,6},{3,7},{4,0},{5,1},{6,2},{7,3},{8,12},{9,13},{10,... | collective-permute-start | bytes 196616 | tf_op jit(solution)/shard_map/ppermute | solution.py:34
  46.3 0.4 collective-permute-start.16
  46.7 2.0 %collective-permute-start.17 = (bf16[256,128]{1,0:T(8,128)(2,1)S(1)}, bf16[256,128]{1,0:T(8,128)(2,1)S(1)}, u32[]{:S(2)}, u32[]{:S(2)}) collective-permute-start(bf16[256,128]{1,0:T(8,128)(2,1)S(1)} %add_convert_fusion.1), channel_id=1, source_target_pairs={{0,12},{1,13},{2,14},{3,15},{4,8},{5,9},{6,10},{7,11},{8,4},{9,5},... | collective-permute-start | bytes 196616 | tf_op jit(solution)/shard_map/ppermute | solution.py:34
  48.7 5.6 %collective-permute-done.16 = bf16[256,128]{1,0:T(8,128)(2,1)S(1)} collective-permute-done((bf16[256,128]{1,0:T(8,128)(2,1)S(1)}, bf16[256,128]{1,0:T(8,128)(2,1)S(1)}, u32[]{:S(2)}, u32[]{:S(2)}) %collective-permute-start.16) | collective-permute-done | bytes 65568 | tf_op jit(solution)/shard_map/ppermute | solution.py:34
  54.3 1.2 %collective-permute-start.23 = (bf16[1024,128]{1,0:T(8,128)(2,1)S(1)}, bf16[1024,128]{1,0:T(8,128)(2,1)S(1)}, u32[]{:S(2)}, u32[]{:S(2)}) collective-permute-start(bf16[1024,128]{1,0:T(8,128)(2,1)S(1)} %pad_maximum_fusion.1.refs_0_), channel_id=1, source_target_pairs={{0,1},{1,0},{2,3},{3,2},{4,5},{5,4},{6,7},{7,6},{8,9},{9,8},{10,11... | collective-permute-start | bytes 786440 | tf_op jit(solution)/shard_map/ppermute | solution.py:34
  55.5 0.6 collective-permute-start.18
  56.1 1.8 %collective-permute-start.20 = (bf16[1024,128]{1,0:T(8,128)(2,1)S(1)}, bf16[1024,128]{1,0:T(8,128)(2,1)S(1)}, u32[]{:S(2)}, u32[]{:S(2)}) collective-permute-start(bf16[1024,128]{1,0:T(8,128)(2,1)S(1)} %pad_maximum_fusion.1.refs_0_), channel_id=1, source_target_pairs={{0,3},{1,2},{2,1},{3,0},{4,7},{5,6},{6,5},{7,4},{8,11},{9,10},{10,... | collective-permute-start | bytes 786440 | tf_op jit(solution)/shard_map/ppermute | solution.py:34
  57.9 5.8 %collective-permute-done.23.refs_2_ = bf16[1024,128]{1,0:T(8,128)(2,1)S(1)} collective-permute-done((bf16[1024,128]{1,0:T(8,128)(2,1)S(1)}, bf16[1024,128]{1,0:T(8,128)(2,1)S(1)}, u32[]{:S(2)}, u32[]{:S(2)}) %collective-permute-start.23) | collective-permute-done | bytes 262176 | tf_op jit(solution)/shard_map/ppermute | solution.py:34
  63.7 3.8 %collective-permute-done.18.refs_0_ = bf16[1024,128]{1,0:T(8,128)(2,1)S(1)} collective-permute-done((bf16[1024,128]{1,0:T(8,128)(2,1)S(1)}, bf16[1024,128]{1,0:T(8,128)(2,1)S(1)}, u32[]{:S(2)}, u32[]{:S(2)}) %collective-permute-start.18) | collective-permute-done | bytes 262176 | tf_op jit(solution)/shard_map/ppermute | solution.py:34
  67.5 0.5 collective-permute-start.21
  68.1 0.0 copy-start.2
  68.1 1.3 %experts_early.1 = (f32[256,768]{1,0:T(8,128)S(1)}, f32[256,16]{1,0:T(8,128)S(1)}, f32[256,128]{1,0:T(8,128)S(1)}, bf16[16,4096]{1,0:T(8,128)(2,1)S(1)}) custom-call(bf16[1024,128]{1,0:T(8,128)(2,1)S(1)} %pad_maximum_fusion.1.refs_0_, bf16[1024,128]{1,0:T(8,128)(2,1)S(1)} %collective-permute-done.22.refs_1_, ...), custom_call_target="tpu_custom_call" | custom-call | flops 797253312 | bytes 3114270 | tf_op jit(solution)/shard_map/experts_early/pallas_call | solution.py:252
  69.4 0.1 collective-permute-done.21.refs_3_
  69.4 0.5 copy-done.2
  69.9 2.8 %experts_late.1 = (bf16[256,1024]{1,0:T(8,128)(2,1)S(1)}, bf16[256,1024]{1,0:T(8,128)(2,1)S(1)}, bf16[256,1024]{1,0:T(8,128)(2,1)S(1)}, bf16[256,1024]{1,0:T(8,128)(2,1)S(1)}, bf16[16,4096]{1,0:T(8,128)(2,1)S(1)}) custom-call(bf16[1024,128]{1,0:T(8,128)(2,1)S(1)} %collective-permute-done.18.refs_0_, bf16[1024,128]{1,0:T(8,128)(2,1)S(1)} %collective-permute-done.19.refs_1_, ...), custom_call_target="tpu_custom_call" | custom-call | flops 1618665856 | bytes 6322913 | tf_op jit(solution)/shard_map/experts_late/pallas_call | solution.py:266
  72.7 0.1 collective-permute-start.26
  72.8 0.5 collective-permute-start.25
  73.3 1.4 %collective-permute-done.26 = bf16[256,1024]{1,0:T(8,128)(2,1)S(1)} collective-permute-done((bf16[256,1024]{1,0:T(8,128)(2,1)S(1)}, bf16[256,1024]{1,0:T(8,128)(2,1)S(1)}, u32[]{:S(2)}, u32[]{:S(2)}) %collective-permute-start.26) | collective-permute-done | bytes 524320 | tf_op jit(solution)/shard_map/ppermute | solution.py:42
  74.7 0.2 add_convert_fusion
  74.9 1.5 %collective-permute-start.27 = (bf16[128,1024]{1,0:T(8,128)(2,1)S(1)}, bf16[128,1024]{1,0:T(8,128)(2,1)S(1)}, u32[]{:S(2)}, u32[]{:S(2)}) collective-permute-start(bf16[128,1024]{1,0:T(8,128)(2,1)S(1)} %get-tuple-element.68), channel_id=1, source_target_pairs={{0,1},{1,0},{2,3},{3,2},{4,5},{5,4},{6,7},{7,6},{8,9},{9,8},{10,11... | collective-permute-start | bytes 786440 | tf_op jit(solution)/shard_map/ppermute | solution.py:34
  76.5 0.2 convert_add_fusion
  76.7 6.7 %collective-permute-done.27 = bf16[128,1024]{1,0:T(8,128)(2,1)S(1)} collective-permute-done((bf16[128,1024]{1,0:T(8,128)(2,1)S(1)}, bf16[128,1024]{1,0:T(8,128)(2,1)S(1)}, u32[]{:S(2)}, u32[]{:S(2)}) %collective-permute-start.27) | collective-permute-done | bytes 262176 | tf_op jit(solution)/shard_map/ppermute | solution.py:34
  83.4 1.2 %collective-permute-done.29 = bf16[128,1024]{1,0:T(8,128)(2,1)S(1)} collective-permute-done((bf16[128,1024]{1,0:T(8,128)(2,1)S(1)}, bf16[128,1024]{1,0:T(8,128)(2,1)S(1)}, u32[]{:S(2)}, u32[]{:S(2)}) %collective-permute-start.29) | collective-permute-done | bytes 262176 | tf_op jit(solution)/shard_map/ppermute | solution.py:34
  84.5 0.2 slice_add_fusion
  84.8 0.6 collective-permute-start.30
  85.4 1.1 %collective-permute-start.28 = (bf16[64,1024]{1,0:T(8,128)(2,1)S(1)}, bf16[64,1024]{1,0:T(8,128)(2,1)S(1)}, u32[]{:S(2)}, u32[]{:S(2)}) collective-permute-start(bf16[64,1024]{1,0:T(8,128)(2,1)S(1)} %slice.114), channel_id=1, source_target_pairs={{0,2},{1,3},{2,0},{3,1},{4,6},{5,7},{6,4},{7,5},{8,10},{9,11},{10,... | collective-permute-start | bytes 393224 | tf_op jit(solution)/shard_map/ppermute | solution.py:34
  86.5 3.3 %collective-permute-done.30 = bf16[64,1024]{1,0:T(8,128)(2,1)S(1)} collective-permute-done((bf16[64,1024]{1,0:T(8,128)(2,1)S(1)}, bf16[64,1024]{1,0:T(8,128)(2,1)S(1)}, u32[]{:S(2)}, u32[]{:S(2)}) %collective-permute-start.30) | collective-permute-done | bytes 131104 | tf_op jit(solution)/shard_map/ppermute | solution.py:34
  89.8 0.6 collective-permute-done.28
  90.5 3.2 %collective-permute-start.31 = (bf16[16,2048]{1,0:T(8,128)(2,1)S(1)}, bf16[16,2048]{1,0:T(8,128)(2,1)S(1)}, u32[]{:S(2)}, u32[]{:S(2)}) collective-permute-start(bf16[16,2048]{1,0:T(8,128)(2,1)S(1)} %get-tuple-element.71), channel_id=1, source_target_pairs={{0,8},{1,9},{2,10},{3,11},{4,12},{5,13},{6,14},{7,15},{8,0},{9,1},... | collective-permute-start | bytes 196616 | tf_op jit(solution)/shard_map/ppermute | solution.py:34
  93.7 1.5 %collective-permute-start.32 = (bf16[16,2048]{1,0:T(8,128)(2,1)S(1)}, bf16[16,2048]{1,0:T(8,128)(2,1)S(1)}, u32[]{:S(2)}, u32[]{:S(2)}) collective-permute-start(bf16[16,2048]{1,0:T(8,128)(2,1)S(1)} %get-tuple-element.73), channel_id=1, source_target_pairs={{0,12},{1,13},{2,14},{3,15},{4,8},{5,9},{6,10},{7,11},{8,4},{9,5},... | collective-permute-start | bytes 196616 | tf_op jit(solution)/shard_map/ppermute | solution.py:34
  95.2 1.5 %collective-permute-done.31 = bf16[16,2048]{1,0:T(8,128)(2,1)S(1)} collective-permute-done((bf16[16,2048]{1,0:T(8,128)(2,1)S(1)}, bf16[16,2048]{1,0:T(8,128)(2,1)S(1)}, u32[]{:S(2)}, u32[]{:S(2)}) %collective-permute-start.31) | collective-permute-done | bytes 65568 | tf_op jit(solution)/shard_map/ppermute | solution.py:34
  96.7 3.1 %collective-permute-done.32 = bf16[16,2048]{1,0:T(8,128)(2,1)S(1)} collective-permute-done((bf16[16,2048]{1,0:T(8,128)(2,1)S(1)}, bf16[16,2048]{1,0:T(8,128)(2,1)S(1)}, u32[]{:S(2)}, u32[]{:S(2)}) %collective-permute-start.32) | collective-permute-done | bytes 65568 | tf_op jit(solution)/shard_map/ppermute | solution.py:34
  99.9 0.3 collective-permute-done.33
  100.2 0.1 collective-permute-start.34
  100.3 1.2 %collective-permute-done.34 = bf16[16,2048]{1,0:T(8,128)(2,1)S(1)} collective-permute-done((bf16[16,2048]{1,0:T(8,128)(2,1)S(1)}, bf16[16,2048]{1,0:T(8,128)(2,1)S(1)}, u32[]{:S(2)}, u32[]{:S(2)}) %collective-permute-start.34) | collective-permute-done | bytes 65568 | tf_op jit(solution)/shard_map/ppermute | solution.py:42
  101.6 0.7 maximum_select_fusion
  (45 shorter events, 0.4 us)
Async XLA Ops:
  0.0 40.9 %copy-start.3 = (bf16[4096,256]{1,0:T(8,128)(2,1)S(1)}, bf16[4096,256]{1,0:T(8,128)(2,1)}, u32[]{:S(2)}) copy-start(bf16[4096,256]{1,0:T(8,128)(2,1)} %refs_7_.5) | copy-start | bytes 6291460
  7.3 8.9 %collective-permute-start.3 = (bf16[16,1664]{1,0:T(8,128)(2,1)}, bf16[16,1664]{1,0:T(8,128)(2,1)S(1)}, u32[]{:S(2)}, u32[]{:S(2)}) collective-permute-start(bf16[16,1664]{1,0:T(8,128)(2,1)} %get-tuple-element.37), channel_id=1, source_target_pairs={{0,1},{1,0},{2,3},{3,2},{4,5},{5,4},{6,7},{7,6},{8,9},{9,8},{10,11... | collective-permute-start | bytes 159752 | tf_op jit(solution)/shard_map/ppermute | solution.py:34
  10.2 12.1 %collective-permute-start = (bf16[16,3072]{1,0:T(8,128)(2,1)}, bf16[16,3072]{1,0:T(8,128)(2,1)S(1)}, u32[]{:S(2)}, u32[]{:S(2)}) collective-permute-start(bf16[16,3072]{1,0:T(8,128)(2,1)} %get-tuple-element.35.refs_0_), channel_id=1, source_target_pairs={{0,4},{1,5},{2,6},{3,7},{4,0},{5,1},{6,2},{7,3},{8,12},{9,13},{10,... | collective-permute-start | bytes 294920 | tf_op jit(solution)/shard_map/ppermute | solution.py:34
  12.1 10.3 %collective-permute-start.1 = (bf16[16,3072]{1,0:T(8,128)(2,1)}, bf16[16,3072]{1,0:T(8,128)(2,1)S(1)}, u32[]{:S(2)}, u32[]{:S(2)}) collective-permute-start(bf16[16,3072]{1,0:T(8,128)(2,1)} %get-tuple-element.35.refs_0_), channel_id=1, source_target_pairs={{0,8},{1,9},{2,10},{3,11},{4,12},{5,13},{6,14},{7,15},{8,0},{9,1},... | collective-permute-start | bytes 294920 | tf_op jit(solution)/shard_map/ppermute | solution.py:34
  14.5 8.0 %collective-permute-start.2 = (bf16[16,3072]{1,0:T(8,128)(2,1)}, bf16[16,3072]{1,0:T(8,128)(2,1)S(1)}, u32[]{:S(2)}, u32[]{:S(2)}) collective-permute-start(bf16[16,3072]{1,0:T(8,128)(2,1)} %get-tuple-element.35.refs_0_), channel_id=1, source_target_pairs={{0,12},{1,13},{2,14},{3,15},{4,8},{5,9},{6,10},{7,11},{8,4},{9,5},... | collective-permute-start | bytes 294920 | tf_op jit(solution)/shard_map/ppermute | solution.py:34
  14.6 4.9 %collective-permute-start.4 = (bf16[16,1664]{1,0:T(8,128)(2,1)}, bf16[16,1664]{1,0:T(8,128)(2,1)S(1)}, u32[]{:S(2)}, u32[]{:S(2)}) collective-permute-start(bf16[16,1664]{1,0:T(8,128)(2,1)} %get-tuple-element.38), channel_id=1, source_target_pairs={{0,2},{1,3},{2,0},{3,1},{4,6},{5,7},{6,4},{7,5},{8,10},{9,11},{10,... | collective-permute-start | bytes 159752 | tf_op jit(solution)/shard_map/ppermute | solution.py:34
  16.2 5.2 %collective-permute-start.5 = (bf16[16,1664]{1,0:T(8,128)(2,1)}, bf16[16,1664]{1,0:T(8,128)(2,1)S(1)}, u32[]{:S(2)}, u32[]{:S(2)}) collective-permute-start(bf16[16,1664]{1,0:T(8,128)(2,1)} %get-tuple-element.39), channel_id=1, source_target_pairs={{0,3},{1,2},{2,1},{3,0},{4,7},{5,6},{6,5},{7,4},{8,11},{9,10},{10,... | collective-permute-start | bytes 159752 | tf_op jit(solution)/shard_map/ppermute | solution.py:34
  21.5 0.8 copy-start.7
  22.5 0.9 copy-start.5
  23.4 8.9 %collective-permute-start.9 = (bf16[64,3072]{1,0:T(8,128)(2,1)S(1)}, bf16[64,3072]{1,0:T(8,128)(2,1)S(1)}, u32[]{:S(2)}, u32[]{:S(2)}) collective-permute-start(bf16[64,3072]{1,0:T(8,128)(2,1)S(1)} %pack_line.1.refs_0_), channel_id=1, source_target_pairs={{0,1},{1,0},{2,3},{3,2},{4,5},{5,4},{6,7},{7,6},{8,9},{9,8},{10,11... | collective-permute-start | bytes 1179656 | tf_op jit(solution)/shard_map/ppermute | solution.py:34
  24.3 9.2 %collective-permute-start.10 = (bf16[64,3072]{1,0:T(8,128)(2,1)S(1)}, bf16[64,3072]{1,0:T(8,128)(2,1)S(1)}, u32[]{:S(2)}, u32[]{:S(2)}) collective-permute-start(bf16[64,3072]{1,0:T(8,128)(2,1)S(1)} %pack_line.1.refs_0_), channel_id=1, source_target_pairs={{0,2},{1,3},{2,0},{3,1},{4,6},{5,7},{6,4},{7,5},{8,10},{9,11},{10,... | collective-permute-start | bytes 1179656 | tf_op jit(solution)/shard_map/ppermute | solution.py:34
  25.6 9.3 %collective-permute-start.6 = (bf16[64,1280]{1,0:T(8,128)(2,1)S(1)}, bf16[64,1280]{1,0:T(8,128)(2,1)S(1)}, u32[]{:S(2)}, u32[]{:S(2)}) collective-permute-start(bf16[64,1280]{1,0:T(8,128)(2,1)S(1)} %get-tuple-element.45), channel_id=1, source_target_pairs={{0,4},{1,5},{2,6},{3,7},{4,0},{5,1},{6,2},{7,3},{8,12},{9,13},{10,... | collective-permute-start | bytes 491528 | tf_op jit(solution)/shard_map/ppermute | solution.py:34
  27.3 13.5 %collective-permute-start.7 = (bf16[64,1280]{1,0:T(8,128)(2,1)S(1)}, bf16[64,1280]{1,0:T(8,128)(2,1)S(1)}, u32[]{:S(2)}, u32[]{:S(2)}) collective-permute-start(bf16[64,1280]{1,0:T(8,128)(2,1)S(1)} %get-tuple-element.46), channel_id=1, source_target_pairs={{0,8},{1,9},{2,10},{3,11},{4,12},{5,13},{6,14},{7,15},{8,0},{9,1},... | collective-permute-start | bytes 491528 | tf_op jit(solution)/shard_map/ppermute | solution.py:34
  28.8 12.0 %collective-permute-start.8 = (bf16[64,1280]{1,0:T(8,128)(2,1)S(1)}, bf16[64,1280]{1,0:T(8,128)(2,1)S(1)}, u32[]{:S(2)}, u32[]{:S(2)}) collective-permute-start(bf16[64,1280]{1,0:T(8,128)(2,1)S(1)} %get-tuple-element.47), channel_id=1, source_target_pairs={{0,12},{1,13},{2,14},{3,15},{4,8},{5,9},{6,10},{7,11},{8,4},{9,5},... | collective-permute-start | bytes 491528 | tf_op jit(solution)/shard_map/ppermute | solution.py:34
  32.3 35.7 %copy-start.1 = (bf16[1,4096,384]{2,1,0:T(8,128)(2,1)S(1)}, bf16[1,4096,384]{2,1,0:T(8,128)(2,1)}, u32[]{:S(2)}) copy-start(bf16[1,4096,384]{2,1,0:T(8,128)(2,1)} %refs_7_.7) | copy-start | bytes 9437188
  32.3 35.7 %copy-start = (bf16[1,4096,384]{2,1,0:T(8,128)(2,1)S(1)}, bf16[1,4096,384]{2,1,0:T(8,128)(2,1)}, u32[]{:S(2)}) copy-start(bf16[1,4096,384]{2,1,0:T(8,128)(2,1)} %refs_6_.5) | copy-start | bytes 9437188
  32.3 35.7 %copy-start.4 = (bf16[4096,16]{0,1:T(8,128)(2,1)S(1)}, bf16[4096,16]{0,1:T(8,128)(2,1)}, u32[]{:S(2)}) copy-start(bf16[4096,16]{0,1:T(8,128)(2,1)} %param.23) | copy-start | bytes 393220
  32.3 35.7 %copy-start.6 = (f32[4096]{0:T(1024)S(1)}, f32[4096]{0:T(1024)}, u32[]{:S(2)}) copy-start(f32[4096]{0:T(1024)} %param.22) | copy-start | bytes 49156
  32.3 8.6 %collective-permute-start.11 = (bf16[64,1024]{1,0:T(8,128)(2,1)S(1)}, bf16[64,1024]{1,0:T(8,128)(2,1)S(1)}, u32[]{:S(2)}, u32[]{:S(2)}) collective-permute-start(bf16[64,1024]{1,0:T(8,128)(2,1)S(1)} %get-tuple-element.70), channel_id=1, source_target_pairs={{0,2},{1,3},{2,0},{3,1},{4,6},{5,7},{6,4},{7,5},{8,10},{9,11},{10,... | collective-permute-start | bytes 393224 | tf_op jit(solution)/shard_map/ppermute | solution.py:34
  33.5 7.4 %collective-permute-start.12 = (bf16[64,1024]{1,0:T(8,128)(2,1)S(1)}, bf16[64,1024]{1,0:T(8,128)(2,1)S(1)}, u32[]{:S(2)}, u32[]{:S(2)}) collective-permute-start(bf16[64,1024]{1,0:T(8,128)(2,1)S(1)} %get-tuple-element.69), channel_id=1, source_target_pairs={{0,2},{1,3},{2,0},{3,1},{4,6},{5,7},{6,4},{7,5},{8,10},{9,11},{10,... | collective-permute-start | bytes 393224 | tf_op jit(solution)/shard_map/ppermute | solution.py:34
  34.9 6.0 %collective-permute-start.13 = (bf16[64,1024]{1,0:T(8,128)(2,1)S(1)}, bf16[64,1024]{1,0:T(8,128)(2,1)S(1)}, u32[]{:S(2)}, u32[]{:S(2)}) collective-permute-start(bf16[64,1024]{1,0:T(8,128)(2,1)S(1)} %slice.77), channel_id=1, source_target_pairs={{0,1},{1,0},{2,3},{3,2},{4,5},{5,4},{6,7},{7,6},{8,9},{9,8},{10,11... | collective-permute-start | bytes 393224 | tf_op jit(solution)/shard_map/ppermute | solution.py:34
  42.0 1.4 %collective-permute-start.14 = (f32[256,128]{1,0:T(8,128)S(1)}, f32[256,128]{1,0:T(8,128)S(1)}, u32[]{:S(2)}, u32[]{:S(2)}) collective-permute-start(f32[256,128]{1,0:T(8,128)S(1)} %get-tuple-element.54), channel_id=1, source_target_pairs={{0,16},{16,0},{1,17},{17,1},{2,18},{18,2},{3,19},{19,3},{4,20},{20... | collective-permute-start | bytes 393224 | tf_op jit(solution)/shard_map/ppermute | solution.py:42
  43.4 5.3 %collective-permute-start.15 = (bf16[256,128]{1,0:T(8,128)(2,1)S(1)}, bf16[256,128]{1,0:T(8,128)(2,1)S(1)}, u32[]{:S(2)}, u32[]{:S(2)}) collective-permute-start(bf16[256,128]{1,0:T(8,128)(2,1)S(1)} %add_convert_fusion.1), channel_id=1, source_target_pairs={{0,4},{1,5},{2,6},{3,7},{4,0},{5,1},{6,2},{7,3},{8,12},{9,13},{10,... | collective-permute-start | bytes 196616 | tf_op jit(solution)/shard_map/ppermute | solution.py:34
  46.3 8.0 %collective-permute-start.16 = (bf16[256,128]{1,0:T(8,128)(2,1)S(1)}, bf16[256,128]{1,0:T(8,128)(2,1)S(1)}, u32[]{:S(2)}, u32[]{:S(2)}) collective-permute-start(bf16[256,128]{1,0:T(8,128)(2,1)S(1)} %add_convert_fusion.1), channel_id=1, source_target_pairs={{0,8},{1,9},{2,10},{3,11},{4,12},{5,13},{6,14},{7,15},{8,0},{9,1},... | collective-permute-start | bytes 196616 | tf_op jit(solution)/shard_map/ppermute | solution.py:34
  46.7 7.6 %collective-permute-start.17 = (bf16[256,128]{1,0:T(8,128)(2,1)S(1)}, bf16[256,128]{1,0:T(8,128)(2,1)S(1)}, u32[]{:S(2)}, u32[]{:S(2)}) collective-permute-start(bf16[256,128]{1,0:T(8,128)(2,1)S(1)} %add_convert_fusion.1), channel_id=1, source_target_pairs={{0,12},{1,13},{2,14},{3,15},{4,8},{5,9},{6,10},{7,11},{8,4},{9,5},... | collective-permute-start | bytes 196616 | tf_op jit(solution)/shard_map/ppermute | solution.py:34
  54.3 9.3 %collective-permute-start.23 = (bf16[1024,128]{1,0:T(8,128)(2,1)S(1)}, bf16[1024,128]{1,0:T(8,128)(2,1)S(1)}, u32[]{:S(2)}, u32[]{:S(2)}) collective-permute-start(bf16[1024,128]{1,0:T(8,128)(2,1)S(1)} %pad_maximum_fusion.1.refs_0_), channel_id=1, source_target_pairs={{0,1},{1,0},{2,3},{3,2},{4,5},{5,4},{6,7},{7,6},{8,9},{9,8},{10,11... | collective-permute-start | bytes 786440 | tf_op jit(solution)/shard_map/ppermute | solution.py:34
  55.5 12.0 %collective-permute-start.18 = (bf16[1024,128]{1,0:T(8,128)(2,1)S(1)}, bf16[1024,128]{1,0:T(8,128)(2,1)S(1)}, u32[]{:S(2)}, u32[]{:S(2)}) collective-permute-start(bf16[1024,128]{1,0:T(8,128)(2,1)S(1)} %pad_maximum_fusion.1.refs_0_), channel_id=1, source_target_pairs={{0,2},{1,3},{2,0},{3,1},{4,6},{5,7},{6,4},{7,5},{8,10},{9,11},{10,... | collective-permute-start | bytes 786440 | tf_op jit(solution)/shard_map/ppermute | solution.py:34
  56.1 11.4 %collective-permute-start.20 = (bf16[1024,128]{1,0:T(8,128)(2,1)S(1)}, bf16[1024,128]{1,0:T(8,128)(2,1)S(1)}, u32[]{:S(2)}, u32[]{:S(2)}) collective-permute-start(bf16[1024,128]{1,0:T(8,128)(2,1)S(1)} %pad_maximum_fusion.1.refs_0_), channel_id=1, source_target_pairs={{0,3},{1,2},{2,1},{3,0},{4,7},{5,6},{6,5},{7,4},{8,11},{9,10},{10,... | collective-permute-start | bytes 786440 | tf_op jit(solution)/shard_map/ppermute | solution.py:34
  57.9 10.1 %collective-permute-start.22 = (bf16[1024,128]{1,0:T(8,128)(2,1)S(1)}, bf16[1024,128]{1,0:T(8,128)(2,1)S(1)}, u32[]{:S(2)}, u32[]{:S(2)}) collective-permute-start(bf16[1024,128]{1,0:T(8,128)(2,1)S(1)} %pad_maximum_fusion.1.refs_0_), channel_id=1, source_target_pairs={{0,16},{16,0},{1,17},{17,1},{2,18},{18,2},{3,19},{19,3},{4,20},{20... | collective-permute-start | bytes 786440 | tf_op jit(solution)/shard_map/ppermute | solution.py:42
  63.7 4.4 %collective-permute-start.24 = (bf16[1024,128]{1,0:T(8,128)(2,1)S(1)}, bf16[1024,128]{1,0:T(8,128)(2,1)S(1)}, u32[]{:S(2)}, u32[]{:S(2)}) collective-permute-start(bf16[1024,128]{1,0:T(8,128)(2,1)S(1)} %collective-permute-done.23.refs_2_), channel_id=1, source_target_pairs={{0,16},{16,0},{1,17},{17,1},{2,18},{18,2},{3,19},{19,3},{4,20},{20... | collective-permute-start | bytes 786440 | tf_op jit(solution)/shard_map/ppermute | solution.py:42
  67.5 1.8 %collective-permute-start.19 = (bf16[1024,128]{1,0:T(8,128)(2,1)S(1)}, bf16[1024,128]{1,0:T(8,128)(2,1)S(1)}, u32[]{:S(2)}, u32[]{:S(2)}) collective-permute-start(bf16[1024,128]{1,0:T(8,128)(2,1)S(1)} %collective-permute-done.18.refs_0_), channel_id=1, source_target_pairs={{0,16},{16,0},{1,17},{17,1},{2,18},{18,2},{3,19},{19,3},{4,20},{20... | collective-permute-start | bytes 786440 | tf_op jit(solution)/shard_map/ppermute | solution.py:42
  67.5 1.9 %collective-permute-start.21 = (bf16[1024,128]{1,0:T(8,128)(2,1)S(1)}, bf16[1024,128]{1,0:T(8,128)(2,1)S(1)}, u32[]{:S(2)}, u32[]{:S(2)}) collective-permute-start(bf16[1024,128]{1,0:T(8,128)(2,1)S(1)} %collective-permute-done.20.refs_2_), channel_id=1, source_target_pairs={{0,16},{16,0},{1,17},{17,1},{2,18},{18,2},{3,19},{19,3},{4,20},{20... | collective-permute-start | bytes 786440 | tf_op jit(solution)/shard_map/ppermute | solution.py:42
  68.1 1.9 %copy-start.2 = (bf16[1,384,4096]{2,1,0:T(8,128)(2,1)S(1)}, bf16[1,384,4096]{2,1,0:T(8,128)(2,1)}, u32[]{:S(2)}) copy-start(bf16[1,384,4096]{2,1,0:T(8,128)(2,1)} %refs_12_.1) | copy-start | bytes 9437188
  72.7 2.0 %collective-permute-start.26 = (bf16[256,1024]{1,0:T(8,128)(2,1)S(1)}, bf16[256,1024]{1,0:T(8,128)(2,1)S(1)}, u32[]{:S(2)}, u32[]{:S(2)}) collective-permute-start(bf16[256,1024]{1,0:T(8,128)(2,1)S(1)} %get-tuple-element.64), channel_id=1, source_target_pairs={{0,16},{16,0},{1,17},{17,1},{2,18},{18,2},{3,19},{19,3},{4,20},{20... | collective-permute-start | bytes 1572872 | tf_op jit(solution)/shard_map/ppermute | solution.py:42
  72.8 3.7 %collective-permute-start.25 = (bf16[256,1024]{1,0:T(8,128)(2,1)S(1)}, bf16[256,1024]{1,0:T(8,128)(2,1)S(1)}, u32[]{:S(2)}, u32[]{:S(2)}) collective-permute-start(bf16[256,1024]{1,0:T(8,128)(2,1)S(1)} %get-tuple-element.62), channel_id=1, source_target_pairs={{0,16},{16,0},{1,17},{17,1},{2,18},{18,2},{3,19},{19,3},{4,20},{20... | collective-permute-start | bytes 1572872 | tf_op jit(solution)/shard_map/ppermute | solution.py:42
  74.9 8.4 %collective-permute-start.27 = (bf16[128,1024]{1,0:T(8,128)(2,1)S(1)}, bf16[128,1024]{1,0:T(8,128)(2,1)S(1)}, u32[]{:S(2)}, u32[]{:S(2)}) collective-permute-start(bf16[128,1024]{1,0:T(8,128)(2,1)S(1)} %get-tuple-element.68), channel_id=1, source_target_pairs={{0,1},{1,0},{2,3},{3,2},{4,5},{5,4},{6,7},{7,6},{8,9},{9,8},{10,11... | collective-permute-start | bytes 786440 | tf_op jit(solution)/shard_map/ppermute | solution.py:34
  76.5 8.1 %collective-permute-start.29 = (bf16[128,1024]{1,0:T(8,128)(2,1)S(1)}, bf16[128,1024]{1,0:T(8,128)(2,1)S(1)}, u32[]{:S(2)}, u32[]{:S(2)}) collective-permute-start(bf16[128,1024]{1,0:T(8,128)(2,1)S(1)} %get-tuple-element.67), channel_id=1, source_target_pairs={{0,2},{1,3},{2,0},{3,1},{4,6},{5,7},{6,4},{7,5},{8,10},{9,11},{10,... | collective-permute-start | bytes 786440 | tf_op jit(solution)/shard_map/ppermute | solution.py:34
  84.8 5.0 %collective-permute-start.30 = (bf16[64,1024]{1,0:T(8,128)(2,1)S(1)}, bf16[64,1024]{1,0:T(8,128)(2,1)S(1)}, u32[]{:S(2)}, u32[]{:S(2)}) collective-permute-start(bf16[64,1024]{1,0:T(8,128)(2,1)S(1)} %slice.113), channel_id=1, source_target_pairs={{0,1},{1,0},{2,3},{3,2},{4,5},{5,4},{6,7},{7,6},{8,9},{9,8},{10,11... | collective-permute-start | bytes 393224 | tf_op jit(solution)/shard_map/ppermute | solution.py:34
  85.4 5.0 %collective-permute-start.28 = (bf16[64,1024]{1,0:T(8,128)(2,1)S(1)}, bf16[64,1024]{1,0:T(8,128)(2,1)S(1)}, u32[]{:S(2)}, u32[]{:S(2)}) collective-permute-start(bf16[64,1024]{1,0:T(8,128)(2,1)S(1)} %slice.114), channel_id=1, source_target_pairs={{0,2},{1,3},{2,0},{3,1},{4,6},{5,7},{6,4},{7,5},{8,10},{9,11},{10,... | collective-permute-start | bytes 393224 | tf_op jit(solution)/shard_map/ppermute | solution.py:34
  90.5 6.2 %collective-permute-start.31 = (bf16[16,2048]{1,0:T(8,128)(2,1)S(1)}, bf16[16,2048]{1,0:T(8,128)(2,1)S(1)}, u32[]{:S(2)}, u32[]{:S(2)}) collective-permute-start(bf16[16,2048]{1,0:T(8,128)(2,1)S(1)} %get-tuple-element.71), channel_id=1, source_target_pairs={{0,8},{1,9},{2,10},{3,11},{4,12},{5,13},{6,14},{7,15},{8,0},{9,1},... | collective-permute-start | bytes 196616 | tf_op jit(solution)/shard_map/ppermute | solution.py:34
  93.7 6.2 %collective-permute-start.32 = (bf16[16,2048]{1,0:T(8,128)(2,1)S(1)}, bf16[16,2048]{1,0:T(8,128)(2,1)S(1)}, u32[]{:S(2)}, u32[]{:S(2)}) collective-permute-start(bf16[16,2048]{1,0:T(8,128)(2,1)S(1)} %get-tuple-element.73), channel_id=1, source_target_pairs={{0,12},{1,13},{2,14},{3,15},{4,8},{5,9},{6,10},{7,11},{8,4},{9,5},... | collective-permute-start | bytes 196616 | tf_op jit(solution)/shard_map/ppermute | solution.py:34
  95.2 5.0 %collective-permute-start.33 = (bf16[16,2048]{1,0:T(8,128)(2,1)S(1)}, bf16[16,2048]{1,0:T(8,128)(2,1)S(1)}, u32[]{:S(2)}, u32[]{:S(2)}) collective-permute-start(bf16[16,2048]{1,0:T(8,128)(2,1)S(1)} %get-tuple-element.72), channel_id=1, source_target_pairs={{0,4},{1,5},{2,6},{3,7},{4,0},{5,1},{6,2},{7,3},{8,12},{9,13},{10,... | collective-permute-start | bytes 196616 | tf_op jit(solution)/shard_map/ppermute | solution.py:34
  100.2 1.3 %collective-permute-start.34 = (bf16[16,2048]{1,0:T(8,128)(2,1)S(1)}, bf16[16,2048]{1,0:T(8,128)(2,1)S(1)}, u32[]{:S(2)}, u32[]{:S(2)}) collective-permute-start(bf16[16,2048]{1,0:T(8,128)(2,1)S(1)} %fusion.6), channel_id=1, source_target_pairs={{0,16},{16,0},{1,17},{17,1},{2,18},{18,2},{3,19},{19,3},{4,20},{20... | collective-permute-start | bytes 196616 | tf_op jit(solution)/shard_map/ppermute | solution.py:42

commit v6 on v5

--- a/solution.py
+++ b/solution.py
@@ -625,9 +625,17 @@
     lines = {kz: trade(mixed, dims, kz=kz) for kz in steps}
     stacked = jnp.concatenate([mixed] + [lines[kz] for kz in range(1, nz)], axis=0)
     pairs = []
+    along_x = {kx: trade(stacked, dims, kx=kx) for kx in range(1, nx)}
+    along_y = {ky: trade(stacked, dims, ky=ky) for ky in range(1, ny)}
+    middle = stacked.shape[0] // 2
     for ky in range(ny):
         for kx in range(nx):
-            got = stacked if ky + kx == 0 else trade(stacked, dims, ky=ky, kx=kx)
+            if ky == 0 or kx == 0:
+                got = along_x[kx] if kx else along_y[ky] if ky else stacked
+            else:
+                top = trade(along_x[kx][:middle], dims, ky=ky)
+                bottom = trade(along_y[ky][middle:], dims, kx=kx)
+                got = jnp.concatenate([top, bottom], axis=0)
             pairs.append((ky * nx + kx, got, swap_sec(got)))
     keep_near, keep_far, send_near, send_far, own_mixed = experts(
         pairs,

time: 103 us -> 102 us (level)
    ppermute x27 -> x28, waiting for transfers between devices: 43.1 us -> 42.2 us  [trade(): return lax.ppermute(value, 'dev', [(d, d ^ code) for d in range(n)])]
    ppermute x27 -> x28, starting transfers between devices: 37.3 us -> 37.5 us  [trade(): return lax.ppermute(value, 'dev', [(d, d ^ code) for d in range(n)])]
    unnamed x16 -> x17, local copies, waits for them, and re-layouts: 2.27 us -> 2.18 us
  transfers between devices with their start and end apart: 35 -> 36, of which waited for: 19 -> 21; matrix products, arithmetic and copies ran while one was open for 0% -> 1% of each run, Pallas kernels for 1% -> 1%
where the time goes in v6:
time: 102 us
  waiting for transfers between devices  46.4 us (45%)
  starting transfers between devices  38.9 us (38%)
  Pallas kernels  12.4 us (12%)
  local copies, waits for them, and re-layouts  2.32 us (2%)
  other arithmetic  1.39 us (1%)
    ppermute x28, waiting for transfers between devices, trade(): return lax.ppermute(value, 'dev', [(d, d ^ code) for d in range(n)])  42.2 us
    ppermute x28, starting transfers between devices, trade(): return lax.ppermute(value, 'dev', [(d, d ^ code) for d in range(n)])  37.5 us
    pallas_call x1, Pallas kernels, attention(): pl.pallas_call(functools.partial(attend_kernel, dims, lanes), out_shape=t...  7.09 us
    ppermute x8, waiting for transfers between devices, swap_sec(): return lax.ppermute(value, 'sec', [(0, 1), (1, 0)])  4.2 us
    pallas_call x1, Pallas kernels, experts(): pl.pallas_call(functools.partial(late_kernel, dims, codes and codes[count...  2.78 us
    unnamed x17, local copies, waits for them, and re-layouts  2.18 us
  transfers between devices with their start and end apart: 36, of which 21 were waited for; matrix products, arithmetic and copies ran while one was open for 1% of the time, Pallas kernels for 1%

profile of v6, /device:TPU:0, one launch (start us, length us, event | category | flops | bytes accessed | tf_op | source)
XLA Modules:
  0.0 101.7 jit_solution(657427817040978938)
XLA Ops:
  0.0 7.1 %attend.1 = (bf16[16,3072]{1,0:T(8,128)(2,1)}, bf16[16,1664]{1,0:T(8,128)(2,1)}, bf16[16,1664]{1,0:T(8,128)(2,1)}, bf16[16,1664]{1,0:T(8,128)(2,1)}, bf16[16,1664]{1,0:T(8,128)(2,1)}) custom-call(s32[16]{0:T(128)} %refs_0_.1, s32[8,16]{1,0:T(8,128)} %bitcast.7, bf16[16,4096]{1,0:T(8,128)(2,1)} %refs_2_.1, bf16[16,256]{1,0:T(8,128)(2,1)} %refs_3_.1, ...), custom_call_target="tpu_custom_call" | custom-call | flops 402653184 | bytes 12582912 | tf_op jit(solution)/shard_map/attend/pallas_call | solution.py:402
  7.1 3.0 %collective-permute-start.3 = (bf16[16,1664]{1,0:T(8,128)(2,1)}, bf16[16,1664]{1,0:T(8,128)(2,1)S(1)}, u32[]{:S(2)}, u32[]{:S(2)}) collective-permute-start(bf16[16,1664]{1,0:T(8,128)(2,1)} %get-tuple-element.37), channel_id=1, source_target_pairs={{0,1},{1,0},{2,3},{3,2},{4,5},{5,4},{6,7},{7,6},{8,9},{9,8},{10,11... | collective-permute-start | bytes 159752 | tf_op jit(solution)/shard_map/ppermute | solution.py:34
  10.1 1.8 %collective-permute-start = (bf16[16,3072]{1,0:T(8,128)(2,1)}, bf16[16,3072]{1,0:T(8,128)(2,1)S(1)}, u32[]{:S(2)}, u32[]{:S(2)}) collective-permute-start(bf16[16,3072]{1,0:T(8,128)(2,1)} %get-tuple-element.35.refs_0_), channel_id=1, source_target_pairs={{0,4},{1,5},{2,6},{3,7},{4,0},{5,1},{6,2},{7,3},{8,12},{9,13},{10,... | collective-permute-start | bytes 294920 | tf_op jit(solution)/shard_map/ppermute | solution.py:34
  11.9 2.5 %collective-permute-start.1 = (bf16[16,3072]{1,0:T(8,128)(2,1)}, bf16[16,3072]{1,0:T(8,128)(2,1)S(1)}, u32[]{:S(2)}, u32[]{:S(2)}) collective-permute-start(bf16[16,3072]{1,0:T(8,128)(2,1)} %get-tuple-element.35.refs_0_), channel_id=1, source_target_pairs={{0,8},{1,9},{2,10},{3,11},{4,12},{5,13},{6,14},{7,15},{8,0},{9,1},... | collective-permute-start | bytes 294920 | tf_op jit(solution)/shard_map/ppermute | solution.py:34
  14.4 0.1 collective-permute-start.2
  14.5 1.6 %collective-permute-start.4 = (bf16[16,1664]{1,0:T(8,128)(2,1)}, bf16[16,1664]{1,0:T(8,128)(2,1)S(1)}, u32[]{:S(2)}, u32[]{:S(2)}) collective-permute-start(bf16[16,1664]{1,0:T(8,128)(2,1)} %get-tuple-element.38), channel_id=1, source_target_pairs={{0,2},{1,3},{2,0},{3,1},{4,6},{5,7},{6,4},{7,5},{8,10},{9,11},{10,... | collective-permute-start | bytes 159752 | tf_op jit(solution)/shard_map/ppermute | solution.py:34
  16.1 0.4 collective-permute-start.5
  16.5 2.9 %collective-permute-done.4.refs_2_ = bf16[16,1664]{1,0:T(8,128)(2,1)S(1)} collective-permute-done((bf16[16,1664]{1,0:T(8,128)(2,1)}, bf16[16,1664]{1,0:T(8,128)(2,1)S(1)}, u32[]{:S(2)}, u32[]{:S(2)}) %collective-permute-start.4) | collective-permute-done | bytes 53280 | tf_op jit(solution)/shard_map/ppermute | solution.py:34
  19.4 1.9 %collective-permute-done.5.refs_3_ = bf16[16,1664]{1,0:T(8,128)(2,1)S(1)} collective-permute-done((bf16[16,1664]{1,0:T(8,128)(2,1)}, bf16[16,1664]{1,0:T(8,128)(2,1)S(1)}, u32[]{:S(2)}, u32[]{:S(2)}) %collective-permute-start.5) | collective-permute-done | bytes 53280 | tf_op jit(solution)/shard_map/ppermute | solution.py:34
  21.3 0.8 copy-done.7
  22.3 0.9 copy-done.5
  23.2 0.7 collective-permute-start.9
  23.9 1.4 %collective-permute-start.10 = (bf16[64,3072]{1,0:T(8,128)(2,1)S(1)}, bf16[64,3072]{1,0:T(8,128)(2,1)S(1)}, u32[]{:S(2)}, u32[]{:S(2)}) collective-permute-start(bf16[64,3072]{1,0:T(8,128)(2,1)S(1)} %pack_line.1.refs_0_), channel_id=1, source_target_pairs={{0,2},{1,3},{2,0},{3,1},{4,6},{5,7},{6,4},{7,5},{8,10},{9,11},{10,... | collective-permute-start | bytes 1179656 | tf_op jit(solution)/shard_map/ppermute | solution.py:34
  25.3 1.6 %collective-permute-start.6 = (bf16[64,1280]{1,0:T(8,128)(2,1)S(1)}, bf16[64,1280]{1,0:T(8,128)(2,1)S(1)}, u32[]{:S(2)}, u32[]{:S(2)}) collective-permute-start(bf16[64,1280]{1,0:T(8,128)(2,1)S(1)} %get-tuple-element.45), channel_id=1, source_target_pairs={{0,4},{1,5},{2,6},{3,7},{4,0},{5,1},{6,2},{7,3},{8,12},{9,13},{10,... | collective-permute-start | bytes 491528 | tf_op jit(solution)/shard_map/ppermute | solution.py:34
  26.9 1.7 %collective-permute-start.7 = (bf16[64,1280]{1,0:T(8,128)(2,1)S(1)}, bf16[64,1280]{1,0:T(8,128)(2,1)S(1)}, u32[]{:S(2)}, u32[]{:S(2)}) collective-permute-start(bf16[64,1280]{1,0:T(8,128)(2,1)S(1)} %get-tuple-element.46), channel_id=1, source_target_pairs={{0,8},{1,9},{2,10},{3,11},{4,12},{5,13},{6,14},{7,15},{8,0},{9,1},... | collective-permute-start | bytes 491528 | tf_op jit(solution)/shard_map/ppermute | solution.py:34
  28.6 1.1 %collective-permute-start.8 = (bf16[64,1280]{1,0:T(8,128)(2,1)S(1)}, bf16[64,1280]{1,0:T(8,128)(2,1)S(1)}, u32[]{:S(2)}, u32[]{:S(2)}) collective-permute-start(bf16[64,1280]{1,0:T(8,128)(2,1)S(1)} %get-tuple-element.47), channel_id=1, source_target_pairs={{0,12},{1,13},{2,14},{3,15},{4,8},{5,9},{6,10},{7,11},{8,4},{9,5},... | collective-permute-start | bytes 491528 | tf_op jit(solution)/shard_map/ppermute | solution.py:34
  29.7 2.4 %collective-permute-done.9.refs_1_ = bf16[64,3072]{1,0:T(8,128)(2,1)S(1)} collective-permute-done((bf16[64,3072]{1,0:T(8,128)(2,1)S(1)}, bf16[64,3072]{1,0:T(8,128)(2,1)S(1)}, u32[]{:S(2)}, u32[]{:S(2)}) %collective-permute-start.9) | collective-permute-done | bytes 393248 | tf_op jit(solution)/shard_map/ppermute | solution.py:34
  32.1 1.2 %collective-permute-start.11 = (bf16[64,1024]{1,0:T(8,128)(2,1)S(1)}, bf16[64,1024]{1,0:T(8,128)(2,1)S(1)}, u32[]{:S(2)}, u32[]{:S(2)}) collective-permute-start(bf16[64,1024]{1,0:T(8,128)(2,1)S(1)} %get-tuple-element.70), channel_id=1, source_target_pairs={{0,2},{1,3},{2,0},{3,1},{4,6},{5,7},{6,4},{7,5},{8,10},{9,11},{10,... | collective-permute-start | bytes 393224 | tf_op jit(solution)/shard_map/ppermute | solution.py:34
  33.3 1.3 %collective-permute-start.12 = (bf16[64,1024]{1,0:T(8,128)(2,1)S(1)}, bf16[64,1024]{1,0:T(8,128)(2,1)S(1)}, u32[]{:S(2)}, u32[]{:S(2)}) collective-permute-start(bf16[64,1024]{1,0:T(8,128)(2,1)S(1)} %get-tuple-element.69), channel_id=1, source_target_pairs={{0,2},{1,3},{2,0},{3,1},{4,6},{5,7},{6,4},{7,5},{8,10},{9,11},{10,... | collective-permute-start | bytes 393224 | tf_op jit(solution)/shard_map/ppermute | solution.py:34
  34.6 2.4 %collective-permute-start.13 = (bf16[64,1024]{1,0:T(8,128)(2,1)S(1)}, bf16[64,1024]{1,0:T(8,128)(2,1)S(1)}, u32[]{:S(2)}, u32[]{:S(2)}) collective-permute-start(bf16[64,1024]{1,0:T(8,128)(2,1)S(1)} %slice.85), channel_id=1, source_target_pairs={{0,1},{1,0},{2,3},{3,2},{4,5},{5,4},{6,7},{7,6},{8,9},{9,8},{10,11... | collective-permute-start | bytes 393224 | tf_op jit(solution)/shard_map/ppermute | solution.py:34
  37.0 3.5 %collective-permute-done.7.refs_2_ = bf16[64,1280]{1,0:T(8,128)(2,1)S(1)} collective-permute-done((bf16[64,1280]{1,0:T(8,128)(2,1)S(1)}, bf16[64,1280]{1,0:T(8,128)(2,1)S(1)}, u32[]{:S(2)}, u32[]{:S(2)}) %collective-permute-start.7) | collective-permute-done | bytes 163872 | tf_op jit(solution)/shard_map/ppermute | solution.py:34
  40.5 0.1 settle.1
  40.6 1.0 %project.1 = (f32[256,128]{1,0:T(8,128)S(1)}, f32[256,128]{1,0:T(8,128)S(1)}) custom-call(bf16[64,3072]{1,0:T(8,128)(2,1)S(1)} %pack_line.1.refs_0_, bf16[64,3072]{1,0:T(8,128)(2,1)S(1)} %collective-permute-done.9.refs_1_, bf16[64,3072]{1,0:T(8,128)(2,1)S(1)} %collective-permute-done.10.refs_2_, bf16[64,1024]{1,0:T(8,128)(2,1)S(1)} %collective-permute-done.11.refs_3_, ...), custom_call_target="tpu_custom_call" | custom-call | flops 536870912 | bytes 4194304 | tf_op jit(solution)/shard_map/project/pallas_call | solution.py:515
  41.7 0.1 collective-permute-start.14
  41.8 1.3 %collective-permute-done.14 = f32[256,128]{1,0:T(8,128)S(1)} collective-permute-done((f32[256,128]{1,0:T(8,128)S(1)}, f32[256,128]{1,0:T(8,128)S(1)}, u32[]{:S(2)}, u32[]{:S(2)}) %collective-permute-start.14) | collective-permute-done | bytes 131104 | tf_op jit(solution)/shard_map/ppermute | solution.py:42
  43.1 2.9 %collective-permute-start.15 = (bf16[256,128]{1,0:T(8,128)(2,1)S(1)}, bf16[256,128]{1,0:T(8,128)(2,1)S(1)}, u32[]{:S(2)}, u32[]{:S(2)}) collective-permute-start(bf16[256,128]{1,0:T(8,128)(2,1)S(1)} %add_convert_fusion.1), channel_id=1, source_target_pairs={{0,4},{1,5},{2,6},{3,7},{4,0},{5,1},{6,2},{7,3},{8,12},{9,13},{10,... | collective-permute-start | bytes 196616 | tf_op jit(solution)/shard_map/ppermute | solution.py:34
  46.0 0.4 collective-permute-start.16
  46.4 2.0 %collective-permute-start.17 = (bf16[256,128]{1,0:T(8,128)(2,1)S(1)}, bf16[256,128]{1,0:T(8,128)(2,1)S(1)}, u32[]{:S(2)}, u32[]{:S(2)}) collective-permute-start(bf16[256,128]{1,0:T(8,128)(2,1)S(1)} %add_convert_fusion.1), channel_id=1, source_target_pairs={{0,12},{1,13},{2,14},{3,15},{4,8},{5,9},{6,10},{7,11},{8,4},{9,5},... | collective-permute-start | bytes 196616 | tf_op jit(solution)/shard_map/ppermute | solution.py:34
  48.4 5.6 %collective-permute-done.16 = bf16[256,128]{1,0:T(8,128)(2,1)S(1)} collective-permute-done((bf16[256,128]{1,0:T(8,128)(2,1)S(1)}, bf16[256,128]{1,0:T(8,128)(2,1)S(1)}, u32[]{:S(2)}, u32[]{:S(2)}) %collective-permute-start.16) | collective-permute-done | bytes 65568 | tf_op jit(solution)/shard_map/ppermute | solution.py:34
  54.0 1.4 %collective-permute-start.20 = (bf16[1024,128]{1,0:T(8,128)(2,1)S(1)}, bf16[1024,128]{1,0:T(8,128)(2,1)S(1)}, u32[]{:S(2)}, u32[]{:S(2)}) collective-permute-start(bf16[1024,128]{1,0:T(8,128)(2,1)S(1)} %pad_maximum_fusion.1.refs_0_), channel_id=1, source_target_pairs={{0,1},{1,0},{2,3},{3,2},{4,5},{5,4},{6,7},{7,6},{8,9},{9,8},{10,11... | collective-permute-start | bytes 786440 | tf_op jit(solution)/shard_map/ppermute | solution.py:34
  55.4 0.5 collective-permute-start.18
  55.9 5.4 %collective-permute-done.20.refs_2_ = bf16[1024,128]{1,0:T(8,128)(2,1)S(1)} collective-permute-done((bf16[1024,128]{1,0:T(8,128)(2,1)S(1)}, bf16[1024,128]{1,0:T(8,128)(2,1)S(1)}, u32[]{:S(2)}, u32[]{:S(2)}) %collective-permute-start.20) | collective-permute-done | bytes 262176 | tf_op jit(solution)/shard_map/ppermute | solution.py:34
  61.3 0.8 collective-permute-start.21
  62.0 0.7 collective-permute-done.18.refs_0_
  62.8 0.3 collective-permute-start.22
  63.1 0.5 collective-permute-start.25
  63.6 2.7 %collective-permute-done.21 = bf16[512,128]{1,0:T(8,128)(2,1)S(1)} collective-permute-done((bf16[512,128]{1,0:T(8,128)(2,1)S(1)}, bf16[512,128]{1,0:T(8,128)(2,1)S(1)}, u32[]{:S(2)}, u32[]{:S(2)}) %collective-permute-start.21) | collective-permute-done | bytes 131104 | tf_op jit(solution)/shard_map/ppermute | solution.py:34
  66.3 1.5 %collective-permute-done.22 = bf16[512,128]{1,0:T(8,128)(2,1)S(1)} collective-permute-done((bf16[512,128]{1,0:T(8,128)(2,1)S(1)}, bf16[512,128]{1,0:T(8,128)(2,1)S(1)}, u32[]{:S(2)}, u32[]{:S(2)}) %collective-permute-start.22) | collective-permute-done | bytes 131104 | tf_op jit(solution)/shard_map/ppermute | solution.py:34
  67.8 0.1 collective-permute-start.23
  68.0 1.3 %experts_early.1 = (f32[256,768]{1,0:T(8,128)S(1)}, f32[256,16]{1,0:T(8,128)S(1)}, f32[256,128]{1,0:T(8,128)S(1)}, bf16[16,4096]{1,0:T(8,128)(2,1)S(1)}) custom-call(bf16[1024,128]{1,0:T(8,128)(2,1)S(1)} %pad_maximum_fusion.1.refs_0_, bf16[1024,128]{1,0:T(8,128)(2,1)S(1)} %collective-permute-done.24.refs_1_, ...), custom_call_target="tpu_custom_call" | custom-call | flops 797253312 | bytes 3114270 | tf_op jit(solution)/shard_map/experts_early/pallas_call | solution.py:252
  69.3 0.2 collective-permute-done.23.refs_3_
  69.4 0.4 copy-done.2
  69.9 2.8 %experts_late.1 = (bf16[256,1024]{1,0:T(8,128)(2,1)S(1)}, bf16[256,1024]{1,0:T(8,128)(2,1)S(1)}, bf16[256,1024]{1,0:T(8,128)(2,1)S(1)}, bf16[256,1024]{1,0:T(8,128)(2,1)S(1)}, bf16[16,4096]{1,0:T(8,128)(2,1)S(1)}) custom-call(bf16[1024,128]{1,0:T(8,128)(2,1)S(1)} %collective-permute-done.18.refs_0_, bf16[1024,128]{1,0:T(8,128)(2,1)S(1)} %collective-permute-done.19.refs_1_, ...), custom_call_target="tpu_custom_call" | custom-call | flops 1618665856 | bytes 6322913 | tf_op jit(solution)/shard_map/experts_late/pallas_call | solution.py:266
  72.7 0.5 collective-permute-start.27
  73.2 0.1 collective-permute-start.26
  73.3 1.5 %collective-permute-done.27 = bf16[256,1024]{1,0:T(8,128)(2,1)S(1)} collective-permute-done((bf16[256,1024]{1,0:T(8,128)(2,1)S(1)}, bf16[256,1024]{1,0:T(8,128)(2,1)S(1)}, u32[]{:S(2)}, u32[]{:S(2)}) %collective-permute-start.27) | collective-permute-done | bytes 524320 | tf_op jit(solution)/shard_map/ppermute | solution.py:42
  74.7 0.2 add_convert_fusion
  75.0 0.3 collective-permute-start.28
  75.3 1.8 %collective-permute-start.30 = (bf16[128,1024]{1,0:T(8,128)(2,1)S(1)}, bf16[128,1024]{1,0:T(8,128)(2,1)S(1)}, u32[]{:S(2)}, u32[]{:S(2)}) collective-permute-start(bf16[128,1024]{1,0:T(8,128)(2,1)S(1)} %get-tuple-element.67), channel_id=1, source_target_pairs={{0,2},{1,3},{2,0},{3,1},{4,6},{5,7},{6,4},{7,5},{8,10},{9,11},{10,... | collective-permute-start | bytes 786440 | tf_op jit(solution)/shard_map/ppermute | solution.py:34
  77.1 0.2 convert_add_fusion
  77.3 6.4 %collective-permute-done.28 = bf16[128,1024]{1,0:T(8,128)(2,1)S(1)} collective-permute-done((bf16[128,1024]{1,0:T(8,128)(2,1)S(1)}, bf16[128,1024]{1,0:T(8,128)(2,1)S(1)}, u32[]{:S(2)}, u32[]{:S(2)}) %collective-permute-start.28) | collective-permute-done | bytes 262176 | tf_op jit(solution)/shard_map/ppermute | solution.py:34
  83.6 0.1 collective-permute-done.30
  83.7 0.2 slice_add_fusion
  83.9 1.7 %collective-permute-start.31 = (bf16[64,1024]{1,0:T(8,128)(2,1)S(1)}, bf16[64,1024]{1,0:T(8,128)(2,1)S(1)}, u32[]{:S(2)}, u32[]{:S(2)}) collective-permute-start(bf16[64,1024]{1,0:T(8,128)(2,1)S(1)} %slice.123), channel_id=1, source_target_pairs={{0,1},{1,0},{2,3},{3,2},{4,5},{5,4},{6,7},{7,6},{8,9},{9,8},{10,11... | collective-permute-start | bytes 393224 | tf_op jit(solution)/shard_map/ppermute | solution.py:34
  85.7 0.7 collective-permute-start.29
  86.4 2.6 %collective-permute-done.31 = bf16[64,1024]{1,0:T(8,128)(2,1)S(1)} collective-permute-done((bf16[64,1024]{1,0:T(8,128)(2,1)S(1)}, bf16[64,1024]{1,0:T(8,128)(2,1)S(1)}, u32[]{:S(2)}, u32[]{:S(2)}) %collective-permute-start.31) | collective-permute-done | bytes 131104 | tf_op jit(solution)/shard_map/ppermute | solution.py:34
  89.0 1.7 %collective-permute-done.29 = bf16[64,1024]{1,0:T(8,128)(2,1)S(1)} collective-permute-done((bf16[64,1024]{1,0:T(8,128)(2,1)S(1)}, bf16[64,1024]{1,0:T(8,128)(2,1)S(1)}, u32[]{:S(2)}, u32[]{:S(2)}) %collective-permute-start.29) | collective-permute-done | bytes 131104 | tf_op jit(solution)/shard_map/ppermute | solution.py:34
  90.8 2.1 %collective-permute-start.32 = (bf16[16,2048]{1,0:T(8,128)(2,1)S(1)}, bf16[16,2048]{1,0:T(8,128)(2,1)S(1)}, u32[]{:S(2)}, u32[]{:S(2)}) collective-permute-start(bf16[16,2048]{1,0:T(8,128)(2,1)S(1)} %get-tuple-element.71), channel_id=1, source_target_pairs={{0,8},{1,9},{2,10},{3,11},{4,12},{5,13},{6,14},{7,15},{8,0},{9,1},... | collective-permute-start | bytes 196616 | tf_op jit(solution)/shard_map/ppermute | solution.py:34
  92.9 2.0 %collective-permute-start.33 = (bf16[16,2048]{1,0:T(8,128)(2,1)S(1)}, bf16[16,2048]{1,0:T(8,128)(2,1)S(1)}, u32[]{:S(2)}, u32[]{:S(2)}) collective-permute-start(bf16[16,2048]{1,0:T(8,128)(2,1)S(1)} %get-tuple-element.73), channel_id=1, source_target_pairs={{0,12},{1,13},{2,14},{3,15},{4,8},{5,9},{6,10},{7,11},{8,4},{9,5},... | collective-permute-start | bytes 196616 | tf_op jit(solution)/shard_map/ppermute | solution.py:34
  94.8 1.8 %collective-permute-done.32 = bf16[16,2048]{1,0:T(8,128)(2,1)S(1)} collective-permute-done((bf16[16,2048]{1,0:T(8,128)(2,1)S(1)}, bf16[16,2048]{1,0:T(8,128)(2,1)S(1)}, u32[]{:S(2)}, u32[]{:S(2)}) %collective-permute-start.32) | collective-permute-done | bytes 65568 | tf_op jit(solution)/shard_map/ppermute | solution.py:34
  96.6 2.4 %collective-permute-done.33 = bf16[16,2048]{1,0:T(8,128)(2,1)S(1)} collective-permute-done((bf16[16,2048]{1,0:T(8,128)(2,1)S(1)}, bf16[16,2048]{1,0:T(8,128)(2,1)S(1)}, u32[]{:S(2)}, u32[]{:S(2)}) %collective-permute-start.33) | collective-permute-done | bytes 65568 | tf_op jit(solution)/shard_map/ppermute | solution.py:34
  99.0 0.6 collective-permute-done.34
  99.8 1.2 %collective-permute-done.35 = bf16[16,2048]{1,0:T(8,128)(2,1)S(1)} collective-permute-done((bf16[16,2048]{1,0:T(8,128)(2,1)S(1)}, bf16[16,2048]{1,0:T(8,128)(2,1)S(1)}, u32[]{:S(2)}, u32[]{:S(2)}) %collective-permute-start.35) | collective-permute-done | bytes 65568 | tf_op jit(solution)/shard_map/ppermute | solution.py:42
  101.0 0.7 maximum_select_fusion
  (51 shorter events, 0.6 us)
Async XLA Ops:
  7.1 33.5 %copy-start.3 = (bf16[4096,256]{1,0:T(8,128)(2,1)S(1)}, bf16[4096,256]{1,0:T(8,128)(2,1)}, u32[]{:S(2)}) copy-start(bf16[4096,256]{1,0:T(8,128)(2,1)} %refs_7_.5) | copy-start | bytes 6291460
  7.1 9.0 %collective-permute-start.3 = (bf16[16,1664]{1,0:T(8,128)(2,1)}, bf16[16,1664]{1,0:T(8,128)(2,1)S(1)}, u32[]{:S(2)}, u32[]{:S(2)}) collective-permute-start(bf16[16,1664]{1,0:T(8,128)(2,1)} %get-tuple-element.37), channel_id=1, source_target_pairs={{0,1},{1,0},{2,3},{3,2},{4,5},{5,4},{6,7},{7,6},{8,9},{9,8},{10,11... | collective-permute-start | bytes 159752 | tf_op jit(solution)/shard_map/ppermute | solution.py:34
  10.1 12.1 %collective-permute-start = (bf16[16,3072]{1,0:T(8,128)(2,1)}, bf16[16,3072]{1,0:T(8,128)(2,1)S(1)}, u32[]{:S(2)}, u32[]{:S(2)}) collective-permute-start(bf16[16,3072]{1,0:T(8,128)(2,1)} %get-tuple-element.35.refs_0_), channel_id=1, source_target_pairs={{0,4},{1,5},{2,6},{3,7},{4,0},{5,1},{6,2},{7,3},{8,12},{9,13},{10,... | collective-permute-start | bytes 294920 | tf_op jit(solution)/shard_map/ppermute | solution.py:34
  11.9 10.4 %collective-permute-start.1 = (bf16[16,3072]{1,0:T(8,128)(2,1)}, bf16[16,3072]{1,0:T(8,128)(2,1)S(1)}, u32[]{:S(2)}, u32[]{:S(2)}) collective-permute-start(bf16[16,3072]{1,0:T(8,128)(2,1)} %get-tuple-element.35.refs_0_), channel_id=1, source_target_pairs={{0,8},{1,9},{2,10},{3,11},{4,12},{5,13},{6,14},{7,15},{8,0},{9,1},... | collective-permute-start | bytes 294920 | tf_op jit(solution)/shard_map/ppermute | solution.py:34
  14.4 7.8 %collective-permute-start.2 = (bf16[16,3072]{1,0:T(8,128)(2,1)}, bf16[16,3072]{1,0:T(8,128)(2,1)S(1)}, u32[]{:S(2)}, u32[]{:S(2)}) collective-permute-start(bf16[16,3072]{1,0:T(8,128)(2,1)} %get-tuple-element.35.refs_0_), channel_id=1, source_target_pairs={{0,12},{1,13},{2,14},{3,15},{4,8},{5,9},{6,10},{7,11},{8,4},{9,5},... | collective-permute-start | bytes 294920 | tf_op jit(solution)/shard_map/ppermute | solution.py:34
  14.5 4.9 %collective-permute-start.4 = (bf16[16,1664]{1,0:T(8,128)(2,1)}, bf16[16,1664]{1,0:T(8,128)(2,1)S(1)}, u32[]{:S(2)}, u32[]{:S(2)}) collective-permute-start(bf16[16,1664]{1,0:T(8,128)(2,1)} %get-tuple-element.38), channel_id=1, source_target_pairs={{0,2},{1,3},{2,0},{3,1},{4,6},{5,7},{6,4},{7,5},{8,10},{9,11},{10,... | collective-permute-start | bytes 159752 | tf_op jit(solution)/shard_map/ppermute | solution.py:34
  16.1 5.2 %collective-permute-start.5 = (bf16[16,1664]{1,0:T(8,128)(2,1)}, bf16[16,1664]{1,0:T(8,128)(2,1)S(1)}, u32[]{:S(2)}, u32[]{:S(2)}) collective-permute-start(bf16[16,1664]{1,0:T(8,128)(2,1)} %get-tuple-element.39), channel_id=1, source_target_pairs={{0,3},{1,2},{2,1},{3,0},{4,7},{5,6},{6,5},{7,4},{8,11},{9,10},{10,... | collective-permute-start | bytes 159752 | tf_op jit(solution)/shard_map/ppermute | solution.py:34
  21.3 0.8 copy-start.7
  22.3 0.9 copy-start.5
  23.2 8.9 %collective-permute-start.9 = (bf16[64,3072]{1,0:T(8,128)(2,1)S(1)}, bf16[64,3072]{1,0:T(8,128)(2,1)S(1)}, u32[]{:S(2)}, u32[]{:S(2)}) collective-permute-start(bf16[64,3072]{1,0:T(8,128)(2,1)S(1)} %pack_line.1.refs_0_), channel_id=1, source_target_pairs={{0,1},{1,0},{2,3},{3,2},{4,5},{5,4},{6,7},{7,6},{8,9},{9,8},{10,11... | collective-permute-start | bytes 1179656 | tf_op jit(solution)/shard_map/ppermute | solution.py:34
  23.9 9.4 %collective-permute-start.10 = (bf16[64,3072]{1,0:T(8,128)(2,1)S(1)}, bf16[64,3072]{1,0:T(8,128)(2,1)S(1)}, u32[]{:S(2)}, u32[]{:S(2)}) collective-permute-start(bf16[64,3072]{1,0:T(8,128)(2,1)S(1)} %pack_line.1.refs_0_), channel_id=1, source_target_pairs={{0,2},{1,3},{2,0},{3,1},{4,6},{5,7},{6,4},{7,5},{8,10},{9,11},{10,... | collective-permute-start | bytes 1179656 | tf_op jit(solution)/shard_map/ppermute | solution.py:34
  25.3 9.3 %collective-permute-start.6 = (bf16[64,1280]{1,0:T(8,128)(2,1)S(1)}, bf16[64,1280]{1,0:T(8,128)(2,1)S(1)}, u32[]{:S(2)}, u32[]{:S(2)}) collective-permute-start(bf16[64,1280]{1,0:T(8,128)(2,1)S(1)} %get-tuple-element.45), channel_id=1, source_target_pairs={{0,4},{1,5},{2,6},{3,7},{4,0},{5,1},{6,2},{7,3},{8,12},{9,13},{10,... | collective-permute-start | bytes 491528 | tf_op jit(solution)/shard_map/ppermute | solution.py:34
  26.9 13.5 %collective-permute-start.7 = (bf16[64,1280]{1,0:T(8,128)(2,1)S(1)}, bf16[64,1280]{1,0:T(8,128)(2,1)S(1)}, u32[]{:S(2)}, u32[]{:S(2)}) collective-permute-start(bf16[64,1280]{1,0:T(8,128)(2,1)S(1)} %get-tuple-element.46), channel_id=1, source_target_pairs={{0,8},{1,9},{2,10},{3,11},{4,12},{5,13},{6,14},{7,15},{8,0},{9,1},... | collective-permute-start | bytes 491528 | tf_op jit(solution)/shard_map/ppermute | solution.py:34
  28.6 11.9 %collective-permute-start.8 = (bf16[64,1280]{1,0:T(8,128)(2,1)S(1)}, bf16[64,1280]{1,0:T(8,128)(2,1)S(1)}, u32[]{:S(2)}, u32[]{:S(2)}) collective-permute-start(bf16[64,1280]{1,0:T(8,128)(2,1)S(1)} %get-tuple-element.47), channel_id=1, source_target_pairs={{0,12},{1,13},{2,14},{3,15},{4,8},{5,9},{6,10},{7,11},{8,4},{9,5},... | collective-permute-start | bytes 491528 | tf_op jit(solution)/shard_map/ppermute | solution.py:34
  32.1 8.5 %collective-permute-start.11 = (bf16[64,1024]{1,0:T(8,128)(2,1)S(1)}, bf16[64,1024]{1,0:T(8,128)(2,1)S(1)}, u32[]{:S(2)}, u32[]{:S(2)}) collective-permute-start(bf16[64,1024]{1,0:T(8,128)(2,1)S(1)} %get-tuple-element.70), channel_id=1, source_target_pairs={{0,2},{1,3},{2,0},{3,1},{4,6},{5,7},{6,4},{7,5},{8,10},{9,11},{10,... | collective-permute-start | bytes 393224 | tf_op jit(solution)/shard_map/ppermute | solution.py:34
  33.3 7.3 %collective-permute-start.12 = (bf16[64,1024]{1,0:T(8,128)(2,1)S(1)}, bf16[64,1024]{1,0:T(8,128)(2,1)S(1)}, u32[]{:S(2)}, u32[]{:S(2)}) collective-permute-start(bf16[64,1024]{1,0:T(8,128)(2,1)S(1)} %get-tuple-element.69), channel_id=1, source_target_pairs={{0,2},{1,3},{2,0},{3,1},{4,6},{5,7},{6,4},{7,5},{8,10},{9,11},{10,... | collective-permute-start | bytes 393224 | tf_op jit(solution)/shard_map/ppermute | solution.py:34
  34.6 6.1 %collective-permute-start.13 = (bf16[64,1024]{1,0:T(8,128)(2,1)S(1)}, bf16[64,1024]{1,0:T(8,128)(2,1)S(1)}, u32[]{:S(2)}, u32[]{:S(2)}) collective-permute-start(bf16[64,1024]{1,0:T(8,128)(2,1)S(1)} %slice.85), channel_id=1, source_target_pairs={{0,1},{1,0},{2,3},{3,2},{4,5},{5,4},{6,7},{7,6},{8,9},{9,8},{10,11... | collective-permute-start | bytes 393224 | tf_op jit(solution)/shard_map/ppermute | solution.py:34
  40.5 27.5 %copy-start.1 = (bf16[1,4096,384]{2,1,0:T(8,128)(2,1)S(1)}, bf16[1,4096,384]{2,1,0:T(8,128)(2,1)}, u32[]{:S(2)}) copy-start(bf16[1,4096,384]{2,1,0:T(8,128)(2,1)} %refs_7_.7) | copy-start | bytes 9437188
  40.6 27.4 %copy-start = (bf16[1,4096,384]{2,1,0:T(8,128)(2,1)S(1)}, bf16[1,4096,384]{2,1,0:T(8,128)(2,1)}, u32[]{:S(2)}) copy-start(bf16[1,4096,384]{2,1,0:T(8,128)(2,1)} %refs_6_.5) | copy-start | bytes 9437188
  40.6 27.4 %copy-start.4 = (bf16[4096,16]{0,1:T(8,128)(2,1)S(1)}, bf16[4096,16]{0,1:T(8,128)(2,1)}, u32[]{:S(2)}) copy-start(bf16[4096,16]{0,1:T(8,128)(2,1)} %param.23) | copy-start | bytes 393220
  40.6 27.4 %copy-start.6 = (f32[4096]{0:T(1024)S(1)}, f32[4096]{0:T(1024)}, u32[]{:S(2)}) copy-start(f32[4096]{0:T(1024)} %param.22) | copy-start | bytes 49156
  41.7 1.4 %collective-permute-start.14 = (f32[256,128]{1,0:T(8,128)S(1)}, f32[256,128]{1,0:T(8,128)S(1)}, u32[]{:S(2)}, u32[]{:S(2)}) collective-permute-start(f32[256,128]{1,0:T(8,128)S(1)} %get-tuple-element.54), channel_id=1, source_target_pairs={{0,16},{16,0},{1,17},{17,1},{2,18},{18,2},{3,19},{19,3},{4,20},{20... | collective-permute-start | bytes 393224 | tf_op jit(solution)/shard_map/ppermute | solution.py:42
  43.1 5.3 %collective-permute-start.15 = (bf16[256,128]{1,0:T(8,128)(2,1)S(1)}, bf16[256,128]{1,0:T(8,128)(2,1)S(1)}, u32[]{:S(2)}, u32[]{:S(2)}) collective-permute-start(bf16[256,128]{1,0:T(8,128)(2,1)S(1)} %add_convert_fusion.1), channel_id=1, source_target_pairs={{0,4},{1,5},{2,6},{3,7},{4,0},{5,1},{6,2},{7,3},{8,12},{9,13},{10,... | collective-permute-start | bytes 196616 | tf_op jit(solution)/shard_map/ppermute | solution.py:34
  46.0 8.0 %collective-permute-start.16 = (bf16[256,128]{1,0:T(8,128)(2,1)S(1)}, bf16[256,128]{1,0:T(8,128)(2,1)S(1)}, u32[]{:S(2)}, u32[]{:S(2)}) collective-permute-start(bf16[256,128]{1,0:T(8,128)(2,1)S(1)} %add_convert_fusion.1), channel_id=1, source_target_pairs={{0,8},{1,9},{2,10},{3,11},{4,12},{5,13},{6,14},{7,15},{8,0},{9,1},... | collective-permute-start | bytes 196616 | tf_op jit(solution)/shard_map/ppermute | solution.py:34
  46.4 7.6 %collective-permute-start.17 = (bf16[256,128]{1,0:T(8,128)(2,1)S(1)}, bf16[256,128]{1,0:T(8,128)(2,1)S(1)}, u32[]{:S(2)}, u32[]{:S(2)}) collective-permute-start(bf16[256,128]{1,0:T(8,128)(2,1)S(1)} %add_convert_fusion.1), channel_id=1, source_target_pairs={{0,12},{1,13},{2,14},{3,15},{4,8},{5,9},{6,10},{7,11},{8,4},{9,5},... | collective-permute-start | bytes 196616 | tf_op jit(solution)/shard_map/ppermute | solution.py:34
  54.0 7.2 %collective-permute-start.20 = (bf16[1024,128]{1,0:T(8,128)(2,1)S(1)}, bf16[1024,128]{1,0:T(8,128)(2,1)S(1)}, u32[]{:S(2)}, u32[]{:S(2)}) collective-permute-start(bf16[1024,128]{1,0:T(8,128)(2,1)S(1)} %pad_maximum_fusion.1.refs_0_), channel_id=1, source_target_pairs={{0,1},{1,0},{2,3},{3,2},{4,5},{5,4},{6,7},{7,6},{8,9},{9,8},{10,11... | collective-permute-start | bytes 786440 | tf_op jit(solution)/shard_map/ppermute | solution.py:34
  55.4 7.3 %collective-permute-start.18 = (bf16[1024,128]{1,0:T(8,128)(2,1)S(1)}, bf16[1024,128]{1,0:T(8,128)(2,1)S(1)}, u32[]{:S(2)}, u32[]{:S(2)}) collective-permute-start(bf16[1024,128]{1,0:T(8,128)(2,1)S(1)} %pad_maximum_fusion.1.refs_0_), channel_id=1, source_target_pairs={{0,2},{1,3},{2,0},{3,1},{4,6},{5,7},{6,4},{7,5},{8,10},{9,11},{10,... | collective-permute-start | bytes 786440 | tf_op jit(solution)/shard_map/ppermute | solution.py:34
  61.3 5.0 %collective-permute-start.21 = (bf16[512,128]{1,0:T(8,128)(2,1)S(1)}, bf16[512,128]{1,0:T(8,128)(2,1)S(1)}, u32[]{:S(2)}, u32[]{:S(2)}) collective-permute-start(bf16[512,128]{1,0:T(8,128)(2,1)S(1)} %slice.86), channel_id=1, source_target_pairs={{0,2},{1,3},{2,0},{3,1},{4,6},{5,7},{6,4},{7,5},{8,10},{9,11},{10,... | collective-permute-start | bytes 393224 | tf_op jit(solution)/shard_map/ppermute | solution.py:34
  62.8 5.0 %collective-permute-start.22 = (bf16[512,128]{1,0:T(8,128)(2,1)S(1)}, bf16[512,128]{1,0:T(8,128)(2,1)S(1)}, u32[]{:S(2)}, u32[]{:S(2)}) collective-permute-start(bf16[512,128]{1,0:T(8,128)(2,1)S(1)} %slice.87), channel_id=1, source_target_pairs={{0,1},{1,0},{2,3},{3,2},{4,5},{5,4},{6,7},{7,6},{8,9},{9,8},{10,11... | collective-permute-start | bytes 393224 | tf_op jit(solution)/shard_map/ppermute | solution.py:34
  63.1 4.8 %collective-permute-start.24 = (bf16[1024,128]{1,0:T(8,128)(2,1)S(1)}, bf16[1024,128]{1,0:T(8,128)(2,1)S(1)}, u32[]{:S(2)}, u32[]{:S(2)}) collective-permute-start(bf16[1024,128]{1,0:T(8,128)(2,1)S(1)} %pad_maximum_fusion.1.refs_0_), channel_id=1, source_target_pairs={{0,16},{16,0},{1,17},{17,1},{2,18},{18,2},{3,19},{19,3},{4,20},{20... | collective-permute-start | bytes 786440 | tf_op jit(solution)/shard_map/ppermute | solution.py:42
  63.1 4.8 %collective-permute-start.25 = (bf16[1024,128]{1,0:T(8,128)(2,1)S(1)}, bf16[1024,128]{1,0:T(8,128)(2,1)S(1)}, u32[]{:S(2)}, u32[]{:S(2)}) collective-permute-start(bf16[1024,128]{1,0:T(8,128)(2,1)S(1)} %collective-permute-done.20.refs_2_), channel_id=1, source_target_pairs={{0,16},{16,0},{1,17},{17,1},{2,18},{18,2},{3,19},{19,3},{4,20},{20... | collective-permute-start | bytes 786440 | tf_op jit(solution)/shard_map/ppermute | solution.py:42
  63.6 5.7 %collective-permute-start.19 = (bf16[1024,128]{1,0:T(8,128)(2,1)S(1)}, bf16[1024,128]{1,0:T(8,128)(2,1)S(1)}, u32[]{:S(2)}, u32[]{:S(2)}) collective-permute-start(bf16[1024,128]{1,0:T(8,128)(2,1)S(1)} %collective-permute-done.18.refs_0_), channel_id=1, source_target_pairs={{0,16},{16,0},{1,17},{17,1},{2,18},{18,2},{3,19},{19,3},{4,20},{20... | collective-permute-start | bytes 786440 | tf_op jit(solution)/shard_map/ppermute | solution.py:42
  67.8 1.6 %collective-permute-start.23 = (bf16[1024,128]{1,0:T(8,128)(2,1)S(1)}, bf16[1024,128]{1,0:T(8,128)(2,1)S(1)}, u32[]{:S(2)}, u32[]{:S(2)}) collective-permute-start(bf16[1024,128]{1,0:T(8,128)(2,1)S(1)} %constant_dynamic-update-slice_fusion.refs_2_), channel_id=1, source_target_pairs={{0,16},{16,0},{1,17},{17,1},{2,18},{18,2},{3,19},{19,3},{4,20},{20... | collective-permute-start | bytes 786440 | tf_op jit(solution)/shard_map/ppermute | solution.py:42
  68.0 1.9 %copy-start.2 = (bf16[1,384,4096]{2,1,0:T(8,128)(2,1)S(1)}, bf16[1,384,4096]{2,1,0:T(8,128)(2,1)}, u32[]{:S(2)}) copy-start(bf16[1,384,4096]{2,1,0:T(8,128)(2,1)} %refs_12_.1) | copy-start | bytes 9437188
  72.7 2.1 %collective-permute-start.27 = (bf16[256,1024]{1,0:T(8,128)(2,1)S(1)}, bf16[256,1024]{1,0:T(8,128)(2,1)S(1)}, u32[]{:S(2)}, u32[]{:S(2)}) collective-permute-start(bf16[256,1024]{1,0:T(8,128)(2,1)S(1)} %get-tuple-element.64), channel_id=1, source_target_pairs={{0,16},{16,0},{1,17},{17,1},{2,18},{18,2},{3,19},{19,3},{4,20},{20... | collective-permute-start | bytes 1572872 | tf_op jit(solution)/shard_map/ppermute | solution.py:42
  73.2 3.9 %collective-permute-start.26 = (bf16[256,1024]{1,0:T(8,128)(2,1)S(1)}, bf16[256,1024]{1,0:T(8,128)(2,1)S(1)}, u32[]{:S(2)}, u32[]{:S(2)}) collective-permute-start(bf16[256,1024]{1,0:T(8,128)(2,1)S(1)} %get-tuple-element.62), channel_id=1, source_target_pairs={{0,16},{16,0},{1,17},{17,1},{2,18},{18,2},{3,19},{19,3},{4,20},{20... | collective-permute-start | bytes 1572872 | tf_op jit(solution)/shard_map/ppermute | solution.py:42
  75.0 8.7 %collective-permute-start.28 = (bf16[128,1024]{1,0:T(8,128)(2,1)S(1)}, bf16[128,1024]{1,0:T(8,128)(2,1)S(1)}, u32[]{:S(2)}, u32[]{:S(2)}) collective-permute-start(bf16[128,1024]{1,0:T(8,128)(2,1)S(1)} %get-tuple-element.68), channel_id=1, source_target_pairs={{0,1},{1,0},{2,3},{3,2},{4,5},{5,4},{6,7},{7,6},{8,9},{9,8},{10,11... | collective-permute-start | bytes 786440 | tf_op jit(solution)/shard_map/ppermute | solution.py:34
  75.3 8.4 %collective-permute-start.30 = (bf16[128,1024]{1,0:T(8,128)(2,1)S(1)}, bf16[128,1024]{1,0:T(8,128)(2,1)S(1)}, u32[]{:S(2)}, u32[]{:S(2)}) collective-permute-start(bf16[128,1024]{1,0:T(8,128)(2,1)S(1)} %get-tuple-element.67), channel_id=1, source_target_pairs={{0,2},{1,3},{2,0},{3,1},{4,6},{5,7},{6,4},{7,5},{8,10},{9,11},{10,... | collective-permute-start | bytes 786440 | tf_op jit(solution)/shard_map/ppermute | solution.py:34
  83.9 5.0 %collective-permute-start.31 = (bf16[64,1024]{1,0:T(8,128)(2,1)S(1)}, bf16[64,1024]{1,0:T(8,128)(2,1)S(1)}, u32[]{:S(2)}, u32[]{:S(2)}) collective-permute-start(bf16[64,1024]{1,0:T(8,128)(2,1)S(1)} %slice.123), channel_id=1, source_target_pairs={{0,1},{1,0},{2,3},{3,2},{4,5},{5,4},{6,7},{7,6},{8,9},{9,8},{10,11... | collective-permute-start | bytes 393224 | tf_op jit(solution)/shard_map/ppermute | solution.py:34
  85.7 5.0 %collective-permute-start.29 = (bf16[64,1024]{1,0:T(8,128)(2,1)S(1)}, bf16[64,1024]{1,0:T(8,128)(2,1)S(1)}, u32[]{:S(2)}, u32[]{:S(2)}) collective-permute-start(bf16[64,1024]{1,0:T(8,128)(2,1)S(1)} %slice.124), channel_id=1, source_target_pairs={{0,2},{1,3},{2,0},{3,1},{4,6},{5,7},{6,4},{7,5},{8,10},{9,11},{10,... | collective-permute-start | bytes 393224 | tf_op jit(solution)/shard_map/ppermute | solution.py:34
  90.8 5.8 %collective-permute-start.32 = (bf16[16,2048]{1,0:T(8,128)(2,1)S(1)}, bf16[16,2048]{1,0:T(8,128)(2,1)S(1)}, u32[]{:S(2)}, u32[]{:S(2)}) collective-permute-start(bf16[16,2048]{1,0:T(8,128)(2,1)S(1)} %get-tuple-element.71), channel_id=1, source_target_pairs={{0,8},{1,9},{2,10},{3,11},{4,12},{5,13},{6,14},{7,15},{8,0},{9,1},... | collective-permute-start | bytes 196616 | tf_op jit(solution)/shard_map/ppermute | solution.py:34
  92.9 6.1 %collective-permute-start.33 = (bf16[16,2048]{1,0:T(8,128)(2,1)S(1)}, bf16[16,2048]{1,0:T(8,128)(2,1)S(1)}, u32[]{:S(2)}, u32[]{:S(2)}) collective-permute-start(bf16[16,2048]{1,0:T(8,128)(2,1)S(1)} %get-tuple-element.73), channel_id=1, source_target_pairs={{0,12},{1,13},{2,14},{3,15},{4,8},{5,9},{6,10},{7,11},{8,4},{9,5},... | collective-permute-start | bytes 196616 | tf_op jit(solution)/shard_map/ppermute | solution.py:34
  94.8 4.8 %collective-permute-start.34 = (bf16[16,2048]{1,0:T(8,128)(2,1)S(1)}, bf16[16,2048]{1,0:T(8,128)(2,1)S(1)}, u32[]{:S(2)}, u32[]{:S(2)}) collective-permute-start(bf16[16,2048]{1,0:T(8,128)(2,1)S(1)} %get-tuple-element.72), channel_id=1, source_target_pairs={{0,4},{1,5},{2,6},{3,7},{4,0},{5,1},{6,2},{7,3},{8,12},{9,13},{10,... | collective-permute-start | bytes 196616 | tf_op jit(solution)/shard_map/ppermute | solution.py:34
  99.7 1.3 %collective-permute-start.35 = (bf16[16,2048]{1,0:T(8,128)(2,1)S(1)}, bf16[16,2048]{1,0:T(8,128)(2,1)S(1)}, u32[]{:S(2)}, u32[]{:S(2)}) collective-permute-start(bf16[16,2048]{1,0:T(8,128)(2,1)S(1)} %fusion.6), channel_id=1, source_target_pairs={{0,16},{16,0},{1,17},{17,1},{2,18},{18,2},{3,19},{19,3},{4,20},{20... | collective-permute-start | bytes 196616 | tf_op jit(solution)/shard_map/ppermute | solution.py:42

commit v7 on v6

--- a/solution.py
+++ b/solution.py
@@ -117,7 +117,7 @@
 
 def early_kernel(dims, codes, count, *refs):
     arrays = refs[:count]
-    gain_ref, router_ref, gate_ref, up_ref, acc, route, square, own_ref = refs[count:]
+    gain_ref, router_ref, gate_ref, up_ref, _, acc, route, square, own_ref = refs[count:]
     acc[...] = jnp.zeros_like(acc)
     route[...] = jnp.zeros_like(route)
     square[...] = jnp.zeros_like(square)
@@ -252,12 +252,12 @@
     found = found or pl.pallas_call(
         functools.partial(early_kernel, dims, codes and codes[:count], len(early)),
         out_shape=tuple(sums),
-        in_specs=[VM] * (len(early) + 4),
+        in_specs=[VM] * (len(early) + 5),
         out_specs=(VM,) * 4,
         compiler_params=params,
         cost_estimate=cost(0.33),
         name="experts_early",
-    )(*early, gain, router, gate, up)
+    )(*early, gain, router, gate, up, down)
     near = total_rows // nx + total_rows // ny
     shapes = [
         jax.ShapeDtypeStruct((r, width // 4), BF)

time: 102 us -> 101 us (level)
  transfers between devices with their start and end apart: 36 -> 36, of which waited for: 21 -> 22; matrix products, arithmetic and copies ran while one was open for 1% -> 1% of each run, Pallas kernels for 1% -> 1%
where the time goes in v7:
time: 101 us
  waiting for transfers between devices  47 us (47%)
  starting transfers between devices  38 us (38%)
  Pallas kernels  12.5 us (12%)
  local copies, waits for them, and re-layouts  1.89 us (2%)
  other arithmetic  1.38 us (1%)
    ppermute x28, waiting for transfers between devices, trade(): return lax.ppermute(value, 'dev', [(d, d ^ code) for d in range(n)])  42.8 us
    ppermute x28, starting transfers between devices, trade(): return lax.ppermute(value, 'dev', [(d, d ^ code) for d in range(n)])  36.7 us
    pallas_call x1, Pallas kernels, attention(): pl.pallas_call(functools.partial(attend_kernel, dims, lanes), out_shape=t...  7.24 us
    ppermute x8, waiting for transfers between devices, swap_sec(): return lax.ppermute(value, 'sec', [(0, 1), (1, 0)])  4.14 us
    pallas_call x1, Pallas kernels, experts(): pl.pallas_call(functools.partial(late_kernel, dims, codes and codes[count...  2.78 us
  transfers between devices with their start and end apart: 36, of which 22 were waited for; matrix products, arithmetic and copies ran while one was open for 1% of the time, Pallas kernels for 1%

profile of v7, /device:TPU:0, one launch (start us, length us, event | category | flops | bytes accessed | tf_op | source)
XLA Modules:
  0.0 101.2 jit_solution(8533485897577668284)
XLA Ops:
  0.0 7.2 %attend.1 = (bf16[16,3072]{1,0:T(8,128)(2,1)}, bf16[16,1664]{1,0:T(8,128)(2,1)}, bf16[16,1664]{1,0:T(8,128)(2,1)}, bf16[16,1664]{1,0:T(8,128)(2,1)}, bf16[16,1664]{1,0:T(8,128)(2,1)}) custom-call(s32[16]{0:T(128)} %refs_0_.1, s32[8,16]{1,0:T(8,128)} %bitcast.7, bf16[16,4096]{1,0:T(8,128)(2,1)} %refs_2_.1, bf16[16,256]{1,0:T(8,128)(2,1)} %refs_3_.1, ...), custom_call_target="tpu_custom_call" | custom-call | flops 402653184 | bytes 12582912 | tf_op jit(solution)/shard_map/attend/pallas_call | solution.py:402
  7.3 3.3 %collective-permute-start.3 = (bf16[16,1664]{1,0:T(8,128)(2,1)}, bf16[16,1664]{1,0:T(8,128)(2,1)S(1)}, u32[]{:S(2)}, u32[]{:S(2)}) collective-permute-start(bf16[16,1664]{1,0:T(8,128)(2,1)} %get-tuple-element.37), channel_id=1, source_target_pairs={{0,1},{1,0},{2,3},{3,2},{4,5},{5,4},{6,7},{7,6},{8,9},{9,8},{10,11... | collective-permute-start | bytes 159752 | tf_op jit(solution)/shard_map/ppermute | solution.py:34
  10.6 1.3 %collective-permute-start = (bf16[16,3072]{1,0:T(8,128)(2,1)}, bf16[16,3072]{1,0:T(8,128)(2,1)S(1)}, u32[]{:S(2)}, u32[]{:S(2)}) collective-permute-start(bf16[16,3072]{1,0:T(8,128)(2,1)} %get-tuple-element.35.refs_0_), channel_id=1, source_target_pairs={{0,4},{1,5},{2,6},{3,7},{4,0},{5,1},{6,2},{7,3},{8,12},{9,13},{10,... | collective-permute-start | bytes 294920 | tf_op jit(solution)/shard_map/ppermute | solution.py:34
  11.9 2.9 %collective-permute-start.1 = (bf16[16,3072]{1,0:T(8,128)(2,1)}, bf16[16,3072]{1,0:T(8,128)(2,1)S(1)}, u32[]{:S(2)}, u32[]{:S(2)}) collective-permute-start(bf16[16,3072]{1,0:T(8,128)(2,1)} %get-tuple-element.35.refs_0_), channel_id=1, source_target_pairs={{0,8},{1,9},{2,10},{3,11},{4,12},{5,13},{6,14},{7,15},{8,0},{9,1},... | collective-permute-start | bytes 294920 | tf_op jit(solution)/shard_map/ppermute | solution.py:34
  14.7 0.2 collective-permute-start.2
  15.0 1.3 %collective-permute-start.4 = (bf16[16,1664]{1,0:T(8,128)(2,1)}, bf16[16,1664]{1,0:T(8,128)(2,1)S(1)}, u32[]{:S(2)}, u32[]{:S(2)}) collective-permute-start(bf16[16,1664]{1,0:T(8,128)(2,1)} %get-tuple-element.38), channel_id=1, source_target_pairs={{0,2},{1,3},{2,0},{3,1},{4,6},{5,7},{6,4},{7,5},{8,10},{9,11},{10,... | collective-permute-start | bytes 159752 | tf_op jit(solution)/shard_map/ppermute | solution.py:34
  16.3 0.2 collective-permute-start.5
  16.5 3.1 %collective-permute-done.4.refs_2_ = bf16[16,1664]{1,0:T(8,128)(2,1)S(1)} collective-permute-done((bf16[16,1664]{1,0:T(8,128)(2,1)}, bf16[16,1664]{1,0:T(8,128)(2,1)S(1)}, u32[]{:S(2)}, u32[]{:S(2)}) %collective-permute-start.4) | collective-permute-done | bytes 53280 | tf_op jit(solution)/shard_map/ppermute | solution.py:34
  19.6 1.9 %collective-permute-done.5.refs_3_ = bf16[16,1664]{1,0:T(8,128)(2,1)S(1)} collective-permute-done((bf16[16,1664]{1,0:T(8,128)(2,1)}, bf16[16,1664]{1,0:T(8,128)(2,1)S(1)}, u32[]{:S(2)}, u32[]{:S(2)}) %collective-permute-start.5) | collective-permute-done | bytes 53280 | tf_op jit(solution)/shard_map/ppermute | solution.py:34
  21.5 0.8 copy-done.7
  22.5 0.9 copy-done.5
  23.4 0.8 collective-permute-start.9
  24.2 1.3 %collective-permute-start.10 = (bf16[64,3072]{1,0:T(8,128)(2,1)S(1)}, bf16[64,3072]{1,0:T(8,128)(2,1)S(1)}, u32[]{:S(2)}, u32[]{:S(2)}) collective-permute-start(bf16[64,3072]{1,0:T(8,128)(2,1)S(1)} %pack_line.1.refs_0_), channel_id=1, source_target_pairs={{0,2},{1,3},{2,0},{3,1},{4,6},{5,7},{6,4},{7,5},{8,10},{9,11},{10,... | collective-permute-start | bytes 1179656 | tf_op jit(solution)/shard_map/ppermute | solution.py:34
  25.5 1.6 %collective-permute-start.6 = (bf16[64,1280]{1,0:T(8,128)(2,1)S(1)}, bf16[64,1280]{1,0:T(8,128)(2,1)S(1)}, u32[]{:S(2)}, u32[]{:S(2)}) collective-permute-start(bf16[64,1280]{1,0:T(8,128)(2,1)S(1)} %get-tuple-element.45), channel_id=1, source_target_pairs={{0,4},{1,5},{2,6},{3,7},{4,0},{5,1},{6,2},{7,3},{8,12},{9,13},{10,... | collective-permute-start | bytes 491528 | tf_op jit(solution)/shard_map/ppermute | solution.py:34
  27.1 1.4 %collective-permute-start.7 = (bf16[64,1280]{1,0:T(8,128)(2,1)S(1)}, bf16[64,1280]{1,0:T(8,128)(2,1)S(1)}, u32[]{:S(2)}, u32[]{:S(2)}) collective-permute-start(bf16[64,1280]{1,0:T(8,128)(2,1)S(1)} %get-tuple-element.46), channel_id=1, source_target_pairs={{0,8},{1,9},{2,10},{3,11},{4,12},{5,13},{6,14},{7,15},{8,0},{9,1},... | collective-permute-start | bytes 491528 | tf_op jit(solution)/shard_map/ppermute | solution.py:34
  28.5 1.4 %collective-permute-start.8 = (bf16[64,1280]{1,0:T(8,128)(2,1)S(1)}, bf16[64,1280]{1,0:T(8,128)(2,1)S(1)}, u32[]{:S(2)}, u32[]{:S(2)}) collective-permute-start(bf16[64,1280]{1,0:T(8,128)(2,1)S(1)} %get-tuple-element.47), channel_id=1, source_target_pairs={{0,12},{1,13},{2,14},{3,15},{4,8},{5,9},{6,10},{7,11},{8,4},{9,5},... | collective-permute-start | bytes 491528 | tf_op jit(solution)/shard_map/ppermute | solution.py:34
  29.9 2.2 %collective-permute-done.9.refs_1_ = bf16[64,3072]{1,0:T(8,128)(2,1)S(1)} collective-permute-done((bf16[64,3072]{1,0:T(8,128)(2,1)S(1)}, bf16[64,3072]{1,0:T(8,128)(2,1)S(1)}, u32[]{:S(2)}, u32[]{:S(2)}) %collective-permute-start.9) | collective-permute-done | bytes 393248 | tf_op jit(solution)/shard_map/ppermute | solution.py:34
  32.1 1.3 %collective-permute-start.11 = (bf16[64,1024]{1,0:T(8,128)(2,1)S(1)}, bf16[64,1024]{1,0:T(8,128)(2,1)S(1)}, u32[]{:S(2)}, u32[]{:S(2)}) collective-permute-start(bf16[64,1024]{1,0:T(8,128)(2,1)S(1)} %get-tuple-element.70), channel_id=1, source_target_pairs={{0,2},{1,3},{2,0},{3,1},{4,6},{5,7},{6,4},{7,5},{8,10},{9,11},{10,... | collective-permute-start | bytes 393224 | tf_op jit(solution)/shard_map/ppermute | solution.py:34
  33.4 0.1 collective-permute-done.10.refs_2_
  33.5 1.2 %collective-permute-start.12 = (bf16[64,1024]{1,0:T(8,128)(2,1)S(1)}, bf16[64,1024]{1,0:T(8,128)(2,1)S(1)}, u32[]{:S(2)}, u32[]{:S(2)}) collective-permute-start(bf16[64,1024]{1,0:T(8,128)(2,1)S(1)} %get-tuple-element.69), channel_id=1, source_target_pairs={{0,2},{1,3},{2,0},{3,1},{4,6},{5,7},{6,4},{7,5},{8,10},{9,11},{10,... | collective-permute-start | bytes 393224 | tf_op jit(solution)/shard_map/ppermute | solution.py:34
  34.8 2.3 %collective-permute-start.13 = (bf16[64,1024]{1,0:T(8,128)(2,1)S(1)}, bf16[64,1024]{1,0:T(8,128)(2,1)S(1)}, u32[]{:S(2)}, u32[]{:S(2)}) collective-permute-start(bf16[64,1024]{1,0:T(8,128)(2,1)S(1)} %slice.85), channel_id=1, source_target_pairs={{0,1},{1,0},{2,3},{3,2},{4,5},{5,4},{6,7},{7,6},{8,9},{9,8},{10,11... | collective-permute-start | bytes 393224 | tf_op jit(solution)/shard_map/ppermute | solution.py:34
  37.0 3.6 %collective-permute-done.7.refs_2_ = bf16[64,1280]{1,0:T(8,128)(2,1)S(1)} collective-permute-done((bf16[64,1280]{1,0:T(8,128)(2,1)S(1)}, bf16[64,1280]{1,0:T(8,128)(2,1)S(1)}, u32[]{:S(2)}, u32[]{:S(2)}) %collective-permute-start.7) | collective-permute-done | bytes 163872 | tf_op jit(solution)/shard_map/ppermute | solution.py:34
  40.7 0.1 settle.1
  40.8 1.0 %project.1 = (f32[256,128]{1,0:T(8,128)S(1)}, f32[256,128]{1,0:T(8,128)S(1)}) custom-call(bf16[64,3072]{1,0:T(8,128)(2,1)S(1)} %pack_line.1.refs_0_, bf16[64,3072]{1,0:T(8,128)(2,1)S(1)} %collective-permute-done.9.refs_1_, bf16[64,3072]{1,0:T(8,128)(2,1)S(1)} %collective-permute-done.10.refs_2_, bf16[64,1024]{1,0:T(8,128)(2,1)S(1)} %collective-permute-done.11.refs_3_, ...), custom_call_target="tpu_custom_call" | custom-call | flops 536870912 | bytes 4194304 | tf_op jit(solution)/shard_map/project/pallas_call | solution.py:515
  41.9 0.1 collective-permute-start.14
  42.0 1.3 %collective-permute-done.14 = f32[256,128]{1,0:T(8,128)S(1)} collective-permute-done((f32[256,128]{1,0:T(8,128)S(1)}, f32[256,128]{1,0:T(8,128)S(1)}, u32[]{:S(2)}, u32[]{:S(2)}) %collective-permute-start.14) | collective-permute-done | bytes 131104 | tf_op jit(solution)/shard_map/ppermute | solution.py:42
  43.3 2.5 %collective-permute-start.15 = (bf16[256,128]{1,0:T(8,128)(2,1)S(1)}, bf16[256,128]{1,0:T(8,128)(2,1)S(1)}, u32[]{:S(2)}, u32[]{:S(2)}) collective-permute-start(bf16[256,128]{1,0:T(8,128)(2,1)S(1)} %add_convert_fusion.1), channel_id=1, source_target_pairs={{0,4},{1,5},{2,6},{3,7},{4,0},{5,1},{6,2},{7,3},{8,12},{9,13},{10,... | collective-permute-start | bytes 196616 | tf_op jit(solution)/shard_map/ppermute | solution.py:34
  45.8 0.8 collective-permute-start.16
  46.6 1.6 %collective-permute-start.17 = (bf16[256,128]{1,0:T(8,128)(2,1)S(1)}, bf16[256,128]{1,0:T(8,128)(2,1)S(1)}, u32[]{:S(2)}, u32[]{:S(2)}) collective-permute-start(bf16[256,128]{1,0:T(8,128)(2,1)S(1)} %add_convert_fusion.1), channel_id=1, source_target_pairs={{0,12},{1,13},{2,14},{3,15},{4,8},{5,9},{6,10},{7,11},{8,4},{9,5},... | collective-permute-start | bytes 196616 | tf_op jit(solution)/shard_map/ppermute | solution.py:34
  48.3 5.8 %collective-permute-done.16 = bf16[256,128]{1,0:T(8,128)(2,1)S(1)} collective-permute-done((bf16[256,128]{1,0:T(8,128)(2,1)S(1)}, bf16[256,128]{1,0:T(8,128)(2,1)S(1)}, u32[]{:S(2)}, u32[]{:S(2)}) %collective-permute-start.16) | collective-permute-done | bytes 65568 | tf_op jit(solution)/shard_map/ppermute | solution.py:34
  54.0 1.5 %collective-permute-start.20 = (bf16[1024,128]{1,0:T(8,128)(2,1)S(1)}, bf16[1024,128]{1,0:T(8,128)(2,1)S(1)}, u32[]{:S(2)}, u32[]{:S(2)}) collective-permute-start(bf16[1024,128]{1,0:T(8,128)(2,1)S(1)} %pad_maximum_fusion.1.refs_0_), channel_id=1, source_target_pairs={{0,1},{1,0},{2,3},{3,2},{4,5},{5,4},{6,7},{7,6},{8,9},{9,8},{10,11... | collective-permute-start | bytes 786440 | tf_op jit(solution)/shard_map/ppermute | solution.py:34
  55.5 0.7 collective-permute-start.18
  56.2 4.5 %collective-permute-done.20.refs_2_ = bf16[1024,128]{1,0:T(8,128)(2,1)S(1)} collective-permute-done((bf16[1024,128]{1,0:T(8,128)(2,1)S(1)}, bf16[1024,128]{1,0:T(8,128)(2,1)S(1)}, u32[]{:S(2)}, u32[]{:S(2)}) %collective-permute-start.20) | collective-permute-done | bytes 262176 | tf_op jit(solution)/shard_map/ppermute | solution.py:34
  60.8 0.7 collective-permute-start.21
  61.5 1.3 %collective-permute-done.18.refs_0_ = bf16[1024,128]{1,0:T(8,128)(2,1)S(1)} collective-permute-done((bf16[1024,128]{1,0:T(8,128)(2,1)S(1)}, bf16[1024,128]{1,0:T(8,128)(2,1)S(1)}, u32[]{:S(2)}, u32[]{:S(2)}) %collective-permute-start.18) | collective-permute-done | bytes 262176 | tf_op jit(solution)/shard_map/ppermute | solution.py:34
  62.8 0.4 collective-permute-start.22
  63.2 0.5 collective-permute-start.25
  63.7 2.1 %collective-permute-done.21 = bf16[512,128]{1,0:T(8,128)(2,1)S(1)} collective-permute-done((bf16[512,128]{1,0:T(8,128)(2,1)S(1)}, bf16[512,128]{1,0:T(8,128)(2,1)S(1)}, u32[]{:S(2)}, u32[]{:S(2)}) %collective-permute-start.21) | collective-permute-done | bytes 131104 | tf_op jit(solution)/shard_map/ppermute | solution.py:34
  65.8 2.0 %collective-permute-done.22 = bf16[512,128]{1,0:T(8,128)(2,1)S(1)} collective-permute-done((bf16[512,128]{1,0:T(8,128)(2,1)S(1)}, bf16[512,128]{1,0:T(8,128)(2,1)S(1)}, u32[]{:S(2)}, u32[]{:S(2)}) %collective-permute-start.22) | collective-permute-done | bytes 131104 | tf_op jit(solution)/shard_map/ppermute | solution.py:34
  67.9 0.1 collective-permute-start.23
  68.0 1.3 %experts_early.1 = (f32[256,768]{1,0:T(8,128)S(1)}, f32[256,16]{1,0:T(8,128)S(1)}, f32[256,128]{1,0:T(8,128)S(1)}, bf16[16,4096]{1,0:T(8,128)(2,1)S(1)}) custom-call(bf16[1024,128]{1,0:T(8,128)(2,1)S(1)} %pad_maximum_fusion.1.refs_0_, bf16[1024,128]{1,0:T(8,128)(2,1)S(1)} %collective-permute-done.24.refs_1_, ...), custom_call_target="tpu_custom_call" | custom-call | flops 797253312 | bytes 3114270 | tf_op jit(solution)/shard_map/experts_early/pallas_call | solution.py:252
  69.3 0.2 collective-permute-done.23.refs_3_
  69.5 2.8 %experts_late.1 = (bf16[256,1024]{1,0:T(8,128)(2,1)S(1)}, bf16[256,1024]{1,0:T(8,128)(2,1)S(1)}, bf16[256,1024]{1,0:T(8,128)(2,1)S(1)}, bf16[256,1024]{1,0:T(8,128)(2,1)S(1)}, bf16[16,4096]{1,0:T(8,128)(2,1)S(1)}) custom-call(bf16[1024,128]{1,0:T(8,128)(2,1)S(1)} %collective-permute-done.18.refs_0_, bf16[1024,128]{1,0:T(8,128)(2,1)S(1)} %collective-permute-done.19.refs_1_, ...), custom_call_target="tpu_custom_call" | custom-call | flops 1618665856 | bytes 6322913 | tf_op jit(solution)/shard_map/experts_late/pallas_call | solution.py:266
  72.2 0.4 collective-permute-start.27
  72.6 0.2 collective-permute-start.26
  72.8 1.4 %collective-permute-done.27 = bf16[256,1024]{1,0:T(8,128)(2,1)S(1)} collective-permute-done((bf16[256,1024]{1,0:T(8,128)(2,1)S(1)}, bf16[256,1024]{1,0:T(8,128)(2,1)S(1)}, u32[]{:S(2)}, u32[]{:S(2)}) %collective-permute-start.27) | collective-permute-done | bytes 524320 | tf_op jit(solution)/shard_map/ppermute | solution.py:42
  74.2 0.2 add_convert_fusion
  74.5 0.4 collective-permute-start.28
  74.8 1.1 %collective-permute-start.30 = (bf16[128,1024]{1,0:T(8,128)(2,1)S(1)}, bf16[128,1024]{1,0:T(8,128)(2,1)S(1)}, u32[]{:S(2)}, u32[]{:S(2)}) collective-permute-start(bf16[128,1024]{1,0:T(8,128)(2,1)S(1)} %get-tuple-element.67), channel_id=1, source_target_pairs={{0,2},{1,3},{2,0},{3,1},{4,6},{5,7},{6,4},{7,5},{8,10},{9,11},{10,... | collective-permute-start | bytes 786440 | tf_op jit(solution)/shard_map/ppermute | solution.py:34
  75.9 0.2 convert_add_fusion
  76.1 6.9 %collective-permute-done.28 = bf16[128,1024]{1,0:T(8,128)(2,1)S(1)} collective-permute-done((bf16[128,1024]{1,0:T(8,128)(2,1)S(1)}, bf16[128,1024]{1,0:T(8,128)(2,1)S(1)}, u32[]{:S(2)}, u32[]{:S(2)}) %collective-permute-start.28) | collective-permute-done | bytes 262176 | tf_op jit(solution)/shard_map/ppermute | solution.py:34
  83.1 0.1 collective-permute-done.30
  83.1 0.2 slice_add_fusion
  83.4 1.7 %collective-permute-start.31 = (bf16[64,1024]{1,0:T(8,128)(2,1)S(1)}, bf16[64,1024]{1,0:T(8,128)(2,1)S(1)}, u32[]{:S(2)}, u32[]{:S(2)}) collective-permute-start(bf16[64,1024]{1,0:T(8,128)(2,1)S(1)} %slice.123), channel_id=1, source_target_pairs={{0,1},{1,0},{2,3},{3,2},{4,5},{5,4},{6,7},{7,6},{8,9},{9,8},{10,11... | collective-permute-start | bytes 393224 | tf_op jit(solution)/shard_map/ppermute | solution.py:34
  85.1 0.9 collective-permute-start.29
  86.0 2.4 %collective-permute-done.31 = bf16[64,1024]{1,0:T(8,128)(2,1)S(1)} collective-permute-done((bf16[64,1024]{1,0:T(8,128)(2,1)S(1)}, bf16[64,1024]{1,0:T(8,128)(2,1)S(1)}, u32[]{:S(2)}, u32[]{:S(2)}) %collective-permute-start.31) | collective-permute-done | bytes 131104 | tf_op jit(solution)/shard_map/ppermute | solution.py:34
  88.4 1.7 %collective-permute-done.29 = bf16[64,1024]{1,0:T(8,128)(2,1)S(1)} collective-permute-done((bf16[64,1024]{1,0:T(8,128)(2,1)S(1)}, bf16[64,1024]{1,0:T(8,128)(2,1)S(1)}, u32[]{:S(2)}, u32[]{:S(2)}) %collective-permute-start.29) | collective-permute-done | bytes 131104 | tf_op jit(solution)/shard_map/ppermute | solution.py:34
  90.2 2.1 %collective-permute-start.32 = (bf16[16,2048]{1,0:T(8,128)(2,1)S(1)}, bf16[16,2048]{1,0:T(8,128)(2,1)S(1)}, u32[]{:S(2)}, u32[]{:S(2)}) collective-permute-start(bf16[16,2048]{1,0:T(8,128)(2,1)S(1)} %get-tuple-element.71), channel_id=1, source_target_pairs={{0,8},{1,9},{2,10},{3,11},{4,12},{5,13},{6,14},{7,15},{8,0},{9,1},... | collective-permute-start | bytes 196616 | tf_op jit(solution)/shard_map/ppermute | solution.py:34
  92.4 1.9 %collective-permute-start.33 = (bf16[16,2048]{1,0:T(8,128)(2,1)S(1)}, bf16[16,2048]{1,0:T(8,128)(2,1)S(1)}, u32[]{:S(2)}, u32[]{:S(2)}) collective-permute-start(bf16[16,2048]{1,0:T(8,128)(2,1)S(1)} %get-tuple-element.73), channel_id=1, source_target_pairs={{0,12},{1,13},{2,14},{3,15},{4,8},{5,9},{6,10},{7,11},{8,4},{9,5},... | collective-permute-start | bytes 196616 | tf_op jit(solution)/shard_map/ppermute | solution.py:34
  94.2 2.6 %collective-permute-done.32 = bf16[16,2048]{1,0:T(8,128)(2,1)S(1)} collective-permute-done((bf16[16,2048]{1,0:T(8,128)(2,1)S(1)}, bf16[16,2048]{1,0:T(8,128)(2,1)S(1)}, u32[]{:S(2)}, u32[]{:S(2)}) %collective-permute-start.32) | collective-permute-done | bytes 65568 | tf_op jit(solution)/shard_map/ppermute | solution.py:34
  96.8 1.7 %collective-permute-done.33 = bf16[16,2048]{1,0:T(8,128)(2,1)S(1)} collective-permute-done((bf16[16,2048]{1,0:T(8,128)(2,1)S(1)}, bf16[16,2048]{1,0:T(8,128)(2,1)S(1)}, u32[]{:S(2)}, u32[]{:S(2)}) %collective-permute-start.33) | collective-permute-done | bytes 65568 | tf_op jit(solution)/shard_map/ppermute | solution.py:34
  98.5 0.6 collective-permute-done.34
  99.3 1.2 %collective-permute-done.35 = bf16[16,2048]{1,0:T(8,128)(2,1)S(1)} collective-permute-done((bf16[16,2048]{1,0:T(8,128)(2,1)S(1)}, bf16[16,2048]{1,0:T(8,128)(2,1)S(1)}, u32[]{:S(2)}, u32[]{:S(2)}) %collective-permute-start.35) | collective-permute-done | bytes 65568 | tf_op jit(solution)/shard_map/ppermute | solution.py:42
  100.5 0.7 maximum_select_fusion
  (51 shorter events, 0.7 us)
Async XLA Ops:
  0.0 68.0 %copy-start.2 = (bf16[1,384,4096]{2,1,0:T(8,128)(2,1)S(1)}, bf16[1,384,4096]{2,1,0:T(8,128)(2,1)}, u32[]{:S(2)}) copy-start(bf16[1,384,4096]{2,1,0:T(8,128)(2,1)} %refs_12_.1) | copy-start | bytes 9437188
  7.2 33.6 %copy-start.3 = (bf16[4096,256]{1,0:T(8,128)(2,1)S(1)}, bf16[4096,256]{1,0:T(8,128)(2,1)}, u32[]{:S(2)}) copy-start(bf16[4096,256]{1,0:T(8,128)(2,1)} %refs_7_.5) | copy-start | bytes 6291460
  7.3 9.0 %collective-permute-start.3 = (bf16[16,1664]{1,0:T(8,128)(2,1)}, bf16[16,1664]{1,0:T(8,128)(2,1)S(1)}, u32[]{:S(2)}, u32[]{:S(2)}) collective-permute-start(bf16[16,1664]{1,0:T(8,128)(2,1)} %get-tuple-element.37), channel_id=1, source_target_pairs={{0,1},{1,0},{2,3},{3,2},{4,5},{5,4},{6,7},{7,6},{8,9},{9,8},{10,11... | collective-permute-start | bytes 159752 | tf_op jit(solution)/shard_map/ppermute | solution.py:34
  10.6 11.8 %collective-permute-start = (bf16[16,3072]{1,0:T(8,128)(2,1)}, bf16[16,3072]{1,0:T(8,128)(2,1)S(1)}, u32[]{:S(2)}, u32[]{:S(2)}) collective-permute-start(bf16[16,3072]{1,0:T(8,128)(2,1)} %get-tuple-element.35.refs_0_), channel_id=1, source_target_pairs={{0,4},{1,5},{2,6},{3,7},{4,0},{5,1},{6,2},{7,3},{8,12},{9,13},{10,... | collective-permute-start | bytes 294920 | tf_op jit(solution)/shard_map/ppermute | solution.py:34
  11.9 10.6 %collective-permute-start.1 = (bf16[16,3072]{1,0:T(8,128)(2,1)}, bf16[16,3072]{1,0:T(8,128)(2,1)S(1)}, u32[]{:S(2)}, u32[]{:S(2)}) collective-permute-start(bf16[16,3072]{1,0:T(8,128)(2,1)} %get-tuple-element.35.refs_0_), channel_id=1, source_target_pairs={{0,8},{1,9},{2,10},{3,11},{4,12},{5,13},{6,14},{7,15},{8,0},{9,1},... | collective-permute-start | bytes 294920 | tf_op jit(solution)/shard_map/ppermute | solution.py:34
  14.7 7.7 %collective-permute-start.2 = (bf16[16,3072]{1,0:T(8,128)(2,1)}, bf16[16,3072]{1,0:T(8,128)(2,1)S(1)}, u32[]{:S(2)}, u32[]{:S(2)}) collective-permute-start(bf16[16,3072]{1,0:T(8,128)(2,1)} %get-tuple-element.35.refs_0_), channel_id=1, source_target_pairs={{0,12},{1,13},{2,14},{3,15},{4,8},{5,9},{6,10},{7,11},{8,4},{9,5},... | collective-permute-start | bytes 294920 | tf_op jit(solution)/shard_map/ppermute | solution.py:34
  15.0 4.6 %collective-permute-start.4 = (bf16[16,1664]{1,0:T(8,128)(2,1)}, bf16[16,1664]{1,0:T(8,128)(2,1)S(1)}, u32[]{:S(2)}, u32[]{:S(2)}) collective-permute-start(bf16[16,1664]{1,0:T(8,128)(2,1)} %get-tuple-element.38), channel_id=1, source_target_pairs={{0,2},{1,3},{2,0},{3,1},{4,6},{5,7},{6,4},{7,5},{8,10},{9,11},{10,... | collective-permute-start | bytes 159752 | tf_op jit(solution)/shard_map/ppermute | solution.py:34
  16.3 5.2 %collective-permute-start.5 = (bf16[16,1664]{1,0:T(8,128)(2,1)}, bf16[16,1664]{1,0:T(8,128)(2,1)S(1)}, u32[]{:S(2)}, u32[]{:S(2)}) collective-permute-start(bf16[16,1664]{1,0:T(8,128)(2,1)} %get-tuple-element.39), channel_id=1, source_target_pairs={{0,3},{1,2},{2,1},{3,0},{4,7},{5,6},{6,5},{7,4},{8,11},{9,10},{10,... | collective-permute-start | bytes 159752 | tf_op jit(solution)/shard_map/ppermute | solution.py:34
  21.5 0.8 copy-start.7
  22.5 0.9 copy-start.5
  23.4 8.7 %collective-permute-start.9 = (bf16[64,3072]{1,0:T(8,128)(2,1)S(1)}, bf16[64,3072]{1,0:T(8,128)(2,1)S(1)}, u32[]{:S(2)}, u32[]{:S(2)}) collective-permute-start(bf16[64,3072]{1,0:T(8,128)(2,1)S(1)} %pack_line.1.refs_0_), channel_id=1, source_target_pairs={{0,1},{1,0},{2,3},{3,2},{4,5},{5,4},{6,7},{7,6},{8,9},{9,8},{10,11... | collective-permute-start | bytes 1179656 | tf_op jit(solution)/shard_map/ppermute | solution.py:34
  24.2 9.4 %collective-permute-start.10 = (bf16[64,3072]{1,0:T(8,128)(2,1)S(1)}, bf16[64,3072]{1,0:T(8,128)(2,1)S(1)}, u32[]{:S(2)}, u32[]{:S(2)}) collective-permute-start(bf16[64,3072]{1,0:T(8,128)(2,1)S(1)} %pack_line.1.refs_0_), channel_id=1, source_target_pairs={{0,2},{1,3},{2,0},{3,1},{4,6},{5,7},{6,4},{7,5},{8,10},{9,11},{10,... | collective-permute-start | bytes 1179656 | tf_op jit(solution)/shard_map/ppermute | solution.py:34
  25.5 9.3 %collective-permute-start.6 = (bf16[64,1280]{1,0:T(8,128)(2,1)S(1)}, bf16[64,1280]{1,0:T(8,128)(2,1)S(1)}, u32[]{:S(2)}, u32[]{:S(2)}) collective-permute-start(bf16[64,1280]{1,0:T(8,128)(2,1)S(1)} %get-tuple-element.45), channel_id=1, source_target_pairs={{0,4},{1,5},{2,6},{3,7},{4,0},{5,1},{6,2},{7,3},{8,12},{9,13},{10,... | collective-permute-start | bytes 491528 | tf_op jit(solution)/shard_map/ppermute | solution.py:34
  27.1 13.6 %collective-permute-start.7 = (bf16[64,1280]{1,0:T(8,128)(2,1)S(1)}, bf16[64,1280]{1,0:T(8,128)(2,1)S(1)}, u32[]{:S(2)}, u32[]{:S(2)}) collective-permute-start(bf16[64,1280]{1,0:T(8,128)(2,1)S(1)} %get-tuple-element.46), channel_id=1, source_target_pairs={{0,8},{1,9},{2,10},{3,11},{4,12},{5,13},{6,14},{7,15},{8,0},{9,1},... | collective-permute-start | bytes 491528 | tf_op jit(solution)/shard_map/ppermute | solution.py:34
  28.5 12.2 %collective-permute-start.8 = (bf16[64,1280]{1,0:T(8,128)(2,1)S(1)}, bf16[64,1280]{1,0:T(8,128)(2,1)S(1)}, u32[]{:S(2)}, u32[]{:S(2)}) collective-permute-start(bf16[64,1280]{1,0:T(8,128)(2,1)S(1)} %get-tuple-element.47), channel_id=1, source_target_pairs={{0,12},{1,13},{2,14},{3,15},{4,8},{5,9},{6,10},{7,11},{8,4},{9,5},... | collective-permute-start | bytes 491528 | tf_op jit(solution)/shard_map/ppermute | solution.py:34
  32.1 8.7 %collective-permute-start.11 = (bf16[64,1024]{1,0:T(8,128)(2,1)S(1)}, bf16[64,1024]{1,0:T(8,128)(2,1)S(1)}, u32[]{:S(2)}, u32[]{:S(2)}) collective-permute-start(bf16[64,1024]{1,0:T(8,128)(2,1)S(1)} %get-tuple-element.70), channel_id=1, source_target_pairs={{0,2},{1,3},{2,0},{3,1},{4,6},{5,7},{6,4},{7,5},{8,10},{9,11},{10,... | collective-permute-start | bytes 393224 | tf_op jit(solution)/shard_map/ppermute | solution.py:34
  33.5 7.3 %collective-permute-start.12 = (bf16[64,1024]{1,0:T(8,128)(2,1)S(1)}, bf16[64,1024]{1,0:T(8,128)(2,1)S(1)}, u32[]{:S(2)}, u32[]{:S(2)}) collective-permute-start(bf16[64,1024]{1,0:T(8,128)(2,1)S(1)} %get-tuple-element.69), channel_id=1, source_target_pairs={{0,2},{1,3},{2,0},{3,1},{4,6},{5,7},{6,4},{7,5},{8,10},{9,11},{10,... | collective-permute-start | bytes 393224 | tf_op jit(solution)/shard_map/ppermute | solution.py:34
  34.8 6.0 %collective-permute-start.13 = (bf16[64,1024]{1,0:T(8,128)(2,1)S(1)}, bf16[64,1024]{1,0:T(8,128)(2,1)S(1)}, u32[]{:S(2)}, u32[]{:S(2)}) collective-permute-start(bf16[64,1024]{1,0:T(8,128)(2,1)S(1)} %slice.85), channel_id=1, source_target_pairs={{0,1},{1,0},{2,3},{3,2},{4,5},{5,4},{6,7},{7,6},{8,9},{9,8},{10,11... | collective-permute-start | bytes 393224 | tf_op jit(solution)/shard_map/ppermute | solution.py:34
  40.7 27.3 %copy-start.1 = (bf16[1,4096,384]{2,1,0:T(8,128)(2,1)S(1)}, bf16[1,4096,384]{2,1,0:T(8,128)(2,1)}, u32[]{:S(2)}) copy-start(bf16[1,4096,384]{2,1,0:T(8,128)(2,1)} %refs_7_.7) | copy-start | bytes 9437188
  40.8 27.2 %copy-start = (bf16[1,4096,384]{2,1,0:T(8,128)(2,1)S(1)}, bf16[1,4096,384]{2,1,0:T(8,128)(2,1)}, u32[]{:S(2)}) copy-start(bf16[1,4096,384]{2,1,0:T(8,128)(2,1)} %refs_6_.5) | copy-start | bytes 9437188
  40.8 27.2 %copy-start.4 = (bf16[4096,16]{0,1:T(8,128)(2,1)S(1)}, bf16[4096,16]{0,1:T(8,128)(2,1)}, u32[]{:S(2)}) copy-start(bf16[4096,16]{0,1:T(8,128)(2,1)} %param.23) | copy-start | bytes 393220
  40.8 27.2 %copy-start.6 = (f32[4096]{0:T(1024)S(1)}, f32[4096]{0:T(1024)}, u32[]{:S(2)}) copy-start(f32[4096]{0:T(1024)} %param.22) | copy-start | bytes 49156
  41.9 1.4 %collective-permute-start.14 = (f32[256,128]{1,0:T(8,128)S(1)}, f32[256,128]{1,0:T(8,128)S(1)}, u32[]{:S(2)}, u32[]{:S(2)}) collective-permute-start(f32[256,128]{1,0:T(8,128)S(1)} %get-tuple-element.54), channel_id=1, source_target_pairs={{0,16},{16,0},{1,17},{17,1},{2,18},{18,2},{3,19},{19,3},{4,20},{20... | collective-permute-start | bytes 393224 | tf_op jit(solution)/shard_map/ppermute | solution.py:42
  43.3 4.9 %collective-permute-start.15 = (bf16[256,128]{1,0:T(8,128)(2,1)S(1)}, bf16[256,128]{1,0:T(8,128)(2,1)S(1)}, u32[]{:S(2)}, u32[]{:S(2)}) collective-permute-start(bf16[256,128]{1,0:T(8,128)(2,1)S(1)} %add_convert_fusion.1), channel_id=1, source_target_pairs={{0,4},{1,5},{2,6},{3,7},{4,0},{5,1},{6,2},{7,3},{8,12},{9,13},{10,... | collective-permute-start | bytes 196616 | tf_op jit(solution)/shard_map/ppermute | solution.py:34
  45.8 8.2 %collective-permute-start.16 = (bf16[256,128]{1,0:T(8,128)(2,1)S(1)}, bf16[256,128]{1,0:T(8,128)(2,1)S(1)}, u32[]{:S(2)}, u32[]{:S(2)}) collective-permute-start(bf16[256,128]{1,0:T(8,128)(2,1)S(1)} %add_convert_fusion.1), channel_id=1, source_target_pairs={{0,8},{1,9},{2,10},{3,11},{4,12},{5,13},{6,14},{7,15},{8,0},{9,1},... | collective-permute-start | bytes 196616 | tf_op jit(solution)/shard_map/ppermute | solution.py:34
  46.6 7.4 %collective-permute-start.17 = (bf16[256,128]{1,0:T(8,128)(2,1)S(1)}, bf16[256,128]{1,0:T(8,128)(2,1)S(1)}, u32[]{:S(2)}, u32[]{:S(2)}) collective-permute-start(bf16[256,128]{1,0:T(8,128)(2,1)S(1)} %add_convert_fusion.1), channel_id=1, source_target_pairs={{0,12},{1,13},{2,14},{3,15},{4,8},{5,9},{6,10},{7,11},{8,4},{9,5},... | collective-permute-start | bytes 196616 | tf_op jit(solution)/shard_map/ppermute | solution.py:34
  54.0 6.7 %collective-permute-start.20 = (bf16[1024,128]{1,0:T(8,128)(2,1)S(1)}, bf16[1024,128]{1,0:T(8,128)(2,1)S(1)}, u32[]{:S(2)}, u32[]{:S(2)}) collective-permute-start(bf16[1024,128]{1,0:T(8,128)(2,1)S(1)} %pad_maximum_fusion.1.refs_0_), channel_id=1, source_target_pairs={{0,1},{1,0},{2,3},{3,2},{4,5},{5,4},{6,7},{7,6},{8,9},{9,8},{10,11... | collective-permute-start | bytes 786440 | tf_op jit(solution)/shard_map/ppermute | solution.py:34
  55.5 7.3 %collective-permute-start.18 = (bf16[1024,128]{1,0:T(8,128)(2,1)S(1)}, bf16[1024,128]{1,0:T(8,128)(2,1)S(1)}, u32[]{:S(2)}, u32[]{:S(2)}) collective-permute-start(bf16[1024,128]{1,0:T(8,128)(2,1)S(1)} %pad_maximum_fusion.1.refs_0_), channel_id=1, source_target_pairs={{0,2},{1,3},{2,0},{3,1},{4,6},{5,7},{6,4},{7,5},{8,10},{9,11},{10,... | collective-permute-start | bytes 786440 | tf_op jit(solution)/shard_map/ppermute | solution.py:34
  60.8 5.0 %collective-permute-start.21 = (bf16[512,128]{1,0:T(8,128)(2,1)S(1)}, bf16[512,128]{1,0:T(8,128)(2,1)S(1)}, u32[]{:S(2)}, u32[]{:S(2)}) collective-permute-start(bf16[512,128]{1,0:T(8,128)(2,1)S(1)} %slice.86), channel_id=1, source_target_pairs={{0,2},{1,3},{2,0},{3,1},{4,6},{5,7},{6,4},{7,5},{8,10},{9,11},{10,... | collective-permute-start | bytes 393224 | tf_op jit(solution)/shard_map/ppermute | solution.py:34
  62.8 5.0 %collective-permute-start.22 = (bf16[512,128]{1,0:T(8,128)(2,1)S(1)}, bf16[512,128]{1,0:T(8,128)(2,1)S(1)}, u32[]{:S(2)}, u32[]{:S(2)}) collective-permute-start(bf16[512,128]{1,0:T(8,128)(2,1)S(1)} %slice.87), channel_id=1, source_target_pairs={{0,1},{1,0},{2,3},{3,2},{4,5},{5,4},{6,7},{7,6},{8,9},{9,8},{10,11... | collective-permute-start | bytes 393224 | tf_op jit(solution)/shard_map/ppermute | solution.py:34
  63.2 4.8 %collective-permute-start.24 = (bf16[1024,128]{1,0:T(8,128)(2,1)S(1)}, bf16[1024,128]{1,0:T(8,128)(2,1)S(1)}, u32[]{:S(2)}, u32[]{:S(2)}) collective-permute-start(bf16[1024,128]{1,0:T(8,128)(2,1)S(1)} %pad_maximum_fusion.1.refs_0_), channel_id=1, source_target_pairs={{0,16},{16,0},{1,17},{17,1},{2,18},{18,2},{3,19},{19,3},{4,20},{20... | collective-permute-start | bytes 786440 | tf_op jit(solution)/shard_map/ppermute | solution.py:42
  63.2 4.8 %collective-permute-start.25 = (bf16[1024,128]{1,0:T(8,128)(2,1)S(1)}, bf16[1024,128]{1,0:T(8,128)(2,1)S(1)}, u32[]{:S(2)}, u32[]{:S(2)}) collective-permute-start(bf16[1024,128]{1,0:T(8,128)(2,1)S(1)} %collective-permute-done.20.refs_2_), channel_id=1, source_target_pairs={{0,16},{16,0},{1,17},{17,1},{2,18},{18,2},{3,19},{19,3},{4,20},{20... | collective-permute-start | bytes 786440 | tf_op jit(solution)/shard_map/ppermute | solution.py:42
  63.7 5.6 %collective-permute-start.19 = (bf16[1024,128]{1,0:T(8,128)(2,1)S(1)}, bf16[1024,128]{1,0:T(8,128)(2,1)S(1)}, u32[]{:S(2)}, u32[]{:S(2)}) collective-permute-start(bf16[1024,128]{1,0:T(8,128)(2,1)S(1)} %collective-permute-done.18.refs_0_), channel_id=1, source_target_pairs={{0,16},{16,0},{1,17},{17,1},{2,18},{18,2},{3,19},{19,3},{4,20},{20... | collective-permute-start | bytes 786440 | tf_op jit(solution)/shard_map/ppermute | solution.py:42
  67.9 1.6 %collective-permute-start.23 = (bf16[1024,128]{1,0:T(8,128)(2,1)S(1)}, bf16[1024,128]{1,0:T(8,128)(2,1)S(1)}, u32[]{:S(2)}, u32[]{:S(2)}) collective-permute-start(bf16[1024,128]{1,0:T(8,128)(2,1)S(1)} %constant_dynamic-update-slice_fusion.refs_2_), channel_id=1, source_target_pairs={{0,16},{16,0},{1,17},{17,1},{2,18},{18,2},{3,19},{19,3},{4,20},{20... | collective-permute-start | bytes 786440 | tf_op jit(solution)/shard_map/ppermute | solution.py:42
  72.2 2.0 %collective-permute-start.27 = (bf16[256,1024]{1,0:T(8,128)(2,1)S(1)}, bf16[256,1024]{1,0:T(8,128)(2,1)S(1)}, u32[]{:S(2)}, u32[]{:S(2)}) collective-permute-start(bf16[256,1024]{1,0:T(8,128)(2,1)S(1)} %get-tuple-element.64), channel_id=1, source_target_pairs={{0,16},{16,0},{1,17},{17,1},{2,18},{18,2},{3,19},{19,3},{4,20},{20... | collective-permute-start | bytes 1572872 | tf_op jit(solution)/shard_map/ppermute | solution.py:42
  72.6 3.3 %collective-permute-start.26 = (bf16[256,1024]{1,0:T(8,128)(2,1)S(1)}, bf16[256,1024]{1,0:T(8,128)(2,1)S(1)}, u32[]{:S(2)}, u32[]{:S(2)}) collective-permute-start(bf16[256,1024]{1,0:T(8,128)(2,1)S(1)} %get-tuple-element.62), channel_id=1, source_target_pairs={{0,16},{16,0},{1,17},{17,1},{2,18},{18,2},{3,19},{19,3},{4,20},{20... | collective-permute-start | bytes 1572872 | tf_op jit(solution)/shard_map/ppermute | solution.py:42
  74.5 8.6 %collective-permute-start.28 = (bf16[128,1024]{1,0:T(8,128)(2,1)S(1)}, bf16[128,1024]{1,0:T(8,128)(2,1)S(1)}, u32[]{:S(2)}, u32[]{:S(2)}) collective-permute-start(bf16[128,1024]{1,0:T(8,128)(2,1)S(1)} %get-tuple-element.68), channel_id=1, source_target_pairs={{0,1},{1,0},{2,3},{3,2},{4,5},{5,4},{6,7},{7,6},{8,9},{9,8},{10,11... | collective-permute-start | bytes 786440 | tf_op jit(solution)/shard_map/ppermute | solution.py:34
  74.8 8.3 %collective-permute-start.30 = (bf16[128,1024]{1,0:T(8,128)(2,1)S(1)}, bf16[128,1024]{1,0:T(8,128)(2,1)S(1)}, u32[]{:S(2)}, u32[]{:S(2)}) collective-permute-start(bf16[128,1024]{1,0:T(8,128)(2,1)S(1)} %get-tuple-element.67), channel_id=1, source_target_pairs={{0,2},{1,3},{2,0},{3,1},{4,6},{5,7},{6,4},{7,5},{8,10},{9,11},{10,... | collective-permute-start | bytes 786440 | tf_op jit(solution)/shard_map/ppermute | solution.py:34
  83.4 5.0 %collective-permute-start.31 = (bf16[64,1024]{1,0:T(8,128)(2,1)S(1)}, bf16[64,1024]{1,0:T(8,128)(2,1)S(1)}, u32[]{:S(2)}, u32[]{:S(2)}) collective-permute-start(bf16[64,1024]{1,0:T(8,128)(2,1)S(1)} %slice.123), channel_id=1, source_target_pairs={{0,1},{1,0},{2,3},{3,2},{4,5},{5,4},{6,7},{7,6},{8,9},{9,8},{10,11... | collective-permute-start | bytes 393224 | tf_op jit(solution)/shard_map/ppermute | solution.py:34
  85.1 5.0 %collective-permute-start.29 = (bf16[64,1024]{1,0:T(8,128)(2,1)S(1)}, bf16[64,1024]{1,0:T(8,128)(2,1)S(1)}, u32[]{:S(2)}, u32[]{:S(2)}) collective-permute-start(bf16[64,1024]{1,0:T(8,128)(2,1)S(1)} %slice.124), channel_id=1, source_target_pairs={{0,2},{1,3},{2,0},{3,1},{4,6},{5,7},{6,4},{7,5},{8,10},{9,11},{10,... | collective-permute-start | bytes 393224 | tf_op jit(solution)/shard_map/ppermute | solution.py:34
  90.2 6.6 %collective-permute-start.32 = (bf16[16,2048]{1,0:T(8,128)(2,1)S(1)}, bf16[16,2048]{1,0:T(8,128)(2,1)S(1)}, u32[]{:S(2)}, u32[]{:S(2)}) collective-permute-start(bf16[16,2048]{1,0:T(8,128)(2,1)S(1)} %get-tuple-element.71), channel_id=1, source_target_pairs={{0,8},{1,9},{2,10},{3,11},{4,12},{5,13},{6,14},{7,15},{8,0},{9,1},... | collective-permute-start | bytes 196616 | tf_op jit(solution)/shard_map/ppermute | solution.py:34
  92.4 6.1 %collective-permute-start.33 = (bf16[16,2048]{1,0:T(8,128)(2,1)S(1)}, bf16[16,2048]{1,0:T(8,128)(2,1)S(1)}, u32[]{:S(2)}, u32[]{:S(2)}) collective-permute-start(bf16[16,2048]{1,0:T(8,128)(2,1)S(1)} %get-tuple-element.73), channel_id=1, source_target_pairs={{0,12},{1,13},{2,14},{3,15},{4,8},{5,9},{6,10},{7,11},{8,4},{9,5},... | collective-permute-start | bytes 196616 | tf_op jit(solution)/shard_map/ppermute | solution.py:34
  94.2 4.9 %collective-permute-start.34 = (bf16[16,2048]{1,0:T(8,128)(2,1)S(1)}, bf16[16,2048]{1,0:T(8,128)(2,1)S(1)}, u32[]{:S(2)}, u32[]{:S(2)}) collective-permute-start(bf16[16,2048]{1,0:T(8,128)(2,1)S(1)} %get-tuple-element.72), channel_id=1, source_target_pairs={{0,4},{1,5},{2,6},{3,7},{4,0},{5,1},{6,2},{7,3},{8,12},{9,13},{10,... | collective-permute-start | bytes 196616 | tf_op jit(solution)/shard_map/ppermute | solution.py:34
  99.2 1.3 %collective-permute-start.35 = (bf16[16,2048]{1,0:T(8,128)(2,1)S(1)}, bf16[16,2048]{1,0:T(8,128)(2,1)S(1)}, u32[]{:S(2)}, u32[]{:S(2)}) collective-permute-start(bf16[16,2048]{1,0:T(8,128)(2,1)S(1)} %fusion.6), channel_id=1, source_target_pairs={{0,16},{16,0},{1,17},{17,1},{2,18},{18,2},{3,19},{19,3},{4,20},{20... | collective-permute-start | bytes 196616 | tf_op jit(solution)/shard_map/ppermute | solution.py:42
